TPU v7x, 32 devices: a whole 2x2x4 slice. The times are simulated.
32 devices in a mesh: dp: 8 (over z, core), tensor: 4 (over y, x).
Axes of the slice: x: 2, y: 2, z: 4, core: 2. Of those that a mesh axis runs over, the one named last changes fastest.
Arguments:
- tokens: bfloat16 [8192, 2048], P('dp'), may hold values from -6 to 6
- lengths: int32 [64], P('dp'), may hold values from 1 to 64, 2560 in all
- cotangent: bfloat16 [8192, 2048], P('dp'), may hold values from -6 to 6
- pre_gain: float32 [2048], replicated, may hold values from 0.5 to 1.5
- pre_shift: float32 [2048], replicated, may hold values from -1.5 to 1.5
- qkv_weight: bfloat16 [3, 2048, 2048], P(None, None, 'tensor'), may hold values from -0.125 to 0.125
- qkv_bias: float32 [3, 2048], P(None, 'tensor'), may hold values from -1.5 to 1.5
- mix_gain: float32 [2048], P('tensor'), may hold values from 0.5 to 1.5
- mix_shift: float32 [2048], P('tensor'), may hold values from -1.5 to 1.5
- out_weight: bfloat16 [2048, 2048], P('tensor'), may hold values from -0.125 to 0.125
- out_bias: float32 [2048], replicated, may hold values from -1.5 to 1.5
- ffn_gain: float32 [2048], replicated, may hold values from 0.5 to 1.5
- ffn_shift: float32 [2048], replicated, may hold values from -1.5 to 1.5
- up_weight: bfloat16 [2048, 8192], P(None, 'tensor'), may hold values from -0.125 to 0.125
- up_bias: float32 [8192], P('tensor'), may hold values from -2.5 to 2.5
- hid_gain: float32 [8192], P('tensor'), may hold values from 0.5 to 1.5
- hid_shift: float32 [8192], P('tensor'), may hold values from -1.5 to 1.5
- down_weight: bfloat16 [8192, 2048], P('tensor'), may hold values from -0.0625 to 0.0625
- down_bias: float32 [2048], replicated, may hold values from -1.5 to 1.5
Outputs:
- output: bfloat16 [8192, 2048], P('dp')
- tokens_grad: float32 [8192, 2048], P('dp')
- pre_gain_grad: float32 [2048], replicated
- pre_shift_grad: float32 [2048], replicated
- qkv_weight_grad: float32 [3, 2048, 2048], P(None, 'dp', 'tensor')
- qkv_bias_grad: float32 [3, 2048], P(None, 'tensor')
- mix_gain_grad: float32 [2048], P('tensor')
- mix_shift_grad: float32 [2048], P('tensor')
- out_weight_grad: float32 [2048, 2048], P('tensor', 'dp')
- out_bias_grad: float32 [2048], replicated
- ffn_gain_grad: float32 [2048], replicated
- ffn_shift_grad: float32 [2048], replicated
- up_weight_grad: float32 [2048, 8192], P('dp', 'tensor')
- up_bias_grad: float32 [8192], P('tensor')
- hid_gain_grad: float32 [8192], P('tensor')
- hid_shift_grad: float32 [8192], P('tensor')
- down_weight_grad: float32 [8192, 2048], P('tensor', 'dp')
- down_bias_grad: float32 [2048], replicated
Inputs may be any that keep to these rules, and one draw needn't show every extreme that they name: Caption length of each pair; the lengths sum to 2560 and the longest is 64.
All inputs are finite; a program needn't handle non-finite values. No bound on the sum of `lengths` on one device may be relied on, other than what follows from the above.
Results may differ from a plain program's by a relative error of at most 0.013.
Values sent between devices are 32-bit elements; how exact they have to be, the bound alone decides.
No kernel may reach another device: no remote copies, remote signals or barrier semaphores. Data moves between devices by JAX's collectives and lax.ppermute only.
A program may use at most 256 MiB of HBM per device.

v0:
```python
import math

import jax
import jax.numpy as jnp
from jax import lax
from jax.sharding import PartitionSpec as P

D = 2048
HD = 64
FF = 8192
SLOT = 128
IMG = 64
SCALE_BASE = 512


eps = 1e-05
root_half = 0.7071067811865476
inv_root_two_pi = 0.3989422804014327
masked_score = -1e30


def rounded(value):
    return value.astype(jnp.bfloat16)


def tables():
    place = jnp.arange(SLOT, dtype=jnp.float32)
    index = jnp.arange(HD // 2, dtype=jnp.float32)
    theta = 10000.0 ** (-2.0 * index / HD)
    angle = place[:, None] * theta[None, :]
    zeta = (2.0 * index + 0.4 * HD) / (1.4 * HD)
    growth = zeta[None, :] ** ((place[:, None] - SLOT // 2) / SCALE_BASE)
    return (jnp.cos(angle), jnp.sin(angle), growth)


def rotate(value, cosine, sine, factor):
    shape = value.shape
    pairs = value.reshape(shape[:-1] + (shape[-1] // 2, 2))
    even = pairs[..., 0]
    odd = pairs[..., 1]
    cos_b = cosine[:, None, :]
    sin_b = sine[:, None, :]
    fac_b = factor[:, None, :]
    new_even = (even * cos_b - odd * sin_b) * fac_b
    new_odd = (odd * cos_b + even * sin_b) * fac_b
    return jnp.stack([new_even, new_odd], axis=-1).reshape(shape)


def local_norm(value):
    mean = jnp.mean(value, axis=-1, keepdims=True)
    var = jnp.mean(value * value, axis=-1, keepdims=True) - mean * mean
    inverse = lax.rsqrt(var + eps)
    return ((value - mean) * inverse, inverse)


def local_back(grad, hat, gain, inverse):
    scaled = grad * gain
    return inverse * (
        scaled
        - jnp.mean(scaled, axis=-1, keepdims=True)
        - hat * jnp.mean(scaled * hat, axis=-1, keepdims=True)
    )


def body(
    tokens,
    lengths,
    cotangent,
    pre_gain,
    pre_shift,
    qkv_weight,
    qkv_bias,
    mix_gain,
    mix_shift,
    out_weight,
    out_bias,
    ffn_gain,
    ffn_shift,
    up_weight,
    up_bias,
    hid_gain,
    hid_shift,
    down_weight,
    down_bias,
):
    pairs = lengths.shape[0]
    rows = tokens.shape[0]
    local_width = qkv_weight.shape[2]
    local_heads = local_width // HD
    scale = 1.0 / math.sqrt(HD)
    cosine, sine, growth = tables()
    shrink = 1.0 / growth
    place = jnp.arange(SLOT, dtype=jnp.int32)
    causal = (place[None, :] <= place[:, None])[None, None]
    valid = place[None, None, None, :] < (IMG + lengths)[:, None, None, None]
    allowed = causal & valid
    inputs = tokens.astype(jnp.float32)
    pre_hat, pre_inv = local_norm(inputs)
    first = rounded(pre_hat * pre_gain + pre_shift)
    proj = (
        jnp.einsum("td,cde->cte", first, qkv_weight, preferred_element_type=jnp.float32)
        + qkv_bias[:, None, :]
    )
    shaped = proj.reshape(3, pairs, SLOT, local_heads, HD)
    query = rounded(rotate(shaped[0], cosine, sine, growth))
    key = rounded(rotate(shaped[1], cosine, sine, shrink))
    value = rounded(shaped[2])

    def scores_of():
        raw = jnp.einsum("pqhd,pkhd->phqk", query, key, preferred_element_type=jnp.float32) * scale
        return jnp.where(allowed, raw, masked_score)

    scores = scores_of()
    top = jnp.max(scores, axis=-1, keepdims=True)
    expd = jnp.exp(scores - top)
    total = jnp.sum(expd, axis=-1, keepdims=True)
    probs = expd / total
    log_total = top + jnp.log(total)
    mixed = jnp.einsum(
        "phqk,pkhd->pqhd", rounded(probs), value, preferred_element_type=jnp.float32
    ).reshape(rows, local_width)
    mix_sums = lax.psum((jnp.sum(mixed, 1), jnp.sum(mixed * mixed, 1)), "tensor")
    mix_mean = mix_sums[0] / D
    mix_inv = lax.rsqrt(mix_sums[1] / D - mix_mean * mix_mean + eps)
    mix_hat = (mixed - mix_mean[:, None]) * mix_inv[:, None]
    mix_low = rounded(mix_hat * mix_gain + mix_shift)
    branch = lax.psum(jnp.dot(mix_low, out_weight, preferred_element_type=jnp.float32), "tensor")
    middle = inputs + branch + out_bias
    ffn_hat, ffn_inv = local_norm(middle)
    second = rounded(ffn_hat * ffn_gain + ffn_shift)
    hidden = jnp.dot(second, up_weight, preferred_element_type=jnp.float32) + up_bias
    active = jax.nn.gelu(hidden, approximate=False)
    hid_sums = lax.psum((jnp.sum(active, 1), jnp.sum(active * active, 1)), "tensor")
    hid_mean = hid_sums[0] / FF
    hid_inv = lax.rsqrt(hid_sums[1] / FF - hid_mean * hid_mean + eps)
    hid_hat = (active - hid_mean[:, None]) * hid_inv[:, None]
    hid_low = rounded(hid_hat * hid_gain + hid_shift)
    result = lax.psum(jnp.dot(hid_low, down_weight, preferred_element_type=jnp.float32), "tensor")
    final = middle + result + down_bias
    output = rounded(final)
    upstream = cotangent.astype(jnp.float32)
    down_grad = jnp.einsum("tf,td->fd", hid_low, cotangent, preferred_element_type=jnp.float32)
    down_bias_grad = jnp.sum(upstream, 0)
    hid_back = jnp.einsum("td,fd->tf", cotangent, down_weight, preferred_element_type=jnp.float32)
    hid_gain_grad = jnp.sum(hid_back * hid_hat, 0)
    hid_shift_grad = jnp.sum(hid_back, 0)
    hid_scaled = hid_back * hid_gain
    hid_back_sums = lax.psum((jnp.sum(hid_scaled, 1), jnp.sum(hid_scaled * hid_hat, 1)), "tensor")
    active_grad = hid_inv[:, None] * (
        hid_scaled - hid_back_sums[0][:, None] / FF - hid_hat * hid_back_sums[1][:, None] / FF
    )
    slope = 0.5 * (1.0 + lax.erf(hidden * root_half)) + hidden * inv_root_two_pi * jnp.exp(
        -0.5 * hidden * hidden
    )
    hidden_grad = rounded(active_grad * slope)
    up_grad = jnp.einsum("td,tf->df", second, hidden_grad, preferred_element_type=jnp.float32)
    up_bias_grad = jnp.sum(hidden_grad, 0, dtype=jnp.float32)
    second_grad = lax.psum(
        jnp.einsum("tf,df->td", hidden_grad, up_weight, preferred_element_type=jnp.float32),
        "tensor",
    )
    ffn_gain_grad = jnp.sum(second_grad * ffn_hat, 0)
    ffn_shift_grad = jnp.sum(second_grad, 0)
    middle_grad = upstream + local_back(second_grad, ffn_hat, ffn_gain, ffn_inv)
    branch_low = rounded(middle_grad)
    out_bias_grad = jnp.sum(middle_grad, 0)
    out_grad = jnp.einsum("te,td->ed", mix_low, branch_low, preferred_element_type=jnp.float32)
    mix_back = jnp.einsum("td,ed->te", branch_low, out_weight, preferred_element_type=jnp.float32)
    mix_gain_grad = jnp.sum(mix_back * mix_hat, 0)
    mix_shift_grad = jnp.sum(mix_back, 0)
    mix_scaled = mix_back * mix_gain
    mix_back_sums = lax.psum((jnp.sum(mix_scaled, 1), jnp.sum(mix_scaled * mix_hat, 1)), "tensor")
    mixed_grad = mix_inv[:, None] * (
        mix_scaled - mix_back_sums[0][:, None] / D - mix_hat * mix_back_sums[1][:, None] / D
    )
    mixed_grad = rounded(mixed_grad).reshape(pairs, SLOT, local_heads, HD)
    again = jnp.exp(scores_of() - log_total)
    prob_grad = jnp.einsum("pqhd,pkhd->phqk", mixed_grad, value, preferred_element_type=jnp.float32)
    carried = jnp.sum(again * prob_grad, axis=-1, keepdims=True)
    score_grad = rounded(again * (prob_grad - carried))
    query_grad = (
        jnp.einsum("phqk,pkhd->pqhd", score_grad, key, preferred_element_type=jnp.float32) * scale
    )
    key_grad = (
        jnp.einsum("phqk,pqhd->pkhd", score_grad, query, preferred_element_type=jnp.float32) * scale
    )
    value_grad = jnp.einsum(
        "phqk,pqhd->pkhd", rounded(again), mixed_grad, preferred_element_type=jnp.float32
    )
    query_pre = rotate(query_grad, cosine, -sine, growth)
    key_pre = rotate(key_grad, cosine, -sine, shrink)
    proj_grad = rounded(jnp.stack([query_pre, key_pre, value_grad]).reshape(3, rows, local_width))
    qkv_grad = jnp.einsum("td,cte->cde", first, proj_grad, preferred_element_type=jnp.float32)
    qkv_bias_grad = jnp.sum(proj_grad, 1, dtype=jnp.float32)
    first_grad = lax.psum(
        jnp.einsum("cte,cde->td", proj_grad, qkv_weight, preferred_element_type=jnp.float32),
        "tensor",
    )
    pre_gain_grad = jnp.sum(first_grad * pre_hat, 0)
    pre_shift_grad = jnp.sum(first_grad, 0)
    tokens_grad = middle_grad + local_back(first_grad, pre_hat, pre_gain, pre_inv)
    qkv_part, out_part, up_part, down_part = (
        lax.psum_scatter(qkv_grad, "dp", scatter_dimension=1, tiled=True),
        lax.psum_scatter(out_grad, "dp", scatter_dimension=1, tiled=True),
        lax.psum_scatter(up_grad, "dp", scatter_dimension=0, tiled=True),
        lax.psum_scatter(down_grad, "dp", scatter_dimension=1, tiled=True),
    )
    small = lax.psum(
        (
            pre_gain_grad,
            pre_shift_grad,
            qkv_bias_grad,
            mix_gain_grad,
            mix_shift_grad,
            out_bias_grad,
            ffn_gain_grad,
            ffn_shift_grad,
            up_bias_grad,
            hid_gain_grad,
            hid_shift_grad,
            down_bias_grad,
        ),
        "dp",
    )
    return (
        output,
        tokens_grad,
        small[0],
        small[1],
        qkv_part,
        small[2],
        small[3],
        small[4],
        out_part,
        small[5],
        small[6],
        small[7],
        up_part,
        small[8],
        small[9],
        small[10],
        down_part,
        small[11],
    )


def solution(mesh):
    in_specs = (
        P("dp", None),
        P("dp"),
        P("dp", None),
        P(),
        P(),
        P(None, None, "tensor"),
        P(None, "tensor"),
        P("tensor"),
        P("tensor"),
        P("tensor", None),
        P(),
        P(),
        P(),
        P(None, "tensor"),
        P("tensor"),
        P("tensor"),
        P("tensor"),
        P("tensor", None),
        P(),
    )
    out_specs = (
        P("dp", None),
        P("dp", None),
        P(),
        P(),
        P(None, "dp", "tensor"),
        P(None, "tensor"),
        P("tensor"),
        P("tensor"),
        P("tensor", "dp"),
        P(),
        P(),
        P(),
        P("dp", "tensor"),
        P("tensor"),
        P("tensor"),
        P("tensor"),
        P("tensor", "dp"),
        P(),
    )
    return jax.shard_map(body, mesh=mesh, in_specs=in_specs, out_specs=out_specs, check_vma=False)
```

profile of v0, /device:TPU:0, one launch (start us, length us, event | category | flops | bytes accessed | tf_op | source)
XLA Modules:
  0.0 1522.8 jit_solution(11128239787350795962)
XLA Ops:
  10.9 11.5 add_bitcast_fusion
  65.7 11.5 all-reduce.4
  84.8 171.5 %all-reduce.11.cloned.1.call-done = f32[1024,2048]{1,0:T(8,128)} async-done(((f32[1024,2048]{1,0:T(8,128)}), f32[1024,2048]{1,0:T(8,128)}) %all-reduce.11.cloned.1.call-update) | async-done | bytes 8388624 | tf_op jit(solution)/shard_map/psum | solution.py:127
  262.0 36.0 %fusion.57 = (f32[1024]{0:T(1024)S(1)}, f32[1024]{0:T(1024)S(1)}, f32[1024,2048]{1,0:T(8,128)}, f32[1024,2048]{1,0:T(8,128)}) fusion(f32[2048]{0:T(1024)S(1)} %copy-done.37, bf16[2048,2048]{1,0:T(8,128)(2,1)} %param.32, f32[1024,2048]{1,0:T(8,128)S(1)} %get-tuple-element.105, f32[2048]{0:T(1024)S(1)} %copy-done.44, f32[2048]{0:T(1024)S(1)} %copy-done.30, ...), kind=kOutput, calls=%fused_computation.139 | convolution fusion | flops 8743024640 | bytes 33595392 | tf_op jit(solution)/shard_map/dot_general | solution.py:131
  298.0 9.8 all-reduce.3
  307.8 17.3 %multiply_reduce_fusion = (f32[2048]{0:T(1024)}, f32[1024]{0:T(1024)S(1)}, f32[1024]{0:T(1024)S(1)}, f32[2048]{0:T(1024)}, f32[1024,2048]{1,0:T(8,128)}) fusion(f32[1024,2048]{1,0:T(8,128)} %get-tuple-element.104, f32[1024]{0:T(1024)S(1)} %get-tuple-element.126, f32[1024]{0:T(1024)S(1)} %get-tuple-element.125, f32[2048]{0:T(1024)S(1)} %copy-done.38, ...), kind=kOutput, calls=%fused_computation.29 | convolution fusion | flops 8608802816 | bytes 29401088 | tf_op jit(solution)/shard_map/td,fd->tf/dot_general | solution.py:144
  333.3 12.3 convert_reduce_fusion.2
  347.6 13.2 fusion.68
  361.5 15.9 %fusion.56 = f32[1024,2048]{1,0:T(8,128)} fusion(bf16[2048,2048]{1,0:T(8,128)(2,1)} %param.36, f32[1024,2048]{1,0:T(8,128)} %get-tuple-element.104, f32[2048]{0:T(1024)S(1)} %copy-done.43, f32[2048]{0:T(1024)S(1)} %copy-done.38, f32[1024]{0:T(1024)S(1)} %get-tuple-element.126, f32[1024]{0:T(1024)S(1)} %get-tuple-element.125), kind=kOutput, calls=%fused_computation.138 | convolution fusion | flops 8600420352 | bytes 25190400 | tf_op jit(solution)/shard_map/dot_general | solution.py:138
  377.4 155.8 %all-reduce.13.cloned.1.call-done = f32[1024,2048]{1,0:T(8,128)} async-done(((f32[1024,2048]{1,0:T(8,128)}), f32[1024,2048]{1,0:T(8,128)}) %all-reduce.13.cloned.1.call-update) | async-done | bytes 8388624 | tf_op jit(solution)/shard_map/psum | solution.py:158
  533.2 8.3 multiply_reduce_fusion.1
  554.9 9.8 all-reduce.1
  597.9 11.4 convolution_bitcast_fusion.1
  610.8 12.5 convolution_bitcast_fusion
  636.0 281.0 %all-reduce.17.cloned.1.call-done = (f32[1024,2048]{1,0:T(8,128)}, f32[1024,2048]{1,0:T(8,128)}) async-done(((f32[1024,2048]{1,0:T(8,128)}, f32[1024,2048]{1,0:T(8,128)}), (f32[1024,2048]{1,0:T(8,128)}, f32[1024,2048]{1,0:T(8,128)})) %all-reduce.17.cloned.1.call-update) | async-done | bytes 16777232 | tf_op jit(solution)/shard_map/psum | solution.py:138
  924.3 17.5 %fusion.55 = f32[2048,2048]{1,0:T(8,128)} fusion(bf16[1024,2048]{1,0:T(8,128)(2,1)} %param.21, f32[1024,2048]{1,0:T(8,128)} %get-tuple-element.104, f32[2048]{0:T(1024)S(1)} %copy-done.43, f32[2048]{0:T(1024)S(1)} %copy-done.38, f32[1024]{0:T(1024)S(1)} %get-tuple-element.126, f32[1024]{0:T(1024)S(1)} %get-tuple-element.125), kind=kOutput, calls=%fused_computation.137 | convolution fusion | flops 8600420352 | bytes 29384704 | tf_op jit(solution)/shard_map/tf,td->fd/dot_general | solution.py:142
  942.4 16.4 %fusion.53 = f32[2048,2048]{1,0:T(8,128)} fusion(bf16[1024,2048]{1,0:T(8,128)(2,1)} %copy-done.14, f32[1024,2048]{1,0:T(8,128)} %copy-done.2, f32[2048]{0:T(1024)S(1)} %copy-done.45, f32[2048]{0:T(1024)S(1)} %copy-done.30, f32[1024]{0:T(1024)S(1)} %get-tuple-element.128, f32[1024]{0:T(1024)S(1)} %get-tuple-element.127), kind=kOutput, calls=%fused_computation.135 | convolution fusion | flops 8600420352 | bytes 29384704 | tf_op jit(solution)/shard_map/td,tf->df/dot_general | solution.py:156
  959.6 10.4 add_convert_fusion
  969.9 9.8 fusion.17
  979.7 69.9 %reduce-scatter.5.cloned.1.call-done = f32[3,256,512]{1,2,0:T(8,128)} async-done(((f32[3,2048,512]{1,2,0:T(8,128)}), f32[3,256,512]{1,2,0:T(8,128)}) %reduce-scatter.5.cloned.1.call-update) | async-done | bytes 1572880 | tf_op jit(solution)/shard_map/reduce_scatter | solution.py:203
  1052.6 48.2 %reduce-scatter.7.cloned.1.call-done = f32[512,256]{1,0:T(8,128)} async-done(((f32[512,2048]{1,0:T(8,128)}), f32[512,256]{1,0:T(8,128)}) %reduce-scatter.7.cloned.1.call-update) | async-done | bytes 524304 | tf_op jit(solution)/shard_map/reduce_scatter | solution.py:204
  1100.8 56.3 %all-reduce.15.cloned.1.call-done = (f32[2048]{0:T(1024)}, f32[2048]{0:T(1024)}, f32[3,512]{1,0:T(4,128)}, f32[512]{0:T(512)}, f32[512]{0:T(512)}, /*index=5*/f3...) async-done(((f32[2048]{0:T(1024)}, f32[2048]{0:T(1024)}, f32[3,512]{1,0:T(4,128)}, ...) | async-done | bytes 83984 | tf_op jit(solution)/shard_map/psum | solution.py:208
  1157.2 173.4 %reduce-scatter.11.cloned.1.call-done = f32[2048,256]{1,0:T(8,128)} async-done(((f32[2048,2048]{1,0:T(8,128)}), f32[2048,256]{1,0:T(8,128)}) %reduce-scatter.11.cloned.1.call-update) | async-done | bytes 2097168 | tf_op jit(solution)/shard_map/reduce_scatter | solution.py:206
  1330.5 169.6 %reduce-scatter.9.cloned.1.call-done = f32[256,2048]{1,0:T(8,128)} async-done(((f32[2048,2048]{1,0:T(8,128)}), f32[256,2048]{1,0:T(8,128)}) %reduce-scatter.9.cloned.1.call-update) | async-done | bytes 2097168 | tf_op jit(solution)/shard_map/reduce_scatter | solution.py:205
  (193 shorter events, 158.3 us)
Async XLA Ops:
  7.2 70.1 %copy-start = (bf16[512,2048]{1,0:T(8,128)(2,1)S(1)}, bf16[512,2048]{1,0:T(8,128)(2,1)}, u32[]{:S(2)}) copy-start(bf16[512,2048]{1,0:T(8,128)(2,1)} %param.28) | copy-start | bytes 6291460
  7.2 249.1 %all-reduce.11.cloned.1.call-start = ((), (), s32[]{:S(2)}) async-start(), calls=%async_computation.4 | async-start | bytes 16777216 | tf_op jit(solution)/shard_map/psum | solution.py:127
  10.9 11.6 copy-start.26
  10.9 11.6 copy-start.28
  41.7 12.0 copy-start.8
  57.1 20.2 %copy-start.40 = (f32[512]{0:T(512)S(1)}, f32[512]{0:T(512)}, u32[]{:S(2)}) copy-start(f32[512]{0:T(512)} %param.26) | copy-start | bytes 6148
  57.1 20.2 %copy-start.46 = (f32[512]{0:T(512)S(1)}, f32[512]{0:T(512)}, u32[]{:S(2)}) copy-start(f32[512]{0:T(512)} %param.27) | copy-start | bytes 6148
  77.3 179.1 %copy-start.36 = (f32[2048]{0:T(1024)S(1)}, f32[2048]{0:T(1024)}, u32[]{:S(2)}) copy-start(f32[2048]{0:T(1024)} %param.29) | copy-start | bytes 24580
  84.8 177.2 %copy-start.30 = (f32[2048]{0:T(1024)S(1)}, f32[2048]{0:T(1024)}, u32[]{:S(2)}) copy-start(f32[2048]{0:T(1024)} %param.30) | copy-start | bytes 24580
  84.8 177.2 %copy-start.37 = (f32[2048]{0:T(1024)S(1)}, f32[2048]{0:T(1024)}, u32[]{:S(2)}) copy-start(f32[2048]{0:T(1024)} %param.33) | copy-start | bytes 24580
  84.8 177.2 %copy-start.44 = (f32[2048]{0:T(1024)S(1)}, f32[2048]{0:T(1024)}, u32[]{:S(2)}) copy-start(f32[2048]{0:T(1024)} %param.31) | copy-start | bytes 24580
  84.8 448.4 %all-reduce.13.cloned.1.call-start = ((), (), s32[]{:S(2)}) async-start(), calls=%async_computation.5 | async-start | bytes 16777216 | tf_op jit(solution)/shard_map/psum | solution.py:158
  261.9 36.0 %copy-start.2 = (f32[1024,2048]{1,0:T(8,128)}, f32[1024,2048]{1,0:T(8,128)S(1)}, u32[]{:S(2)}) copy-start(f32[1024,2048]{1,0:T(8,128)S(1)} %get-tuple-element.105) | copy-start | bytes 25165828
  262.0 45.8 %copy-start.38 = (f32[2048]{0:T(1024)S(1)}, f32[2048]{0:T(1024)}, u32[]{:S(2)}) copy-start(f32[2048]{0:T(1024)} %param.34) | copy-start | bytes 24580
  360.8 556.2 %all-reduce.17.cloned.1.call-start = ((), (), s32[]{:S(2)}) async-start(), calls=%async_computation.11 | async-start | bytes 33554432 | tf_op jit(solution)/shard_map/psum | solution.py:138
  533.2 9.4 copy-start.13
  584.9 10.5 copy-start.18
  609.3 440.3 %reduce-scatter.5.cloned.1.call-start = ((), (), s32[]{:S(2)}) async-start(), calls=%async_computation.6 | async-start | bytes 14155776 | tf_op jit(solution)/shard_map/reduce_scatter | solution.py:203
  623.3 477.5 %reduce-scatter.7.cloned.1.call-start = ((), (), s32[]{:S(2)}) async-start(), calls=%async_computation.7 | async-start | bytes 4718592 | tf_op jit(solution)/shard_map/reduce_scatter | solution.py:204
  633.2 524.0 %all-reduce.15.cloned.1.call-start = ((), (), s32[]{:S(2)}) async-start(), calls=%async_computation.10 | async-start | bytes 172032 | tf_op jit(solution)/shard_map/psum | solution.py:208
  924.2 406.3 %reduce-scatter.11.cloned.1.call-start = ((), (), s32[]{:S(2)}) async-start(), calls=%async_computation.9 | async-start | bytes 18874368 | tf_op jit(solution)/shard_map/reduce_scatter | solution.py:206
  941.8 558.3 %reduce-scatter.9.cloned.1.call-start = ((), (), s32[]{:S(2)}) async-start(), calls=%async_computation.8 | async-start | bytes 18874368 | tf_op jit(solution)/shard_map/reduce_scatter | solution.py:205
  959.6 10.4 copy-start.5
  969.9 545.5 %copy-start.1 = (bf16[512,2048]{1,0:T(8,128)(2,1)S(1)}, bf16[512,2048]{1,0:T(8,128)(2,1)}, u32[]{:S(2)}) copy-start(bf16[512,2048]{1,0:T(8,128)(2,1)} %param.28) | copy-start | bytes 6291460
  (33 other events, 147.8 us)
Sparse Core Ops, SparseCore 0:
  84.9 171.4 all-reduce.10
  361.0 172.1 all-reduce.12
  609.4 307.5 all-reduce.16
  919.3 130.2 reduce-scatter.4
  1052.4 48.3 reduce-scatter.6
  1106.2 50.9 all-reduce.14
  1160.1 170.4 reduce-scatter.10
  1333.5 166.5 reduce-scatter.8
where the time goes:
time: 1530 us; the launch traced here: 1520 us
  waiting for transfers between devices  1130 us (74%)
  matrix products  185 us (12%)
  other arithmetic  82.8 us (5%)
  local copies, waits for them, and re-layouts  73.6 us (5%)
  blocking collectives  39.2 us (3%)
  between operations  15.4 us (1%)
    psum x1, waiting for transfers between devices, body(): lax.psum(jnp.dot(hid_low, down_weight, preferred_element_type=jnp.float32...  281 us
    reduce_scatter x1, waiting for transfers between devices, body(): lax.psum_scatter(down_grad, 'dp', scatter_dimension=1, tiled=True)  173 us
    psum x1, waiting for transfers between devices, body(): lax.psum(jnp.dot(mix_low, out_weight, preferred_element_type=jnp.float32)...  172 us
    reduce_scatter x1, waiting for transfers between devices, body(): lax.psum_scatter(up_grad, 'dp', scatter_dimension=0, tiled=True)  170 us
    psum x1, waiting for transfers between devices, body(): lax.psum(jnp.einsum('tf,df->td', hidden_grad, up_weight, preferred_elemen...  156 us
    reduce_scatter x1, waiting for transfers between devices, body(): lax.psum_scatter(qkv_grad, 'dp', scatter_dimension=1, tiled=True)  69.9 us
    psum x1, waiting for transfers between devices, body(): lax.psum((pre_gain_grad, pre_shift_grad, qkv_bias_grad, mix_gain_grad, mi...  56.3 us
    reduce_scatter x1, waiting for transfers between devices, body(): lax.psum_scatter(out_grad, 'dp', scatter_dimension=1, tiled=True)  48.2 us
  transfers between devices with their start and end apart: 8, of which 8 were waited for; matrix products, arithmetic and copies ran while one was open for 7% of the time, Pallas kernels for 0%

commit v1 on v0

v1 whole, which is shorter than its diff:
```python
import functools
import math

import jax
import jax.numpy as jnp
import numpy as np
from jax import lax
from jax.experimental import pallas as pl
from jax.experimental.pallas import tpu as pltpu
from jax.sharding import PartitionSpec as P

D = 2048
HD = 64
FF = 8192
SLOT = 128
IMG = 64
SCALE_BASE = 512
HALF = D // 2

eps = 1e-05
root_half = 0.7071067811865476
inv_root_two_pi = 0.3989422804014327
masked_score = -1e30
MEGA = 1 << 20

F32 = jnp.float32
BF16 = jnp.bfloat16
NN = (((1,), (0,)), ((), ()))
NT = (((1,), (1,)), ((), ()))
TN = (((0,), (0,)), ((), ()))


def rounded(value):
    return value.astype(BF16)


def mul(left, right, dims=NN):
    return lax.dot_general(left, right, dims, preferred_element_type=F32)


def xpos_tables():
    place = np.arange(SLOT, dtype=np.float64)[:, None]
    lane = np.arange(128)[None, :]
    index = (lane % HD) // 2
    angle = place * 10000.0 ** (-2.0 * index / HD)
    zeta = (2.0 * index + 0.4 * HD) / (1.4 * HD)
    growth = zeta ** ((place - SLOT // 2) / SCALE_BASE)
    even = lane % 2 == 0
    found = []
    for factor in (growth / math.sqrt(HD), 1.0 / growth):
        found += [
            np.cos(angle) * factor,
            np.where(even, -np.sin(angle), 0.0) * factor,
            np.where(even, 0.0, np.sin(angle)) * factor,
        ]
    return jnp.asarray(np.tile(np.stack(found), (1, 2, 1)).astype(np.float32))


def rotate(value, tables, base, sign):
    up = pltpu.roll(value, 127, axis=1)
    down = pltpu.roll(value, 1, axis=1)
    turned = up * tables[base + 1] + down * tables[base + 2]
    return value * tables[base] + turned if sign > 0 else value * tables[base] - turned


def columns_of(parts):
    return jnp.transpose(parts)


def rows_of(columns):
    size = columns[0].shape[0]
    lane = lax.broadcasted_iota(jnp.int32, (size, 128), 1)
    tile = jnp.zeros((size, 128), F32)
    for at, column in enumerate(columns):
        tile = jnp.where(lane == at, column, tile)
    return jnp.transpose(tile)[:8]


def norm_parts(value):
    mean = jnp.mean(value, axis=-1, keepdims=True)
    var = jnp.mean(value * value, axis=-1, keepdims=True) - mean * mean
    inverse = lax.rsqrt(var + eps)
    return (value - mean) * inverse, inverse


def sum_rows(value):
    return jnp.sum(value, axis=0, keepdims=True)


def whole(array, **kw):
    rank = array.ndim
    return (array, array.shape, lambda *at: (0,) * rank)


def run(kernel, grid, ins, outs, scratch=(), prefetch=(), after=(), alias=None, limit=56, name=None):
    prefetch = tuple(prefetch)

    def body(*refs):
        refs = list(refs)
        first = len(prefetch) + len(ins)
        del refs[first : first + len(after)]
        kernel(*refs)

    in_specs = []
    for array, block, where in ins:
        if block is None:
            in_specs.append(pl.BlockSpec(memory_space=pl.ANY))
        elif tuple(block) == tuple(array.shape):
            in_specs.append(pl.BlockSpec(block, where, pipeline_mode=pl.Buffered(1)))
        else:
            in_specs.append(pl.BlockSpec(block, where))
    in_specs += [pl.BlockSpec(memory_space=pl.ANY)] * len(after)
    out_specs = [pl.BlockSpec(block, where) for shape, dtype, block, where in outs]
    out_shape = [jax.ShapeDtypeStruct(shape, dtype) for shape, dtype, block, where in outs]
    return pl.pallas_call(
        body,
        grid_spec=pltpu.PrefetchScalarGridSpec(
            num_scalar_prefetch=len(prefetch),
            grid=grid,
            in_specs=in_specs,
            out_specs=out_specs,
            scratch_shapes=list(scratch),
        ),
        out_shape=out_shape,
        input_output_aliases=alias or {},
        compiler_params=pltpu.CompilerParams(
            dimension_semantics=("arbitrary",) * len(grid), vmem_limit_bytes=limit * MEGA
        ),
        cost_estimate=pl.CostEstimate(flops=1000, bytes_accessed=1000, transcendentals=0),
        name=name,
    )(*prefetch, *[array for array, block, where in ins], *after)


def flip(value, bit, size):
    return lax.ppermute(value, "tensor", [(t, t ^ (1 << bit)) for t in range(size)])


def gather_pieces(own, bits, order):
    pieces = {0: own}
    for bit in order:
        for block in list(pieces):
            pieces[block | 1 << bit] = flip(pieces[block], bit, 1 << bits)
    return [pieces[block] for block in range(1 << bits)]


class Line:
    def __init__(self):
        self.last = None

    def tie(self, value):
        if self.last is None:
            return value
        return lax.optimization_barrier((value, self.last))[0]

    def mark(self, value):
        self.last = value


class Total:
    def __init__(self, line, parts, bits):
        self.line, self.bits = line, bits
        self.orders = [list(range(bits)), list(range(bits))[::-1]]
        self.left = [[bit for bit in range(bits) if bit != order[0]] for order in self.orders]
        self.keep = [parts[0], parts[2]]
        self.got = [flip(parts[1], self.orders[0][0], 1 << bits), flip(parts[3], self.orders[1][0], 1 << bits)]
        self.step = 1

    def advance(self):
        line, size = self.line, 1 << self.bits
        if self.step == self.bits:
            for half in range(2):
                self.keep[half] = line.tie(self.keep[half]) + self.got[half]
                line.mark(self.keep[half])
            return
        picks = []
        for half in range(2):
            left, bit = self.left[half], self.orders[half][self.step]
            keep, got = self.keep[half], self.got[half]
            cube = (2,) * len(left) + keep.shape[1:]
            axis = len(left) - 1 - left.index(bit)
            shape = (keep.shape[0] // 2,) + keep.shape[1:]
            pick = lambda value, at, cube=cube, axis=axis, shape=shape: lax.index_in_dim(
                value.reshape(cube), at, axis, keepdims=False
            ).reshape(shape)
            send = pick(line.tie(keep), 1) + pick(got, 1)
            line.mark(send)
            picks.append((pick, keep, got))
            self.got[half] = flip(send, bit, size)
            left.remove(bit)
        for half in range(2):
            pick, keep, got = picks[half]
            self.keep[half] = pick(line.tie(keep), 0) + pick(got, 0)
            line.mark(self.keep[half])
        self.step += 1

    def pieces(self):
        up, down = self.orders
        return gather_pieces(self.keep[0], self.bits, down), gather_pieces(self.keep[1], self.bits, up)


class Ring:
    def __init__(self, line, first, rest, size):
        self.line, self.rest, self.size = line, rest, size
        self.step = 0
        self.got = self.send(first)

    def send(self, value):
        return lax.ppermute(value, "dp", [(d, (d + 2) % self.size) for d in range(self.size)])

    def advance(self):
        value = self.line.tie(self.rest)[self.step] + self.got
        self.line.mark(value)
        self.step += 1
        if self.step < self.size // 2 - 1:
            self.got = self.send(value)
        return value


def butterfly(value, bits):
    for bit in range(bits):
        value = value + flip(value, bit, 1 << bits)
    return value


def tree_sum(value):
    while value.shape[0] > 1:
        value = value.reshape((value.shape[0] // 2, 2) + value.shape[1:])
        value = value[:, 0] + value[:, 1]
    return value[0]


def combine(pieces, block, blocks):
    level = [pieces[other][:, (block ^ other) * SLOT : (block ^ other) * SLOT + SLOT] for other in range(blocks)]
    while len(level) > 1:
        level = [level[at] + level[at + 1] for at in range(0, len(level), 2)]
    return level[0]


def attention_scores(query, both_keys, length):
    scores = mul(query, both_keys, NT)
    row = lax.broadcasted_iota(jnp.int32, scores.shape, 0)
    place = lax.broadcasted_iota(jnp.int32, scores.shape, 1) % SLOT
    scores = jnp.where((place <= row) & (place < IMG + length), scores, masked_score)
    parts = []
    for at in range(2):
        part = scores[:, at * SLOT : (at + 1) * SLOT]
        expd = jnp.exp(part - jnp.max(part, axis=-1, keepdims=True))
        parts.append(expd / jnp.sum(expd, axis=-1, keepdims=True))
    return parts


def split_heads(value, mask):
    return jnp.concatenate([value * mask[0:1], value * mask[1:2]], axis=0)


def store_parts(refs, value, step, steps, only=None):
    left_keep, left_send, right_keep, right_send = refs
    left_keep[0] = value[:SLOT, :HALF]
    left_send[0] = value[SLOT:, :HALF]

    @pl.when(step < steps // 2)
    def _():
        right_keep[0] = value[:SLOT, HALF:]
        right_keep[1] = value[SLOT:, HALF:]

    @pl.when(step >= steps // 2)
    def _():
        right_send[0] = value[:SLOT, HALF:]
        right_send[1] = value[SLOT:, HALF:]


def part_outs(blocks):
    half = blocks // 2
    steps = blocks // 2
    shape = (half, SLOT, HALF)
    low = max(steps // 2, 1)
    return [
        (shape, F32, (1, SLOT, HALF), lambda s, *_: (s, 0, 0)),
        (shape, F32, (1, SLOT, HALF), lambda s, *_: (s, 0, 0)),
        (shape, F32, (2, SLOT, HALF), lambda s, *_: (jnp.minimum(s, low - 1), 0, 0)),
        (shape, F32, (2, SLOT, HALF), lambda s, *_: (jnp.maximum(s - steps // 2, 0), 0, 0)),
    ]


def front(order, lengths, tokens, gain, shift, weight, bias, tables, mask, mix_gain, uw_rows, out_weight, after=()):
    blocks = order.shape[0]
    steps = blocks // 2
    width = weight.shape[2]
    groups = width // 128
    rows = blocks * SLOT

    def kernel(order_ref, length_ref, x0, x1, g, b, w, wb, tab, msk, mg, uwr, ow, own, first, qkv, mixed, sums, uw, *parts):
        step = pl.program_id(0)

        @pl.when(step == 0)
        def _():
            found = mul(uwr[...], ow[...])
            uw[...] = jnp.concatenate(
                [found[0:1] + found[1:2] + found[2:3], found[3:4] + found[4:5] + found[5:6], found[6:8], jnp.zeros((4, D), F32)],
                axis=0,
            )

        x = jnp.concatenate([x0[0], x1[0]], axis=0)
        own[...] = x
        hat, _ = norm_parts(x.astype(F32))
        one = rounded(hat * g[...] + b[...])
        first[...] = one
        for c in range(3):
            proj = mul(one, w[c]) + wb[c : c + 1]
            for group in range(groups):
                part = proj[:, group * 128 : group * 128 + 128]
                if c < 2:
                    part = rotate(part, tab, 3 * c, 1)
                at = c * width + group * 128
                qkv[:, at : at + 128] = rounded(part)
        for pair in range(2):
            r = slice(pair * SLOT, pair * SLOT + SLOT)
            length = length_ref[order_ref[2 * step + pair]]
            for group in range(groups):
                at = group * 128
                query = qkv[r, at : at + 128]
                keys = split_heads(qkv[r, width + at : width + at + 128], msk)
                values = split_heads(qkv[r, 2 * width + at : 2 * width + at + 128], msk)
                probs = attention_scores(query, keys, length)
                mixed[r, at : at + 128] = mul(rounded(jnp.concatenate(probs, axis=1)), values)
        m = mixed[...]
        total = jnp.sum(m, axis=-1, keepdims=True)
        sums[...] = rows_of([total, jnp.sum(m * m, axis=-1, keepdims=True)])
        middle = total * (1.0 / width)
        partial = mul(rounded((m - middle) * mg[...]), ow[...]) + middle * uw[0:1]
        store_parts(parts, partial, step, steps)

    row2 = lambda s, *_: (s, 0)
    pair_of = lambda offset: lambda s, order_ref, length_ref: (order_ref[2 * s + offset], 0, 0)
    return run(
        kernel,
        (steps,),
        [
            (tokens, (1, SLOT, D), pair_of(0)),
            (tokens, (1, SLOT, D), pair_of(1)),
            whole(gain), whole(shift), whole(weight), whole(bias), whole(tables), whole(mask),
            whole(mix_gain), whole(uw_rows), whole(out_weight),
        ],
        [
            ((rows, D), BF16, (2 * SLOT, D), row2),
            ((rows, D), BF16, (2 * SLOT, D), row2),
            ((rows, 3 * width), BF16, (2 * SLOT, 3 * width), row2),
            ((rows, width), F32, (2 * SLOT, width), row2),
            ((8, rows), F32, (8, 2 * SLOT), lambda s, *_: (0, s)),
            ((8, D), F32, (8, D), lambda s, *_: (0, 0)),
        ]
        + part_outs(blocks),
        prefetch=(order, lengths),
        after=after,
        name="front",
    )


def pieces_in(pieces):
    return [whole(piece) for half in pieces for piece in half]


def load_pieces(refs, total, step, blocks):
    for block in range(blocks):

        @pl.when(step == block)
        def _(block=block):
            total[:, :HALF] = refs[block][0]
            total[:, HALF:] = refs[blocks + block][0]


def middle_norm(own, pieces, sums, uw, out_bias, gain, shift, after=()):
    blocks = len(pieces[0])
    rows = blocks * SLOT

    def kernel(*refs):
        x, parts, stats = refs[0], refs[1 : 1 + 2 * blocks], refs[1 + 2 * blocks : 1 + 3 * blocks]
        uw_ref, bias, g, b, mid, second, stat, total, tot8 = refs[1 + 3 * blocks :]
        step = pl.program_id(0)
        load_pieces(parts, total, step, blocks)
        for block in range(blocks):

            @pl.when(step == block)
            def _(block=block):
                tot8[...] = combine(stats, block, blocks)

        cols = columns_of(tot8[...])
        mean = cols[:, 0:1] * (1.0 / D)
        inverse = lax.rsqrt(cols[:, 1:2] * (1.0 / D) - mean * mean + eps)
        branch = inverse * (total[...] - mean * uw_ref[0:1]) + uw_ref[1:2]
        value = x[...].astype(F32) + branch + bias[...]
        mid[...] = value
        hat, _ = norm_parts(value)
        second[...] = rounded(hat * g[...] + b[...])
        lane = lax.broadcasted_iota(jnp.int32, (SLOT, 128), 1)
        stat[...] = jnp.where(lane == 0, mean, inverse)

    row = lambda k, *_: (k, 0)
    return run(
        kernel,
        (blocks,),
        [(own, (SLOT, D), row)]
        + pieces_in(pieces)
        + [whole(part) for part in sums]
        + [whole(uw), whole(out_bias), whole(gain), whole(shift)],
        [
            ((rows, D), F32, (SLOT, D), row),
            ((rows, D), BF16, (SLOT, D), row),
            ((rows, 128), F32, (SLOT, 128), row),
        ],
        scratch=[pltpu.VMEM((SLOT, D), F32), pltpu.VMEM((8, SLOT), F32)],
        after=after,
        name="middle_norm",
    )


def hidden_back(cot, down_weight, after=()):
    rows, units = cot.shape[0], down_weight.shape[0]
    tile = min(512, units)

    def kernel(c, w, out):
        out[...] = rounded(mul(c[...], w[...], NT))

    return run(
        kernel,
        (units // tile,),
        [whole(cot), (down_weight, (tile, D), lambda j: (j, 0))],
        [((rows, units), BF16, (rows, tile), lambda j: (0, j))],
        after=after,
        name="hidden_back",
    )[0]


def hidden_front(chunk, second, up_weight, up_bias, back, gain, after=()):
    rows, units = second.shape[0], up_weight.shape[1]
    tile = 256
    steps = units // tile

    def kernel(s_ref, w, b, hb, g, act, slp, sums, acc):
        step = pl.program_id(0)
        hidden = mul(s_ref[...], w[...]) + b[...]
        tail = jnp.exp(-0.5 * hidden * hidden)
        t = 1.0 / (1.0 + (0.3275911 * root_half) * jnp.abs(hidden))
        poly = 1.061405429 * t - 1.453152027
        poly = poly * t + 1.421413741
        poly = poly * t - 0.284496736
        poly = poly * t + 0.254829592
        half = 0.5 * poly * t * tail
        phi = jnp.where(hidden >= 0.0, 1.0 - half, half)
        active = hidden * phi
        act[...] = rounded(active)
        slp[...] = rounded(phi + hidden * (inv_root_two_pi * tail))
        scaled = hb[...].astype(F32) * g[...]
        for at, value in enumerate((active, active * active, scaled, scaled * active)):
            part = value[:, :128] + value[:, 128:]

            @pl.when(step == 0)
            def _():
                acc[at] = part

            @pl.when(step > 0)
            def _():
                acc[at] += part

        @pl.when(step == steps - 1)
        def _():
            for block in range(rows // SLOT):
                r = slice(block * SLOT, block * SLOT + SLOT)
                sums[:, r] = rows_of([jnp.sum(acc[at, r], axis=-1, keepdims=True) for at in range(4)])

    return run(
        kernel,
        (steps,),
        [
            whole(second),
            (up_weight, (D, tile), lambda j: (0, j)),
            (up_bias, (1, tile), lambda j: (0, j)),
            (back, (rows, tile), lambda j: (chunk, j)),
            (gain, (1, tile), lambda j: (0, j)),
        ],
        [
            ((rows, units), BF16, (rows, tile), lambda j: (0, j)),
            ((rows, units), BF16, (rows, tile), lambda j: (0, j)),
            ((8, rows), F32, (8, rows), lambda j: (0, 0)),
        ],
        scratch=[pltpu.VMEM((4, rows, 128), F32)],
        after=after,
        name="hidden_front",
    )


def hidden_grad(chunk, active, slope, back, sums, gain, shift, up_weight, after=()):
    blocks = len(sums)
    rows, units = active.shape
    tile = 256
    steps = D // tile
    half = steps // 2

    def kernel(act, slp, hb, *refs):
        stats = refs[:blocks]
        g, b, w, low, grad, vecs, left_keep, left_send, right_keep, right_send, acc = refs[blocks:]
        step = pl.program_id(0)

        @pl.when(step == 0)
        def _():
            for block in range(blocks):
                r = slice(block * SLOT, block * SLOT + SLOT)
                cols = columns_of(combine(stats, block, blocks)) * (1.0 / FF)
                mean = cols[:, 0:1]
                inverse = lax.rsqrt(cols[:, 1:2] - mean * mean + eps)
                one = cols[:, 2:3]
                two = inverse * (cols[:, 3:4] - mean * one)
                for at in range(0, units, 512):
                    c = slice(at, at + 512)
                    hat = (act[r, c].astype(F32) - mean) * inverse
                    low[r, c] = rounded(hat * g[:, c] + b[:, c])
                    raw = hb[r, c].astype(F32)
                    grown = rounded(inverse * (raw * g[:, c] - one - hat * two) * slp[r, c].astype(F32))
                    grad[r, c] = grown
                    found = [sum_rows(raw * hat), sum_rows(raw), sum_rows(grown.astype(F32))]
                    for i, value in enumerate(found):
                        if block == 0:
                            vecs[i : i + 1, c] = value
                        else:
                            vecs[i : i + 1, c] += value

        value = mul(grad[...], w[...], NT)

        @pl.when(step < half)
        def _():
            for block in range(blocks):
                r = slice(block * SLOT, block * SLOT + SLOT)
                (left_send if block & 1 else left_keep)[block // 2] = value[r]

        @pl.when(step >= half)
        def _():
            for block in range(blocks):
                r = slice(block * SLOT, block * SLOT + SLOT)
                (right_send if block >= blocks // 2 else right_keep)[block % (blocks // 2)] = value[r]

    shape = (blocks // 2, SLOT, HALF)
    block_shape = (blocks // 2, SLOT, tile)
    lefts = lambda j: (0, 0, jnp.minimum(j, half - 1))
    rights = lambda j: (0, 0, jnp.maximum(j - half, 0))
    fixed = lambda j: (0, 0)
    return run(
        kernel,
        (steps,),
        [whole(active), whole(slope), (back, (rows, units), lambda j: (chunk, 0))]
        + [whole(part) for part in sums]
        + [whole(gain), whole(shift), (up_weight, (tile, units), lambda j: (j, 0))],
        [
            ((rows, units), BF16, (rows, units), fixed),
            ((rows, units), BF16, (rows, units), fixed),
            ((8, units), F32, (8, units), fixed),
            (shape, F32, block_shape, lefts),
            (shape, F32, block_shape, lefts),
            (shape, F32, block_shape, rights),
            (shape, F32, block_shape, rights),
        ],
        scratch=[pltpu.VMEM((8, 128), F32)],
        after=after,
        name="hidden_grad",
    )


def result_part(order, lows, down_weight, after=()):
    blocks = order.shape[0]
    units = down_weight.shape[0]

    def kernel(order_ref, low, w, out):
        out[0] = mul(low[...], w[...])

    return run(
        kernel,
        (blocks,),
        [(lows, (SLOT, units), lambda k, *_: (k, 0)), whole(down_weight)],
        [((blocks, SLOT, D), F32, (1, SLOT, D), lambda k, o: (o[k], 0, 0))],
        prefetch=(order,),
        after=after,
        name="result_part",
    )[0]


def middle_back(own, cot, pieces, middle, stat, uw, out_bias, gain, after=()):
    blocks = len(pieces[0])
    rows = blocks * SLOT

    def kernel(*refs):
        x, c, parts = refs[0], refs[1], refs[2 : 2 + 2 * blocks]
        mid, st, uw_ref, bias, g, grad, low, stat2, vecs, total = refs[2 + 2 * blocks :]
        load_pieces(parts, total, pl.program_id(0), blocks)
        value = mid[...]
        hat, inverse = norm_parts(value)
        sec = total[...]
        scaled = sec * g[...]
        up = c[...].astype(F32)
        out = up + inverse * (
            scaled
            - jnp.mean(scaled, axis=-1, keepdims=True)
            - hat * jnp.mean(scaled * hat, axis=-1, keepdims=True)
        )
        grad[...] = out
        lowered = rounded(out)
        low[...] = lowered
        low32 = lowered.astype(F32)
        one = jnp.mean(low32 * uw_ref[0:1], axis=-1, keepdims=True)
        moved = value - x[...].astype(F32) - bias[...] - uw_ref[1:2]
        two = jnp.mean(low32 * moved, axis=-1, keepdims=True)
        lane = lax.broadcasted_iota(jnp.int32, (SLOT, 128), 1)
        stat2[...] = jnp.where(lane == 2, one, jnp.where(lane == 3, two, st[...]))
        vecs[0, 0:1] = sum_rows(sec * hat)
        vecs[0, 1:2] = sum_rows(sec)
        vecs[0, 2:3] = sum_rows(out)
        vecs[0, 3:4] = sum_rows(up)

    row = lambda k, *_: (k, 0)
    return run(
        kernel,
        (blocks,),
        [(own, (SLOT, D), row), (cot, (SLOT, D), row)]
        + pieces_in(pieces)
        + [(middle, (SLOT, D), row), (stat, (SLOT, 128), row), whole(uw), whole(out_bias), whole(gain)],
        [
            ((rows, D), F32, (SLOT, D), row),
            ((rows, D), BF16, (SLOT, D), row),
            ((rows, 128), F32, (SLOT, 128), row),
            ((blocks, 8, D), F32, (1, 8, D), lambda k, *_: (k, 0, 0)),
        ],
        scratch=[pltpu.VMEM((SLOT, D), F32)],
        after=after,
        name="middle_back",
    )


def attention_back(order, lengths, low, stat, mixed, qkv, own, mix_gain, mix_shift, out_weight, weight, tables, mask, after=()):
    blocks = order.shape[0]
    steps = blocks // 2
    width = out_weight.shape[0]
    groups = width // 128
    rows = blocks * SLOT

    def kernel(
        order_ref, length_ref, low_ref, st, mx, qkv_ref, x, mg, ms, ow, w, tab, msk,
        mix_low, dproj, vecs, wide, left_keep, left_send, right_keep, right_send, dmixed,
    ):
        step = pl.program_id(0)
        mean, inverse, one, two = (st[:, at : at + 1] for at in range(4))
        back = mul(low_ref[...], ow[...], NT)
        hat = (mx[...] - mean) * inverse
        mix_low[...] = rounded(hat * mg[...] + ms[...])
        dmixed[...] = rounded(inverse * (back * mg[...] - one - hat * two))
        vecs[0, 0:1, :width] = sum_rows(back * hat)
        vecs[0, 1:2, :width] = sum_rows(back)
        first_half = lax.broadcasted_iota(jnp.int32, (SLOT, 128), 1) < HD
        for pair in range(2):
            r = slice(pair * SLOT, pair * SLOT + SLOT)
            length = length_ref[order_ref[2 * step + pair]]
            for group in range(groups):
                at = group * 128
                query = qkv_ref[r, at : at + 128]
                keys = split_heads(qkv_ref[r, width + at : width + at + 128], msk)
                values = split_heads(qkv_ref[r, 2 * width + at : 2 * width + at + 128], msk)
                grad = dmixed[r, at : at + 128]
                probs = attention_scores(query, keys, length)
                dprobs = mul(grad, values, NT)
                dscores = []
                for i in range(2):
                    dp = dprobs[:, i * SLOT : (i + 1) * SLOT]
                    carried = jnp.sum(probs[i] * dp, axis=-1, keepdims=True)
                    dscores.append(rounded(probs[i] * (dp - carried)))
                dscores = jnp.concatenate(dscores, axis=1)
                dquery = mul(dscores, keys)
                dkey = mul(dscores, query, TN)
                dvalue = mul(rounded(jnp.concatenate(probs, axis=1)), grad, TN)
                dkey = jnp.where(first_half, dkey[:SLOT], dkey[SLOT:])
                dvalue = jnp.where(first_half, dvalue[:SLOT], dvalue[SLOT:])
                tabs = [tab[i, :SLOT] for i in range(6)]
                dproj[r, at : at + 128] = rounded(rotate(dquery, tabs, 0, -1))
                dproj[r, width + at : width + at + 128] = rounded(rotate(dkey, tabs, 3, -1))
                dproj[r, 2 * width + at : 2 * width + at + 128] = rounded(dvalue)
        vecs[0, 2:3] = sum_rows(dproj[...].astype(F32))
        partial = mul(dproj[:, :width], w[0], NT)
        for c in (1, 2):
            partial += mul(dproj[:, c * width : (c + 1) * width], w[c], NT)
        pre_hat, _ = norm_parts(x[...].astype(F32))
        grown = partial * pre_hat
        wide[0, 0:1] = sum_rows(grown[:SLOT]) + sum_rows(grown[SLOT:])
        wide[0, 1:2] = sum_rows(partial[:SLOT]) + sum_rows(partial[SLOT:])
        store_parts((left_keep, left_send, right_keep, right_send), partial, step, steps)

    row2 = lambda s, *_: (s, 0)
    return run(
        kernel,
        (steps,),
        [
            (low, (2 * SLOT, D), row2),
            (stat, (2 * SLOT, 128), row2),
            (mixed, (2 * SLOT, width), row2),
            (qkv, (2 * SLOT, 3 * width), row2),
            (own, (2 * SLOT, D), row2),
            whole(mix_gain), whole(mix_shift), whole(out_weight), whole(weight), whole(tables), whole(mask),
        ],
        [
            ((rows, width), BF16, (2 * SLOT, width), row2),
            ((rows, 3 * width), BF16, (2 * SLOT, 3 * width), row2),
            ((steps, 8, 3 * width), F32, (1, 8, 3 * width), lambda s, *_: (s, 0, 0)),
            ((steps, 8, D), F32, (1, 8, D), lambda s, *_: (s, 0, 0)),
        ]
        + part_outs(blocks),
        scratch=[pltpu.VMEM((2 * SLOT, width), BF16)],
        prefetch=(order, lengths),
        after=after,
        name="attention_back",
    )


def tokens_back(order, own, grad, pieces, gain, before, pairs, after=()):
    blocks = len(pieces[0])

    def kernel(order_ref, x, gr, *refs):
        parts = refs[: 2 * blocks]
        g = refs[2 * blocks]
        out, total = refs[-2:]
        load_pieces(parts, total, pl.program_id(0), blocks)
        hat, inverse = norm_parts(x[...].astype(F32))
        scaled = total[...] * g[...]
        out[0] = gr[...] + inverse * (
            scaled
            - jnp.mean(scaled, axis=-1, keepdims=True)
            - hat * jnp.mean(scaled * hat, axis=-1, keepdims=True)
        )

    row = lambda k, *_: (k, 0)
    ins = [(own, (SLOT, D), row), (grad, (SLOT, D), row)] + pieces_in(pieces) + [whole(gain)]
    alias = None
    if before is not None:
        alias = {1 + len(ins): 0}
        ins = ins + [(before, None, None)]
    return run(
        kernel,
        (blocks,),
        ins,
        [((pairs, SLOT, D), F32, (1, SLOT, D), lambda k, o: (o[k], 0, 0))],
        scratch=[pltpu.VMEM((SLOT, D), F32)],
        prefetch=(order,),
        after=after,
        alias=alias,
        name="tokens_back",
    )[0]


def output_of(order, middle, result, bias, before, after=()):
    blocks = order.shape[0]

    def kernel(order_ref, mid, res, b, *refs):
        out = refs[-1]
        out[0] = rounded(mid[...] + res[0] + b[...])

    ins = [
        (middle, (SLOT, D), lambda k, *_: (k, 0)),
        (result, (1, SLOT, D), lambda k, o: (o[k], 0, 0)),
        whole(bias),
    ]
    alias = None
    if before is not None:
        alias = {1 + len(ins): 0}
        ins = ins + [(before, None, None)]
    return run(
        kernel,
        (blocks,),
        ins,
        [(result.shape, BF16, (1, SLOT, D), lambda k, o: (o[k], 0, 0))],
        prefetch=(order,),
        after=after,
        alias=alias,
        name="output",
    )[0]


def weight_grad(ids, lefts, rights, left_blocked, got=None):
    count = ids.shape[0]
    rows = lefts[0].shape[0]
    many = len(lefts)
    wide, tall = lefts[0].shape[1], rights[0].shape[1]
    block = D // (2 * count)
    shape = (block, tall) if left_blocked else (wide, block)

    def kernel(ids_ref, *refs):
        left, right = refs[:many], refs[many : 2 * many]
        outs = refs[2 * many + (got is not None) :]
        value = mul(left[0][...], right[0][...], TN)
        for at in range(1, many):
            value += mul(left[at][...], right[at][...], TN)
        if got is None:
            outs[0][0] = value
            return
        value += refs[2 * many][0]
        step = pl.program_id(0)

        @pl.when(step == 0)
        def _():
            outs[0][...] = value

        @pl.when(step > 0)
        def _():
            outs[1][0] = value

    fixed = lambda i, *_: (0, 0)
    moving = lambda i, ids_ref: (0, ids_ref[i])
    lead = lambda i, *_: (i, 0, 0)
    ins = [(left, (rows, block), moving) if left_blocked else (left, (rows, wide), fixed) for left in lefts]
    ins += [(right, (rows, tall), fixed) if left_blocked else (right, (rows, block), moving) for right in rights]
    if got is None:
        outs = [((count,) + shape, F32, (1,) + shape, lead)]
    else:
        ins += [(got, (1,) + shape, lead)]
        outs = [
            (shape, F32, shape, fixed),
            ((count - 1,) + shape, F32, (1,) + shape, lambda i, *_: (jnp.maximum(i - 1, 0), 0, 0)),
        ]
    return run(kernel, (count,), ins, outs, prefetch=(ids,), name="weight_grad")


def split_rows(value):
    found = []
    for _ in range(3):
        part = lax.reduce_precision(value, 8, 7)
        found.append(part.astype(BF16))
        value = value - part
    return found


def body(
    tokens,
    lengths,
    cotangent,
    pre_gain,
    pre_shift,
    qkv_weight,
    qkv_bias,
    mix_gain,
    mix_shift,
    out_weight,
    out_bias,
    ffn_gain,
    ffn_shift,
    up_weight,
    up_bias,
    hid_gain,
    hid_shift,
    down_weight,
    down_bias,
):
    pairs = lengths.shape[0]
    blocks = lax.axis_size("tensor")
    bits = blocks.bit_length() - 1
    chunks = pairs // blocks
    width = qkv_weight.shape[2]
    mine = lax.axis_index("tensor").astype(jnp.int32)
    orders = [jnp.arange(c * blocks, (c + 1) * blocks, dtype=jnp.int32) ^ mine for c in range(chunks)]
    tokens3 = tokens.reshape(pairs, SLOT, D)
    row = lambda v: v.reshape(1, -1)
    pre_gain, pre_shift, mix_gain, mix_shift = map(row, (pre_gain, pre_shift, mix_gain, mix_shift))
    out_bias, ffn_gain, ffn_shift, up_bias = map(row, (out_bias, ffn_gain, ffn_shift, up_bias))
    hid_gain, hid_shift, down_bias = map(row, (hid_gain, hid_shift, down_bias))
    tables = xpos_tables()
    lane = np.arange(128)[None, :] < HD
    mask = jnp.asarray(np.concatenate([lane, ~lane], 0).astype(np.float32)).astype(BF16)
    zero = jnp.zeros((2, width), BF16)
    uw_rows = jnp.concatenate(split_rows(mix_gain) + split_rows(mix_shift) + [zero], 0)

    line = Line()
    dp_size = lax.axis_size("dp")
    place = lax.axis_index("dp").astype(jnp.int32)
    count = dp_size // 2
    around = lax.rem(place // 2 + count - 1 - jnp.arange(count, dtype=jnp.int32), count)
    mine_ids, other_ids = 2 * around + lax.rem(place, 2), 2 * around + 1 - lax.rem(place, 2)

    def send_half(lefts, rights, left_blocked):
        sent = weight_grad(other_ids, [line.tie(lefts[0])] + lefts[1:], rights, left_blocked)[0]
        line.mark(sent)
        return lax.ppermute(sent, "dp", [(d, d ^ 1) for d in range(dp_size)])

    def keep_half(lefts, rights, left_blocked, got):
        first, rest = weight_grad(mine_ids, [line.tie(lefts[0])] + lefts[1:], rights, left_blocked, got)
        line.mark(rest)
        return Ring(line, first, rest, dp_size)

    ones, twos, threes = [], [], []
    up_order = list(range(bits))
    for c in range(chunks):
        found = front(
            orders[c], lengths, line.tie(tokens3), pre_gain, pre_shift, qkv_weight, qkv_bias, tables, mask, mix_gain, uw_rows,
            out_weight,
        )
        own, first, qkv, mixed, sums, uw = found[:6]
        line.mark(sums)
        if c == 0:
            uw_total = butterfly(uw, bits)
        one = dict(own=own, first=first, qkv=qkv, mixed=mixed, parts=found[6:])
        one["sums"] = gather_pieces(sums, bits, up_order)
        if c == 0:
            one["branch"] = Total(line, one["parts"], bits)
        ones.append(one)
    cot3 = cotangent.reshape(pairs, SLOT, D)
    cot_own = line.tie(cot3)[jnp.concatenate(orders)].reshape(chunks, -1, D)
    cots = [cot_own[c] for c in range(chunks)]
    back = hidden_back(cot_own.reshape(-1, D), down_weight)
    line.mark(back)
    for c in range(chunks):
        one = ones[c]
        if c > 0:
            one["branch"] = Total(line, [line.tie(part) for part in one["parts"]], bits)
        for step in range(bits):
            one["branch"].advance()
        one["pieces"] = one["branch"].pieces()

    for c in range(chunks):
        one = ones[c]
        mid, second, stat = middle_norm(
            line.tie(one["own"]), one["pieces"], one["sums"], uw_total, out_bias, ffn_gain, ffn_shift
        )
        line.mark(stat)
        active, slope, sums = hidden_front(c, line.tie(second), up_weight, up_bias, back, hid_gain)
        line.mark(sums)
        twos.append(
            dict(middle=mid, second=second, stat=stat, active=active, slope=slope, sums=gather_pieces(sums, bits, up_order))
        )
    for c in range(chunks):
        two = twos[c]
        found = hidden_grad(c, line.tie(two["active"]), two["slope"], back, two["sums"], hid_gain, hid_shift, up_weight)
        line.mark(found[2])
        two.update(low=found[0], grad=found[1], vecs=found[2], parts=found[3:])
        two["total"] = Total(line, two["parts"], bits)
    every = lambda items, name: [item[name] for item in items]
    down_args = (every(twos, "low"), cots, False)
    up_args = (every(twos, "second"), every(twos, "grad"), True)
    down_got = send_half(*down_args)
    up_got = send_half(*up_args)
    twos[0]["total"].advance()
    down_ring = keep_half(*down_args, down_got)
    up_ring = keep_half(*up_args, up_got)
    for step in range(1, bits):
        twos[0]["total"].advance()
    twos[0]["pieces"] = twos[0]["total"].pieces()
    for c in range(1, chunks):
        for step in range(bits):
            twos[c]["total"].advance()
        twos[c]["pieces"] = twos[c]["total"].pieces()
    result = result_part(jnp.concatenate(orders), line.tie(jnp.concatenate(every(twos, "low"), 0)), down_weight)
    line.mark(result)
    result = lax.psum(result, "tensor")

    for c in range(chunks):
        one, two = ones[c], twos[c]
        grad, low, stat2, vecs = middle_back(
            line.tie(one["own"]), cots[c], two["pieces"], two["middle"], two["stat"], uw_total, out_bias, ffn_gain
        )
        line.mark(stat2)
        found = attention_back(
            orders[c], lengths, line.tie(low), stat2, one["mixed"], one["qkv"], one["own"], mix_gain, mix_shift, out_weight,
            qkv_weight, tables, mask,
        )
        line.mark(found[2])
        three = dict(grad=grad, low=low, vecs=tree_sum(vecs), mix_low=found[0], dproj=found[1])
        three["narrow"] = tree_sum(found[2])
        three["wide"] = tree_sum(found[3])
        three["total"] = Total(line, found[4:], bits)
        threes.append(three)
        if c == 0:
            down_ring.advance()
            up_ring.advance()

    out_args = (every(threes, "mix_low"), every(threes, "low"), False)
    qkv_args = (every(ones, "first"), every(threes, "dproj"), True)
    out_got = send_half(*out_args)
    threes[0]["total"].advance()
    qkv_got = send_half(*qkv_args)
    out_ring = keep_half(*out_args, out_got)
    for step in range(1, bits):
        threes[0]["total"].advance()
    threes[0]["pieces"] = threes[0]["total"].pieces()
    qkv_ring = keep_half(*qkv_args, qkv_got)
    for c in range(1, chunks):
        threes[c]["total"].advance()

    add = lambda items, name, size: functools.reduce(jnp.add, [item[name] for item in items])[:size]
    hid_vecs, mid_vecs, narrow = add(twos, "vecs", 3), add(threes, "vecs", 4), add(threes, "narrow", 3)
    wide = butterfly(line.tie(add(threes, "wide", 2)), bits)
    line.mark(wide)
    pad = lambda v: jnp.pad(v, ((0, 0), (0, D - v.shape[1])))
    vecs = jnp.concatenate([pad(hid_vecs), mid_vecs, pad(narrow), wide], 0)
    for bit in range(dp_size.bit_length() - 1):
        vecs = vecs + lax.ppermute(vecs, "dp", [(d, d ^ (1 << bit)) for d in range(dp_size)])
    hid_vecs, mid_vecs, narrow, wide = vecs[:3], vecs[3:7], vecs[7:10], vecs[10:12]
    for c in range(1, chunks):
        for step in range(1, bits):
            threes[c]["total"].advance()
        threes[c]["pieces"] = threes[c]["total"].pieces()
    for step in range(1, count - 1):
        down_part, up_part = down_ring.advance(), up_ring.advance()
        if step == 1:
            out_ring.advance()
            qkv_ring.advance()
    tokens_grad, output = None, None
    for c in range(chunks):
        tokens_grad = tokens_back(
            orders[c], line.tie(ones[c]["own"]), threes[c]["grad"], threes[c]["pieces"], pre_gain, tokens_grad, pairs
        )
        line.mark(tokens_grad)
        output = output_of(orders[c], line.tie(twos[c]["middle"]), result, down_bias, output)
        line.mark(output)
    for step in range(1, count - 1):
        out_part, qkv_part = out_ring.advance(), qkv_ring.advance()
    qkv_part = jnp.swapaxes(qkv_part.reshape(-1, 3, width), 0, 1)
    units = hid_gain.shape[1]
    return (
        output.reshape(-1, D),
        tokens_grad.reshape(-1, D),
        wide[0],
        wide[1],
        qkv_part,
        narrow[2, : 3 * width].reshape(3, width),
        narrow[0, :width],
        narrow[1, :width],
        out_part,
        mid_vecs[2],
        mid_vecs[0],
        mid_vecs[1],
        up_part,
        hid_vecs[2, :units],
        hid_vecs[0, :units],
        hid_vecs[1, :units],
        down_part,
        mid_vecs[3],
    )


def solution(mesh):
    in_specs = (
        P("dp", None),
        P("dp"),
        P("dp", None),
        P(),
        P(),
        P(None, None, "tensor"),
        P(None, "tensor"),
        P("tensor"),
        P("tensor"),
        P("tensor", None),
        P(),
        P(),
        P(),
        P(None, "tensor"),
        P("tensor"),
        P("tensor"),
        P("tensor"),
        P("tensor", None),
        P(),
    )
    out_specs = (
        P("dp", None),
        P("dp", None),
        P(),
        P(),
        P(None, "dp", "tensor"),
        P(None, "tensor"),
        P("tensor"),
        P("tensor"),
        P("tensor", "dp"),
        P(),
        P(),
        P(),
        P("dp", "tensor"),
        P("tensor"),
        P("tensor"),
        P("tensor"),
        P("tensor", "dp"),
        P(),
    )
    return jax.shard_map(body, mesh=mesh, in_specs=in_specs, out_specs=out_specs, check_vma=False)
```

time: 1530 us -> 920 us (0.60)
  waiting for transfers between devices: 1130 us -> 420 us
  Pallas kernels: 0 us -> 314 us
  matrix products: 185 us -> 0 us
  starting transfers between devices: 0.8 us -> 92.8 us
  local copies, waits for them, and re-layouts: 73.6 us -> 20.7 us
  blocking collectives: 39.2 us -> 0 us
  other arithmetic: 82.8 us -> 46.1 us
    psum x4 -> x1, waiting for transfers between devices: 665 us -> 0.01 us  [body(): result = lax.psum(result, 'tensor')]
    reduce_scatter x4 -> x0, waiting for transfers between devices: 461 us -> none  [the longest x1 173 us: body(): lax.psum_scatter(down_grad, 'dp', scatter_dimension=1, tiled=True)]
    ppermute x0 -> x95, waiting for transfers between devices: none -> 420 us  [the longest x76 302 us: flip(): lax.ppermute(value, 'tensor', [(t, t ^ 1 << bit) for t in range(size)])]
    pallas_call x0 -> x26, Pallas kernels: none -> 314 us  [run(): pl.pallas_call(body, grid_spec=pltpu.PrefetchScalarGridSpec(num_scalar_pr...]
    dot_general x18 -> x0, matrix products: 185 us -> none  [the longest x1 36 us: body(): jnp.dot(second, up_weight, preferred_element_type=jnp.float32) + up_bias]
    ppermute x0 -> x95, starting transfers between devices: none -> 92.8 us  [the longest x76 73.5 us: flip(): lax.ppermute(value, 'tensor', [(t, t ^ 1 << bit) for t in range(size)])]
    reduce_sum x8 -> x0, other arithmetic: 48.2 us -> none  [the longest x1 12.3 us: body(): up_bias_grad = jnp.sum(hidden_grad, 0, dtype=jnp.float32)]
    psum x4 -> x0, blocking collectives: 39.2 us -> none  [the longest x1 11.5 us: body(): lax.psum((jnp.sum(mixed, 1), jnp.sum(mixed * mixed, 1)), 'tensor')]
  transfers between devices with their start and end apart: 8 -> 96, of which waited for: 8 -> 39; matrix products, arithmetic and copies ran while one was open for 7% -> 6% of each run, Pallas kernels for 0% -> 29%
where the time goes in v1:
time: 920 us; the launch traced here: 910 us
  waiting for transfers between devices  420 us (46%)
  Pallas kernels  314 us (34%)
  starting transfers between devices  92.8 us (10%)
  other arithmetic  46.1 us (5%)
  local copies, waits for them, and re-layouts  20.7 us (2%)
  between operations  15.8 us (2%)
    pallas_call x26, Pallas kernels, run(): pl.pallas_call(body, grid_spec=pltpu.PrefetchScalarGridSpec(num_scalar_pr...  314 us
    ppermute x76, waiting for transfers between devices, flip(): lax.ppermute(value, 'tensor', [(t, t ^ 1 << bit) for t in range(size)])  302 us
    ppermute x12, waiting for transfers between devices, send(): lax.ppermute(value, 'dp', [(d, (d + 2) % self.size) for d in range(self.s...  81 us
    ppermute x76, starting transfers between devices, flip(): lax.ppermute(value, 'tensor', [(t, t ^ 1 << bit) for t in range(size)])  73.5 us
    ppermute x3, waiting for transfers between devices, body(): lax.ppermute(vecs, 'dp', [(d, d ^ 1 << bit) for d in range(dp_size)])  36.1 us
    add x12, other arithmetic, advance(): value = self.line.tie(self.rest)[self.step] + self.got  25.5 us
  transfers between devices with their start and end apart: 96, of which 39 were waited for; matrix products, arithmetic and copies ran while one was open for 6% of the time, Pallas kernels for 29%

profile of v1, /device:TPU:0, one launch (start us, length us, event | category | flops | bytes accessed | tf_op | source)
XLA Modules:
  0.0 909.6 jit_solution(11570021554946467689)
XLA Ops:
  9.8 15.7 %front.2 = (bf16[512,2048]{1,0:T(8,128)(2,1)}, bf16[512,2048]{1,0:T(8,128)(2,1)}, bf16[512,1536]{1,0:T(8,128)(2,1)}, f32[512,512]{1,0:T(8,128)}, f32[8,512]{1,0:...) custom-call(s32[4]{0:T(128)} %iota_xor_fusion.refs_0_, ...), custom_call_target="tpu_custom_call" | custom-call | flops 1000 | bytes 1000 | tf_op jit(solution)/shard_map/front/pallas_call | solution.py:115
  30.6 15.7 %front.3 = (bf16[512,2048]{1,0:T(8,128)(2,1)}, bf16[512,2048]{1,0:T(8,128)(2,1)}, bf16[512,1536]{1,0:T(8,128)(2,1)}, f32[512,512]{1,0:T(8,128)}, f32[8,512]{1,0:...) custom-call(s32[4]{0:T(128)} %add_xor_fusion.refs_0_, ...), custom_call_target="tpu_custom_call" | custom-call | flops 1000 | bytes 1000 | tf_op jit(solution)/shard_map/front/pallas_call | solution.py:115
  51.4 13.6 %hidden_back.1.refs_3_.refs_2_ = bf16[1024,2048]{1,0:T(8,128)(2,1)} custom-call(bf16[1024,2048]{1,0:T(8,128)(2,1)} %bitcast.92, bf16[2048,2048]{1,0:T(8,128)(2,1)} %refs_2_.1), custom_call_target="tpu_custom_call" | custom-call | flops 1000 | bytes 1000 | tf_op jit(solution)/shard_map/hidden_back/pallas_call | solution.py:115
  66.1 12.3 %collective-permute-done.2 = f32[1,128,1024]{2,1,0:T(8,128)S(1)} collective-permute-done((f32[1,128,1024]{2,1,0:T(8,128)S(1)}, f32[1,128,1024]{2,1,0:T(8,128)S(1)}, u32[]{:S(2)}, u32[]{:S(2)}) %collective-permute-start.2) | collective-permute-done | bytes 524320 | tf_op jit(solution)/shard_map/ppermute | solution.py:135
  80.9 21.2 %collective-permute-done.4 = f32[2,128,1024]{2,1,0:T(8,128)S(1)} collective-permute-done((f32[2,128,1024]{2,1,0:T(8,128)S(1)}, f32[2,128,1024]{2,1,0:T(8,128)S(1)}, u32[]{:S(2)}, u32[]{:S(2)}) %collective-permute-start.4) | collective-permute-done | bytes 1048608 | tf_op jit(solution)/shard_map/ppermute | solution.py:135
  182.3 14.6 %hidden_front.2 = (bf16[512,2048]{1,0:T(8,128)(2,1)}, bf16[512,2048]{1,0:T(8,128)(2,1)}, f32[8,512]{1,0:T(8,128)}) custom-call(bf16[512,2048]{1,0:T(8,128)(2,1)} %get-tuple-element.240.refs_0_.refs_1_, bf16[2048,2048]{1,0:T(8,128)(2,1)} %refs_9_.5, f32[1,2048]{1,0:T(1,128)} %bitcast.139, bf16[1024,2048]{1,0:T(8,128)(2,1)} %hidden_back.1.refs_3_.refs_2_, ...), custom_call_target="tpu_custom_call" | custom-call | flops 1000 | bytes 1000 | tf_op jit(solution)/shard_map/hidden_front/pallas_call | solution.py:115
  206.9 14.7 %hidden_front.3 = (bf16[512,2048]{1,0:T(8,128)(2,1)}, bf16[512,2048]{1,0:T(8,128)(2,1)}, f32[8,512]{1,0:T(8,128)}) custom-call(bf16[512,2048]{1,0:T(8,128)(2,1)} %get-tuple-element.215.refs_0_.refs_2_, bf16[2048,2048]{1,0:T(8,128)(2,1)} %refs_9_.5, f32[1,2048]{1,0:T(1,128)} %bitcast.140, bf16[1024,2048]{1,0:T(8,128)(2,1)} %hidden_back.1.refs_3_.refs_2_, ...), custom_call_target="tpu_custom_call" | custom-call | flops 1000 | bytes 1000 | tf_op jit(solution)/shard_map/hidden_front/pallas_call | solution.py:115
  231.1 18.5 %hidden_grad.2 = (bf16[512,2048]{1,0:T(8,128)(2,1)}, bf16[512,2048]{1,0:T(8,128)(2,1)}, f32[8,2048]{1,0:T(8,128)}, f32[2,128,1024]{2,1,0:T(8,128)}, f32[2,128,10...) custom-call(bf16[512,2048]{1,0:T(8,128)(2,1)} %get-tuple-element.217.refs_0_, ...), custom_call_target="tpu_custom_call" | custom-call | flops 1000 | bytes 1000 | tf_op jit(solution)/shard_map/hidden_grad/pallas_call | solution.py:115
  250.2 18.1 %hidden_grad.3 = (bf16[512,2048]{1,0:T(8,128)(2,1)}, bf16[512,2048]{1,0:T(8,128)(2,1)}, f32[8,2048]{1,0:T(8,128)}, f32[2,128,1024]{2,1,0:T(8,128)}, f32[2,128,10...) custom-call(bf16[512,2048]{1,0:T(8,128)(2,1)} %get-tuple-element.224.refs_0_, ...), custom_call_target="tpu_custom_call" | custom-call | flops 1000 | bytes 1000 | tf_op jit(solution)/shard_map/hidden_grad/pallas_call | solution.py:115
  293.2 22.3 %collective-permute-done.34 = f32[2,128,1024]{2,1,0:T(8,128)S(1)} collective-permute-done((f32[2,128,1024]{2,1,0:T(8,128)S(1)}, f32[2,128,1024]{2,1,0:T(8,128)S(1)}, u32[]{:S(2)}, u32[]{:S(2)}) %collective-permute-start.34) | collective-permute-done | bytes 1048608 | tf_op jit(solution)/shard_map/ppermute | solution.py:135
  319.1 13.1 %weight_grad.10 = (f32[2048,256]{1,0:T(8,128)}, f32[3,2048,256]{2,1,0:T(8,128)}) custom-call(s32[4]{0:T(128)} %broadcast_add_fusion.refs_0_, bf16[512,2048]{1,0:T(8,128)(2,1)} %get-tuple-element.238.refs_1_, bf16[512,2048]{1,0:T(8,128)(2,1)} %get-tuple-element.228.refs_2_, bf16[512,2048]{1,0:T(8,128)(2,1)} %bitcast.97, bf16[512,2048]{1,0:T(8,128)(2,1)} %bitcast.94, ...), custom_call_target="tpu_custom_call" | custom-call | flops 1000 | bytes 1000 | tf_op jit(solution)/shard_map/weight_grad/pallas_call | solution.py:115
  332.2 12.8 %weight_grad.11 = (f32[256,2048]{1,0:T(8,128)}, f32[3,256,2048]{2,1,0:T(8,128)}) custom-call(s32[4]{0:T(128)} %broadcast_add_fusion.refs_0_, bf16[512,2048]{1,0:T(8,128)(2,1)} %get-tuple-element.240.refs_0_.refs_1_, bf16[512,2048]{1,0:T(8,128)(2,1)} %get-tuple-element.215.refs_0_.refs_2_, bf16[512,2048]{1,0:T(8,128)(2,1)} %get-tuple-element.230.refs_3_, ...), custom_call_target="tpu_custom_call" | custom-call | flops 1000 | bytes 1000 | tf_op jit(solution)/shard_map/weight_grad/pallas_call | solution.py:115
  397.3 16.0 %result_part.1 = f32[8,128,2048]{2,1,0:T(8,128)} custom-call(s32[8]{0:T(128)} %pad_add_fusion.refs_0_, bf16[1024,2048]{1,0:T(8,128)(2,1)} %pad_maximum_fusion.refs_1_, bf16[2048,2048]{1,0:T(8,128)(2,1)} %refs_2_.1), custom_call_target="tpu_custom_call" | custom-call | flops 1000 | bytes 1000 | tf_op jit(solution)/shard_map/result_part/pallas_call | solution.py:115
  426.1 21.4 %attention_back.2 = (bf16[512,512]{1,0:T(8,128)(2,1)}, bf16[512,1536]{1,0:T(8,128)(2,1)}, f32[2,8,1536]{2,1,0:T(8,128)}, f32[2,8,2048]{2,1,0:T(8,128)}, f32[2,12...) custom-call(s32[4]{0:T(128)} %iota_xor_fusion.refs_0_, ...), custom_call_target="tpu_custom_call" | custom-call | flops 1000 | bytes 1000 | tf_op jit(solution)/shard_map/attention_back/pallas_call | solution.py:115
  459.8 20.5 %collective-permute-done.52.refs_3_ = f32[1,128,1024]{2,1,0:T(8,128)S(1)} collective-permute-done((f32[1,128,1024]{2,1,0:T(8,128)S(1)}, f32[1,128,1024]{2,1,0:T(8,128)S(1)}, u32[]{:S(2)}, u32[]{:S(2)}) %collective-permute-start.52) | collective-permute-done | bytes 524320 | tf_op jit(solution)/shard_map/ppermute | solution.py:135
  497.6 21.6 %attention_back.3 = (bf16[512,512]{1,0:T(8,128)(2,1)}, bf16[512,1536]{1,0:T(8,128)(2,1)}, f32[2,8,1536]{2,1,0:T(8,128)}, f32[2,8,2048]{2,1,0:T(8,128)}, f32[2,12...) custom-call(s32[4]{0:T(128)} %add_xor_fusion.refs_0_, ...), custom_call_target="tpu_custom_call" | custom-call | flops 1000 | bytes 1000 | tf_op jit(solution)/shard_map/attention_back/pallas_call | solution.py:115
  542.1 20.1 %collective-permute-done.61 = f32[1,128,1024]{2,1,0:T(8,128)S(1)} collective-permute-done((f32[1,128,1024]{2,1,0:T(8,128)}, f32[1,128,1024]{2,1,0:T(8,128)S(1)}, u32[]{:S(2)}, u32[]{:S(2)}) %collective-permute-start.61) | collective-permute-done | bytes 524320 | tf_op jit(solution)/shard_map/ppermute | solution.py:135
  571.9 38.3 %collective-permute-done.62 = f32[1,128,1024]{2,1,0:T(8,128)S(1)} collective-permute-done((f32[1,128,1024]{2,1,0:T(8,128)}, f32[1,128,1024]{2,1,0:T(8,128)S(1)}, u32[]{:S(2)}, u32[]{:S(2)}) %collective-permute-start.62) | collective-permute-done | bytes 524320 | tf_op jit(solution)/shard_map/ppermute | solution.py:135
  631.2 19.2 %collective-permute-done.66 = f32[2,2048]{1,0:T(2,128)S(1)} collective-permute-done((f32[2,2048]{1,0:T(2,128)S(1)}, f32[2,2048]{1,0:T(2,128)S(1)}, u32[]{:S(2)}, u32[]{:S(2)}) %collective-permute-start.66) | collective-permute-done | bytes 16416 | tf_op jit(solution)/shard_map/ppermute | solution.py:135
  677.9 20.3 %collective-permute-done.77.refs_5_ = f32[1,128,1024]{2,1,0:T(8,128)S(1)} collective-permute-done((f32[1,128,1024]{2,1,0:T(8,128)S(1)}, f32[1,128,1024]{2,1,0:T(8,128)S(1)}, u32[]{:S(2)}, u32[]{:S(2)}) %collective-permute-start.77) | collective-permute-done | bytes 524320 | tf_op jit(solution)/shard_map/ppermute | solution.py:135
  725.9 27.4 %collective-permute-done.74 = f32[2048,256]{1,0:T(8,128)S(1)} collective-permute-done((f32[2048,256]{1,0:T(8,128)S(1)}, f32[2048,256]{1,0:T(8,128)S(1)}, u32[]{:S(2)}, u32[]{:S(2)}) %collective-permute-start.74) | collective-permute-done | bytes 2097184 | tf_op jit(solution)/shard_map/ppermute | solution.py:208
  756.0 22.5 %collective-permute-done.83.refs_5_ = f32[1,128,1024]{2,1,0:T(8,128)} collective-permute-done((f32[1,128,1024]{2,1,0:T(8,128)S(1)}, f32[1,128,1024]{2,1,0:T(8,128)}, u32[]{:S(2)}, u32[]{:S(2)}) %collective-permute-start.83) | collective-permute-done | bytes 524320 | tf_op jit(solution)/shard_map/ppermute | solution.py:135
  779.2 19.1 %collective-permute-done.75 = f32[256,2048]{1,0:T(8,128)S(1)} collective-permute-done((f32[256,2048]{1,0:T(8,128)S(1)}, f32[256,2048]{1,0:T(8,128)S(1)}, u32[]{:S(2)}, u32[]{:S(2)}) %collective-permute-start.75) | collective-permute-done | bytes 2097184 | tf_op jit(solution)/shard_map/ppermute | solution.py:208
  842.2 31.8 %collective-permute-done.89 = f32[12,2048]{1,0:T(8,128)S(1)} collective-permute-done((f32[12,2048]{1,0:T(8,128)S(1)}, f32[12,2048]{1,0:T(8,128)S(1)}, u32[]{:S(2)}, u32[]{:S(2)}) %collective-permute-start.89) | collective-permute-done | bytes 98336 | tf_op jit(solution)/shard_map/ppermute | solution.py:995
  (480 shorter events, 422.8 us)
Async XLA Ops:
  7.2 802.0 %all-reduce.3.cloned.1.call-start = ((), (), s32[]{:S(2)}) async-start(), calls=%async_computation | async-start | bytes 16777216 | tf_op jit(solution)/shard_map/psum | solution.py:953
  151.6 45.8 %collective-permute-start.23 = (f32[1,128,1024]{2,1,0:T(8,128)S(1)}, f32[1,128,1024]{2,1,0:T(8,128)S(1)}, u32[]{:S(2)}, u32[]{:S(2)}) collective-permute-start(f32[1,128,1024]{2,1,0:T(8,128)S(1)} %add.304.refs_5_), channel_id=1, source_target_pairs={{0,2},{1,3},{2,0},{3,1},{4,6},{5,7},{6,4},{7,5},{8,10},{9,11},{10,... | collective-permute-start | bytes 1572872 | tf_op jit(solution)/shard_map/ppermute | solution.py:135
  288.9 43.3 %collective-permute-start.37 = (f32[4,256,2048]{2,1,0:T(8,128)}, f32[4,256,2048]{2,1,0:T(8,128)}, u32[]{:S(2)}, u32[]{:S(2)}) collective-permute-start(f32[4,256,2048]{2,1,0:T(8,128)} %weight_grad.9), channel_id=1, source_target_pairs={{0,4},{4,0},{8,12},{12,8},{16,20},{20,16},{24,28},{28,24},{1,5},{5... | collective-permute-start | bytes 25165832 | tf_op jit(solution)/shard_map/ppermute | solution.py:883
  291.9 59.9 %collective-permute-start.40 = (f32[2,128,1024]{2,1,0:T(8,128)}, f32[2,128,1024]{2,1,0:T(8,128)S(1)}, u32[]{:S(2)}, u32[]{:S(2)}) collective-permute-start(f32[2,128,1024]{2,1,0:T(8,128)} %get-tuple-element.248), channel_id=1, source_target_pairs={{0,1},{1,0},{2,3},{3,2},{4,5},{5,4},{6,7},{7,6},{8,9},{9,8},{10,11... | collective-permute-start | bytes 3145736 | tf_op jit(solution)/shard_map/ppermute | solution.py:135
  353.1 95.5 %collective-permute-start.50 = (f32[2048,256]{1,0:T(8,128)}, f32[2048,256]{1,0:T(8,128)}, u32[]{:S(2)}, u32[]{:S(2)}) collective-permute-start(f32[2048,256]{1,0:T(8,128)} %get-tuple-element.267), channel_id=1, source_target_pairs={{0,8},{4,12},{8,16},{12,20},{16,24},{20,28},{24,0},{28,4},{1,9},{5... | collective-permute-start | bytes 6291464 | tf_op jit(solution)/shard_map/ppermute | solution.py:208
  356.7 98.8 %collective-permute-start.51 = (f32[256,2048]{1,0:T(8,128)}, f32[256,2048]{1,0:T(8,128)S(1)}, u32[]{:S(2)}, u32[]{:S(2)}) collective-permute-start(f32[256,2048]{1,0:T(8,128)} %get-tuple-element.269), channel_id=1, source_target_pairs={{0,8},{4,12},{8,16},{12,20},{16,24},{20,28},{24,0},{28,4},{1,9},{5... | collective-permute-start | bytes 6291464 | tf_op jit(solution)/shard_map/ppermute | solution.py:208
  393.1 54.4 %collective-permute-start.55 = (f32[1,128,1024]{2,1,0:T(8,128)}, f32[1,128,1024]{2,1,0:T(8,128)S(1)}, u32[]{:S(2)}, u32[]{:S(2)}) collective-permute-start(f32[1,128,1024]{2,1,0:T(8,128)} %add.321.refs_6_), channel_id=1, source_target_pairs={{0,1},{1,0},{2,3},{3,2},{4,5},{5,4},{6,7},{7,6},{8,9},{9,8},{10,11... | collective-permute-start | bytes 1572872 | tf_op jit(solution)/shard_map/ppermute | solution.py:135
  413.2 40.1 %collective-permute-start.56 = (f32[1,128,1024]{2,1,0:T(8,128)}, f32[1,128,1024]{2,1,0:T(8,128)S(1)}, u32[]{:S(2)}, u32[]{:S(2)}) collective-permute-start(f32[1,128,1024]{2,1,0:T(8,128)} %add.321.refs_6_), channel_id=1, source_target_pairs={{0,2},{1,3},{2,0},{3,1},{4,6},{5,7},{6,4},{7,5},{8,10},{9,11},{10,... | collective-permute-start | bytes 1572872 | tf_op jit(solution)/shard_map/ppermute | solution.py:135
  414.5 40.3 %collective-permute-start.53 = (f32[1,128,1024]{2,1,0:T(8,128)S(1)}, f32[1,128,1024]{2,1,0:T(8,128)S(1)}, u32[]{:S(2)}, u32[]{:S(2)}) collective-permute-start(f32[1,128,1024]{2,1,0:T(8,128)S(1)} %add.320.refs_2_), channel_id=1, source_target_pairs={{0,2},{1,3},{2,0},{3,1},{4,6},{5,7},{6,4},{7,5},{8,10},{9,11},{10,... | collective-permute-start | bytes 1572872 | tf_op jit(solution)/shard_map/ppermute | solution.py:135
  447.5 77.6 %collective-permute-start.58 = (f32[2,128,1024]{2,1,0:T(8,128)}, f32[2,128,1024]{2,1,0:T(8,128)S(1)}, u32[]{:S(2)}, u32[]{:S(2)}) collective-permute-start(f32[2,128,1024]{2,1,0:T(8,128)} %get-tuple-element.280), channel_id=1, source_target_pairs={{0,1},{1,0},{2,3},{3,2},{4,5},{5,4},{6,7},{7,6},{8,9},{9,8},{10,11... | collective-permute-start | bytes 3145736 | tf_op jit(solution)/shard_map/ppermute | solution.py:135
  448.7 77.3 %collective-permute-start.59 = (f32[2,128,1024]{2,1,0:T(8,128)}, f32[2,128,1024]{2,1,0:T(8,128)S(1)}, u32[]{:S(2)}, u32[]{:S(2)}) collective-permute-start(f32[2,128,1024]{2,1,0:T(8,128)} %get-tuple-element.282), channel_id=1, source_target_pairs={{0,2},{1,3},{2,0},{3,1},{4,6},{5,7},{6,4},{7,5},{8,10},{9,11},{10,... | collective-permute-start | bytes 3145736 | tf_op jit(solution)/shard_map/ppermute | solution.py:135
  535.6 76.1 %collective-permute-start.63 = (f32[4,256,1536]{2,1,0:T(8,128)}, f32[4,256,1536]{2,1,0:T(8,128)}, u32[]{:S(2)}, u32[]{:S(2)}) collective-permute-start(f32[4,256,1536]{2,1,0:T(8,128)} %weight_grad.13), channel_id=1, source_target_pairs={{0,4},{4,0},{8,12},{12,8},{16,20},{20,16},{24,28},{28,24},{1,5},{5... | collective-permute-start | bytes 18874376 | tf_op jit(solution)/shard_map/ppermute | solution.py:883
  540.2 83.0 %collective-permute-start.64 = (f32[2,128,1024]{2,1,0:T(8,128)}, f32[2,128,1024]{2,1,0:T(8,128)}, u32[]{:S(2)}, u32[]{:S(2)}) collective-permute-start(f32[2,128,1024]{2,1,0:T(8,128)} %get-tuple-element.298), channel_id=1, source_target_pairs={{0,1},{1,0},{2,3},{3,2},{4,5},{5,4},{6,7},{7,6},{8,9},{9,8},{10,11... | collective-permute-start | bytes 3145736 | tf_op jit(solution)/shard_map/ppermute | solution.py:135
  541.0 84.1 %collective-permute-start.65 = (f32[2,128,1024]{2,1,0:T(8,128)}, f32[2,128,1024]{2,1,0:T(8,128)}, u32[]{:S(2)}, u32[]{:S(2)}) collective-permute-start(f32[2,128,1024]{2,1,0:T(8,128)} %get-tuple-element.300), channel_id=1, source_target_pairs={{0,2},{1,3},{2,0},{3,1},{4,6},{5,7},{6,4},{7,5},{8,10},{9,11},{10,... | collective-permute-start | bytes 3145736 | tf_op jit(solution)/shard_map/ppermute | solution.py:135
  562.2 47.9 %collective-permute-start.62 = (f32[1,128,1024]{2,1,0:T(8,128)}, f32[1,128,1024]{2,1,0:T(8,128)S(1)}, u32[]{:S(2)}, u32[]{:S(2)}) collective-permute-start(f32[1,128,1024]{2,1,0:T(8,128)} %slice_add_fusion.6), channel_id=1, source_target_pairs={{0,1},{1,0},{2,3},{3,2},{4,5},{5,4},{6,7},{7,6},{8,9},{9,8},{10,11... | collective-permute-start | bytes 1572872 | tf_op jit(solution)/shard_map/ppermute | solution.py:135
  563.9 95.7 %collective-permute-start.70 = (f32[2048,256]{1,0:T(8,128)}, f32[2048,256]{1,0:T(8,128)}, u32[]{:S(2)}, u32[]{:S(2)}) collective-permute-start(f32[2048,256]{1,0:T(8,128)} %bitcast_add_fusion.5), channel_id=1, source_target_pairs={{0,8},{4,12},{8,16},{12,20},{16,24},{20,28},{24,0},{28,4},{1,9},{5... | collective-permute-start | bytes 6291464 | tf_op jit(solution)/shard_map/ppermute | solution.py:208
  610.2 52.9 %collective-permute-start.71 = (f32[256,2048]{1,0:T(8,128)}, f32[256,2048]{1,0:T(8,128)}, u32[]{:S(2)}, u32[]{:S(2)}) collective-permute-start(f32[256,2048]{1,0:T(8,128)} %bitcast_add_fusion.4), channel_id=1, source_target_pairs={{0,8},{4,12},{8,16},{12,20},{16,24},{20,28},{24,0},{28,4},{1,9},{5... | collective-permute-start | bytes 6291464 | tf_op jit(solution)/shard_map/ppermute | solution.py:208
  659.7 48.7 %collective-permute-start.73 = (f32[256,1536]{1,0:T(8,128)S(1)}, f32[256,1536]{1,0:T(8,128)S(1)}, u32[]{:S(2)}, u32[]{:S(2)}) collective-permute-start(f32[256,1536]{1,0:T(8,128)S(1)} %copy-done.84), channel_id=1, source_target_pairs={{0,8},{4,12},{8,16},{12,20},{16,24},{20,28},{24,0},{28,4},{1,9},{5... | collective-permute-start | bytes 4718600 | tf_op jit(solution)/shard_map/ppermute | solution.py:208
  663.1 90.2 %collective-permute-start.74 = (f32[2048,256]{1,0:T(8,128)S(1)}, f32[2048,256]{1,0:T(8,128)S(1)}, u32[]{:S(2)}, u32[]{:S(2)}) collective-permute-start(f32[2048,256]{1,0:T(8,128)S(1)} %bitcast_add_fusion.3), channel_id=1, source_target_pairs={{0,8},{4,12},{8,16},{12,20},{16,24},{20,28},{24,0},{28,4},{1,9},{5... | collective-permute-start | bytes 6291464 | tf_op jit(solution)/shard_map/ppermute | solution.py:208
  675.4 122.9 %collective-permute-start.75 = (f32[256,2048]{1,0:T(8,128)S(1)}, f32[256,2048]{1,0:T(8,128)S(1)}, u32[]{:S(2)}, u32[]{:S(2)}) collective-permute-start(f32[256,2048]{1,0:T(8,128)S(1)} %bitcast_add_fusion.2), channel_id=1, source_target_pairs={{0,8},{4,12},{8,16},{12,20},{16,24},{20,28},{24,0},{28,4},{1,9},{5... | collective-permute-start | bytes 6291464 | tf_op jit(solution)/shard_map/ppermute | solution.py:208
  712.0 126.9 %collective-permute-start.92 = (f32[256,1536]{1,0:T(8,128)}, f32[256,1536]{1,0:T(8,128)}, u32[]{:S(2)}, u32[]{:S(2)}) collective-permute-start(f32[256,1536]{1,0:T(8,128)} %bitcast_add_fusion.8), channel_id=1, source_target_pairs={{0,8},{4,12},{8,16},{12,20},{16,24},{20,28},{24,0},{28,4},{1,9},{5... | collective-permute-start | bytes 4718600 | tf_op jit(solution)/shard_map/ppermute | solution.py:208
  755.7 59.4 %collective-permute-start.82 = (f32[1,128,1024]{2,1,0:T(8,128)S(1)}, f32[1,128,1024]{2,1,0:T(8,128)S(1)}, u32[]{:S(2)}, u32[]{:S(2)}) collective-permute-start(f32[1,128,1024]{2,1,0:T(8,128)S(1)} %add.339.refs_3_), channel_id=1, source_target_pairs={{0,1},{1,0},{2,3},{3,2},{4,5},{5,4},{6,7},{7,6},{8,9},{9,8},{10,11... | collective-permute-start | bytes 1572872 | tf_op jit(solution)/shard_map/ppermute | solution.py:135
  756.0 82.0 %collective-permute-start.91 = (f32[512,256]{1,0:T(8,128)}, f32[512,256]{1,0:T(8,128)S(1)}, u32[]{:S(2)}, u32[]{:S(2)}) collective-permute-start(f32[512,256]{1,0:T(8,128)} %bitcast_add_fusion.11), channel_id=1, source_target_pairs={{0,8},{4,12},{8,16},{12,20},{16,24},{20,28},{24,0},{28,4},{1,9},{5... | collective-permute-start | bytes 1572872 | tf_op jit(solution)/shard_map/ppermute | solution.py:208
  841.0 57.1 %collective-permute-start.94 = (f32[256,1536]{1,0:T(8,128)S(1)}, f32[256,1536]{1,0:T(8,128)}, u32[]{:S(2)}, u32[]{:S(2)}) collective-permute-start(f32[256,1536]{1,0:T(8,128)S(1)} %bitcast_add_fusion.7), channel_id=1, source_target_pairs={{0,8},{4,12},{8,16},{12,20},{16,24},{20,28},{24,0},{28,4},{1,9},{5... | collective-permute-start | bytes 4718600 | tf_op jit(solution)/shard_map/ppermute | solution.py:208
  (166 other events, 3610.6 us)
Sparse Core Ops, SparseCore 0:
  535.9 264.3 all-reduce.2

commit v2 on v1

--- a/solution.py
+++ b/solution.py
@@ -22,6 +22,23 @@
 inv_root_two_pi = 0.3989422804014327
 masked_score = -1e30
 MEGA = 1 << 20
+
+COST = {
+    "front": 15.6,
+    "middle_norm": 7.5,
+    "hidden_back": 400.0,
+    "hidden_front": 14.7,
+    "hidden_mid": 6.0,
+    "hidden_grad": 7.0,
+    "full_grad": 15.0,
+    "attention_grads": 12.0,
+    "result_part": 400.0,
+    "middle_back": 11.0,
+    "attention_back": 21.7,
+    "tokens_back": 8.5,
+    "output": 6.0,
+}
+WORK = 5.5e+07
 
 F32 = jnp.float32
 BF16 = jnp.bfloat16
@@ -126,7 +143,7 @@
         compiler_params=pltpu.CompilerParams(
             dimension_semantics=("arbitrary",) * len(grid), vmem_limit_bytes=limit * MEGA
         ),
-        cost_estimate=pl.CostEstimate(flops=1000, bytes_accessed=1000, transcendentals=0),
+        cost_estimate=pl.CostEstimate(flops=int(COST[name] * WORK), bytes_accessed=1000, transcendentals=0),
         name=name,
     )(*prefetch, *[array for array, block, where in ins], *after)
 
@@ -135,12 +152,9 @@
     return lax.ppermute(value, "tensor", [(t, t ^ (1 << bit)) for t in range(size)])
 
 
-def gather_pieces(own, bits, order):
-    pieces = {0: own}
-    for bit in order:
-        for block in list(pieces):
-            pieces[block | 1 << bit] = flip(pieces[block], bit, 1 << bits)
-    return [pieces[block] for block in range(1 << bits)]
+def all_pieces(own, bits):
+    size = 1 << bits
+    return [own] + [lax.ppermute(own, "tensor", [(t, t ^ k) for t in range(size)]) for k in range(1, size)]
 
 
 class Line:
@@ -150,10 +164,10 @@
     def tie(self, value):
         if self.last is None:
             return value
-        return lax.optimization_barrier((value, self.last))[0]
-
-    def mark(self, value):
-        self.last = value
+        return lax.optimization_barrier((value,) + self.last)[0]
+
+    def mark(self, *values):
+        self.last = values
 
 
 class Total:
@@ -193,9 +207,27 @@
             line.mark(self.keep[half])
         self.step += 1
 
+    def gather(self):
+        size = 1 << self.bits
+        if self.step == self.bits:
+            self.held = [[0], [0]]
+            self.step += 1
+        else:
+            for half in range(2):
+                self.keep[half] = jnp.concatenate([self.line.tie(self.keep[half]), self.got[half]], 0)
+                self.line.mark(self.keep[half])
+                self.held[half] = self.held[half] + [block | self.last[half] for block in self.held[half]]
+        self.last = [1 << self.orders[half].pop() for half in range(2)]
+        self.got = [flip(self.keep[half], self.last[half].bit_length() - 1, size) for half in range(2)]
+
     def pieces(self):
-        up, down = self.orders
-        return gather_pieces(self.keep[0], self.bits, down), gather_pieces(self.keep[1], self.bits, up)
+        arrays, where = [], []
+        for half in range(2):
+            arrays += [self.keep[half], self.got[half]]
+            found = {block: (2 * half, at) for at, block in enumerate(self.held[half])}
+            found.update({block | self.last[half]: (2 * half + 1, at) for at, block in enumerate(self.held[half])})
+            where.append(found)
+        return arrays, where
 
 
 class Ring:
@@ -229,8 +261,36 @@
     return value[0]
 
 
+class Small:
+    def __init__(self, own, bits):
+        self.bits, self.bit, self.held = bits, 0, [own]
+        self.got = None
+        self.step()
+
+    def step(self):
+        if self.got is not None:
+            many = len(self.held)
+            self.held = self.held + [self.got[at] for at in range(many)]
+        if self.bit < self.bits:
+            self.got = flip(jnp.stack(self.held), self.bit, 1 << self.bits)
+            self.bit += 1
+
+    def pieces(self):
+        while len(self.held) < 1 << self.bits:
+            self.step()
+        return self.held
+
+
+def both_vectors(pieces):
+    level = [piece[8:] for piece in pieces]
+    while len(level) > 1:
+        level = [level[at] + level[at + 1] for at in range(0, len(level), 2)]
+    many = D // level[0].shape[1]
+    return jnp.stack([level[0][:many].reshape(-1), level[0][4 : 4 + many].reshape(-1)])
+
+
 def combine(pieces, block, blocks):
-    level = [pieces[other][:, (block ^ other) * SLOT : (block ^ other) * SLOT + SLOT] for other in range(blocks)]
+    level = [pieces[other][:8, (block ^ other) * SLOT : (block ^ other) * SLOT + SLOT] for other in range(blocks)]
     while len(level) > 1:
         level = [level[at] + level[at + 1] for at in range(0, len(level), 2)]
     return level[0]
@@ -289,16 +349,20 @@
     groups = width // 128
     rows = blocks * SLOT
 
-    def kernel(order_ref, length_ref, x0, x1, g, b, w, wb, tab, msk, mg, uwr, ow, own, first, qkv, mixed, sums, uw, *parts):
+    def kernel(order_ref, length_ref, x0, x1, g, b, w, wb, tab, msk, mg, uwr, ow, own, first, qkv, mixed, small, *parts_uw):
         step = pl.program_id(0)
+        parts, uw = parts_uw[:4], parts_uw[4]
 
         @pl.when(step == 0)
         def _():
             found = mul(uwr[...], ow[...])
-            uw[...] = jnp.concatenate(
-                [found[0:1] + found[1:2] + found[2:3], found[3:4] + found[4:5] + found[5:6], found[6:8], jnp.zeros((4, D), F32)],
-                axis=0,
-            )
+            uw[0:1] = found[0:1] + found[1:2] + found[2:3]
+            uw[1:2] = found[3:4] + found[4:5] + found[5:6]
+            small[8:] = jnp.zeros((8, rows), F32)
+            for at in range(D // rows):
+                c = slice(at * rows, at * rows + rows)
+                small[8 + at : 9 + at] = uw[0:1, c]
+                small[12 + at : 13 + at] = uw[1:2, c]
 
         x = jnp.concatenate([x0[0], x1[0]], axis=0)
         own[...] = x
@@ -325,7 +389,8 @@
                 mixed[r, at : at + 128] = mul(rounded(jnp.concatenate(probs, axis=1)), values)
         m = mixed[...]
         total = jnp.sum(m, axis=-1, keepdims=True)
-        sums[...] = rows_of([total, jnp.sum(m * m, axis=-1, keepdims=True)])
+        here = pl.ds(pl.multiple_of(step * 2 * SLOT, 2 * SLOT), 2 * SLOT)
+        small[:8, here] = rows_of([total, jnp.sum(m * m, axis=-1, keepdims=True)])
         middle = total * (1.0 / width)
         partial = mul(rounded((m - middle) * mg[...]), ow[...]) + middle * uw[0:1]
         store_parts(parts, partial, step, steps)
@@ -346,10 +411,10 @@
             ((rows, D), BF16, (2 * SLOT, D), row2),
             ((rows, 3 * width), BF16, (2 * SLOT, 3 * width), row2),
             ((rows, width), F32, (2 * SLOT, width), row2),
-            ((8, rows), F32, (8, 2 * SLOT), lambda s, *_: (0, s)),
-            ((8, D), F32, (8, D), lambda s, *_: (0, 0)),
+            ((16, rows), F32, (16, rows), lambda s, *_: (0, 0)),
         ]
         + part_outs(blocks),
+        scratch=[pltpu.VMEM((8, D), F32)],
         prefetch=(order, lengths),
         after=after,
         name="front",
@@ -357,27 +422,28 @@
 
 
 def pieces_in(pieces):
-    return [whole(piece) for half in pieces for piece in half]
-
-
-def load_pieces(refs, total, step, blocks):
+    return [whole(piece) for piece in pieces[0]]
+
+
+def load_pieces(refs, where, total, step, blocks):
     for block in range(blocks):
 
         @pl.when(step == block)
         def _(block=block):
-            total[:, :HALF] = refs[block][0]
-            total[:, HALF:] = refs[blocks + block][0]
+            for half in range(2):
+                array, at = where[half][block]
+                total[:, half * HALF : half * HALF + HALF] = refs[array][at]
 
 
 def middle_norm(own, pieces, sums, uw, out_bias, gain, shift, after=()):
-    blocks = len(pieces[0])
+    blocks = len(pieces[1][0])
     rows = blocks * SLOT
 
     def kernel(*refs):
-        x, parts, stats = refs[0], refs[1 : 1 + 2 * blocks], refs[1 + 2 * blocks : 1 + 3 * blocks]
-        uw_ref, bias, g, b, mid, second, stat, total, tot8 = refs[1 + 3 * blocks :]
+        x, parts, stats = refs[0], refs[1:5], refs[5 : 5 + blocks]
+        uw_ref, bias, g, b, mid, second, stat, total, tot8 = refs[5 + blocks :]
         step = pl.program_id(0)
-        load_pieces(parts, total, step, blocks)
+        load_pieces(parts, pieces[1], total, step, blocks)
         for block in range(blocks):
 
             @pl.when(step == block)
@@ -414,31 +480,31 @@
     )
 
 
-def hidden_back(cot, down_weight, after=()):
-    rows, units = cot.shape[0], down_weight.shape[0]
+def hidden_back(cots, down_weight):
+    many, rows, units = len(cots), cots[0].shape[0], down_weight.shape[0]
     tile = min(512, units)
 
-    def kernel(c, w, out):
-        out[...] = rounded(mul(c[...], w[...], NT))
+    def kernel(*refs):
+        w, out = refs[many:]
+        for at in range(many):
+            out[at * rows : at * rows + rows] = rounded(mul(refs[at][...], w[...], NT))
 
     return run(
         kernel,
         (units // tile,),
-        [whole(cot), (down_weight, (tile, D), lambda j: (j, 0))],
-        [((rows, units), BF16, (rows, tile), lambda j: (0, j))],
-        after=after,
+        [whole(cot) for cot in cots] + [(down_weight, (tile, D), lambda j: (j, 0))],
+        [((many * rows, units), BF16, (many * rows, tile), lambda j: (0, j))],
         name="hidden_back",
     )[0]
 
 
 def hidden_front(chunk, second, up_weight, up_bias, back, gain, after=()):
     rows, units = second.shape[0], up_weight.shape[1]
-    tile = 256
+    tile = 512
     steps = units // tile
 
-    def kernel(s_ref, w, b, hb, g, act, slp, sums, acc):
-        step = pl.program_id(0)
-        hidden = mul(s_ref[...], w[...]) + b[...]
+    def part_of(c, s_ref, w, b, hb, g, act, slp):
+        hidden = mul(s_ref[...], w[:, c]) + b[:, c]
         tail = jnp.exp(-0.5 * hidden * hidden)
         t = 1.0 / (1.0 + (0.3275911 * root_half) * jnp.abs(hidden))
         poly = 1.061405429 * t - 1.453152027
@@ -448,19 +514,24 @@
         half = 0.5 * poly * t * tail
         phi = jnp.where(hidden >= 0.0, 1.0 - half, half)
         active = hidden * phi
-        act[...] = rounded(active)
-        slp[...] = rounded(phi + hidden * (inv_root_two_pi * tail))
-        scaled = hb[...].astype(F32) * g[...]
-        for at, value in enumerate((active, active * active, scaled, scaled * active)):
-            part = value[:, :128] + value[:, 128:]
-
-            @pl.when(step == 0)
-            def _():
-                acc[at] = part
-
-            @pl.when(step > 0)
-            def _():
-                acc[at] += part
+        act[:, c] = rounded(active)
+        slp[:, c] = rounded(phi + hidden * (inv_root_two_pi * tail))
+        scaled = hb[:, c].astype(F32) * g[:, c]
+        return [value[:, :128] + value[:, 128:] for value in (active, active * active, scaled, scaled * active)]
+
+    def kernel(s_ref, w, b, hb, g, act, slp, sums, acc):
+        step = pl.program_id(0)
+        found = [part_of(slice(at, at + 256), s_ref, w, b, hb, g, act, slp) for at in range(0, tile, 256)]
+
+        @pl.when(step == 0)
+        def _():
+            for at in range(4):
+                acc[at] = found[0][at] + found[1][at]
+
+        @pl.when(step > 0)
+        def _():
+            for at in range(4):
+                acc[at] += found[0][at] + found[1][at]
 
         @pl.when(step == steps - 1)
         def _():
@@ -489,42 +560,67 @@
     )
 
 
-def hidden_grad(chunk, active, slope, back, sums, gain, shift, up_weight, after=()):
+def hidden_mid(chunk, active, slope, back, sums, gain, shift):
     blocks = len(sums)
     rows, units = active.shape
+
+    def kernel(act, slp, hb, *refs):
+        stats = refs[:blocks]
+        g, b, low, grad, vecs, tot8 = refs[blocks:]
+        step = pl.program_id(0)
+        for block in range(blocks):
+
+            @pl.when(step == block)
+            def _(block=block):
+                tot8[...] = combine(stats, block, blocks)
+
+        cols = columns_of(tot8[...]) * (1.0 / FF)
+        mean = cols[:, 0:1]
+        inverse = lax.rsqrt(cols[:, 1:2] - mean * mean + eps)
+        one = cols[:, 2:3]
+        two = inverse * (cols[:, 3:4] - mean * one)
+        for at in range(0, units, 256):
+            c = slice(at, at + 256)
+            hat = (act[:, c].astype(F32) - mean) * inverse
+            low[:, c] = rounded(hat * g[:, c] + b[:, c])
+            raw = hb[:, c].astype(F32)
+            grown = rounded(inverse * (raw * g[:, c] - one - hat * two) * slp[:, c].astype(F32))
+            grad[:, c] = grown
+            vecs[0, 0:1, c] = sum_rows(raw * hat)
+            vecs[0, 1:2, c] = sum_rows(raw)
+            vecs[0, 2:3, c] = sum_rows(grown.astype(F32))
+
+    row = lambda k: (k, 0)
+    return run(
+        kernel,
+        (blocks,),
+        [
+            (active, (SLOT, units), row),
+            (slope, (SLOT, units), row),
+            (back, (SLOT, units), lambda k: (chunk * blocks + k, 0)),
+        ]
+        + [whole(part) for part in sums]
+        + [whole(gain), whole(shift)],
+        [
+            ((rows, units), BF16, (SLOT, units), row),
+            ((rows, units), BF16, (SLOT, units), row),
+            ((blocks, 8, units), F32, (1, 8, units), lambda k: (k, 0, 0)),
+        ],
+        scratch=[pltpu.VMEM((8, SLOT), F32)],
+        name="hidden_mid",
+    )
+
+
+def hidden_grad(grad, up_weight):
+    rows, units = grad.shape
+    blocks = rows // SLOT
     tile = 256
     steps = D // tile
     half = steps // 2
 
-    def kernel(act, slp, hb, *refs):
-        stats = refs[:blocks]
-        g, b, w, low, grad, vecs, left_keep, left_send, right_keep, right_send, acc = refs[blocks:]
+    def kernel(gr, w, left_keep, left_send, right_keep, right_send):
         step = pl.program_id(0)
-
-        @pl.when(step == 0)
-        def _():
-            for block in range(blocks):
-                r = slice(block * SLOT, block * SLOT + SLOT)
-                cols = columns_of(combine(stats, block, blocks)) * (1.0 / FF)
-                mean = cols[:, 0:1]
-                inverse = lax.rsqrt(cols[:, 1:2] - mean * mean + eps)
-                one = cols[:, 2:3]
-                two = inverse * (cols[:, 3:4] - mean * one)
-                for at in range(0, units, 512):
-                    c = slice(at, at + 512)
-                    hat = (act[r, c].astype(F32) - mean) * inverse
-                    low[r, c] = rounded(hat * g[:, c] + b[:, c])
-                    raw = hb[r, c].astype(F32)
-                    grown = rounded(inverse * (raw * g[:, c] - one - hat * two) * slp[r, c].astype(F32))
-                    grad[r, c] = grown
-                    found = [sum_rows(raw * hat), sum_rows(raw), sum_rows(grown.astype(F32))]
-                    for i, value in enumerate(found):
-                        if block == 0:
-                            vecs[i : i + 1, c] = value
-                        else:
-                            vecs[i : i + 1, c] += value
-
-        value = mul(grad[...], w[...], NT)
+        value = mul(gr[...], w[...], NT)
 
         @pl.when(step < half)
         def _():
@@ -542,54 +638,53 @@
     block_shape = (blocks // 2, SLOT, tile)
     lefts = lambda j: (0, 0, jnp.minimum(j, half - 1))
     rights = lambda j: (0, 0, jnp.maximum(j - half, 0))
-    fixed = lambda j: (0, 0)
     return run(
         kernel,
         (steps,),
-        [whole(active), whole(slope), (back, (rows, units), lambda j: (chunk, 0))]
-        + [whole(part) for part in sums]
-        + [whole(gain), whole(shift), (up_weight, (tile, units), lambda j: (j, 0))],
+        [whole(grad), (up_weight, (tile, units), lambda j: (j, 0))],
         [
-            ((rows, units), BF16, (rows, units), fixed),
-            ((rows, units), BF16, (rows, units), fixed),
-            ((8, units), F32, (8, units), fixed),
             (shape, F32, block_shape, lefts),
             (shape, F32, block_shape, lefts),
             (shape, F32, block_shape, rights),
             (shape, F32, block_shape, rights),
         ],
-        scratch=[pltpu.VMEM((8, 128), F32)],
-        after=after,
         name="hidden_grad",
     )
 
 
-def result_part(order, lows, down_weight, after=()):
-    blocks = order.shape[0]
+def result_part(order, lows, down_weight):
+    pairs = order.shape[0]
     units = down_weight.shape[0]
-
-    def kernel(order_ref, low, w, out):
-        out[0] = mul(low[...], w[...])
+    many = len(lows)
+    rows = lows[0].shape[0]
+    each = rows // SLOT
+    tile = 256
+
+    def kernel(order_ref, *refs):
+        w, out = refs[many:]
+        for at in range(many):
+            value = mul(refs[at][...], w[...])
+            for block in range(each):
+                out[order_ref[at * each + block]] = value[block * SLOT : block * SLOT + SLOT]
 
     return run(
         kernel,
-        (blocks,),
-        [(lows, (SLOT, units), lambda k, *_: (k, 0)), whole(down_weight)],
-        [((blocks, SLOT, D), F32, (1, SLOT, D), lambda k, o: (o[k], 0, 0))],
+        (D // tile,),
+        [whole(low) for low in lows] + [(down_weight, (units, tile), lambda j, *_: (0, j))],
+        [((pairs, SLOT, D), F32, (pairs, SLOT, tile), lambda j, *_: (0, 0, j))],
         prefetch=(order,),
-        after=after,
         name="result_part",
     )[0]
 
 
 def middle_back(own, cot, pieces, middle, stat, uw, out_bias, gain, after=()):
-    blocks = len(pieces[0])
+    blocks = len(pieces[1][0])
     rows = blocks * SLOT
 
     def kernel(*refs):
-        x, c, parts = refs[0], refs[1], refs[2 : 2 + 2 * blocks]
-        mid, st, uw_ref, bias, g, grad, low, stat2, vecs, total = refs[2 + 2 * blocks :]
-        load_pieces(parts, total, pl.program_id(0), blocks)
+        x, c, parts = refs[0], refs[1], refs[2:6]
+        mid, st, uw_ref, bias, g, grad, low, stat2, vecs, total = refs[6:]
+        load_pieces(parts, pieces[1], total, pl.program_id(0), blocks)
         value = mid[...]
         hat, inverse = norm_parts(value)
         sec = total[...]
@@ -716,13 +811,13 @@
 
 
 def tokens_back(order, own, grad, pieces, gain, before, pairs, after=()):
-    blocks = len(pieces[0])
+    blocks = len(pieces[1][0])
 
     def kernel(order_ref, x, gr, *refs):
-        parts = refs[: 2 * blocks]
-        g = refs[2 * blocks]
+        parts = refs[:4]
+        g = refs[4]
         out, total = refs[-2:]
-        load_pieces(parts, total, pl.program_id(0), blocks)
+        load_pieces(parts, pieces[1], total, pl.program_id(0), blocks)
         hat, inverse = norm_parts(x[...].astype(F32))
         scaled = total[...] * g[...]
         out[0] = gr[...] + inverse * (
@@ -778,39 +873,44 @@
     )[0]
 
 
-def weight_grad(ids, lefts, rights, left_blocked, got=None):
-    count = ids.shape[0]
-    rows = lefts[0].shape[0]
-    many = len(lefts)
-    wide, tall = lefts[0].shape[1], rights[0].shape[1]
+def attention_grads(ids, firsts, dprojs, lows, mixes, got=None):
+    count, many = ids.shape[0], len(firsts)
+    rows = firsts[0].shape[0]
+    wide, tall = dprojs[0].shape[1], mixes[0].shape[1]
     block = D // (2 * count)
-    shape = (block, tall) if left_blocked else (wide, block)
+    shape = (block, wide + tall)
 
     def kernel(ids_ref, *refs):
-        left, right = refs[:many], refs[many : 2 * many]
-        outs = refs[2 * many + (got is not None) :]
-        value = mul(left[0][...], right[0][...], TN)
-        for at in range(1, many):
-            value += mul(left[at][...], right[at][...], TN)
+        parts = [refs[at * many : (at + 1) * many] for at in range(4)]
+        outs = refs[4 * many + (got is not None) :]
+        total = []
+        for left, right in ((parts[0], parts[1]), (parts[2], parts[3])):
+            value = mul(left[0][...], right[0][...], TN)
+            for at in range(1, many):
+                value += mul(left[at][...], right[at][...], TN)
+            total.append(value)
         if got is None:
-            outs[0][0] = value
+            outs[0][0, :, :wide] = total[0]
+            outs[0][0, :, wide:] = total[1]
             return
-        value += refs[2 * many][0]
+        more = refs[4 * many]
         step = pl.program_id(0)
 
         @pl.when(step == 0)
         def _():
-            outs[0][...] = value
+            outs[0][:, :wide] = total[0] + more[0, :, :wide]
+            outs[0][:, wide:] = total[1] + more[0, :, wide:]
 
         @pl.when(step > 0)
         def _():
-            outs[1][0] = value
+            outs[1][0, :, :wide] = total[0] + more[0, :, :wide]
+            outs[1][0, :, wide:] = total[1] + more[0, :, wide:]
 
     fixed = lambda i, *_: (0, 0)
     moving = lambda i, ids_ref: (0, ids_ref[i])
     lead = lambda i, *_: (i, 0, 0)
-    ins = [(left, (rows, block), moving) if left_blocked else (left, (rows, wide), fixed) for left in lefts]
-    ins += [(right, (rows, tall), fixed) if left_blocked else (right, (rows, block), moving) for right in rights]
+    ins = [(left, (rows, block), moving) for left in firsts] + [(right, (rows, wide), fixed) for right in dprojs]
+    ins += [(left, (rows, block), moving) for left in lows] + [(right, (rows, tall), fixed) for right in mixes]
     if got is None:
         outs = [((count,) + shape, F32, (1,) + shape, lead)]
     else:
@@ -819,7 +919,45 @@
             (shape, F32, shape, fixed),
             ((count - 1,) + shape, F32, (1,) + shape, lambda i, *_: (jnp.maximum(i - 1, 0), 0, 0)),
         ]
-    return run(kernel, (count,), ins, outs, prefetch=(ids,), name="weight_grad")
+    return run(kernel, (count,), ins, outs, prefetch=(ids,), name="attention_grads")
+
+
+def full_grad(lefts, rights):
+    rows, many, block = lefts[0].shape[0], len(lefts), 512
+    wide, tall = lefts[0].shape[1], rights[0].shape[1]
+
+    def kernel(*refs):
+        left, right, out = refs[:many], refs[many : 2 * many], refs[2 * many]
+        value = mul(left[0][...], right[0][...], TN)
+        for at in range(1, many):
+            value += mul(left[at][...], right[at][...], TN)
+        out[...] = value
+
+    ins = [(left, (rows, block), lambda i: (0, i)) for left in lefts]
+    ins += [(right, (rows, tall), lambda i: (0, 0)) for right in rights]
+    return run(
+        kernel, (wide // block,), ins, [((wide, tall), F32, (block, tall), lambda i: (i, 0))], name="full_grad"
+    )[0]
+
+
+def steps_of(totals, bits, done, until):
+    done = list(done)
+
+    def step(at):
+        if done[at] < bits:
+            totals[at].advance()
+        else:
+            totals[at].gather()
+        done[at] += 1
+        if done[at] == bits and until == 2 * bits:
+            totals[at].gather()
+            done[at] += 1
+
+    limits = [until] + [until if until == 2 * bits else bits - 1] * (len(totals) - 1)
+    while any(have < limit for have, limit in zip(done, limits)):
+        for at in range(len(totals)):
+            if done[at] < limits[at]:
+                step(at)
 
 
 def split_rows(value):
@@ -877,80 +1015,105 @@
     around = lax.rem(place // 2 + count - 1 - jnp.arange(count, dtype=jnp.int32), count)
     mine_ids, other_ids = 2 * around + lax.rem(place, 2), 2 * around + 1 - lax.rem(place, 2)
 
-    def send_half(lefts, rights, left_blocked):
-        sent = weight_grad(other_ids, [line.tie(lefts[0])] + lefts[1:], rights, left_blocked)[0]
-        line.mark(sent)
-        return lax.ppermute(sent, "dp", [(d, d ^ 1) for d in range(dp_size)])
-
-    def keep_half(lefts, rights, left_blocked, got):
-        first, rest = weight_grad(mine_ids, [line.tie(lefts[0])] + lefts[1:], rights, left_blocked, got)
-        line.mark(rest)
-        return Ring(line, first, rest, dp_size)
+    def full(lefts, rights):
+        grad = full_grad([line.tie(lefts[0])] + lefts[1:], rights)
+        line.mark(grad)
+        return grad
+
+    every = lambda items, name: [item[name] for item in items]
 
     ones, twos, threes = [], [], []
-    up_order = list(range(bits))
     for c in range(chunks):
         found = front(
             orders[c], lengths, line.tie(tokens3), pre_gain, pre_shift, qkv_weight, qkv_bias, tables, mask, mix_gain, uw_rows,
             out_weight,
         )
-        own, first, qkv, mixed, sums, uw = found[:6]
-        line.mark(sums)
+        own, first, qkv, mixed, small = found[:5]
+        one = dict(own=own, first=first, qkv=qkv, mixed=mixed, parts=found[5:])
+        line.mark(small)
+        one["small"] = small
         if c == 0:
-            uw_total = butterfly(uw, bits)
-        one = dict(own=own, first=first, qkv=qkv, mixed=mixed, parts=found[6:])
-        one["sums"] = gather_pieces(sums, bits, up_order)
-        if c == 0:
-            one["branch"] = Total(line, one["parts"], bits)
+            one["total"] = Total(line, one["parts"], bits)
+            one["sums"] = Small(small, bits)
         ones.append(one)
+    sums0 = ones[0]["sums"]
+    if bits > 1:
+        ones[0]["total"].advance()
+    for c in range(1, chunks):
+        ones[c]["total"] = Total(line, [line.tie(part) for part in ones[c]["parts"]], bits)
+    sums0.held[0] = line.tie(sums0.held[0])
+    sums0.step()
     cot3 = cotangent.reshape(pairs, SLOT, D)
-    cot_own = line.tie(cot3)[jnp.concatenate(orders)].reshape(chunks, -1, D)
-    cots = [cot_own[c] for c in range(chunks)]
-    back = hidden_back(cot_own.reshape(-1, D), down_weight)
+    cots = []
+    for c in range(chunks):
+        cots.append(line.tie(cot3)[orders[c]].reshape(-1, D))
+        line.mark(cots[-1])
+    totals = every(ones, "total")
+    for step in range(1, bits):
+        totals[0].advance()
+    back = hidden_back([line.tie(cots[0])] + cots[1:], down_weight)
     line.mark(back)
+    for one in ones[1:]:
+        one["sums"] = Small(line.tie(one["small"]), bits)
+    done = [bits] + [0] * (chunks - 1)
+    steps_of(totals, bits, done, 2 * bits - 1)
+    for one in ones[1:]:
+        line.mark(*line.last, one["sums"].got)
+        one["sums"].step()
+    uw_total = both_vectors(sums0.pieces())
+
     for c in range(chunks):
         one = ones[c]
-        if c > 0:
-            one["branch"] = Total(line, [line.tie(part) for part in one["parts"]], bits)
-        for step in range(bits):
-            one["branch"].advance()
-        one["pieces"] = one["branch"].pieces()
-
-    for c in range(chunks):
-        one = ones[c]
+        if c == 0:
+            totals[0].gather()
+            for total in totals[1:]:
+                total.advance()
+                total.gather()
+            for other in ones[1:]:
+                line.mark(*line.last, *other["sums"].pieces())
         mid, second, stat = middle_norm(
-            line.tie(one["own"]), one["pieces"], one["sums"], uw_total, out_bias, ffn_gain, ffn_shift
+            line.tie(one["own"]), totals[c].pieces(), one["sums"].pieces(), uw_total, out_bias, ffn_gain, ffn_shift
         )
         line.mark(stat)
+        if c == 0:
+            for total in totals[1:]:
+                for step in range(1, bits):
+                    total.gather()
+        else:
+            line.mark(stat, *twos[c - 1]["sums"][1:])
         active, slope, sums = hidden_front(c, line.tie(second), up_weight, up_bias, back, hid_gain)
         line.mark(sums)
-        twos.append(
-            dict(middle=mid, second=second, stat=stat, active=active, slope=slope, sums=gather_pieces(sums, bits, up_order))
-        )
+        twos.append(dict(middle=mid, second=second, stat=stat, active=active, slope=slope, sums=all_pieces(sums, bits)))
     for c in range(chunks):
         two = twos[c]
-        found = hidden_grad(c, line.tie(two["active"]), two["slope"], back, two["sums"], hid_gain, hid_shift, up_weight)
-        line.mark(found[2])
-        two.update(low=found[0], grad=found[1], vecs=found[2], parts=found[3:])
-        two["total"] = Total(line, two["parts"], bits)
-    every = lambda items, name: [item[name] for item in items]
-    down_args = (every(twos, "low"), cots, False)
-    up_args = (every(twos, "second"), every(twos, "grad"), True)
-    down_got = send_half(*down_args)
-    up_got = send_half(*up_args)
-    twos[0]["total"].advance()
-    down_ring = keep_half(*down_args, down_got)
-    up_ring = keep_half(*up_args, up_got)
+        low, grad, vecs = hidden_mid(c, line.tie(two["active"]), two["slope"], back, two["sums"], hid_gain, hid_shift)
+        two.update(low=low, grad=grad, vecs=functools.reduce(jnp.add, [vecs[k] for k in range(blocks)]))
+        line.mark(vecs)
+    lows = every(twos, "low")
+    down_grad = full(lows, cots)
+    down_part = lax.psum_scatter(down_grad, "dp", scatter_dimension=1, tiled=True)
+    up_grad = full(every(twos, "second"), every(twos, "grad"))
+    up_part = lax.psum_scatter(up_grad, "dp", scatter_dimension=0, tiled=True)
+    parts = []
+    for two in twos:
+        parts.append(hidden_grad(line.tie(two["grad"]), up_weight))
+        line.mark(parts[-1][0])
+        if not totals[1:] or two is twos[0]:
+            twos[0]["total"] = Total(line, parts[0], bits)
+    for step in range(bits):
+        twos[0]["total"].advance()
+    twos[0]["total"].gather()
+    for c in range(1, chunks):
+        twos[c]["total"] = Total(line, [line.tie(part) for part in parts[c]], bits)
+    totals = every(twos, "total")
     for step in range(1, bits):
-        twos[0]["total"].advance()
-    twos[0]["pieces"] = twos[0]["total"].pieces()
-    for c in range(1, chunks):
-        for step in range(bits):
-            twos[c]["total"].advance()
-        twos[c]["pieces"] = twos[c]["total"].pieces()
-    result = result_part(jnp.concatenate(orders), line.tie(jnp.concatenate(every(twos, "low"), 0)), down_weight)
+        totals[0].gather()
+    result = result_part(jnp.concatenate(orders), [line.tie(lows[0])] + lows[1:], down_weight)
     line.mark(result)
-    result = lax.psum(result, "tensor")
+    steps_of(totals, bits, [2 * bits] + [0] * (chunks - 1), 2 * bits)
+    result = lax.psum(line.tie(result), "tensor")
+    for two in twos:
+        two["pieces"] = two["total"].pieces()
 
     for c in range(chunks):
         one, two = ones[c], twos[c]
@@ -968,52 +1131,76 @@
         three["wide"] = tree_sum(found[3])
         three["total"] = Total(line, found[4:], bits)
         threes.append(three)
-        if c == 0:
-            down_ring.advance()
-            up_ring.advance()
-
-    out_args = (every(threes, "mix_low"), every(threes, "low"), False)
-    qkv_args = (every(ones, "first"), every(threes, "dproj"), True)
-    out_got = send_half(*out_args)
-    threes[0]["total"].advance()
-    qkv_got = send_half(*qkv_args)
-    out_ring = keep_half(*out_args, out_got)
+
+    first, last = threes[0]["total"], threes[-1]["total"]
+    if chunks > 1:
+        first.advance()
+    add = lambda items, name, size: functools.reduce(jnp.add, [item[name] for item in items])[:size]
+    pad = lambda v: jnp.pad(v, ((0, 0), (0, D - v.shape[1])))
+    wide = add(threes, "wide", 2)
+    got = flip(wide, 0, blocks)
+    grads_of = lambda ids, sent: attention_grads(
+        ids, [line.tie(ones[0]["first"])] + every(ones, "first")[1:], every(threes, "dproj"), every(threes, "low"),
+        every(threes, "mix_low"), sent,
+    )
+    sent = grads_of(other_ids, None)[0]
+    line.mark(sent)
+    sent = lax.ppermute(sent, "dp", [(d, d ^ 1) for d in range(dp_size)])
+    for step in range(1 if chunks > 1 else 0, bits):
+        first.advance()
+    first.gather()
+    line.mark(*line.last, down_part)
+    ring_first, ring_rest = grads_of(mine_ids, sent)
+    line.mark(ring_rest)
+    ring = Ring(line, ring_first, ring_rest, dp_size)
+    for bit in range(1, bits):
+        wide = line.tie(wide) + got
+        got = flip(wide, bit, blocks)
+        line.mark(wide)
+    if chunks > 1:
+        last.advance()
     for step in range(1, bits):
-        threes[0]["total"].advance()
-    threes[0]["pieces"] = threes[0]["total"].pieces()
-    qkv_ring = keep_half(*qkv_args, qkv_got)
-    for c in range(1, chunks):
-        threes[c]["total"].advance()
-
-    add = lambda items, name, size: functools.reduce(jnp.add, [item[name] for item in items])[:size]
-    hid_vecs, mid_vecs, narrow = add(twos, "vecs", 3), add(threes, "vecs", 4), add(threes, "narrow", 3)
-    wide = butterfly(line.tie(add(threes, "wide", 2)), bits)
-    line.mark(wide)
-    pad = lambda v: jnp.pad(v, ((0, 0), (0, D - v.shape[1])))
-    vecs = jnp.concatenate([pad(hid_vecs), mid_vecs, pad(narrow), wide], 0)
-    for bit in range(dp_size.bit_length() - 1):
-        vecs = vecs + lax.ppermute(vecs, "dp", [(d, d ^ (1 << bit)) for d in range(dp_size)])
-    hid_vecs, mid_vecs, narrow, wide = vecs[:3], vecs[3:7], vecs[7:10], vecs[10:12]
-    for c in range(1, chunks):
+        first.gather()
+    wide = line.tie(wide) + got
+    vecs = jnp.concatenate([pad(add(twos, "vecs", 3)), add(threes, "vecs", 4), pad(add(threes, "narrow", 3)), wide], 0)
+    line.mark(vecs)
+    hop = lambda v, bit: lax.ppermute(v, "dp", [(d, d ^ (1 << bit)) for d in range(dp_size)])
+    dp_bits = dp_size.bit_length() - 1
+    got = hop(vecs, 0)
+    if chunks > 1:
         for step in range(1, bits):
-            threes[c]["total"].advance()
-        threes[c]["pieces"] = threes[c]["total"].pieces()
-    for step in range(1, count - 1):
-        down_part, up_part = down_ring.advance(), up_ring.advance()
-        if step == 1:
-            out_ring.advance()
-            qkv_ring.advance()
+            last.advance()
+        last.gather()
+        line.mark(*line.last, *last.got)
+    vecs = line.tie(vecs) + got
+    line.mark(vecs)
+    got = hop(vecs, 1)
+    attention_part = ring.advance()
     tokens_grad, output = None, None
     for c in range(chunks):
         tokens_grad = tokens_back(
-            orders[c], line.tie(ones[c]["own"]), threes[c]["grad"], threes[c]["pieces"], pre_gain, tokens_grad, pairs
+            orders[c], line.tie(ones[c]["own"]), threes[c]["grad"], threes[c]["total"].pieces(), pre_gain, tokens_grad, pairs
         )
         line.mark(tokens_grad)
+        if c == 0:
+            if chunks > 1:
+                for step in range(1, bits):
+                    last.gather()
+    for bit in range(2, dp_bits):
+        vecs = line.tie(vecs) + got
+        line.mark(vecs)
+        got = hop(vecs, bit)
+        attention_part = ring.advance()
+    line.mark(attention_part, up_part)
+    for step in range(dp_bits - 1, count - 1):
+        attention_part = ring.advance()
+    vecs = vecs + got
+    hid_vecs, mid_vecs, narrow, wide = vecs[:3], vecs[3:7], vecs[7:10], vecs[10:12]
+    for c in range(chunks):
         output = output_of(orders[c], line.tie(twos[c]["middle"]), result, down_bias, output)
         line.mark(output)
-    for step in range(1, count - 1):
-        out_part, qkv_part = out_ring.advance(), qkv_ring.advance()
-    qkv_part = jnp.swapaxes(qkv_part.reshape(-1, 3, width), 0, 1)
+    qkv_part = jnp.swapaxes(attention_part[:, : 3 * width].reshape(-1, 3, width), 0, 1)
+    out_part = jnp.transpose(attention_part[:, 3 * width :])
     units = hid_gain.shape[1]
     return (
         output.reshape(-1, D),

time: 920 us -> 788 us (0.86)
  waiting for transfers between devices: 420 us -> 333 us
  Pallas kernels: 314 us -> 290 us
  starting transfers between devices: 92.8 us -> 75.6 us
  other arithmetic: 46.1 us -> 29.2 us
  local copies, waits for them, and re-layouts: 20.7 us -> 33.5 us
    ppermute x12 -> x3, waiting for transfers between devices: 81 us -> 13.6 us  [send(): lax.ppermute(value, 'dp', [(d, (d + 2) % self.size) for d in range(self.s...]
    ppermute x76 -> x54, waiting for transfers between devices: 302 us -> 271 us  [flip(): lax.ppermute(value, 'tensor', [(t, t ^ 1 << bit) for t in range(size)])]
    pallas_call x26 -> x24, Pallas kernels: 314 us -> 290 us  [run(): pl.pallas_call(body, grid_spec=pltpu.PrefetchScalarGridSpec(num_scalar_pr...]
    add x12 -> x3, other arithmetic: 25.5 us -> 7.57 us  [advance(): value = self.line.tie(self.rest)[self.step] + self.got]
    ppermute x76 -> x54, starting transfers between devices: 73.5 us -> 61 us  [flip(): lax.ppermute(value, 'tensor', [(t, t ^ 1 << bit) for t in range(size)])]
    ppermute x7 -> x10, waiting for transfers between devices: 36.1 us -> 48.5 us  [the longest x3 48.5 us: body(): lax.ppermute(v, 'dp', [(d, d ^ 1 << bit) for d in range(dp_size)])]
  transfers between devices with their start and end apart: 96 -> 70, of which waited for: 39 -> 30; matrix products, arithmetic and copies ran while one was open for 6% -> 6% of each run, Pallas kernels for 29% -> 29%
where the time goes in v2:
time: 788 us; the launch traced here: 778 us
  waiting for transfers between devices  333 us (42%)
  Pallas kernels  290 us (37%)
  starting transfers between devices  75.6 us (10%)
  local copies, waits for them, and re-layouts  33.5 us (4%)
  other arithmetic  29.2 us (4%)
  between operations  17.1 us (2%)
    pallas_call x24, Pallas kernels, run(): pl.pallas_call(body, grid_spec=pltpu.PrefetchScalarGridSpec(num_scalar_pr...  290 us
    ppermute x54, waiting for transfers between devices, flip(): lax.ppermute(value, 'tensor', [(t, t ^ 1 << bit) for t in range(size)])  271 us
    ppermute x54, starting transfers between devices, flip(): lax.ppermute(value, 'tensor', [(t, t ^ 1 << bit) for t in range(size)])  61 us
    ppermute x3, waiting for transfers between devices, body(): lax.ppermute(v, 'dp', [(d, d ^ 1 << bit) for d in range(dp_size)])  48.5 us
  transfers between devices with their start and end apart: 70, of which 30 were waited for; matrix products, arithmetic and copies ran while one was open for 6% of the time, Pallas kernels for 29%

profile of v2, /device:TPU:0, one launch (start us, length us, event | category | flops | bytes accessed | tf_op | source)
XLA Modules:
  0.0 778.0 jit_solution(2718497521214812388)
XLA Ops:
  10.7 15.7 %front.2 = (bf16[512,2048]{1,0:T(8,128)(2,1)}, bf16[512,2048]{1,0:T(8,128)(2,1)}, bf16[512,1536]{1,0:T(8,128)(2,1)}, f32[512,512]{1,0:T(8,128)}, f32[16,512]{1,0...) custom-call(s32[4]{0:T(128)} %get-tuple-element.421.refs_0_, ...), custom_call_target="tpu_custom_call" | custom-call | flops 858000000 | bytes 1000 | tf_op jit(solution)/shard_map/front/pallas_call | solution.py:132
  31.5 15.8 %front.3 = (bf16[512,2048]{1,0:T(8,128)(2,1)}, bf16[512,2048]{1,0:T(8,128)(2,1)}, bf16[512,1536]{1,0:T(8,128)(2,1)}, f32[512,512]{1,0:T(8,128)}, f32[16,512]{1,0...) custom-call(s32[4]{0:T(128)} %get-tuple-element.422.refs_0_, ...), custom_call_target="tpu_custom_call" | custom-call | flops 858000000 | bytes 1000 | tf_op jit(solution)/shard_map/front/pallas_call | solution.py:132
  76.2 13.5 %hidden_back.1.refs_3_.refs_2_ = bf16[1024,2048]{1,0:T(8,128)(2,1)} custom-call(bf16[512,2048]{1,0:T(8,128)(2,1)} %bitcast.110, bf16[512,2048]{1,0:T(8,128)(2,1)} %bitcast.107, bf16[2048,2048]{1,0:T(8,128)(2,1)} %refs_3_.1), custom_call_target="tpu_custom_call" | custom-call | flops 22000001024 | bytes 1000 | tf_op jit(solution)/shard_map/hidden_back/pallas_call | solution.py:132
  110.9 30.0 %collective-permute-done.9 = f32[1,128,1024]{2,1,0:T(8,128)S(1)} collective-permute-done((f32[1,128,1024]{2,1,0:T(8,128)S(1)}, f32[1,128,1024]{2,1,0:T(8,128)S(1)}, u32[]{:S(2)}, u32[]{:S(2)}) %collective-permute-start.9) | collective-permute-done | bytes 524320 | tf_op jit(solution)/shard_map/ppermute | solution.py:152
  156.3 13.7 %hidden_front.2 = (bf16[512,2048]{1,0:T(8,128)(2,1)}, bf16[512,2048]{1,0:T(8,128)(2,1)}, f32[8,512]{1,0:T(8,128)}) custom-call(bf16[512,2048]{1,0:T(8,128)(2,1)} %get-tuple-element.243.refs_0_, bf16[2048,2048]{1,0:T(8,128)(2,1)} %refs_1_.13, f32[1,2048]{1,0:T(1,128)} %bitcast.155, bf16[1024,2048]{1,0:T(8,128)(2,1)} %hidden_back.1.refs_3_.refs_2_, ...), custom_call_target="tpu_custom_call" | custom-call | flops 808499968 | bytes 1000 | tf_op jit(solution)/shard_map/hidden_front/pallas_call | solution.py:132
  183.7 13.7 %hidden_front.3 = (bf16[512,2048]{1,0:T(8,128)(2,1)}, bf16[512,2048]{1,0:T(8,128)(2,1)}, f32[8,512]{1,0:T(8,128)}) custom-call(bf16[512,2048]{1,0:T(8,128)(2,1)} %get-tuple-element.228.refs_0_.refs_1_, bf16[2048,2048]{1,0:T(8,128)(2,1)} %refs_1_.13, f32[1,2048]{1,0:T(1,128)} %bitcast.156, bf16[1024,2048]{1,0:T(8,128)(2,1)} %hidden_back.1.refs_3_.refs_2_, ...), custom_call_target="tpu_custom_call" | custom-call | flops 808499968 | bytes 1000 | tf_op jit(solution)/shard_map/hidden_front/pallas_call | solution.py:132
  216.4 14.3 %full_grad.2 = f32[2048,2048]{1,0:T(8,128)} custom-call(bf16[512,2048]{1,0:T(8,128)(2,1)} %get-tuple-element.262.refs_0_.refs_1_, bf16[512,2048]{1,0:T(8,128)(2,1)} %get-tuple-element.242.refs_1_.refs_2_, bf16[512,2048]{1,0:T(8,128)(2,1)} %bitcast.111, bf16[512,2048]{1,0:T(8,128)(2,1)} %bitcast.108), custom_call_target="tpu_custom_call" | custom-call | flops 825000000 | bytes 1000 | tf_op jit(solution)/shard_map/full_grad/pallas_call | solution.py:132
  230.8 14.1 %full_grad.3 = f32[2048,2048]{1,0:T(8,128)} custom-call(bf16[512,2048]{1,0:T(8,128)(2,1)} %get-tuple-element.243.refs_0_, bf16[512,2048]{1,0:T(8,128)(2,1)} %get-tuple-element.228.refs_0_.refs_1_, bf16[512,2048]{1,0:T(8,128)(2,1)} %get-tuple-element.244.refs_2_.refs_0_, bf16[512,2048]{1,0:T(8,128)(2,1)} %get-tuple-element.246.refs_3_.refs_0_), custom_call_target="tpu_custom_call" | custom-call | flops 825000000 | bytes 1000 | tf_op jit(solution)/shard_map/full_grad/pallas_call | solution.py:132
  259.1 11.5 %hidden_grad.3 = (f32[2,128,1024]{2,1,0:T(8,128)}, f32[2,128,1024]{2,1,0:T(8,128)}, f32[2,128,1024]{2,1,0:T(8,128)}, f32[2,128,1024]{2,1,0:T(8,128)}) custom-call(bf16[512,2048]{1,0:T(8,128)(2,1)} %get-tuple-element.246.refs_3_.refs_0_, bf16[2048,2048]{1,0:T(8,128)(2,1)} %refs_1_.13), custom_call_target="tpu_custom_call" | custom-call | flops 385000000 | bytes 1000 | tf_op jit(solution)/shard_map/hidden_grad/pallas_call | solution.py:132
  282.7 13.4 %collective-permute-done.28 = f32[1,128,1024]{2,1,0:T(8,128)S(1)} collective-permute-done((f32[1,128,1024]{2,1,0:T(8,128)S(1)}, f32[1,128,1024]{2,1,0:T(8,128)S(1)}, u32[]{:S(2)}, u32[]{:S(2)}) %collective-permute-start.28) | collective-permute-done | bytes 524320 | tf_op jit(solution)/shard_map/ppermute | solution.py:152
  315.2 15.8 %result_part.1 = f32[8,128,2048]{2,1,0:T(8,128)} custom-call(s32[8]{0:T(128)} %pad_add_fusion.refs_0_, bf16[512,2048]{1,0:T(8,128)(2,1)} %get-tuple-element.262.refs_0_.refs_1_, bf16[512,2048]{1,0:T(8,128)(2,1)} %get-tuple-element.242.refs_1_.refs_2_, bf16[2048,2048]{1,0:T(8,128)(2,1)} %refs_3_.1), custom_call_target="tpu_custom_call" | custom-call | flops 22000001024 | bytes 1000 | tf_op jit(solution)/shard_map/result_part/pallas_call | solution.py:132
  342.3 20.9 %collective-permute-done.34 = f32[1,128,1024]{2,1,0:T(8,128)S(1)} collective-permute-done((f32[1,128,1024]{2,1,0:T(8,128)S(1)}, f32[1,128,1024]{2,1,0:T(8,128)S(1)}, u32[]{:S(2)}, u32[]{:S(2)}) %collective-permute-start.34) | collective-permute-done | bytes 524320 | tf_op jit(solution)/shard_map/ppermute | solution.py:152
  365.5 12.5 %collective-permute-done.36 = f32[1,128,1024]{2,1,0:T(8,128)S(1)} collective-permute-done((f32[1,128,1024]{2,1,0:T(8,128)S(1)}, f32[1,128,1024]{2,1,0:T(8,128)S(1)}, u32[]{:S(2)}, u32[]{:S(2)}) %collective-permute-start.36) | collective-permute-done | bytes 524320 | tf_op jit(solution)/shard_map/ppermute | solution.py:152
  392.9 21.9 %attention_back.2 = (bf16[512,512]{1,0:T(8,128)(2,1)}, bf16[512,1536]{1,0:T(8,128)(2,1)}, f32[2,8,1536]{2,1,0:T(8,128)}, f32[2,8,2048]{2,1,0:T(8,128)}, f32[2,12...) custom-call(s32[4]{0:T(128)} %get-tuple-element.421.refs_0_, ...), custom_call_target="tpu_custom_call" | custom-call | flops 1193500032 | bytes 1000 | tf_op jit(solution)/shard_map/attention_back/pallas_call | solution.py:132
  429.1 21.8 %attention_back.3 = (bf16[512,512]{1,0:T(8,128)(2,1)}, bf16[512,1536]{1,0:T(8,128)(2,1)}, f32[2,8,1536]{2,1,0:T(8,128)}, f32[2,8,2048]{2,1,0:T(8,128)}, f32[2,12...) custom-call(s32[4]{0:T(128)} %get-tuple-element.422.refs_0_, ...), custom_call_target="tpu_custom_call" | custom-call | flops 1193500032 | bytes 1000 | tf_op jit(solution)/shard_map/attention_back/pallas_call | solution.py:132
  470.6 20.3 %collective-permute-done.44 = f32[1,128,1024]{2,1,0:T(8,128)S(1)} collective-permute-done((f32[1,128,1024]{2,1,0:T(8,128)S(1)}, f32[1,128,1024]{2,1,0:T(8,128)S(1)}, u32[]{:S(2)}, u32[]{:S(2)}) %collective-permute-start.44) | collective-permute-done | bytes 524320 | tf_op jit(solution)/shard_map/ppermute | solution.py:152
  495.2 14.3 %attention_grads.3 = (f32[256,2048]{1,0:T(8,128)}, f32[3,256,2048]{2,1,0:T(8,128)}) custom-call(s32[4]{0:T(128)} %broadcast_add_fusion.refs_0_, bf16[512,2048]{1,0:T(8,128)(2,1)} %get-tuple-element.305.refs_1_, bf16[512,2048]{1,0:T(8,128)(2,1)} %get-tuple-element.298.refs_2_, bf16[512,1536]{1,0:T(8,128)(2,1)} %get-tuple-element.299.refs_3_, ...), custom_call_target="tpu_custom_call" | custom-call | flops 660000000 | bytes 1000 | tf_op jit(solution)/shard_map/attention_grads/pallas_call | solution.py:132
  509.6 25.7 %collective-permute-done.47 = f32[2,2048]{1,0:T(2,128)S(1)} collective-permute-done((f32[2,2048]{1,0:T(2,128)S(1)}, f32[2,2048]{1,0:T(2,128)S(1)}, u32[]{:S(2)}, u32[]{:S(2)}) %collective-permute-start.47) | collective-permute-done | bytes 16416 | tf_op jit(solution)/shard_map/ppermute | solution.py:152
  544.1 13.8 %collective-permute-done.50 = f32[1,128,1024]{2,1,0:T(8,128)} collective-permute-done((f32[1,128,1024]{2,1,0:T(8,128)}, f32[1,128,1024]{2,1,0:T(8,128)}, u32[]{:S(2)}, u32[]{:S(2)}) %collective-permute-start.50) | collective-permute-done | bytes 524320 | tf_op jit(solution)/shard_map/ppermute | solution.py:152
  575.2 22.0 %collective-permute-done.56 = f32[1,128,1024]{2,1,0:T(8,128)S(1)} collective-permute-done((f32[1,128,1024]{2,1,0:T(8,128)S(1)}, f32[1,128,1024]{2,1,0:T(8,128)S(1)}, u32[]{:S(2)}, u32[]{:S(2)}) %collective-permute-start.56) | collective-permute-done | bytes 524320 | tf_op jit(solution)/shard_map/ppermute | solution.py:152
  600.0 13.6 %collective-permute-done.58 = f32[256,2048]{1,0:T(8,128)S(1)} collective-permute-done((f32[256,2048]{1,0:T(8,128)}, f32[256,2048]{1,0:T(8,128)S(1)}, u32[]{:S(2)}, u32[]{:S(2)}) %collective-permute-start.58) | collective-permute-done | bytes 2097184 | tf_op jit(solution)/shard_map/ppermute | solution.py:240
  615.2 17.1 %collective-permute-done.60.refs_6_ = f32[2,128,1024]{2,1,0:T(8,128)S(1)} collective-permute-done((f32[2,128,1024]{2,1,0:T(8,128)S(1)}, f32[2,128,1024]{2,1,0:T(8,128)S(1)}, u32[]{:S(2)}, u32[]{:S(2)}) %collective-permute-start.60) | collective-permute-done | bytes 1048608 | tf_op jit(solution)/shard_map/ppermute | solution.py:152
  647.7 35.0 %collective-permute-done.62.refs_6_ = f32[2,128,1024]{2,1,0:T(8,128)S(1)} collective-permute-done((f32[2,128,1024]{2,1,0:T(8,128)S(1)}, f32[2,128,1024]{2,1,0:T(8,128)S(1)}, u32[]{:S(2)}, u32[]{:S(2)}) %collective-permute-start.62) | collective-permute-done | bytes 1048608 | tf_op jit(solution)/shard_map/ppermute | solution.py:152
  700.9 48.5 %collective-permute-done.66 = f32[12,2048]{1,0:T(8,128)S(1)} collective-permute-done((f32[12,2048]{1,0:T(8,128)S(1)}, f32[12,2048]{1,0:T(8,128)S(1)}, u32[]{:S(2)}, u32[]{:S(2)}) %collective-permute-start.66) | collective-permute-done | bytes 98336 | tf_op jit(solution)/shard_map/ppermute | solution.py:1167
  (389 shorter events, 301.6 us)
Async XLA Ops:
  8.0 485.9 %reduce-scatter.3.cloned.1.call-start = ((), (), s32[]{:S(2)}) async-start(), calls=%async_computation.2 | async-start | bytes 18874368 | tf_op jit(solution)/shard_map/reduce_scatter | solution.py:1094
  58.3 48.2 %collective-permute-start.15 = (f32[2,16,512]{2,1,0:T(8,128)S(1)}, f32[2,16,512]{2,1,0:T(8,128)S(1)}, u32[]{:S(2)}, u32[]{:S(2)}) collective-permute-start(f32[2,16,512]{2,1,0:T(8,128)S(1)} %pad_maximum_fusion.1), channel_id=1, source_target_pairs={{0,2},{1,3},{2,0},{3,1},{4,6},{5,7},{6,4},{7,5},{8,10},{9,11},{10,... | collective-permute-start | bytes 196616 | tf_op jit(solution)/shard_map/ppermute | solution.py:152
  59.4 36.2 %collective-permute-start.5 = (f32[2,128,1024]{2,1,0:T(8,128)}, f32[2,128,1024]{2,1,0:T(8,128)S(1)}, u32[]{:S(2)}, u32[]{:S(2)}) collective-permute-start(f32[2,128,1024]{2,1,0:T(8,128)} %get-tuple-element.206), channel_id=1, source_target_pairs={{0,2},{1,3},{2,0},{3,1},{4,6},{5,7},{6,4},{7,5},{8,10},{9,11},{10,... | collective-permute-start | bytes 3145736 | tf_op jit(solution)/shard_map/ppermute | solution.py:152
  104.2 41.1 %collective-permute-start.12 = (f32[2,128,1024]{2,1,0:T(8,128)S(1)}, f32[2,128,1024]{2,1,0:T(8,128)S(1)}, u32[]{:S(2)}, u32[]{:S(2)}) collective-permute-start(f32[2,128,1024]{2,1,0:T(8,128)S(1)} %constant_dynamic-update-slice_fusion.refs_1_), channel_id=1, source_target_pairs={{0,1},{1,0},{2,3},{3,2},{4,5},{5,4},{6,7},{7,6},{8,9},{9,8},{10,11... | collective-permute-start | bytes 3145736 | tf_op jit(solution)/shard_map/ppermute | solution.py:152
  105.0 40.3 %collective-permute-start.13 = (f32[2,128,1024]{2,1,0:T(8,128)S(1)}, f32[2,128,1024]{2,1,0:T(8,128)S(1)}, u32[]{:S(2)}, u32[]{:S(2)}) collective-permute-start(f32[2,128,1024]{2,1,0:T(8,128)S(1)} %constant_dynamic-update-slice_fusion.2.refs_3_), channel_id=1, source_target_pairs={{0,2},{1,3},{2,0},{3,1},{4,6},{5,7},{6,4},{7,5},{8,10},{9,11},{10,... | collective-permute-start | bytes 3145736 | tf_op jit(solution)/shard_map/ppermute | solution.py:152
  230.8 520.6 %reduce-scatter.5.cloned.1.call-start = ((), (), s32[]{:S(2)}) async-start(), calls=%async_computation.3 | async-start | bytes 18874368 | tf_op jit(solution)/shard_map/reduce_scatter | solution.py:1096
  245.0 510.4 %all-reduce.3.cloned.1.call-start = ((), (), s32[]{:S(2)}) async-start(), calls=%async_computation.4 | async-start | bytes 16777216 | tf_op jit(solution)/shard_map/psum | solution.py:1114
  312.5 69.4 %collective-permute-start.39 = (f32[2,128,1024]{2,1,0:T(8,128)S(1)}, f32[2,128,1024]{2,1,0:T(8,128)}, u32[]{:S(2)}, u32[]{:S(2)}) collective-permute-start(f32[2,128,1024]{2,1,0:T(8,128)S(1)} %constant_dynamic-update-slice_fusion.10.refs_4_), channel_id=1, source_target_pairs={{0,2},{1,3},{2,0},{3,1},{4,6},{5,7},{6,4},{7,5},{8,10},{9,11},{10,... | collective-permute-start | bytes 3145736 | tf_op jit(solution)/shard_map/ppermute | solution.py:152
  313.3 68.5 %collective-permute-start.38 = (f32[2,128,1024]{2,1,0:T(8,128)S(1)}, f32[2,128,1024]{2,1,0:T(8,128)}, u32[]{:S(2)}, u32[]{:S(2)}) collective-permute-start(f32[2,128,1024]{2,1,0:T(8,128)S(1)} %constant_dynamic-update-slice_fusion.8.refs_2_), channel_id=1, source_target_pairs={{0,1},{1,0},{2,3},{3,2},{4,5},{5,4},{6,7},{7,6},{8,9},{9,8},{10,11... | collective-permute-start | bytes 3145736 | tf_op jit(solution)/shard_map/ppermute | solution.py:152
  380.6 37.6 %collective-permute-start.41 = (f32[2,128,1024]{2,1,0:T(8,128)}, f32[2,128,1024]{2,1,0:T(8,128)}, u32[]{:S(2)}, u32[]{:S(2)}) collective-permute-start(f32[2,128,1024]{2,1,0:T(8,128)} %constant_dynamic-update-slice_fusion.14.refs_4_), channel_id=1, source_target_pairs={{0,2},{1,3},{2,0},{3,1},{4,6},{5,7},{6,4},{7,5},{8,10},{9,11},{10,... | collective-permute-start | bytes 3145736 | tf_op jit(solution)/shard_map/ppermute | solution.py:152
  381.1 37.1 %collective-permute-start.40 = (f32[2,128,1024]{2,1,0:T(8,128)S(1)}, f32[2,128,1024]{2,1,0:T(8,128)}, u32[]{:S(2)}, u32[]{:S(2)}) collective-permute-start(f32[2,128,1024]{2,1,0:T(8,128)S(1)} %constant_dynamic-update-slice_fusion.12.refs_2_), channel_id=1, source_target_pairs={{0,1},{1,0},{2,3},{3,2},{4,5},{5,4},{6,7},{7,6},{8,9},{9,8},{10,11... | collective-permute-start | bytes 3145736 | tf_op jit(solution)/shard_map/ppermute | solution.py:152
  467.8 67.6 %collective-permute-start.48 = (f32[2,128,1024]{2,1,0:T(8,128)}, f32[2,128,1024]{2,1,0:T(8,128)}, u32[]{:S(2)}, u32[]{:S(2)}) collective-permute-start(f32[2,128,1024]{2,1,0:T(8,128)} %get-tuple-element.315), channel_id=1, source_target_pairs={{0,1},{1,0},{2,3},{3,2},{4,5},{5,4},{6,7},{7,6},{8,9},{9,8},{10,11... | collective-permute-start | bytes 3145736 | tf_op jit(solution)/shard_map/ppermute | solution.py:152
  469.0 69.7 %collective-permute-start.49 = (f32[2,128,1024]{2,1,0:T(8,128)}, f32[2,128,1024]{2,1,0:T(8,128)}, u32[]{:S(2)}, u32[]{:S(2)}) collective-permute-start(f32[2,128,1024]{2,1,0:T(8,128)} %get-tuple-element.317), channel_id=1, source_target_pairs={{0,2},{1,3},{2,0},{3,1},{4,6},{5,7},{6,4},{7,5},{8,10},{9,11},{10,... | collective-permute-start | bytes 3145736 | tf_op jit(solution)/shard_map/ppermute | solution.py:152
  490.9 44.4 %collective-permute-start.47 = (f32[2,2048]{1,0:T(2,128)S(1)}, f32[2,2048]{1,0:T(2,128)S(1)}, u32[]{:S(2)}, u32[]{:S(2)}) collective-permute-start(f32[2,2048]{1,0:T(2,128)S(1)} %fusion.12), channel_id=1, source_target_pairs={{0,1},{1,0},{2,3},{3,2},{4,5},{5,4},{6,7},{7,6},{8,9},{9,8},{10,11... | collective-permute-start | bytes 49160 | tf_op jit(solution)/shard_map/ppermute | solution.py:152
  493.2 67.1 %collective-permute-start.51 = (f32[1,128,1024]{2,1,0:T(8,128)S(1)}, f32[1,128,1024]{2,1,0:T(8,128)}, u32[]{:S(2)}, u32[]{:S(2)}) collective-permute-start(f32[1,128,1024]{2,1,0:T(8,128)S(1)} %add.346), channel_id=1, source_target_pairs={{0,1},{1,0},{2,3},{3,2},{4,5},{5,4},{6,7},{7,6},{8,9},{9,8},{10,11... | collective-permute-start | bytes 1572872 | tf_op jit(solution)/shard_map/ppermute | solution.py:152
  494.0 64.0 %collective-permute-start.50 = (f32[1,128,1024]{2,1,0:T(8,128)}, f32[1,128,1024]{2,1,0:T(8,128)}, u32[]{:S(2)}, u32[]{:S(2)}) collective-permute-start(f32[1,128,1024]{2,1,0:T(8,128)} %add.345), channel_id=1, source_target_pairs={{0,2},{1,3},{2,0},{3,1},{4,6},{5,7},{6,4},{7,5},{8,10},{9,11},{10,... | collective-permute-start | bytes 1572872 | tf_op jit(solution)/shard_map/ppermute | solution.py:152
  535.4 78.2 %collective-permute-start.58 = (f32[256,2048]{1,0:T(8,128)}, f32[256,2048]{1,0:T(8,128)S(1)}, u32[]{:S(2)}, u32[]{:S(2)}) collective-permute-start(f32[256,2048]{1,0:T(8,128)} %get-tuple-element.327), channel_id=1, source_target_pairs={{0,8},{4,12},{8,16},{12,20},{16,24},{20,28},{24,0},{28,4},{1,9},{5... | collective-permute-start | bytes 6291464 | tf_op jit(solution)/shard_map/ppermute | solution.py:240
  573.2 59.2 %collective-permute-start.60 = (f32[2,128,1024]{2,1,0:T(8,128)S(1)}, f32[2,128,1024]{2,1,0:T(8,128)S(1)}, u32[]{:S(2)}, u32[]{:S(2)}) collective-permute-start(f32[2,128,1024]{2,1,0:T(8,128)S(1)} %constant_dynamic-update-slice_fusion.18.refs_5_), channel_id=1, source_target_pairs={{0,2},{1,3},{2,0},{3,1},{4,6},{5,7},{6,4},{7,5},{8,10},{9,11},{10,... | collective-permute-start | bytes 3145736 | tf_op jit(solution)/shard_map/ppermute | solution.py:152
  615.2 78.3 %collective-permute-start.64 = (f32[256,2048]{1,0:T(8,128)}, f32[256,2048]{1,0:T(8,128)}, u32[]{:S(2)}, u32[]{:S(2)}) collective-permute-start(f32[256,2048]{1,0:T(8,128)} %bitcast_add_fusion.2), channel_id=1, source_target_pairs={{0,8},{4,12},{8,16},{12,20},{16,24},{20,28},{24,0},{28,4},{1,9},{5... | collective-permute-start | bytes 6291464 | tf_op jit(solution)/shard_map/ppermute | solution.py:240
  644.6 38.1 %collective-permute-start.62 = (f32[2,128,1024]{2,1,0:T(8,128)S(1)}, f32[2,128,1024]{2,1,0:T(8,128)S(1)}, u32[]{:S(2)}, u32[]{:S(2)}) collective-permute-start(f32[2,128,1024]{2,1,0:T(8,128)S(1)} %constant_dynamic-update-slice_fusion.22.refs_5_), channel_id=1, source_target_pairs={{0,2},{1,3},{2,0},{3,1},{4,6},{5,7},{6,4},{7,5},{8,10},{9,11},{10,... | collective-permute-start | bytes 3145736 | tf_op jit(solution)/shard_map/ppermute | solution.py:152
  645.5 37.7 %collective-permute-start.61 = (f32[2,128,1024]{2,1,0:T(8,128)S(1)}, f32[2,128,1024]{2,1,0:T(8,128)S(1)}, u32[]{:S(2)}, u32[]{:S(2)}) collective-permute-start(f32[2,128,1024]{2,1,0:T(8,128)S(1)} %constant_dynamic-update-slice_fusion.20.refs_3_), channel_id=1, source_target_pairs={{0,1},{1,0},{2,3},{3,2},{4,5},{5,4},{6,7},{7,6},{8,9},{9,8},{10,11... | collective-permute-start | bytes 3145736 | tf_op jit(solution)/shard_map/ppermute | solution.py:152
  646.2 47.4 %collective-permute-start.63 = (f32[12,2048]{1,0:T(8,128)S(1)}, f32[12,2048]{1,0:T(8,128)S(1)}, u32[]{:S(2)}, u32[]{:S(2)}) collective-permute-start(f32[12,2048]{1,0:T(8,128)S(1)} %add.375), channel_id=1, source_target_pairs={{0,8},{4,12},{8,0},{12,4},{16,24},{20,28},{24,16},{28,20},{1,9},{5... | collective-permute-start | bytes 294920 | tf_op jit(solution)/shard_map/ppermute | solution.py:1167
  697.0 54.3 %collective-permute-start.65 = (f32[256,2048]{1,0:T(8,128)}, f32[256,2048]{1,0:T(8,128)}, u32[]{:S(2)}, u32[]{:S(2)}) collective-permute-start(f32[256,2048]{1,0:T(8,128)} %bitcast_add_fusion.1), channel_id=1, source_target_pairs={{0,8},{4,12},{8,16},{12,20},{16,24},{20,28},{24,0},{28,4},{1,9},{5... | collective-permute-start | bytes 6291464 | tf_op jit(solution)/shard_map/ppermute | solution.py:240
  698.5 50.9 %collective-permute-start.66 = (f32[12,2048]{1,0:T(8,128)S(1)}, f32[12,2048]{1,0:T(8,128)S(1)}, u32[]{:S(2)}, u32[]{:S(2)}) collective-permute-start(f32[12,2048]{1,0:T(8,128)S(1)} %add.377), channel_id=1, source_target_pairs={{0,16},{4,20},{8,24},{12,28},{16,0},{20,4},{24,8},{28,12},{1,17},{... | collective-permute-start | bytes 294920 | tf_op jit(solution)/shard_map/ppermute | solution.py:1167
  (109 other events, 2086.4 us)
Sparse Core Ops, SparseCore 0:
  230.9 169.1 reduce-scatter.2
  403.2 195.2 reduce-scatter.4
Sparse Core Ops, SparseCore 1:
  465.4 252.9 all-reduce.2

commit v3 on v2

--- a/solution.py
+++ b/solution.py
@@ -614,7 +614,7 @@
 def hidden_grad(grad, up_weight):
     rows, units = grad.shape
     blocks = rows // SLOT
-    tile = 256
+    tile = 512
     steps = D // tile
     half = steps // 2
 
@@ -1049,6 +1049,7 @@
         cots.append(line.tie(cot3)[orders[c]].reshape(-1, D))
         line.mark(cots[-1])
     totals = every(ones, "total")
+    line.mark(*line.last, *sums0.pieces())
     for step in range(1, bits):
         totals[0].advance()
     back = hidden_back([line.tie(cots[0])] + cots[1:], down_weight)
@@ -1062,33 +1063,36 @@
         one["sums"].step()
     uw_total = both_vectors(sums0.pieces())
 
+    def mid_of(c):
+        two = twos[c]
+        low, grad, vecs = hidden_mid(c, line.tie(two["active"]), two["slope"], back, two["sums"], hid_gain, hid_shift)
+        two.update(low=low, grad=grad, vecs=functools.reduce(jnp.add, [vecs[k] for k in range(blocks)]))
+        line.mark(vecs)
+
+    totals[0].gather()
+    for other in ones[1:]:
+        line.mark(*line.last, *other["sums"].pieces())
     for c in range(chunks):
         one = ones[c]
-        if c == 0:
-            totals[0].gather()
-            for total in totals[1:]:
-                total.advance()
-                total.gather()
-            for other in ones[1:]:
-                line.mark(*line.last, *other["sums"].pieces())
         mid, second, stat = middle_norm(
             line.tie(one["own"]), totals[c].pieces(), one["sums"].pieces(), uw_total, out_bias, ffn_gain, ffn_shift
         )
         line.mark(stat)
         if c == 0:
             for total in totals[1:]:
-                for step in range(1, bits):
-                    total.gather()
-        else:
-            line.mark(stat, *twos[c - 1]["sums"][1:])
+                total.advance()
+                total.gather()
         active, slope, sums = hidden_front(c, line.tie(second), up_weight, up_bias, back, hid_gain)
         line.mark(sums)
         twos.append(dict(middle=mid, second=second, stat=stat, active=active, slope=slope, sums=all_pieces(sums, bits)))
+        if c == 0:
+            for total in totals[1:]:
+                for step in range(1, bits):
+                    total.gather()
+        if c > 0:
+            line.mark(sums, *twos[c - 1]["sums"][1:])
     for c in range(chunks):
-        two = twos[c]
-        low, grad, vecs = hidden_mid(c, line.tie(two["active"]), two["slope"], back, two["sums"], hid_gain, hid_shift)
-        two.update(low=low, grad=grad, vecs=functools.reduce(jnp.add, [vecs[k] for k in range(blocks)]))
-        line.mark(vecs)
+        mid_of(c)
     lows = every(twos, "low")
     down_grad = full(lows, cots)
     down_part = lax.psum_scatter(down_grad, "dp", scatter_dimension=1, tiled=True)
@@ -1110,17 +1114,20 @@
         totals[0].gather()
     result = result_part(jnp.concatenate(orders), [line.tie(lows[0])] + lows[1:], down_weight)
     line.mark(result)
-    steps_of(totals, bits, [2 * bits] + [0] * (chunks - 1), 2 * bits)
+    steps_of(totals, bits, [2 * bits] + [0] * (chunks - 1), bits)
     result = lax.psum(line.tie(result), "tensor")
-    for two in twos:
-        two["pieces"] = two["total"].pieces()
 
     for c in range(chunks):
         one, two = ones[c], twos[c]
         grad, low, stat2, vecs = middle_back(
-            line.tie(one["own"]), cots[c], two["pieces"], two["middle"], two["stat"], uw_total, out_bias, ffn_gain
+            line.tie(one["own"]), cots[c], two["total"].pieces(), two["middle"], two["stat"], uw_total, out_bias, ffn_gain
         )
         line.mark(stat2)
+        if c == 0:
+            for total in totals[1:]:
+                total.advance()
+                for step in range(bits):
+                    total.gather()
         found = attention_back(
             orders[c], lengths, line.tie(low), stat2, one["mixed"], one["qkv"], one["own"], mix_gain, mix_shift, out_weight,
             qkv_weight, tables, mask,
@@ -1146,36 +1153,30 @@
     sent = grads_of(other_ids, None)[0]
     line.mark(sent)
     sent = lax.ppermute(sent, "dp", [(d, d ^ 1) for d in range(dp_size)])
-    for step in range(1 if chunks > 1 else 0, bits):
-        first.advance()
-    first.gather()
     line.mark(*line.last, down_part)
     ring_first, ring_rest = grads_of(mine_ids, sent)
     line.mark(ring_rest)
     ring = Ring(line, ring_first, ring_rest, dp_size)
+    for step in range(1 if chunks > 1 else 0, bits):
+        first.advance()
+    first.gather()
+    if chunks > 1:
+        last.advance()
+    for step in range(1, bits):
+        first.gather()
+    attention_part = ring.advance()
+    if chunks > 1:
+        for step in range(1, bits):
+            last.advance()
+        last.gather()
     for bit in range(1, bits):
         wide = line.tie(wide) + got
         got = flip(wide, bit, blocks)
         line.mark(wide)
     if chunks > 1:
-        last.advance()
-    for step in range(1, bits):
-        first.gather()
-    wide = line.tie(wide) + got
-    vecs = jnp.concatenate([pad(add(twos, "vecs", 3)), add(threes, "vecs", 4), pad(add(threes, "narrow", 3)), wide], 0)
-    line.mark(vecs)
+        line.mark(*line.last, *last.got)
     hop = lambda v, bit: lax.ppermute(v, "dp", [(d, d ^ (1 << bit)) for d in range(dp_size)])
     dp_bits = dp_size.bit_length() - 1
-    got = hop(vecs, 0)
-    if chunks > 1:
-        for step in range(1, bits):
-            last.advance()
-        last.gather()
-        line.mark(*line.last, *last.got)
-    vecs = line.tie(vecs) + got
-    line.mark(vecs)
-    got = hop(vecs, 1)
-    attention_part = ring.advance()
     tokens_grad, output = None, None
     for c in range(chunks):
         tokens_grad = tokens_back(
@@ -1183,16 +1184,25 @@
         )
         line.mark(tokens_grad)
         if c == 0:
+            wide = line.tie(wide) + got
+            vecs = jnp.concatenate(
+                [pad(add(twos, "vecs", 3)), add(threes, "vecs", 4), pad(add(threes, "narrow", 3)), wide], 0
+            )
+            line.mark(vecs)
+            got = hop(vecs, 0)
             if chunks > 1:
                 for step in range(1, bits):
                     last.gather()
+            vecs = line.tie(vecs) + got
+            line.mark(vecs)
+            got = hop(vecs, 1)
+            attention_part = ring.advance()
     for bit in range(2, dp_bits):
         vecs = line.tie(vecs) + got
         line.mark(vecs)
         got = hop(vecs, bit)
-        attention_part = ring.advance()
-    line.mark(attention_part, up_part)
-    for step in range(dp_bits - 1, count - 1):
+    line.mark(*line.last, up_part)
+    for step in range(2, count - 1):
         attention_part = ring.advance()
     vecs = vecs + got
     hid_vecs, mid_vecs, narrow, wide = vecs[:3], vecs[3:7], vecs[7:10], vecs[10:12]

time: 788 us -> 780 us (0.990)
    ppermute x3, waiting for transfers between devices: 48.5 us -> 6.66 us  [body(): lax.ppermute(v, 'dp', [(d, d ^ 1 << bit) for d in range(dp_size)])]
    ppermute x54, waiting for transfers between devices: 271 us -> 292 us  [flip(): lax.ppermute(value, 'tensor', [(t, t ^ 1 << bit) for t in range(size)])]
    ppermute x3, waiting for transfers between devices: 13.6 us -> 26.3 us  [send(): lax.ppermute(value, 'dp', [(d, (d + 2) % self.size) for d in range(self.s...]
  transfers between devices with their start and end apart: 70 -> 70, of which waited for: 30 -> 30; matrix products, arithmetic and copies ran while one was open for 6% -> 6% of each run, Pallas kernels for 29% -> 31%
where the time goes in v3:
time: 780 us; the launch traced here: 770 us
  waiting for transfers between devices  333 us (43%)
  Pallas kernels  286 us (37%)
  starting transfers between devices  76.5 us (10%)
  other arithmetic  29.7 us (4%)
  local copies, waits for them, and re-layouts  27.9 us (4%)
  between operations  17.1 us (2%)
    ppermute x54, waiting for transfers between devices, flip(): lax.ppermute(value, 'tensor', [(t, t ^ 1 << bit) for t in range(size)])  292 us
    pallas_call x24, Pallas kernels, run(): pl.pallas_call(body, grid_spec=pltpu.PrefetchScalarGridSpec(num_scalar_pr...  286 us
    ppermute x54, starting transfers between devices, flip(): lax.ppermute(value, 'tensor', [(t, t ^ 1 << bit) for t in range(size)])  65.2 us
    ppermute x3, waiting for transfers between devices, send(): lax.ppermute(value, 'dp', [(d, (d + 2) % self.size) for d in range(self.s...  26.3 us
  transfers between devices with their start and end apart: 70, of which 30 were waited for; matrix products, arithmetic and copies ran while one was open for 6% of the time, Pallas kernels for 31%

profile of v3, /device:TPU:0, one launch (start us, length us, event | category | flops | bytes accessed | tf_op | source)
XLA Modules:
  0.0 769.7 jit_solution(2470335925854810219)
XLA Ops:
  10.7 15.7 %front.2 = (bf16[512,2048]{1,0:T(8,128)(2,1)}, bf16[512,2048]{1,0:T(8,128)(2,1)}, bf16[512,1536]{1,0:T(8,128)(2,1)}, f32[512,512]{1,0:T(8,128)}, f32[16,512]{1,0...) custom-call(s32[4]{0:T(128)} %get-tuple-element.421.refs_0_, ...), custom_call_target="tpu_custom_call" | custom-call | flops 858000000 | bytes 1000 | tf_op jit(solution)/shard_map/front/pallas_call | solution.py:132
  31.5 15.9 %front.3 = (bf16[512,2048]{1,0:T(8,128)(2,1)}, bf16[512,2048]{1,0:T(8,128)(2,1)}, bf16[512,1536]{1,0:T(8,128)(2,1)}, f32[512,512]{1,0:T(8,128)}, f32[16,512]{1,0...) custom-call(s32[4]{0:T(128)} %get-tuple-element.422.refs_0_, ...), custom_call_target="tpu_custom_call" | custom-call | flops 858000000 | bytes 1000 | tf_op jit(solution)/shard_map/front/pallas_call | solution.py:132
  78.1 13.5 %hidden_back.1.refs_3_.refs_2_ = bf16[1024,2048]{1,0:T(8,128)(2,1)} custom-call(bf16[512,2048]{1,0:T(8,128)(2,1)} %bitcast.110, bf16[512,2048]{1,0:T(8,128)(2,1)} %bitcast.107, bf16[2048,2048]{1,0:T(8,128)(2,1)} %refs_3_.1), custom_call_target="tpu_custom_call" | custom-call | flops 22000001024 | bytes 1000 | tf_op jit(solution)/shard_map/hidden_back/pallas_call | solution.py:132
  110.7 28.7 %collective-permute-done.11 = f32[2,16,512]{2,1,0:T(8,128)S(1)} collective-permute-done((f32[2,16,512]{2,1,0:T(8,128)S(1)}, f32[2,16,512]{2,1,0:T(8,128)S(1)}, u32[]{:S(2)}, u32[]{:S(2)}) %collective-permute-start.11) | collective-permute-done | bytes 65568 | tf_op jit(solution)/shard_map/ppermute | solution.py:152
  151.2 13.7 %hidden_front.2 = (bf16[512,2048]{1,0:T(8,128)(2,1)}, bf16[512,2048]{1,0:T(8,128)(2,1)}, f32[8,512]{1,0:T(8,128)}) custom-call(bf16[512,2048]{1,0:T(8,128)(2,1)} %get-tuple-element.243.refs_0_, bf16[2048,2048]{1,0:T(8,128)(2,1)} %refs_1_.13, f32[1,2048]{1,0:T(1,128)} %bitcast.153, bf16[1024,2048]{1,0:T(8,128)(2,1)} %hidden_back.1.refs_3_.refs_2_, ...), custom_call_target="tpu_custom_call" | custom-call | flops 808499968 | bytes 1000 | tf_op jit(solution)/shard_map/hidden_front/pallas_call | solution.py:132
  170.6 15.9 %collective-permute-done.19.refs_4_ = f32[2,128,1024]{2,1,0:T(8,128)S(1)} collective-permute-done((f32[2,128,1024]{2,1,0:T(8,128)S(1)}, f32[2,128,1024]{2,1,0:T(8,128)S(1)}, u32[]{:S(2)}, u32[]{:S(2)}) %collective-permute-start.19) | collective-permute-done | bytes 1048608 | tf_op jit(solution)/shard_map/ppermute | solution.py:152
  196.0 13.7 %hidden_front.3 = (bf16[512,2048]{1,0:T(8,128)(2,1)}, bf16[512,2048]{1,0:T(8,128)(2,1)}, f32[8,512]{1,0:T(8,128)}) custom-call(bf16[512,2048]{1,0:T(8,128)(2,1)} %get-tuple-element.228.refs_0_.refs_1_, bf16[2048,2048]{1,0:T(8,128)(2,1)} %refs_1_.13, f32[1,2048]{1,0:T(1,128)} %bitcast.154, bf16[1024,2048]{1,0:T(8,128)(2,1)} %hidden_back.1.refs_3_.refs_2_, ...), custom_call_target="tpu_custom_call" | custom-call | flops 808499968 | bytes 1000 | tf_op jit(solution)/shard_map/hidden_front/pallas_call | solution.py:132
  229.3 14.3 %full_grad.2 = f32[2048,2048]{1,0:T(8,128)} custom-call(bf16[512,2048]{1,0:T(8,128)(2,1)} %get-tuple-element.262.refs_0_.refs_1_, bf16[512,2048]{1,0:T(8,128)(2,1)} %get-tuple-element.242.refs_1_.refs_2_, bf16[512,2048]{1,0:T(8,128)(2,1)} %bitcast.111, bf16[512,2048]{1,0:T(8,128)(2,1)} %bitcast.108), custom_call_target="tpu_custom_call" | custom-call | flops 825000000 | bytes 1000 | tf_op jit(solution)/shard_map/full_grad/pallas_call | solution.py:132
  243.7 14.1 %full_grad.3 = f32[2048,2048]{1,0:T(8,128)} custom-call(bf16[512,2048]{1,0:T(8,128)(2,1)} %get-tuple-element.243.refs_0_, bf16[512,2048]{1,0:T(8,128)(2,1)} %get-tuple-element.228.refs_0_.refs_1_, bf16[512,2048]{1,0:T(8,128)(2,1)} %get-tuple-element.244.refs_2_.refs_0_, bf16[512,2048]{1,0:T(8,128)(2,1)} %get-tuple-element.246.refs_3_.refs_0_), custom_call_target="tpu_custom_call" | custom-call | flops 825000000 | bytes 1000 | tf_op jit(solution)/shard_map/full_grad/pallas_call | solution.py:132
  293.3 13.4 %collective-permute-done.28 = f32[1,128,1024]{2,1,0:T(8,128)S(1)} collective-permute-done((f32[1,128,1024]{2,1,0:T(8,128)S(1)}, f32[1,128,1024]{2,1,0:T(8,128)S(1)}, u32[]{:S(2)}, u32[]{:S(2)}) %collective-permute-start.28) | collective-permute-done | bytes 524320 | tf_op jit(solution)/shard_map/ppermute | solution.py:152
  326.1 16.1 %result_part.1 = f32[8,128,2048]{2,1,0:T(8,128)} custom-call(s32[8]{0:T(128)} %pad_add_fusion.refs_0_, bf16[512,2048]{1,0:T(8,128)(2,1)} %get-tuple-element.262.refs_0_.refs_1_, bf16[512,2048]{1,0:T(8,128)(2,1)} %get-tuple-element.242.refs_1_.refs_2_, bf16[2048,2048]{1,0:T(8,128)(2,1)} %refs_3_.1), custom_call_target="tpu_custom_call" | custom-call | flops 22000001024 | bytes 1000 | tf_op jit(solution)/shard_map/result_part/pallas_call | solution.py:132
  363.7 11.0 %middle_back.2 = (f32[512,2048]{1,0:T(8,128)}, bf16[512,2048]{1,0:T(8,128)(2,1)}, f32[512,128]{1,0:T(8,128)}, f32[4,8,2048]{2,1,0:T(8,128)}) custom-call(bf16[512,2048]{1,0:T(8,128)(2,1)} %get-tuple-element.326.refs_0_.refs_6_.refs_1_, bf16[512,2048]{1,0:T(8,128)(2,1)} %bitcast.112, f32[2,128,1024]{2,1,0:T(8,128)} %copy-done.7, ...), custom_call_target="tpu_custom_call" | custom-call | flops 605000000 | bytes 1000 | tf_op jit(solution)/shard_map/middle_back/pallas_call | solution.py:132
  377.7 12.0 %collective-permute-done.38 = f32[1,128,1024]{2,1,0:T(8,128)S(1)} collective-permute-done((f32[1,128,1024]{2,1,0:T(8,128)S(1)}, f32[1,128,1024]{2,1,0:T(8,128)S(1)}, u32[]{:S(2)}, u32[]{:S(2)}) %collective-permute-start.38) | collective-permute-done | bytes 524320 | tf_op jit(solution)/shard_map/ppermute | solution.py:152
  394.1 21.8 %attention_back.2 = (bf16[512,512]{1,0:T(8,128)(2,1)}, bf16[512,1536]{1,0:T(8,128)(2,1)}, f32[2,8,1536]{2,1,0:T(8,128)}, f32[2,8,2048]{2,1,0:T(8,128)}, f32[2,12...) custom-call(s32[4]{0:T(128)} %get-tuple-element.421.refs_0_, ...), custom_call_target="tpu_custom_call" | custom-call | flops 1193500032 | bytes 1000 | tf_op jit(solution)/shard_map/attention_back/pallas_call | solution.py:132
  417.4 11.5 %middle_back.3 = (f32[512,2048]{1,0:T(8,128)}, bf16[512,2048]{1,0:T(8,128)(2,1)}, f32[512,128]{1,0:T(8,128)}, f32[4,8,2048]{2,1,0:T(8,128)}) custom-call(bf16[512,2048]{1,0:T(8,128)(2,1)} %get-tuple-element.333.refs_0_.refs_6_.refs_1_, bf16[512,2048]{1,0:T(8,128)(2,1)} %bitcast.109, f32[2,128,1024]{2,1,0:T(8,128)} %copy-done.9, ...), custom_call_target="tpu_custom_call" | custom-call | flops 605000000 | bytes 1000 | tf_op jit(solution)/shard_map/middle_back/pallas_call | solution.py:132
  429.0 21.8 %attention_back.3 = (bf16[512,512]{1,0:T(8,128)(2,1)}, bf16[512,1536]{1,0:T(8,128)(2,1)}, f32[2,8,1536]{2,1,0:T(8,128)}, f32[2,8,2048]{2,1,0:T(8,128)}, f32[2,12...) custom-call(s32[4]{0:T(128)} %get-tuple-element.422.refs_0_, ...), custom_call_target="tpu_custom_call" | custom-call | flops 1193500032 | bytes 1000 | tf_op jit(solution)/shard_map/attention_back/pallas_call | solution.py:132
  454.8 10.7 %attention_grads.2 = f32[4,256,2048]{2,1,0:T(8,128)} custom-call(s32[4]{0:T(128)} %add_subtract_fusion.refs_0_, bf16[512,2048]{1,0:T(8,128)(2,1)} %get-tuple-element.303.refs_1_, bf16[512,2048]{1,0:T(8,128)(2,1)} %get-tuple-element.298.refs_2_, bf16[512,1536]{1,0:T(8,128)(2,1)} %get-tuple-element.299.refs_3_, bf16[512,1536]{1,0:T(8,128)(2,1)} %get-tuple-element.300.refs_4_, ...), custom_call_target="tpu_custom_call" | custom-call | flops 660000000 | bytes 1000 | tf_op jit(solution)/shard_map/attention_grads/pallas_call | solution.py:132
  479.3 13.4 %attention_grads.3 = (f32[256,2048]{1,0:T(8,128)}, f32[3,256,2048]{2,1,0:T(8,128)}) custom-call(s32[4]{0:T(128)} %broadcast_add_fusion.refs_0_, bf16[512,2048]{1,0:T(8,128)(2,1)} %get-tuple-element.303.refs_1_, bf16[512,2048]{1,0:T(8,128)(2,1)} %get-tuple-element.298.refs_2_, bf16[512,1536]{1,0:T(8,128)(2,1)} %get-tuple-element.299.refs_3_, ...), custom_call_target="tpu_custom_call" | custom-call | flops 660000000 | bytes 1000 | tf_op jit(solution)/shard_map/attention_grads/pallas_call | solution.py:132
  497.9 37.5 %collective-permute-done.47 = f32[2,128,1024]{2,1,0:T(8,128)S(1)} collective-permute-done((f32[2,128,1024]{2,1,0:T(8,128)}, f32[2,128,1024]{2,1,0:T(8,128)S(1)}, u32[]{:S(2)}, u32[]{:S(2)}) %collective-permute-start.47) | collective-permute-done | bytes 1048608 | tf_op jit(solution)/shard_map/ppermute | solution.py:152
  544.9 17.9 %collective-permute-done.49 = f32[1,128,1024]{2,1,0:T(8,128)S(1)} collective-permute-done((f32[1,128,1024]{2,1,0:T(8,128)S(1)}, f32[1,128,1024]{2,1,0:T(8,128)S(1)}, u32[]{:S(2)}, u32[]{:S(2)}) %collective-permute-start.49) | collective-permute-done | bytes 524320 | tf_op jit(solution)/shard_map/ppermute | solution.py:152
  563.5 14.0 %collective-permute-done.50 = f32[1,128,1024]{2,1,0:T(8,128)S(1)} collective-permute-done((f32[1,128,1024]{2,1,0:T(8,128)S(1)}, f32[1,128,1024]{2,1,0:T(8,128)S(1)}, u32[]{:S(2)}, u32[]{:S(2)}) %collective-permute-start.50) | collective-permute-done | bytes 524320 | tf_op jit(solution)/shard_map/ppermute | solution.py:152
  593.8 40.5 %collective-permute-done.56 = f32[1,128,1024]{2,1,0:T(8,128)S(1)} collective-permute-done((f32[1,128,1024]{2,1,0:T(8,128)S(1)}, f32[1,128,1024]{2,1,0:T(8,128)S(1)}, u32[]{:S(2)}, u32[]{:S(2)}) %collective-permute-start.56) | collective-permute-done | bytes 524320 | tf_op jit(solution)/shard_map/ppermute | solution.py:152
  654.2 16.7 %collective-permute-done.61 = f32[256,2048]{1,0:T(8,128)} collective-permute-done((f32[256,2048]{1,0:T(8,128)}, f32[256,2048]{1,0:T(8,128)}, u32[]{:S(2)}, u32[]{:S(2)}) %collective-permute-start.61) | collective-permute-done | bytes 2097184 | tf_op jit(solution)/shard_map/ppermute | solution.py:240
  677.6 44.6 %collective-permute-done.63.refs_6_ = f32[2,128,1024]{2,1,0:T(8,128)S(1)} collective-permute-done((f32[2,128,1024]{2,1,0:T(8,128)S(1)}, f32[2,128,1024]{2,1,0:T(8,128)S(1)}, u32[]{:S(2)}, u32[]{:S(2)}) %collective-permute-start.63) | collective-permute-done | bytes 1048608 | tf_op jit(solution)/shard_map/ppermute | solution.py:152
  (390 shorter events, 304.0 us)
Async XLA Ops:
  8.0 464.0 %reduce-scatter.3.cloned.1.call-start = ((), (), s32[]{:S(2)}) async-start(), calls=%async_computation.2 | async-start | bytes 18874368 | tf_op jit(solution)/shard_map/reduce_scatter | solution.py:1098
  106.5 42.4 %collective-permute-start.14 = (f32[1,128,1024]{2,1,0:T(8,128)}, f32[1,128,1024]{2,1,0:T(8,128)S(1)}, u32[]{:S(2)}, u32[]{:S(2)}) collective-permute-start(f32[1,128,1024]{2,1,0:T(8,128)} %slice_add_fusion.19), channel_id=1, source_target_pairs={{0,2},{1,3},{2,0},{3,1},{4,6},{5,7},{6,4},{7,5},{8,10},{9,11},{10,... | collective-permute-start | bytes 1572872 | tf_op jit(solution)/shard_map/ppermute | solution.py:152
  108.6 41.9 %collective-permute-start.15 = (f32[1,128,1024]{2,1,0:T(8,128)S(1)}, f32[1,128,1024]{2,1,0:T(8,128)S(1)}, u32[]{:S(2)}, u32[]{:S(2)}) collective-permute-start(f32[1,128,1024]{2,1,0:T(8,128)S(1)} %slice_add_fusion.18), channel_id=1, source_target_pairs={{0,1},{1,0},{2,3},{3,2},{4,5},{5,4},{6,7},{7,6},{8,9},{9,8},{10,11... | collective-permute-start | bytes 1572872 | tf_op jit(solution)/shard_map/ppermute | solution.py:152
  167.1 45.5 %collective-permute-start.22 = (f32[8,512]{1,0:T(8,128)S(1)}, f32[8,512]{1,0:T(8,128)S(1)}, u32[]{:S(2)}, u32[]{:S(2)}) collective-permute-start(f32[8,512]{1,0:T(8,128)S(1)} %copy-done.54), channel_id=1, source_target_pairs={{0,3},{1,2},{2,1},{3,0},{4,7},{5,6},{6,5},{7,4},{8,11},{9,10},{10,... | collective-permute-start | bytes 49160 | tf_op jit(solution)/shard_map/ppermute | solution.py:157
  168.7 44.6 %collective-permute-start.21 = (f32[8,512]{1,0:T(8,128)S(1)}, f32[8,512]{1,0:T(8,128)S(1)}, u32[]{:S(2)}, u32[]{:S(2)}) collective-permute-start(f32[8,512]{1,0:T(8,128)S(1)} %copy-done.54), channel_id=1, source_target_pairs={{0,2},{1,3},{2,0},{3,1},{4,6},{5,7},{6,4},{7,5},{8,10},{9,11},{10,... | collective-permute-start | bytes 49160 | tf_op jit(solution)/shard_map/ppermute | solution.py:157
  169.3 43.9 %collective-permute-start.20 = (f32[8,512]{1,0:T(8,128)S(1)}, f32[8,512]{1,0:T(8,128)S(1)}, u32[]{:S(2)}, u32[]{:S(2)}) collective-permute-start(f32[8,512]{1,0:T(8,128)S(1)} %copy-done.54), channel_id=1, source_target_pairs={{0,1},{1,0},{2,3},{3,2},{4,5},{5,4},{6,7},{7,6},{8,9},{9,8},{10,11... | collective-permute-start | bytes 49160 | tf_op jit(solution)/shard_map/ppermute | solution.py:157
  243.6 490.8 %reduce-scatter.5.cloned.1.call-start = ((), (), s32[]{:S(2)}) async-start(), calls=%async_computation.3 | async-start | bytes 18874368 | tf_op jit(solution)/shard_map/reduce_scatter | solution.py:1100
  257.8 489.2 %all-reduce.3.cloned.1.call-start = ((), (), s32[]{:S(2)}) async-start(), calls=%async_computation.4 | async-start | bytes 16777216 | tf_op jit(solution)/shard_map/psum | solution.py:1118
  322.8 41.0 %collective-permute-start.35 = (f32[2,128,1024]{2,1,0:T(8,128)S(1)}, f32[2,128,1024]{2,1,0:T(8,128)}, u32[]{:S(2)}, u32[]{:S(2)}) collective-permute-start(f32[2,128,1024]{2,1,0:T(8,128)S(1)} %constant_dynamic-update-slice_fusion.10.refs_4_), channel_id=1, source_target_pairs={{0,2},{1,3},{2,0},{3,1},{4,6},{5,7},{6,4},{7,5},{8,10},{9,11},{10,... | collective-permute-start | bytes 3145736 | tf_op jit(solution)/shard_map/ppermute | solution.py:152
  324.1 39.6 %collective-permute-start.34 = (f32[2,128,1024]{2,1,0:T(8,128)S(1)}, f32[2,128,1024]{2,1,0:T(8,128)}, u32[]{:S(2)}, u32[]{:S(2)}) collective-permute-start(f32[2,128,1024]{2,1,0:T(8,128)S(1)} %constant_dynamic-update-slice_fusion.8.refs_2_), channel_id=1, source_target_pairs={{0,1},{1,0},{2,3},{3,2},{4,5},{5,4},{6,7},{7,6},{8,9},{9,8},{10,11... | collective-permute-start | bytes 3145736 | tf_op jit(solution)/shard_map/ppermute | solution.py:152
  470.8 64.6 %collective-permute-start.47 = (f32[2,128,1024]{2,1,0:T(8,128)}, f32[2,128,1024]{2,1,0:T(8,128)S(1)}, u32[]{:S(2)}, u32[]{:S(2)}) collective-permute-start(f32[2,128,1024]{2,1,0:T(8,128)} %get-tuple-element.314), channel_id=1, source_target_pairs={{0,1},{1,0},{2,3},{3,2},{4,5},{5,4},{6,7},{7,6},{8,9},{9,8},{10,11... | collective-permute-start | bytes 3145736 | tf_op jit(solution)/shard_map/ppermute | solution.py:152
  470.9 66.8 %collective-permute-start.48 = (f32[2,128,1024]{2,1,0:T(8,128)}, f32[2,128,1024]{2,1,0:T(8,128)}, u32[]{:S(2)}, u32[]{:S(2)}) collective-permute-start(f32[2,128,1024]{2,1,0:T(8,128)} %get-tuple-element.316), channel_id=1, source_target_pairs={{0,2},{1,3},{2,0},{3,1},{4,6},{5,7},{6,4},{7,5},{8,10},{9,11},{10,... | collective-permute-start | bytes 3145736 | tf_op jit(solution)/shard_map/ppermute | solution.py:152
  492.8 95.3 %collective-permute-start.51 = (f32[256,2048]{1,0:T(8,128)}, f32[256,2048]{1,0:T(8,128)S(1)}, u32[]{:S(2)}, u32[]{:S(2)}) collective-permute-start(f32[256,2048]{1,0:T(8,128)} %get-tuple-element.322), channel_id=1, source_target_pairs={{0,8},{4,12},{8,16},{12,20},{16,24},{20,28},{24,0},{28,4},{1,9},{5... | collective-permute-start | bytes 6291464 | tf_op jit(solution)/shard_map/ppermute | solution.py:240
  495.2 98.5 %collective-permute-start.54 = (f32[2,2048]{1,0:T(2,128)S(1)}, f32[2,2048]{1,0:T(2,128)S(1)}, u32[]{:S(2)}, u32[]{:S(2)}) collective-permute-start(f32[2,2048]{1,0:T(2,128)S(1)} %fusion.12), channel_id=1, source_target_pairs={{0,1},{1,0},{2,3},{3,2},{4,5},{5,4},{6,7},{7,6},{8,9},{9,8},{10,11... | collective-permute-start | bytes 49160 | tf_op jit(solution)/shard_map/ppermute | solution.py:152
  538.9 52.9 %collective-permute-start.53 = (f32[1,128,1024]{2,1,0:T(8,128)S(1)}, f32[1,128,1024]{2,1,0:T(8,128)S(1)}, u32[]{:S(2)}, u32[]{:S(2)}) collective-permute-start(f32[1,128,1024]{2,1,0:T(8,128)S(1)} %slice_add_fusion.2), channel_id=1, source_target_pairs={{0,1},{1,0},{2,3},{3,2},{4,5},{5,4},{6,7},{7,6},{8,9},{9,8},{10,11... | collective-permute-start | bytes 1572872 | tf_op jit(solution)/shard_map/ppermute | solution.py:152
  577.5 64.1 %collective-permute-start.58 = (f32[2,128,1024]{2,1,0:T(8,128)S(1)}, f32[2,128,1024]{2,1,0:T(8,128)S(1)}, u32[]{:S(2)}, u32[]{:S(2)}) collective-permute-start(f32[2,128,1024]{2,1,0:T(8,128)S(1)} %constant_dynamic-update-slice_fusion.18.refs_5_), channel_id=1, source_target_pairs={{0,2},{1,3},{2,0},{3,1},{4,6},{5,7},{6,4},{7,5},{8,10},{9,11},{10,... | collective-permute-start | bytes 3145736 | tf_op jit(solution)/shard_map/ppermute | solution.py:152
  588.1 53.4 %collective-permute-start.57 = (f32[2,128,1024]{2,1,0:T(8,128)S(1)}, f32[2,128,1024]{2,1,0:T(8,128)S(1)}, u32[]{:S(2)}, u32[]{:S(2)}) collective-permute-start(f32[2,128,1024]{2,1,0:T(8,128)S(1)} %constant_dynamic-update-slice_fusion.16.refs_3_), channel_id=1, source_target_pairs={{0,1},{1,0},{2,3},{3,2},{4,5},{5,4},{6,7},{7,6},{8,9},{9,8},{10,11... | collective-permute-start | bytes 3145736 | tf_op jit(solution)/shard_map/ppermute | solution.py:152
  591.4 79.6 %collective-permute-start.61 = (f32[256,2048]{1,0:T(8,128)}, f32[256,2048]{1,0:T(8,128)}, u32[]{:S(2)}, u32[]{:S(2)}) collective-permute-start(f32[256,2048]{1,0:T(8,128)} %bitcast_add_fusion.2), channel_id=1, source_target_pairs={{0,8},{4,12},{8,16},{12,20},{16,24},{20,28},{24,0},{28,4},{1,9},{5... | collective-permute-start | bytes 6291464 | tf_op jit(solution)/shard_map/ppermute | solution.py:240
  591.8 49.7 %collective-permute-start.55 = (f32[1,128,1024]{2,1,0:T(8,128)S(1)}, f32[1,128,1024]{2,1,0:T(8,128)S(1)}, u32[]{:S(2)}, u32[]{:S(2)}) collective-permute-start(f32[1,128,1024]{2,1,0:T(8,128)S(1)} %add.372), channel_id=1, source_target_pairs={{0,2},{1,3},{2,0},{3,1},{4,6},{5,7},{6,4},{7,5},{8,10},{9,11},{10,... | collective-permute-start | bytes 1572872 | tf_op jit(solution)/shard_map/ppermute | solution.py:152
  593.7 40.7 %collective-permute-start.56 = (f32[1,128,1024]{2,1,0:T(8,128)S(1)}, f32[1,128,1024]{2,1,0:T(8,128)S(1)}, u32[]{:S(2)}, u32[]{:S(2)}) collective-permute-start(f32[1,128,1024]{2,1,0:T(8,128)S(1)} %add.373), channel_id=1, source_target_pairs={{0,1},{1,0},{2,3},{3,2},{4,5},{5,4},{6,7},{7,6},{8,9},{9,8},{10,11... | collective-permute-start | bytes 1572872 | tf_op jit(solution)/shard_map/ppermute | solution.py:152
  674.3 68.8 %collective-permute-start.65 = (f32[256,2048]{1,0:T(8,128)}, f32[256,2048]{1,0:T(8,128)}, u32[]{:S(2)}, u32[]{:S(2)}) collective-permute-start(f32[256,2048]{1,0:T(8,128)} %bitcast_add_fusion.1), channel_id=1, source_target_pairs={{0,8},{4,12},{8,16},{12,20},{16,24},{20,28},{24,0},{28,4},{1,9},{5... | collective-permute-start | bytes 6291464 | tf_op jit(solution)/shard_map/ppermute | solution.py:240
  674.3 48.0 %collective-permute-start.63 = (f32[2,128,1024]{2,1,0:T(8,128)S(1)}, f32[2,128,1024]{2,1,0:T(8,128)S(1)}, u32[]{:S(2)}, u32[]{:S(2)}) collective-permute-start(f32[2,128,1024]{2,1,0:T(8,128)S(1)} %constant_dynamic-update-slice_fusion.22.refs_5_), channel_id=1, source_target_pairs={{0,2},{1,3},{2,0},{3,1},{4,6},{5,7},{6,4},{7,5},{8,10},{9,11},{10,... | collective-permute-start | bytes 3145736 | tf_op jit(solution)/shard_map/ppermute | solution.py:152
  675.7 47.9 %collective-permute-start.62 = (f32[2,128,1024]{2,1,0:T(8,128)S(1)}, f32[2,128,1024]{2,1,0:T(8,128)S(1)}, u32[]{:S(2)}, u32[]{:S(2)}) collective-permute-start(f32[2,128,1024]{2,1,0:T(8,128)S(1)} %constant_dynamic-update-slice_fusion.20.refs_3_), channel_id=1, source_target_pairs={{0,1},{1,0},{2,3},{3,2},{4,5},{5,4},{6,7},{7,6},{8,9},{9,8},{10,11... | collective-permute-start | bytes 3145736 | tf_op jit(solution)/shard_map/ppermute | solution.py:152
  677.4 55.8 %collective-permute-start.64 = (f32[12,2048]{1,0:T(8,128)S(1)}, f32[12,2048]{1,0:T(8,128)S(1)}, u32[]{:S(2)}, u32[]{:S(2)}) collective-permute-start(f32[12,2048]{1,0:T(8,128)S(1)} %add.376), channel_id=1, source_target_pairs={{0,8},{4,12},{8,0},{12,4},{16,24},{20,28},{24,16},{28,20},{1,9},{5... | collective-permute-start | bytes 294920 | tf_op jit(solution)/shard_map/ppermute | solution.py:1178
  (110 other events, 1914.5 us)
Sparse Core Ops, SparseCore 0:
  243.7 168.6 reduce-scatter.2
  415.5 241.1 reduce-scatter.4
Sparse Core Ops, SparseCore 1:
  466.2 265.0 all-reduce.2

commit v4 on v3

--- a/solution.py
+++ b/solution.py
@@ -1069,6 +1069,11 @@
         two.update(low=low, grad=grad, vecs=functools.reduce(jnp.add, [vecs[k] for k in range(blocks)]))
         line.mark(vecs)
 
+    def hidden_of(c):
+        parts = hidden_grad(line.tie(twos[c]["grad"]), up_weight)
+        line.mark(parts[0])
+        return parts
+
     totals[0].gather()
     for other in ones[1:]:
         line.mark(*line.last, *other["sums"].pieces())
@@ -1086,35 +1091,38 @@
         line.mark(sums)
         twos.append(dict(middle=mid, second=second, stat=stat, active=active, slope=slope, sums=all_pieces(sums, bits)))
         if c == 0:
+            line.mark(sums, *twos[0]["sums"][1:])
             for total in totals[1:]:
                 for step in range(1, bits):
                     total.gather()
-        if c > 0:
-            line.mark(sums, *twos[c - 1]["sums"][1:])
-    for c in range(chunks):
+        else:
+            twos[0]["total"].advance()
+            line.mark(*line.last, *twos[c]["sums"][1:], *twos[0]["total"].got)
         mid_of(c)
+        if c == 0 and chunks > 1:
+            twos[0]["total"] = Total(line, hidden_of(0), bits)
     lows = every(twos, "low")
     down_grad = full(lows, cots)
     down_part = lax.psum_scatter(down_grad, "dp", scatter_dimension=1, tiled=True)
     up_grad = full(every(twos, "second"), every(twos, "grad"))
     up_part = lax.psum_scatter(up_grad, "dp", scatter_dimension=0, tiled=True)
-    parts = []
-    for two in twos:
-        parts.append(hidden_grad(line.tie(two["grad"]), up_weight))
-        line.mark(parts[-1][0])
-        if not totals[1:] or two is twos[0]:
-            twos[0]["total"] = Total(line, parts[0], bits)
-    for step in range(bits):
-        twos[0]["total"].advance()
-    twos[0]["total"].gather()
+    if chunks > 1:
+        for step in range(1, bits):
+            twos[0]["total"].advance()
+        twos[0]["total"].gather()
+        parts = [None] + [hidden_of(c) for c in range(1, chunks)]
+    else:
+        twos[0]["total"] = Total(line, hidden_of(0), bits)
+        for step in range(bits):
+            twos[0]["total"].advance()
+        twos[0]["total"].gather()
+    for step in range(1, bits):
+        twos[0]["total"].gather()
     for c in range(1, chunks):
         twos[c]["total"] = Total(line, [line.tie(part) for part in parts[c]], bits)
     totals = every(twos, "total")
-    for step in range(1, bits):
-        totals[0].gather()
     result = result_part(jnp.concatenate(orders), [line.tie(lows[0])] + lows[1:], down_weight)
     line.mark(result)
-    steps_of(totals, bits, [2 * bits] + [0] * (chunks - 1), bits)
     result = lax.psum(line.tie(result), "tensor")
 
     for c in range(chunks):
@@ -1126,8 +1134,6 @@
         if c == 0:
             for total in totals[1:]:
                 total.advance()
-                for step in range(bits):
-                    total.gather()
         found = attention_back(
             orders[c], lengths, line.tie(low), stat2, one["mixed"], one["qkv"], one["own"], mix_gain, mix_shift, out_weight,
             qkv_weight, tables, mask,
@@ -1136,7 +1142,15 @@
         three = dict(grad=grad, low=low, vecs=tree_sum(vecs), mix_low=found[0], dproj=found[1])
         three["narrow"] = tree_sum(found[2])
         three["wide"] = tree_sum(found[3])
-        three["total"] = Total(line, found[4:], bits)
+        parts = found[4:]
+        if c == 0 and chunks > 1:
+            for total in totals[1:]:
+                for step in range(1, bits):
+                    total.advance()
+                for step in range(bits):
+                    total.gather()
+            parts = [line.tie(part) for part in parts]
+        three["total"] = Total(line, parts, bits)
         threes.append(three)
 
     first, last = threes[0]["total"], threes[-1]["total"]

time: 780 us -> 786 us (level)
  Pallas kernels: 286 us -> 295 us
    ppermute x54, waiting for transfers between devices: 292 us -> 260 us  [flip(): lax.ppermute(value, 'tensor', [(t, t ^ 1 << bit) for t in range(size)])]
    ppermute x3, waiting for transfers between devices: 26.3 us -> 41.2 us  [send(): lax.ppermute(value, 'dp', [(d, (d + 2) % self.size) for d in range(self.s...]
    ppermute x3, waiting for transfers between devices: 6.66 us -> 18.9 us  [body(): lax.ppermute(v, 'dp', [(d, d ^ 1 << bit) for d in range(dp_size)])]
    pallas_call x24, Pallas kernels: 286 us -> 295 us  [run(): pl.pallas_call(body, grid_spec=pltpu.PrefetchScalarGridSpec(num_scalar_pr...]
  transfers between devices with their start and end apart: 70 -> 70, of which waited for: 30 -> 37; matrix products, arithmetic and copies ran while one was open for 6% -> 5% of each run, Pallas kernels for 31% -> 30%
where the time goes in v4:
time: 786 us; the launch traced here: 776 us
  waiting for transfers between devices  331 us (42%)
  Pallas kernels  295 us (38%)
  starting transfers between devices  77.5 us (10%)
  other arithmetic  27.6 us (4%)
  local copies, waits for them, and re-layouts  27 us (3%)
  between operations  17.2 us (2%)
    pallas_call x24, Pallas kernels, run(): pl.pallas_call(body, grid_spec=pltpu.PrefetchScalarGridSpec(num_scalar_pr...  295 us
    ppermute x54, waiting for transfers between devices, flip(): lax.ppermute(value, 'tensor', [(t, t ^ 1 << bit) for t in range(size)])  260 us
    ppermute x54, starting transfers between devices, flip(): lax.ppermute(value, 'tensor', [(t, t ^ 1 << bit) for t in range(size)])  64.3 us
    ppermute x3, waiting for transfers between devices, send(): lax.ppermute(value, 'dp', [(d, (d + 2) % self.size) for d in range(self.s...  41.2 us
    ppermute x3, waiting for transfers between devices, body(): lax.ppermute(v, 'dp', [(d, d ^ 1 << bit) for d in range(dp_size)])  18.9 us
  transfers between devices with their start and end apart: 70, of which 37 were waited for; matrix products, arithmetic and copies ran while one was open for 5% of the time, Pallas kernels for 30%

profile of v4, /device:TPU:0, one launch (start us, length us, event | category | flops | bytes accessed | tf_op | source)
XLA Modules:
  0.0 776.0 jit_solution(13939036105346747396)
XLA Ops:
  10.7 15.8 %front.2 = (bf16[512,2048]{1,0:T(8,128)(2,1)}, bf16[512,2048]{1,0:T(8,128)(2,1)}, bf16[512,1536]{1,0:T(8,128)(2,1)}, f32[512,512]{1,0:T(8,128)}, f32[16,512]{1,0...) custom-call(s32[4]{0:T(128)} %get-tuple-element.429.refs_0_, ...), custom_call_target="tpu_custom_call" | custom-call | flops 858000000 | bytes 1000 | tf_op jit(solution)/shard_map/front/pallas_call | solution.py:132
  31.5 15.8 %front.3 = (bf16[512,2048]{1,0:T(8,128)(2,1)}, bf16[512,2048]{1,0:T(8,128)(2,1)}, bf16[512,1536]{1,0:T(8,128)(2,1)}, f32[512,512]{1,0:T(8,128)}, f32[16,512]{1,0...) custom-call(s32[4]{0:T(128)} %get-tuple-element.430.refs_0_, ...), custom_call_target="tpu_custom_call" | custom-call | flops 858000000 | bytes 1000 | tf_op jit(solution)/shard_map/front/pallas_call | solution.py:132
  78.1 13.6 %hidden_back.1.refs_3_.refs_2_ = bf16[1024,2048]{1,0:T(8,128)(2,1)} custom-call(bf16[512,2048]{1,0:T(8,128)(2,1)} %bitcast.110, bf16[512,2048]{1,0:T(8,128)(2,1)} %bitcast.107, bf16[2048,2048]{1,0:T(8,128)(2,1)} %refs_3_.1), custom_call_target="tpu_custom_call" | custom-call | flops 22000001024 | bytes 1000 | tf_op jit(solution)/shard_map/hidden_back/pallas_call | solution.py:132
  110.8 28.7 %collective-permute-done.11 = f32[2,16,512]{2,1,0:T(8,128)S(1)} collective-permute-done((f32[2,16,512]{2,1,0:T(8,128)S(1)}, f32[2,16,512]{2,1,0:T(8,128)S(1)}, u32[]{:S(2)}, u32[]{:S(2)}) %collective-permute-start.11) | collective-permute-done | bytes 65568 | tf_op jit(solution)/shard_map/ppermute | solution.py:152
  151.3 13.6 %hidden_front.2 = (bf16[512,2048]{1,0:T(8,128)(2,1)}, bf16[512,2048]{1,0:T(8,128)(2,1)}, f32[8,512]{1,0:T(8,128)}) custom-call(bf16[512,2048]{1,0:T(8,128)(2,1)} %get-tuple-element.255.refs_0_, bf16[2048,2048]{1,0:T(8,128)(2,1)} %refs_1_.13, f32[1,2048]{1,0:T(1,128)} %bitcast.153, bf16[1024,2048]{1,0:T(8,128)(2,1)} %hidden_back.1.refs_3_.refs_2_, ...), custom_call_target="tpu_custom_call" | custom-call | flops 808499968 | bytes 1000 | tf_op jit(solution)/shard_map/hidden_front/pallas_call | solution.py:132
  205.3 13.8 %hidden_front.3 = (bf16[512,2048]{1,0:T(8,128)(2,1)}, bf16[512,2048]{1,0:T(8,128)(2,1)}, f32[8,512]{1,0:T(8,128)}) custom-call(bf16[512,2048]{1,0:T(8,128)(2,1)} %get-tuple-element.241.refs_0_.refs_1_, bf16[2048,2048]{1,0:T(8,128)(2,1)} %refs_1_.13, f32[1,2048]{1,0:T(1,128)} %bitcast.154, bf16[1024,2048]{1,0:T(8,128)(2,1)} %hidden_back.1.refs_3_.refs_2_, ...), custom_call_target="tpu_custom_call" | custom-call | flops 808499968 | bytes 1000 | tf_op jit(solution)/shard_map/hidden_front/pallas_call | solution.py:132
  232.4 18.5 %hidden_mid.3 = (bf16[512,2048]{1,0:T(8,128)(2,1)}, bf16[512,2048]{1,0:T(8,128)(2,1)}, f32[4,8,2048]{2,1,0:T(8,128)}) custom-call(bf16[512,2048]{1,0:T(8,128)(2,1)} %get-tuple-element.250.refs_0_, bf16[512,2048]{1,0:T(8,128)(2,1)} %get-tuple-element.251.refs_1_, bf16[1024,2048]{1,0:T(8,128)(2,1)} %hidden_back.1.refs_3_.refs_2_, ...), custom_call_target="tpu_custom_call" | custom-call | flops 330000000 | bytes 1000 | tf_op jit(solution)/shard_map/hidden_mid/pallas_call | solution.py:132
  250.9 14.1 %full_grad.2 = f32[2048,2048]{1,0:T(8,128)} custom-call(bf16[512,2048]{1,0:T(8,128)(2,1)} %get-tuple-element.263.refs_0_.refs_1_, bf16[512,2048]{1,0:T(8,128)(2,1)} %get-tuple-element.254.refs_1_.refs_2_, bf16[512,2048]{1,0:T(8,128)(2,1)} %bitcast.111, bf16[512,2048]{1,0:T(8,128)(2,1)} %bitcast.108), custom_call_target="tpu_custom_call" | custom-call | flops 825000000 | bytes 1000 | tf_op jit(solution)/shard_map/full_grad/pallas_call | solution.py:132
  265.0 14.1 %full_grad.3 = f32[2048,2048]{1,0:T(8,128)} custom-call(bf16[512,2048]{1,0:T(8,128)(2,1)} %get-tuple-element.255.refs_0_, bf16[512,2048]{1,0:T(8,128)(2,1)} %get-tuple-element.241.refs_0_.refs_1_, bf16[512,2048]{1,0:T(8,128)(2,1)} %get-tuple-element.231.refs_0_.refs_2_, bf16[512,2048]{1,0:T(8,128)(2,1)} %get-tuple-element.259.refs_3_.refs_0_), custom_call_target="tpu_custom_call" | custom-call | flops 825000000 | bytes 1000 | tf_op jit(solution)/shard_map/full_grad/pallas_call | solution.py:132
  299.9 15.8 %result_part.1 = f32[8,128,2048]{2,1,0:T(8,128)} custom-call(s32[8]{0:T(128)} %pad_add_fusion.refs_0_, bf16[512,2048]{1,0:T(8,128)(2,1)} %get-tuple-element.263.refs_0_.refs_1_, bf16[512,2048]{1,0:T(8,128)(2,1)} %get-tuple-element.254.refs_1_.refs_2_, bf16[2048,2048]{1,0:T(8,128)(2,1)} %refs_3_.1), custom_call_target="tpu_custom_call" | custom-call | flops 22000001024 | bytes 1000 | tf_op jit(solution)/shard_map/result_part/pallas_call | solution.py:132
  322.6 11.1 %middle_back.2 = (f32[512,2048]{1,0:T(8,128)}, bf16[512,2048]{1,0:T(8,128)(2,1)}, f32[512,128]{1,0:T(8,128)}, f32[4,8,2048]{2,1,0:T(8,128)}) custom-call(bf16[512,2048]{1,0:T(8,128)(2,1)} %get-tuple-element.334.refs_0_.refs_6_.refs_1_, bf16[512,2048]{1,0:T(8,128)(2,1)} %bitcast.112, f32[2,128,1024]{2,1,0:T(8,128)} %copy-done.7, ...), custom_call_target="tpu_custom_call" | custom-call | flops 605000000 | bytes 1000 | tf_op jit(solution)/shard_map/middle_back/pallas_call | solution.py:132
  344.0 21.7 %attention_back.2 = (bf16[512,512]{1,0:T(8,128)(2,1)}, bf16[512,1536]{1,0:T(8,128)(2,1)}, f32[2,8,1536]{2,1,0:T(8,128)}, f32[2,8,2048]{2,1,0:T(8,128)}, f32[2,12...) custom-call(s32[4]{0:T(128)} %get-tuple-element.429.refs_0_, ...), custom_call_target="tpu_custom_call" | custom-call | flops 1193500032 | bytes 1000 | tf_op jit(solution)/shard_map/attention_back/pallas_call | solution.py:132
  368.7 12.0 %collective-permute-done.38 = f32[1,128,1024]{2,1,0:T(8,128)S(1)} collective-permute-done((f32[1,128,1024]{2,1,0:T(8,128)S(1)}, f32[1,128,1024]{2,1,0:T(8,128)S(1)}, u32[]{:S(2)}, u32[]{:S(2)}) %collective-permute-start.38) | collective-permute-done | bytes 524320 | tf_op jit(solution)/shard_map/ppermute | solution.py:152
  386.8 14.0 %collective-permute-done.41.refs_5_ = f32[2,128,1024]{2,1,0:T(8,128)} collective-permute-done((f32[2,128,1024]{2,1,0:T(8,128)S(1)}, f32[2,128,1024]{2,1,0:T(8,128)}, u32[]{:S(2)}, u32[]{:S(2)}) %collective-permute-start.41) | collective-permute-done | bytes 1048608 | tf_op jit(solution)/shard_map/ppermute | solution.py:152
  401.0 11.1 %middle_back.3 = (f32[512,2048]{1,0:T(8,128)}, bf16[512,2048]{1,0:T(8,128)(2,1)}, f32[512,128]{1,0:T(8,128)}, f32[4,8,2048]{2,1,0:T(8,128)}) custom-call(bf16[512,2048]{1,0:T(8,128)(2,1)} %get-tuple-element.341.refs_0_.refs_6_.refs_1_, bf16[512,2048]{1,0:T(8,128)(2,1)} %bitcast.109, f32[2,128,1024]{2,1,0:T(8,128)} %copy-done.9, ...), custom_call_target="tpu_custom_call" | custom-call | flops 605000000 | bytes 1000 | tf_op jit(solution)/shard_map/middle_back/pallas_call | solution.py:132
  412.2 21.6 %attention_back.3 = (bf16[512,512]{1,0:T(8,128)(2,1)}, bf16[512,1536]{1,0:T(8,128)(2,1)}, f32[2,8,1536]{2,1,0:T(8,128)}, f32[2,8,2048]{2,1,0:T(8,128)}, f32[2,12...) custom-call(s32[4]{0:T(128)} %get-tuple-element.430.refs_0_, ...), custom_call_target="tpu_custom_call" | custom-call | flops 1193500032 | bytes 1000 | tf_op jit(solution)/shard_map/attention_back/pallas_call | solution.py:132
  462.5 13.4 %attention_grads.3 = (f32[256,2048]{1,0:T(8,128)}, f32[3,256,2048]{2,1,0:T(8,128)}) custom-call(s32[4]{0:T(128)} %broadcast_add_fusion.refs_0_, bf16[512,2048]{1,0:T(8,128)(2,1)} %get-tuple-element.311.refs_1_, bf16[512,2048]{1,0:T(8,128)(2,1)} %get-tuple-element.306.refs_2_, bf16[512,1536]{1,0:T(8,128)(2,1)} %get-tuple-element.307.refs_3_, ...), custom_call_target="tpu_custom_call" | custom-call | flops 660000000 | bytes 1000 | tf_op jit(solution)/shard_map/attention_grads/pallas_call | solution.py:132
  480.1 38.8 %collective-permute-done.47 = f32[2,128,1024]{2,1,0:T(8,128)S(1)} collective-permute-done((f32[2,128,1024]{2,1,0:T(8,128)}, f32[2,128,1024]{2,1,0:T(8,128)S(1)}, u32[]{:S(2)}, u32[]{:S(2)}) %collective-permute-start.47) | collective-permute-done | bytes 1048608 | tf_op jit(solution)/shard_map/ppermute | solution.py:152
  528.9 17.0 %collective-permute-done.49 = f32[1,128,1024]{2,1,0:T(8,128)S(1)} collective-permute-done((f32[1,128,1024]{2,1,0:T(8,128)S(1)}, f32[1,128,1024]{2,1,0:T(8,128)S(1)}, u32[]{:S(2)}, u32[]{:S(2)}) %collective-permute-start.49) | collective-permute-done | bytes 524320 | tf_op jit(solution)/shard_map/ppermute | solution.py:152
  546.8 13.9 %collective-permute-done.50 = f32[1,128,1024]{2,1,0:T(8,128)S(1)} collective-permute-done((f32[1,128,1024]{2,1,0:T(8,128)S(1)}, f32[1,128,1024]{2,1,0:T(8,128)S(1)}, u32[]{:S(2)}, u32[]{:S(2)}) %collective-permute-start.50) | collective-permute-done | bytes 524320 | tf_op jit(solution)/shard_map/ppermute | solution.py:152
  577.0 40.6 %collective-permute-done.56 = f32[1,128,1024]{2,1,0:T(8,128)S(1)} collective-permute-done((f32[1,128,1024]{2,1,0:T(8,128)S(1)}, f32[1,128,1024]{2,1,0:T(8,128)S(1)}, u32[]{:S(2)}, u32[]{:S(2)}) %collective-permute-start.56) | collective-permute-done | bytes 524320 | tf_op jit(solution)/shard_map/ppermute | solution.py:152
  637.5 32.3 %collective-permute-done.61 = f32[256,2048]{1,0:T(8,128)} collective-permute-done((f32[256,2048]{1,0:T(8,128)}, f32[256,2048]{1,0:T(8,128)}, u32[]{:S(2)}, u32[]{:S(2)}) %collective-permute-start.61) | collective-permute-done | bytes 2097184 | tf_op jit(solution)/shard_map/ppermute | solution.py:240
  675.0 38.7 %collective-permute-done.63.refs_6_ = f32[2,128,1024]{2,1,0:T(8,128)S(1)} collective-permute-done((f32[2,128,1024]{2,1,0:T(8,128)S(1)}, f32[2,128,1024]{2,1,0:T(8,128)S(1)}, u32[]{:S(2)}, u32[]{:S(2)}) %collective-permute-start.63) | collective-permute-done | bytes 1048608 | tf_op jit(solution)/shard_map/ppermute | solution.py:152
  723.7 13.2 %collective-permute-done.64 = f32[12,2048]{1,0:T(8,128)S(1)} collective-permute-done((f32[12,2048]{1,0:T(8,128)S(1)}, f32[12,2048]{1,0:T(8,128)S(1)}, u32[]{:S(2)}, u32[]{:S(2)}) %collective-permute-start.64) | collective-permute-done | bytes 98336 | tf_op jit(solution)/shard_map/ppermute | solution.py:1192
  (388 shorter events, 295.5 us)
Async XLA Ops:
  8.0 447.0 %reduce-scatter.3.cloned.1.call-start = ((), (), s32[]{:S(2)}) async-start(), calls=%async_computation.2 | async-start | bytes 18874368 | tf_op jit(solution)/shard_map/reduce_scatter | solution.py:1106
  106.5 42.3 %collective-permute-start.14 = (f32[1,128,1024]{2,1,0:T(8,128)}, f32[1,128,1024]{2,1,0:T(8,128)S(1)}, u32[]{:S(2)}, u32[]{:S(2)}) collective-permute-start(f32[1,128,1024]{2,1,0:T(8,128)} %slice_add_fusion.19), channel_id=1, source_target_pairs={{0,2},{1,3},{2,0},{3,1},{4,6},{5,7},{6,4},{7,5},{8,10},{9,11},{10,... | collective-permute-start | bytes 1572872 | tf_op jit(solution)/shard_map/ppermute | solution.py:152
  108.7 41.9 %collective-permute-start.15 = (f32[1,128,1024]{2,1,0:T(8,128)S(1)}, f32[1,128,1024]{2,1,0:T(8,128)S(1)}, u32[]{:S(2)}, u32[]{:S(2)}) collective-permute-start(f32[1,128,1024]{2,1,0:T(8,128)S(1)} %slice_add_fusion.18), channel_id=1, source_target_pairs={{0,1},{1,0},{2,3},{3,2},{4,5},{5,4},{6,7},{7,6},{8,9},{9,8},{10,11... | collective-permute-start | bytes 1572872 | tf_op jit(solution)/shard_map/ppermute | solution.py:152
  264.9 476.6 %reduce-scatter.5.cloned.1.call-start = ((), (), s32[]{:S(2)}) async-start(), calls=%async_computation.3 | async-start | bytes 18874368 | tf_op jit(solution)/shard_map/reduce_scatter | solution.py:1108
  279.2 474.0 %all-reduce.3.cloned.1.call-start = ((), (), s32[]{:S(2)}) async-start(), calls=%async_computation.4 | async-start | bytes 16777216 | tf_op jit(solution)/shard_map/psum | solution.py:1126
  298.1 42.1 %collective-permute-start.34 = (f32[2,128,1024]{2,1,0:T(8,128)}, f32[2,128,1024]{2,1,0:T(8,128)S(1)}, u32[]{:S(2)}, u32[]{:S(2)}) collective-permute-start(f32[2,128,1024]{2,1,0:T(8,128)} %get-tuple-element.272), channel_id=1, source_target_pairs={{0,1},{1,0},{2,3},{3,2},{4,5},{5,4},{6,7},{7,6},{8,9},{9,8},{10,11... | collective-permute-start | bytes 3145736 | tf_op jit(solution)/shard_map/ppermute | solution.py:152
  298.4 41.9 %collective-permute-start.35 = (f32[2,128,1024]{2,1,0:T(8,128)}, f32[2,128,1024]{2,1,0:T(8,128)}, u32[]{:S(2)}, u32[]{:S(2)}) collective-permute-start(f32[2,128,1024]{2,1,0:T(8,128)} %get-tuple-element.275), channel_id=1, source_target_pairs={{0,2},{1,3},{2,0},{3,1},{4,6},{5,7},{6,4},{7,5},{8,10},{9,11},{10,... | collective-permute-start | bytes 3145736 | tf_op jit(solution)/shard_map/ppermute | solution.py:152
  384.0 49.8 %collective-permute-start.42 = (f32[2,128,1024]{2,1,0:T(8,128)}, f32[2,128,1024]{2,1,0:T(8,128)S(1)}, u32[]{:S(2)}, u32[]{:S(2)}) collective-permute-start(f32[2,128,1024]{2,1,0:T(8,128)} %get-tuple-element.299), channel_id=1, source_target_pairs={{0,1},{1,0},{2,3},{3,2},{4,5},{5,4},{6,7},{7,6},{8,9},{9,8},{10,11... | collective-permute-start | bytes 3145736 | tf_op jit(solution)/shard_map/ppermute | solution.py:152
  385.0 49.7 %collective-permute-start.43 = (f32[2,128,1024]{2,1,0:T(8,128)}, f32[2,128,1024]{2,1,0:T(8,128)}, u32[]{:S(2)}, u32[]{:S(2)}) collective-permute-start(f32[2,128,1024]{2,1,0:T(8,128)} %get-tuple-element.302), channel_id=1, source_target_pairs={{0,2},{1,3},{2,0},{3,1},{4,6},{5,7},{6,4},{7,5},{8,10},{9,11},{10,... | collective-permute-start | bytes 3145736 | tf_op jit(solution)/shard_map/ppermute | solution.py:152
  454.2 64.7 %collective-permute-start.47 = (f32[2,128,1024]{2,1,0:T(8,128)}, f32[2,128,1024]{2,1,0:T(8,128)S(1)}, u32[]{:S(2)}, u32[]{:S(2)}) collective-permute-start(f32[2,128,1024]{2,1,0:T(8,128)} %get-tuple-element.322), channel_id=1, source_target_pairs={{0,1},{1,0},{2,3},{3,2},{4,5},{5,4},{6,7},{7,6},{8,9},{9,8},{10,11... | collective-permute-start | bytes 3145736 | tf_op jit(solution)/shard_map/ppermute | solution.py:152
  454.5 67.3 %collective-permute-start.48 = (f32[2,128,1024]{2,1,0:T(8,128)}, f32[2,128,1024]{2,1,0:T(8,128)}, u32[]{:S(2)}, u32[]{:S(2)}) collective-permute-start(f32[2,128,1024]{2,1,0:T(8,128)} %get-tuple-element.324), channel_id=1, source_target_pairs={{0,2},{1,3},{2,0},{3,1},{4,6},{5,7},{6,4},{7,5},{8,10},{9,11},{10,... | collective-permute-start | bytes 3145736 | tf_op jit(solution)/shard_map/ppermute | solution.py:152
  476.0 95.6 %collective-permute-start.51 = (f32[256,2048]{1,0:T(8,128)}, f32[256,2048]{1,0:T(8,128)S(1)}, u32[]{:S(2)}, u32[]{:S(2)}) collective-permute-start(f32[256,2048]{1,0:T(8,128)} %get-tuple-element.330), channel_id=1, source_target_pairs={{0,8},{4,12},{8,16},{12,20},{16,24},{20,28},{24,0},{28,4},{1,9},{5... | collective-permute-start | bytes 6291464 | tf_op jit(solution)/shard_map/ppermute | solution.py:240
  477.6 99.0 %collective-permute-start.54 = (f32[2,2048]{1,0:T(2,128)S(1)}, f32[2,2048]{1,0:T(2,128)S(1)}, u32[]{:S(2)}, u32[]{:S(2)}) collective-permute-start(f32[2,2048]{1,0:T(2,128)S(1)} %fusion.12), channel_id=1, source_target_pairs={{0,1},{1,0},{2,3},{3,2},{4,5},{5,4},{6,7},{7,6},{8,9},{9,8},{10,11... | collective-permute-start | bytes 49160 | tf_op jit(solution)/shard_map/ppermute | solution.py:152
  522.9 52.0 %collective-permute-start.53 = (f32[1,128,1024]{2,1,0:T(8,128)S(1)}, f32[1,128,1024]{2,1,0:T(8,128)S(1)}, u32[]{:S(2)}, u32[]{:S(2)}) collective-permute-start(f32[1,128,1024]{2,1,0:T(8,128)S(1)} %slice_add_fusion.2), channel_id=1, source_target_pairs={{0,1},{1,0},{2,3},{3,2},{4,5},{5,4},{6,7},{7,6},{8,9},{9,8},{10,11... | collective-permute-start | bytes 1572872 | tf_op jit(solution)/shard_map/ppermute | solution.py:152
  523.0 37.7 %collective-permute-start.50 = (f32[1,128,1024]{2,1,0:T(8,128)S(1)}, f32[1,128,1024]{2,1,0:T(8,128)S(1)}, u32[]{:S(2)}, u32[]{:S(2)}) collective-permute-start(f32[1,128,1024]{2,1,0:T(8,128)S(1)} %add.366), channel_id=1, source_target_pairs={{0,1},{1,0},{2,3},{3,2},{4,5},{5,4},{6,7},{7,6},{8,9},{9,8},{10,11... | collective-permute-start | bytes 1572872 | tf_op jit(solution)/shard_map/ppermute | solution.py:152
  560.8 64.3 %collective-permute-start.58 = (f32[2,128,1024]{2,1,0:T(8,128)S(1)}, f32[2,128,1024]{2,1,0:T(8,128)S(1)}, u32[]{:S(2)}, u32[]{:S(2)}) collective-permute-start(f32[2,128,1024]{2,1,0:T(8,128)S(1)} %constant_dynamic-update-slice_fusion.18.refs_5_), channel_id=1, source_target_pairs={{0,2},{1,3},{2,0},{3,1},{4,6},{5,7},{6,4},{7,5},{8,10},{9,11},{10,... | collective-permute-start | bytes 3145736 | tf_op jit(solution)/shard_map/ppermute | solution.py:152
  571.5 53.6 %collective-permute-start.57 = (f32[2,128,1024]{2,1,0:T(8,128)S(1)}, f32[2,128,1024]{2,1,0:T(8,128)S(1)}, u32[]{:S(2)}, u32[]{:S(2)}) collective-permute-start(f32[2,128,1024]{2,1,0:T(8,128)S(1)} %constant_dynamic-update-slice_fusion.16.refs_3_), channel_id=1, source_target_pairs={{0,1},{1,0},{2,3},{3,2},{4,5},{5,4},{6,7},{7,6},{8,9},{9,8},{10,11... | collective-permute-start | bytes 3145736 | tf_op jit(solution)/shard_map/ppermute | solution.py:152
  574.7 95.0 %collective-permute-start.61 = (f32[256,2048]{1,0:T(8,128)}, f32[256,2048]{1,0:T(8,128)}, u32[]{:S(2)}, u32[]{:S(2)}) collective-permute-start(f32[256,2048]{1,0:T(8,128)} %bitcast_add_fusion.2), channel_id=1, source_target_pairs={{0,8},{4,12},{8,16},{12,20},{16,24},{20,28},{24,0},{28,4},{1,9},{5... | collective-permute-start | bytes 6291464 | tf_op jit(solution)/shard_map/ppermute | solution.py:240
  574.9 50.2 %collective-permute-start.55 = (f32[1,128,1024]{2,1,0:T(8,128)S(1)}, f32[1,128,1024]{2,1,0:T(8,128)S(1)}, u32[]{:S(2)}, u32[]{:S(2)}) collective-permute-start(f32[1,128,1024]{2,1,0:T(8,128)S(1)} %add.372), channel_id=1, source_target_pairs={{0,2},{1,3},{2,0},{3,1},{4,6},{5,7},{6,4},{7,5},{8,10},{9,11},{10,... | collective-permute-start | bytes 1572872 | tf_op jit(solution)/shard_map/ppermute | solution.py:152
  576.6 41.1 %collective-permute-start.56 = (f32[1,128,1024]{2,1,0:T(8,128)S(1)}, f32[1,128,1024]{2,1,0:T(8,128)S(1)}, u32[]{:S(2)}, u32[]{:S(2)}) collective-permute-start(f32[1,128,1024]{2,1,0:T(8,128)S(1)} %add.373), channel_id=1, source_target_pairs={{0,1},{1,0},{2,3},{3,2},{4,5},{5,4},{6,7},{7,6},{8,9},{9,8},{10,11... | collective-permute-start | bytes 1572872 | tf_op jit(solution)/shard_map/ppermute | solution.py:152
  673.2 76.0 %collective-permute-start.65 = (f32[256,2048]{1,0:T(8,128)}, f32[256,2048]{1,0:T(8,128)}, u32[]{:S(2)}, u32[]{:S(2)}) collective-permute-start(f32[256,2048]{1,0:T(8,128)} %bitcast_add_fusion.1), channel_id=1, source_target_pairs={{0,8},{4,12},{8,16},{12,20},{16,24},{20,28},{24,0},{28,4},{1,9},{5... | collective-permute-start | bytes 6291464 | tf_op jit(solution)/shard_map/ppermute | solution.py:240
  673.2 40.5 %collective-permute-start.63 = (f32[2,128,1024]{2,1,0:T(8,128)S(1)}, f32[2,128,1024]{2,1,0:T(8,128)S(1)}, u32[]{:S(2)}, u32[]{:S(2)}) collective-permute-start(f32[2,128,1024]{2,1,0:T(8,128)S(1)} %constant_dynamic-update-slice_fusion.22.refs_5_), channel_id=1, source_target_pairs={{0,2},{1,3},{2,0},{3,1},{4,6},{5,7},{6,4},{7,5},{8,10},{9,11},{10,... | collective-permute-start | bytes 3145736 | tf_op jit(solution)/shard_map/ppermute | solution.py:152
  674.8 39.0 %collective-permute-start.62 = (f32[2,128,1024]{2,1,0:T(8,128)S(1)}, f32[2,128,1024]{2,1,0:T(8,128)S(1)}, u32[]{:S(2)}, u32[]{:S(2)}) collective-permute-start(f32[2,128,1024]{2,1,0:T(8,128)S(1)} %constant_dynamic-update-slice_fusion.20.refs_3_), channel_id=1, source_target_pairs={{0,1},{1,0},{2,3},{3,2},{4,5},{5,4},{6,7},{7,6},{8,9},{9,8},{10,11... | collective-permute-start | bytes 3145736 | tf_op jit(solution)/shard_map/ppermute | solution.py:152
  675.0 61.9 %collective-permute-start.64 = (f32[12,2048]{1,0:T(8,128)S(1)}, f32[12,2048]{1,0:T(8,128)S(1)}, u32[]{:S(2)}, u32[]{:S(2)}) collective-permute-start(f32[12,2048]{1,0:T(8,128)S(1)} %add.376), channel_id=1, source_target_pairs={{0,8},{4,12},{8,0},{12,4},{16,24},{20,28},{24,16},{28,20},{1,9},{5... | collective-permute-start | bytes 294920 | tf_op jit(solution)/shard_map/ppermute | solution.py:1192
  (109 other events, 1775.7 us)
Sparse Core Ops, SparseCore 0:
  265.1 169.6 reduce-scatter.2
  437.8 272.2 reduce-scatter.4
Sparse Core Ops, SparseCore 1:
  449.2 258.9 all-reduce.2

commit v5 on v4

--- a/solution.py
+++ b/solution.py
@@ -1097,8 +1097,10 @@
                     total.gather()
         else:
             twos[0]["total"].advance()
-            line.mark(*line.last, *twos[c]["sums"][1:], *twos[0]["total"].got)
+            line.mark(*line.last, *twos[c]["sums"][1:])
         mid_of(c)
+        if c > 0:
+            line.mark(*line.last, *twos[0]["total"].got)
         if c == 0 and chunks > 1:
             twos[0]["total"] = Total(line, hidden_of(0), bits)
     lows = every(twos, "low")
@@ -1215,14 +1217,15 @@
         vecs = line.tie(vecs) + got
         line.mark(vecs)
         got = hop(vecs, bit)
-    line.mark(*line.last, up_part)
-    for step in range(2, count - 1):
+    for step in range(2, count - 2):
         attention_part = ring.advance()
-    vecs = vecs + got
-    hid_vecs, mid_vecs, narrow, wide = vecs[:3], vecs[3:7], vecs[7:10], vecs[10:12]
     for c in range(chunks):
         output = output_of(orders[c], line.tie(twos[c]["middle"]), result, down_bias, output)
         line.mark(output)
+    line.mark(*line.last, up_part)
+    attention_part = ring.advance()
+    vecs = vecs + got
+    hid_vecs, mid_vecs, narrow, wide = vecs[:3], vecs[3:7], vecs[7:10], vecs[10:12]
     qkv_part = jnp.swapaxes(attention_part[:, : 3 * width].reshape(-1, 3, width), 0, 1)
     out_part = jnp.transpose(attention_part[:, 3 * width :])
     units = hid_gain.shape[1]

time: 786 us -> 776 us (0.987)
  Pallas kernels: 295 us -> 285 us
    ppermute x54, waiting for transfers between devices: 260 us -> 272 us  [flip(): lax.ppermute(value, 'tensor', [(t, t ^ 1 << bit) for t in range(size)])]
    pallas_call x24, Pallas kernels: 295 us -> 285 us  [run(): pl.pallas_call(body, grid_spec=pltpu.PrefetchScalarGridSpec(num_scalar_pr...]
  transfers between devices with their start and end apart: 70 -> 70, of which waited for: 37 -> 30; matrix products, arithmetic and copies ran while one was open for 5% -> 5% of each run, Pallas kernels for 30% -> 33%
where the time goes in v5:
time: 776 us; the launch traced here: 766 us
  waiting for transfers between devices  337 us (43%)
  Pallas kernels  285 us (37%)
  starting transfers between devices  74.3 us (10%)
  local copies, waits for them, and re-layouts  26.4 us (3%)
  other arithmetic  26.3 us (3%)
  between operations  17.2 us (2%)
    pallas_call x24, Pallas kernels, run(): pl.pallas_call(body, grid_spec=pltpu.PrefetchScalarGridSpec(num_scalar_pr...  285 us
    ppermute x54, waiting for transfers between devices, flip(): lax.ppermute(value, 'tensor', [(t, t ^ 1 << bit) for t in range(size)])  272 us
    ppermute x54, starting transfers between devices, flip(): lax.ppermute(value, 'tensor', [(t, t ^ 1 << bit) for t in range(size)])  63.4 us
    ppermute x3, waiting for transfers between devices, send(): lax.ppermute(value, 'dp', [(d, (d + 2) % self.size) for d in range(self.s...  35.8 us
    ppermute x3, waiting for transfers between devices, body(): lax.ppermute(v, 'dp', [(d, d ^ 1 << bit) for d in range(dp_size)])  16.4 us
  transfers between devices with their start and end apart: 70, of which 30 were waited for; matrix products, arithmetic and copies ran while one was open for 5% of the time, Pallas kernels for 33%

profile of v5, /device:TPU:0, one launch (start us, length us, event | category | flops | bytes accessed | tf_op | source)
XLA Modules:
  0.0 766.1 jit_solution(13990431088022601007)
XLA Ops:
  10.7 15.7 %front.2 = (bf16[512,2048]{1,0:T(8,128)(2,1)}, bf16[512,2048]{1,0:T(8,128)(2,1)}, bf16[512,1536]{1,0:T(8,128)(2,1)}, f32[512,512]{1,0:T(8,128)}, f32[16,512]{1,0...) custom-call(s32[4]{0:T(128)} %get-tuple-element.429.refs_0_, ...), custom_call_target="tpu_custom_call" | custom-call | flops 858000000 | bytes 1000 | tf_op jit(solution)/shard_map/front/pallas_call | solution.py:132
  31.4 15.8 %front.3 = (bf16[512,2048]{1,0:T(8,128)(2,1)}, bf16[512,2048]{1,0:T(8,128)(2,1)}, bf16[512,1536]{1,0:T(8,128)(2,1)}, f32[512,512]{1,0:T(8,128)}, f32[16,512]{1,0...) custom-call(s32[4]{0:T(128)} %get-tuple-element.430.refs_0_, ...), custom_call_target="tpu_custom_call" | custom-call | flops 858000000 | bytes 1000 | tf_op jit(solution)/shard_map/front/pallas_call | solution.py:132
  78.1 13.5 %hidden_back.1.refs_3_.refs_2_ = bf16[1024,2048]{1,0:T(8,128)(2,1)} custom-call(bf16[512,2048]{1,0:T(8,128)(2,1)} %bitcast.110, bf16[512,2048]{1,0:T(8,128)(2,1)} %bitcast.107, bf16[2048,2048]{1,0:T(8,128)(2,1)} %refs_3_.1), custom_call_target="tpu_custom_call" | custom-call | flops 22000001024 | bytes 1000 | tf_op jit(solution)/shard_map/hidden_back/pallas_call | solution.py:132
  110.7 28.7 %collective-permute-done.11 = f32[2,16,512]{2,1,0:T(8,128)S(1)} collective-permute-done((f32[2,16,512]{2,1,0:T(8,128)S(1)}, f32[2,16,512]{2,1,0:T(8,128)S(1)}, u32[]{:S(2)}, u32[]{:S(2)}) %collective-permute-start.11) | collective-permute-done | bytes 65568 | tf_op jit(solution)/shard_map/ppermute | solution.py:152
  151.2 13.6 %hidden_front.2 = (bf16[512,2048]{1,0:T(8,128)(2,1)}, bf16[512,2048]{1,0:T(8,128)(2,1)}, f32[8,512]{1,0:T(8,128)}) custom-call(bf16[512,2048]{1,0:T(8,128)(2,1)} %get-tuple-element.254.refs_0_, bf16[2048,2048]{1,0:T(8,128)(2,1)} %refs_1_.13, f32[1,2048]{1,0:T(1,128)} %bitcast.153, bf16[1024,2048]{1,0:T(8,128)(2,1)} %hidden_back.1.refs_3_.refs_2_, ...), custom_call_target="tpu_custom_call" | custom-call | flops 808499968 | bytes 1000 | tf_op jit(solution)/shard_map/hidden_front/pallas_call | solution.py:132
  205.3 13.8 %hidden_front.3 = (bf16[512,2048]{1,0:T(8,128)(2,1)}, bf16[512,2048]{1,0:T(8,128)(2,1)}, f32[8,512]{1,0:T(8,128)}) custom-call(bf16[512,2048]{1,0:T(8,128)(2,1)} %get-tuple-element.238.refs_0_.refs_1_, bf16[2048,2048]{1,0:T(8,128)(2,1)} %refs_1_.13, f32[1,2048]{1,0:T(1,128)} %bitcast.154, bf16[1024,2048]{1,0:T(8,128)(2,1)} %hidden_back.1.refs_3_.refs_2_, ...), custom_call_target="tpu_custom_call" | custom-call | flops 808499968 | bytes 1000 | tf_op jit(solution)/shard_map/hidden_front/pallas_call | solution.py:132
  233.3 14.1 %full_grad.2 = f32[2048,2048]{1,0:T(8,128)} custom-call(bf16[512,2048]{1,0:T(8,128)(2,1)} %get-tuple-element.262.refs_0_.refs_1_, bf16[512,2048]{1,0:T(8,128)(2,1)} %get-tuple-element.253.refs_1_.refs_2_, bf16[512,2048]{1,0:T(8,128)(2,1)} %bitcast.111, bf16[512,2048]{1,0:T(8,128)(2,1)} %bitcast.108), custom_call_target="tpu_custom_call" | custom-call | flops 825000000 | bytes 1000 | tf_op jit(solution)/shard_map/full_grad/pallas_call | solution.py:132
  247.4 14.1 %full_grad.3 = f32[2048,2048]{1,0:T(8,128)} custom-call(bf16[512,2048]{1,0:T(8,128)(2,1)} %get-tuple-element.254.refs_0_, bf16[512,2048]{1,0:T(8,128)(2,1)} %get-tuple-element.238.refs_0_.refs_1_, bf16[512,2048]{1,0:T(8,128)(2,1)} %get-tuple-element.231.refs_0_.refs_2_, bf16[512,2048]{1,0:T(8,128)(2,1)} %get-tuple-element.258.refs_3_.refs_0_), custom_call_target="tpu_custom_call" | custom-call | flops 825000000 | bytes 1000 | tf_op jit(solution)/shard_map/full_grad/pallas_call | solution.py:132
  275.5 15.9 %result_part.1 = f32[8,128,2048]{2,1,0:T(8,128)} custom-call(s32[8]{0:T(128)} %pad_add_fusion.refs_0_, bf16[512,2048]{1,0:T(8,128)(2,1)} %get-tuple-element.262.refs_0_.refs_1_, bf16[512,2048]{1,0:T(8,128)(2,1)} %get-tuple-element.253.refs_1_.refs_2_, bf16[2048,2048]{1,0:T(8,128)(2,1)} %refs_3_.1), custom_call_target="tpu_custom_call" | custom-call | flops 22000001024 | bytes 1000 | tf_op jit(solution)/shard_map/result_part/pallas_call | solution.py:132
  296.3 40.9 %collective-permute-done.33.refs_5_ = f32[2,128,1024]{2,1,0:T(8,128)S(1)} collective-permute-done((f32[2,128,1024]{2,1,0:T(8,128)S(1)}, f32[2,128,1024]{2,1,0:T(8,128)S(1)}, u32[]{:S(2)}, u32[]{:S(2)}) %collective-permute-start.33) | collective-permute-done | bytes 1048608 | tf_op jit(solution)/shard_map/ppermute | solution.py:152
  339.1 11.3 %middle_back.2 = (f32[512,2048]{1,0:T(8,128)}, bf16[512,2048]{1,0:T(8,128)(2,1)}, f32[512,128]{1,0:T(8,128)}, f32[4,8,2048]{2,1,0:T(8,128)}) custom-call(bf16[512,2048]{1,0:T(8,128)(2,1)} %get-tuple-element.334.refs_0_.refs_6_.refs_1_, bf16[512,2048]{1,0:T(8,128)(2,1)} %bitcast.112, f32[2,128,1024]{2,1,0:T(8,128)} %copy-done.6, f32[2,128,1024]{2,1,0:T(8,128)} %copy-done.35, ...), custom_call_target="tpu_custom_call" | custom-call | flops 605000000 | bytes 1000 | tf_op jit(solution)/shard_map/middle_back/pallas_call | solution.py:132
  350.3 31.2 %collective-permute-done.34 = f32[2,128,1024]{2,1,0:T(8,128)S(1)} collective-permute-done((f32[2,128,1024]{2,1,0:T(8,128)}, f32[2,128,1024]{2,1,0:T(8,128)S(1)}, u32[]{:S(2)}, u32[]{:S(2)}) %collective-permute-start.34) | collective-permute-done | bytes 1048608 | tf_op jit(solution)/shard_map/ppermute | solution.py:152
  383.4 21.7 %attention_back.2 = (bf16[512,512]{1,0:T(8,128)(2,1)}, bf16[512,1536]{1,0:T(8,128)(2,1)}, f32[2,8,1536]{2,1,0:T(8,128)}, f32[2,8,2048]{2,1,0:T(8,128)}, f32[2,12...) custom-call(s32[4]{0:T(128)} %get-tuple-element.429.refs_0_, ...), custom_call_target="tpu_custom_call" | custom-call | flops 1193500032 | bytes 1000 | tf_op jit(solution)/shard_map/attention_back/pallas_call | solution.py:132
  407.8 23.4 %collective-permute-done.38 = f32[1,128,1024]{2,1,0:T(8,128)S(1)} collective-permute-done((f32[1,128,1024]{2,1,0:T(8,128)S(1)}, f32[1,128,1024]{2,1,0:T(8,128)S(1)}, u32[]{:S(2)}, u32[]{:S(2)}) %collective-permute-start.38) | collective-permute-done | bytes 524320 | tf_op jit(solution)/shard_map/ppermute | solution.py:152
  437.5 29.9 %collective-permute-done.41.refs_5_ = f32[2,128,1024]{2,1,0:T(8,128)} collective-permute-done((f32[2,128,1024]{2,1,0:T(8,128)S(1)}, f32[2,128,1024]{2,1,0:T(8,128)}, u32[]{:S(2)}, u32[]{:S(2)}) %collective-permute-start.41) | collective-permute-done | bytes 1048608 | tf_op jit(solution)/shard_map/ppermute | solution.py:152
  467.4 11.0 %middle_back.3 = (f32[512,2048]{1,0:T(8,128)}, bf16[512,2048]{1,0:T(8,128)(2,1)}, f32[512,128]{1,0:T(8,128)}, f32[4,8,2048]{2,1,0:T(8,128)}) custom-call(bf16[512,2048]{1,0:T(8,128)(2,1)} %get-tuple-element.341.refs_0_.refs_6_.refs_1_, bf16[512,2048]{1,0:T(8,128)(2,1)} %bitcast.109, f32[2,128,1024]{2,1,0:T(8,128)} %copy-done.8, ...), custom_call_target="tpu_custom_call" | custom-call | flops 605000000 | bytes 1000 | tf_op jit(solution)/shard_map/middle_back/pallas_call | solution.py:132
  478.4 21.9 %attention_back.3 = (bf16[512,512]{1,0:T(8,128)(2,1)}, bf16[512,1536]{1,0:T(8,128)(2,1)}, f32[2,8,1536]{2,1,0:T(8,128)}, f32[2,8,2048]{2,1,0:T(8,128)}, f32[2,12...) custom-call(s32[4]{0:T(128)} %get-tuple-element.430.refs_0_, ...), custom_call_target="tpu_custom_call" | custom-call | flops 1193500032 | bytes 1000 | tf_op jit(solution)/shard_map/attention_back/pallas_call | solution.py:132
  504.4 10.8 %attention_grads.2 = f32[4,256,2048]{2,1,0:T(8,128)} custom-call(s32[4]{0:T(128)} %add_subtract_fusion.refs_0_, bf16[512,2048]{1,0:T(8,128)(2,1)} %get-tuple-element.317.refs_1_, bf16[512,2048]{1,0:T(8,128)(2,1)} %get-tuple-element.312.refs_2_, bf16[512,1536]{1,0:T(8,128)(2,1)} %get-tuple-element.313.refs_3_, bf16[512,1536]{1,0:T(8,128)(2,1)} %get-tuple-element.314.refs_4_, ...), custom_call_target="tpu_custom_call" | custom-call | flops 660000000 | bytes 1000 | tf_op jit(solution)/shard_map/attention_grads/pallas_call | solution.py:132
  529.1 13.4 %attention_grads.3 = (f32[256,2048]{1,0:T(8,128)}, f32[3,256,2048]{2,1,0:T(8,128)}) custom-call(s32[4]{0:T(128)} %broadcast_add_fusion.refs_0_, bf16[512,2048]{1,0:T(8,128)(2,1)} %get-tuple-element.317.refs_1_, bf16[512,2048]{1,0:T(8,128)(2,1)} %get-tuple-element.312.refs_2_, bf16[512,1536]{1,0:T(8,128)(2,1)} %get-tuple-element.313.refs_3_, ...), custom_call_target="tpu_custom_call" | custom-call | flops 660000000 | bytes 1000 | tf_op jit(solution)/shard_map/attention_grads/pallas_call | solution.py:132
  548.5 20.9 %collective-permute-done.47 = f32[2,128,1024]{2,1,0:T(8,128)S(1)} collective-permute-done((f32[2,128,1024]{2,1,0:T(8,128)}, f32[2,128,1024]{2,1,0:T(8,128)S(1)}, u32[]{:S(2)}, u32[]{:S(2)}) %collective-permute-start.47) | collective-permute-done | bytes 1048608 | tf_op jit(solution)/shard_map/ppermute | solution.py:152
  597.2 33.4 %collective-permute-done.51 = f32[256,2048]{1,0:T(8,128)S(1)} collective-permute-done((f32[256,2048]{1,0:T(8,128)}, f32[256,2048]{1,0:T(8,128)S(1)}, u32[]{:S(2)}, u32[]{:S(2)}) %collective-permute-start.51) | collective-permute-done | bytes 2097184 | tf_op jit(solution)/shard_map/ppermute | solution.py:240
  636.2 30.7 %collective-permute-done.56 = f32[1,128,1024]{2,1,0:T(8,128)S(1)} collective-permute-done((f32[1,128,1024]{2,1,0:T(8,128)S(1)}, f32[1,128,1024]{2,1,0:T(8,128)S(1)}, u32[]{:S(2)}, u32[]{:S(2)}) %collective-permute-start.56) | collective-permute-done | bytes 524320 | tf_op jit(solution)/shard_map/ppermute | solution.py:152
  688.3 21.7 %collective-permute-done.63.refs_6_ = f32[2,128,1024]{2,1,0:T(8,128)S(1)} collective-permute-done((f32[2,128,1024]{2,1,0:T(8,128)S(1)}, f32[2,128,1024]{2,1,0:T(8,128)S(1)}, u32[]{:S(2)}, u32[]{:S(2)}) %collective-permute-start.63) | collective-permute-done | bytes 1048608 | tf_op jit(solution)/shard_map/ppermute | solution.py:152
  720.8 16.0 %collective-permute-done.64 = f32[12,2048]{1,0:T(8,128)S(1)} collective-permute-done((f32[12,2048]{1,0:T(8,128)S(1)}, f32[12,2048]{1,0:T(8,128)S(1)}, u32[]{:S(2)}, u32[]{:S(2)}) %collective-permute-start.64) | collective-permute-done | bytes 98336 | tf_op jit(solution)/shard_map/ppermute | solution.py:1194
  (381 shorter events, 265.4 us)
Async XLA Ops:
  8.0 513.0 %reduce-scatter.3.cloned.1.call-start = ((), (), s32[]{:S(2)}) async-start(), calls=%async_computation.2 | async-start | bytes 18874368 | tf_op jit(solution)/shard_map/reduce_scatter | solution.py:1108
  59.4 36.2 %collective-permute-start.7 = (f32[2,128,1024]{2,1,0:T(8,128)}, f32[2,128,1024]{2,1,0:T(8,128)S(1)}, u32[]{:S(2)}, u32[]{:S(2)}) collective-permute-start(f32[2,128,1024]{2,1,0:T(8,128)} %get-tuple-element.211), channel_id=1, source_target_pairs={{0,2},{1,3},{2,0},{3,1},{4,6},{5,7},{6,4},{7,5},{8,10},{9,11},{10,... | collective-permute-start | bytes 3145736 | tf_op jit(solution)/shard_map/ppermute | solution.py:152
  104.2 35.8 %collective-permute-start.13 = (f32[2,128,1024]{2,1,0:T(8,128)S(1)}, f32[2,128,1024]{2,1,0:T(8,128)S(1)}, u32[]{:S(2)}, u32[]{:S(2)}) collective-permute-start(f32[2,128,1024]{2,1,0:T(8,128)S(1)} %constant_dynamic-update-slice_fusion.2.refs_3_), channel_id=1, source_target_pairs={{0,2},{1,3},{2,0},{3,1},{4,6},{5,7},{6,4},{7,5},{8,10},{9,11},{10,... | collective-permute-start | bytes 3145736 | tf_op jit(solution)/shard_map/ppermute | solution.py:152
  106.5 42.3 %collective-permute-start.14 = (f32[1,128,1024]{2,1,0:T(8,128)}, f32[1,128,1024]{2,1,0:T(8,128)S(1)}, u32[]{:S(2)}, u32[]{:S(2)}) collective-permute-start(f32[1,128,1024]{2,1,0:T(8,128)} %slice_add_fusion.19), channel_id=1, source_target_pairs={{0,2},{1,3},{2,0},{3,1},{4,6},{5,7},{6,4},{7,5},{8,10},{9,11},{10,... | collective-permute-start | bytes 1572872 | tf_op jit(solution)/shard_map/ppermute | solution.py:152
  108.6 41.9 %collective-permute-start.15 = (f32[1,128,1024]{2,1,0:T(8,128)S(1)}, f32[1,128,1024]{2,1,0:T(8,128)S(1)}, u32[]{:S(2)}, u32[]{:S(2)}) collective-permute-start(f32[1,128,1024]{2,1,0:T(8,128)S(1)} %slice_add_fusion.18), channel_id=1, source_target_pairs={{0,1},{1,0},{2,3},{3,2},{4,5},{5,4},{6,7},{7,6},{8,9},{9,8},{10,11... | collective-permute-start | bytes 1572872 | tf_op jit(solution)/shard_map/ppermute | solution.py:152
  247.4 490.6 %all-reduce.3.cloned.1.call-start = ((), (), s32[]{:S(2)}) async-start(), calls=%async_computation.3 | async-start | bytes 16777216 | tf_op jit(solution)/shard_map/psum | solution.py:1128
  291.4 458.3 %reduce-scatter.5.cloned.1.call-start = ((), (), s32[]{:S(2)}) async-start(), calls=%async_computation.4 | async-start | bytes 18874368 | tf_op jit(solution)/shard_map/reduce_scatter | solution.py:1110
  292.2 45.0 %collective-permute-start.33 = (f32[2,128,1024]{2,1,0:T(8,128)S(1)}, f32[2,128,1024]{2,1,0:T(8,128)S(1)}, u32[]{:S(2)}, u32[]{:S(2)}) collective-permute-start(f32[2,128,1024]{2,1,0:T(8,128)S(1)} %constant_dynamic-update-slice_fusion.10.refs_4_), channel_id=1, source_target_pairs={{0,2},{1,3},{2,0},{3,1},{4,6},{5,7},{6,4},{7,5},{8,10},{9,11},{10,... | collective-permute-start | bytes 3145736 | tf_op jit(solution)/shard_map/ppermute | solution.py:152
  292.9 45.2 %collective-permute-start.32 = (f32[2,128,1024]{2,1,0:T(8,128)S(1)}, f32[2,128,1024]{2,1,0:T(8,128)S(1)}, u32[]{:S(2)}, u32[]{:S(2)}) collective-permute-start(f32[2,128,1024]{2,1,0:T(8,128)S(1)} %constant_dynamic-update-slice_fusion.8.refs_2_), channel_id=1, source_target_pairs={{0,1},{1,0},{2,3},{3,2},{4,5},{5,4},{6,7},{7,6},{8,9},{9,8},{10,11... | collective-permute-start | bytes 3145736 | tf_op jit(solution)/shard_map/ppermute | solution.py:152
  293.0 88.5 %collective-permute-start.34 = (f32[2,128,1024]{2,1,0:T(8,128)}, f32[2,128,1024]{2,1,0:T(8,128)S(1)}, u32[]{:S(2)}, u32[]{:S(2)}) collective-permute-start(f32[2,128,1024]{2,1,0:T(8,128)} %get-tuple-element.271), channel_id=1, source_target_pairs={{0,1},{1,0},{2,3},{3,2},{4,5},{5,4},{6,7},{7,6},{8,9},{9,8},{10,11... | collective-permute-start | bytes 3145736 | tf_op jit(solution)/shard_map/ppermute | solution.py:152
  294.9 86.7 %collective-permute-start.35 = (f32[2,128,1024]{2,1,0:T(8,128)S(1)}, f32[2,128,1024]{2,1,0:T(8,128)S(1)}, u32[]{:S(2)}, u32[]{:S(2)}) collective-permute-start(f32[2,128,1024]{2,1,0:T(8,128)S(1)} %copy-done.58), channel_id=1, source_target_pairs={{0,2},{1,3},{2,0},{3,1},{4,6},{5,7},{6,4},{7,5},{8,10},{9,11},{10,... | collective-permute-start | bytes 3145736 | tf_op jit(solution)/shard_map/ppermute | solution.py:152
  435.4 64.9 %collective-permute-start.42 = (f32[2,128,1024]{2,1,0:T(8,128)}, f32[2,128,1024]{2,1,0:T(8,128)S(1)}, u32[]{:S(2)}, u32[]{:S(2)}) collective-permute-start(f32[2,128,1024]{2,1,0:T(8,128)} %get-tuple-element.304), channel_id=1, source_target_pairs={{0,1},{1,0},{2,3},{3,2},{4,5},{5,4},{6,7},{7,6},{8,9},{9,8},{10,11... | collective-permute-start | bytes 3145736 | tf_op jit(solution)/shard_map/ppermute | solution.py:152
  435.5 65.7 %collective-permute-start.43 = (f32[2,128,1024]{2,1,0:T(8,128)}, f32[2,128,1024]{2,1,0:T(8,128)}, u32[]{:S(2)}, u32[]{:S(2)}) collective-permute-start(f32[2,128,1024]{2,1,0:T(8,128)} %get-tuple-element.307), channel_id=1, source_target_pairs={{0,2},{1,3},{2,0},{3,1},{4,6},{5,7},{6,4},{7,5},{8,10},{9,11},{10,... | collective-permute-start | bytes 3145736 | tf_op jit(solution)/shard_map/ppermute | solution.py:152
  519.7 49.7 %collective-permute-start.47 = (f32[2,128,1024]{2,1,0:T(8,128)}, f32[2,128,1024]{2,1,0:T(8,128)S(1)}, u32[]{:S(2)}, u32[]{:S(2)}) collective-permute-start(f32[2,128,1024]{2,1,0:T(8,128)} %get-tuple-element.322), channel_id=1, source_target_pairs={{0,1},{1,0},{2,3},{3,2},{4,5},{5,4},{6,7},{7,6},{8,9},{9,8},{10,11... | collective-permute-start | bytes 3145736 | tf_op jit(solution)/shard_map/ppermute | solution.py:152
  520.0 49.5 %collective-permute-start.48 = (f32[2,128,1024]{2,1,0:T(8,128)}, f32[2,128,1024]{2,1,0:T(8,128)}, u32[]{:S(2)}, u32[]{:S(2)}) collective-permute-start(f32[2,128,1024]{2,1,0:T(8,128)} %get-tuple-element.324), channel_id=1, source_target_pairs={{0,2},{1,3},{2,0},{3,1},{4,6},{5,7},{6,4},{7,5},{8,10},{9,11},{10,... | collective-permute-start | bytes 3145736 | tf_op jit(solution)/shard_map/ppermute | solution.py:152
  542.6 88.0 %collective-permute-start.51 = (f32[256,2048]{1,0:T(8,128)}, f32[256,2048]{1,0:T(8,128)S(1)}, u32[]{:S(2)}, u32[]{:S(2)}) collective-permute-start(f32[256,2048]{1,0:T(8,128)} %get-tuple-element.330), channel_id=1, source_target_pairs={{0,8},{4,12},{8,16},{12,20},{16,24},{20,28},{24,0},{28,4},{1,9},{5... | collective-permute-start | bytes 6291464 | tf_op jit(solution)/shard_map/ppermute | solution.py:240
  545.9 89.6 %collective-permute-start.54 = (f32[2,2048]{1,0:T(2,128)S(1)}, f32[2,2048]{1,0:T(2,128)S(1)}, u32[]{:S(2)}, u32[]{:S(2)}) collective-permute-start(f32[2,2048]{1,0:T(2,128)S(1)} %fusion.12), channel_id=1, source_target_pairs={{0,1},{1,0},{2,3},{3,2},{4,5},{5,4},{6,7},{7,6},{8,9},{9,8},{10,11... | collective-permute-start | bytes 49160 | tf_op jit(solution)/shard_map/ppermute | solution.py:152
  570.6 63.2 %collective-permute-start.53 = (f32[1,128,1024]{2,1,0:T(8,128)S(1)}, f32[1,128,1024]{2,1,0:T(8,128)S(1)}, u32[]{:S(2)}, u32[]{:S(2)}) collective-permute-start(f32[1,128,1024]{2,1,0:T(8,128)S(1)} %slice_add_fusion.2), channel_id=1, source_target_pairs={{0,1},{1,0},{2,3},{3,2},{4,5},{5,4},{6,7},{7,6},{8,9},{9,8},{10,11... | collective-permute-start | bytes 1572872 | tf_op jit(solution)/shard_map/ppermute | solution.py:152
  585.8 47.9 %collective-permute-start.52 = (f32[1,128,1024]{2,1,0:T(8,128)S(1)}, f32[1,128,1024]{2,1,0:T(8,128)S(1)}, u32[]{:S(2)}, u32[]{:S(2)}) collective-permute-start(f32[1,128,1024]{2,1,0:T(8,128)S(1)} %slice_add_fusion.3), channel_id=1, source_target_pairs={{0,2},{1,3},{2,0},{3,1},{4,6},{5,7},{6,4},{7,5},{8,10},{9,11},{10,... | collective-permute-start | bytes 1572872 | tf_op jit(solution)/shard_map/ppermute | solution.py:152
  595.6 72.6 %collective-permute-start.58 = (f32[2,128,1024]{2,1,0:T(8,128)S(1)}, f32[2,128,1024]{2,1,0:T(8,128)S(1)}, u32[]{:S(2)}, u32[]{:S(2)}) collective-permute-start(f32[2,128,1024]{2,1,0:T(8,128)S(1)} %constant_dynamic-update-slice_fusion.18.refs_5_), channel_id=1, source_target_pairs={{0,2},{1,3},{2,0},{3,1},{4,6},{5,7},{6,4},{7,5},{8,10},{9,11},{10,... | collective-permute-start | bytes 3145736 | tf_op jit(solution)/shard_map/ppermute | solution.py:152
  630.6 37.7 %collective-permute-start.57 = (f32[2,128,1024]{2,1,0:T(8,128)S(1)}, f32[2,128,1024]{2,1,0:T(8,128)S(1)}, u32[]{:S(2)}, u32[]{:S(2)}) collective-permute-start(f32[2,128,1024]{2,1,0:T(8,128)S(1)} %constant_dynamic-update-slice_fusion.16.refs_3_), channel_id=1, source_target_pairs={{0,1},{1,0},{2,3},{3,2},{4,5},{5,4},{6,7},{7,6},{8,9},{9,8},{10,11... | collective-permute-start | bytes 3145736 | tf_op jit(solution)/shard_map/ppermute | solution.py:152
  633.7 49.3 %collective-permute-start.61 = (f32[256,2048]{1,0:T(8,128)}, f32[256,2048]{1,0:T(8,128)}, u32[]{:S(2)}, u32[]{:S(2)}) collective-permute-start(f32[256,2048]{1,0:T(8,128)} %bitcast_add_fusion.2), channel_id=1, source_target_pairs={{0,8},{4,12},{8,16},{12,20},{16,24},{20,28},{24,0},{28,4},{1,9},{5... | collective-permute-start | bytes 6291464 | tf_op jit(solution)/shard_map/ppermute | solution.py:240
  686.2 65.4 %collective-permute-start.66 = (f32[256,2048]{1,0:T(8,128)}, f32[256,2048]{1,0:T(8,128)}, u32[]{:S(2)}, u32[]{:S(2)}) collective-permute-start(f32[256,2048]{1,0:T(8,128)} %bitcast_add_fusion.1), channel_id=1, source_target_pairs={{0,8},{4,12},{8,16},{12,20},{16,24},{20,28},{24,0},{28,4},{1,9},{5... | collective-permute-start | bytes 6291464 | tf_op jit(solution)/shard_map/ppermute | solution.py:240
  688.3 48.5 %collective-permute-start.64 = (f32[12,2048]{1,0:T(8,128)S(1)}, f32[12,2048]{1,0:T(8,128)S(1)}, u32[]{:S(2)}, u32[]{:S(2)}) collective-permute-start(f32[12,2048]{1,0:T(8,128)S(1)} %add.376), channel_id=1, source_target_pairs={{0,8},{4,12},{8,0},{12,4},{16,24},{20,28},{24,16},{28,20},{1,9},{5... | collective-permute-start | bytes 294920 | tf_op jit(solution)/shard_map/ppermute | solution.py:1194
  (105 other events, 1795.5 us)
Sparse Core Ops, SparseCore 0:
  247.5 169.5 reduce-scatter.2
  420.2 204.1 reduce-scatter.4
Sparse Core Ops, SparseCore 1:
  291.5 259.9 all-reduce.2

commit v6 on v5

--- a/solution.py
+++ b/solution.py
@@ -31,7 +31,7 @@
     "hidden_mid": 6.0,
     "hidden_grad": 7.0,
     "full_grad": 15.0,
-    "attention_grads": 12.0,
+    "ring_grads": 12.0,
     "result_part": 400.0,
     "middle_back": 11.0,
     "attention_back": 21.7,
@@ -873,44 +873,44 @@
     )[0]
 
 
-def attention_grads(ids, firsts, dprojs, lows, mixes, got=None):
-    count, many = ids.shape[0], len(firsts)
-    rows = firsts[0].shape[0]
-    wide, tall = dprojs[0].shape[1], mixes[0].shape[1]
+def ring_grads(ids, products, got=None):
+    count, many = ids.shape[0], len(products[0][0])
+    rows = products[0][0][0].shape[0]
+    widths = [rights[0].shape[1] for lefts, rights in products]
     block = D // (2 * count)
-    shape = (block, wide + tall)
+    shape = (block, sum(widths))
 
     def kernel(ids_ref, *refs):
-        parts = [refs[at * many : (at + 1) * many] for at in range(4)]
-        outs = refs[4 * many + (got is not None) :]
-        total = []
-        for left, right in ((parts[0], parts[1]), (parts[2], parts[3])):
+        outs = refs[2 * many * len(products) + (got is not None) :]
+        step = pl.program_id(0)
+        start = 0
+        for at, width in enumerate(widths):
+            left, right = (refs[(2 * at + side) * many : (2 * at + side + 1) * many] for side in range(2))
             value = mul(left[0][...], right[0][...], TN)
-            for at in range(1, many):
-                value += mul(left[at][...], right[at][...], TN)
-            total.append(value)
-        if got is None:
-            outs[0][0, :, :wide] = total[0]
-            outs[0][0, :, wide:] = total[1]
-            return
-        more = refs[4 * many]
-        step = pl.program_id(0)
-
-        @pl.when(step == 0)
-        def _():
-            outs[0][:, :wide] = total[0] + more[0, :, :wide]
-            outs[0][:, wide:] = total[1] + more[0, :, wide:]
-
-        @pl.when(step > 0)
-        def _():
-            outs[1][0, :, :wide] = total[0] + more[0, :, :wide]
-            outs[1][0, :, wide:] = total[1] + more[0, :, wide:]
+            for k in range(1, many):
+                value += mul(left[k][...], right[k][...], TN)
+            c = slice(start, start + width)
+            start += width
+            if got is None:
+                outs[0][0, :, c] = value
+                continue
+            value += refs[2 * many * len(products)][0, :, c]
+
+            @pl.when(step == 0)
+            def _(value=value, c=c):
+                outs[0][:, c] = value
+
+            @pl.when(step > 0)
+            def _(value=value, c=c):
+                outs[1][0, :, c] = value
 
     fixed = lambda i, *_: (0, 0)
     moving = lambda i, ids_ref: (0, ids_ref[i])
     lead = lambda i, *_: (i, 0, 0)
-    ins = [(left, (rows, block), moving) for left in firsts] + [(right, (rows, wide), fixed) for right in dprojs]
-    ins += [(left, (rows, block), moving) for left in lows] + [(right, (rows, tall), fixed) for right in mixes]
+    ins = []
+    for lefts, rights in products:
+        ins += [(left, (rows, block), moving) for left in lefts]
+        ins += [(right, right.shape, fixed) for right in rights]
     if got is None:
         outs = [((count,) + shape, F32, (1,) + shape, lead)]
     else:
@@ -919,24 +919,31 @@
             (shape, F32, shape, fixed),
             ((count - 1,) + shape, F32, (1,) + shape, lambda i, *_: (jnp.maximum(i - 1, 0), 0, 0)),
         ]
-    return run(kernel, (count,), ins, outs, prefetch=(ids,), name="attention_grads")
-
-
-def full_grad(lefts, rights):
-    rows, many, block = lefts[0].shape[0], len(lefts), 512
-    wide, tall = lefts[0].shape[1], rights[0].shape[1]
+    return run(kernel, (count,), ins, outs, prefetch=(ids,), name="ring_grads")
+
+
+def full_grad(products):
+    many, block = len(products[0][0]), 512
+    rows, tall = products[0][0][0].shape
+    widths = [rights[0].shape[1] for lefts, rights in products]
 
     def kernel(*refs):
-        left, right, out = refs[:many], refs[many : 2 * many], refs[2 * many]
-        value = mul(left[0][...], right[0][...], TN)
-        for at in range(1, many):
-            value += mul(left[at][...], right[at][...], TN)
-        out[...] = value
-
-    ins = [(left, (rows, block), lambda i: (0, i)) for left in lefts]
-    ins += [(right, (rows, tall), lambda i: (0, 0)) for right in rights]
+        out, start = refs[-1], 0
+        for at, width in enumerate(widths):
+            left, right = (refs[(2 * at + side) * many : (2 * at + side + 1) * many] for side in range(2))
+            value = mul(left[0][...], right[0][...], TN)
+            for k in range(1, many):
+                value += mul(left[k][...], right[k][...], TN)
+            out[:, start : start + width] = value
+            start += width
+
+    ins = []
+    for lefts, rights in products:
+        ins += [(left, (rows, block), lambda i: (0, i)) for left in lefts]
+        ins += [(right, right.shape, lambda i: (0, 0)) for right in rights]
+    wide = sum(widths)
     return run(
-        kernel, (wide // block,), ins, [((wide, tall), F32, (block, tall), lambda i: (i, 0))], name="full_grad"
+        kernel, (tall // block,), ins, [((tall, wide), F32, (block, wide), lambda i: (i, 0))], name="full_grad"
     )[0]
 
 
@@ -1015,8 +1022,12 @@
     around = lax.rem(place // 2 + count - 1 - jnp.arange(count, dtype=jnp.int32), count)
     mine_ids, other_ids = 2 * around + lax.rem(place, 2), 2 * around + 1 - lax.rem(place, 2)
 
-    def full(lefts, rights):
-        grad = full_grad([line.tie(lefts[0])] + lefts[1:], rights)
+    def tied(products):
+        (lefts, rights), others = products[0], products[1:]
+        return [([line.tie(lefts[0])] + lefts[1:], rights)] + others
+
+    def full(products):
+        grad = full_grad(tied(products))
         line.mark(grad)
         return grad
 
@@ -1104,10 +1115,12 @@
         if c == 0 and chunks > 1:
             twos[0]["total"] = Total(line, hidden_of(0), bits)
     lows = every(twos, "low")
-    down_grad = full(lows, cots)
+    down_grad = full([(lows, cots)])
     down_part = lax.psum_scatter(down_grad, "dp", scatter_dimension=1, tiled=True)
-    up_grad = full(every(twos, "second"), every(twos, "grad"))
-    up_part = lax.psum_scatter(up_grad, "dp", scatter_dimension=0, tiled=True)
+    up_products = [(every(twos, "second"), every(twos, "grad"))]
+    sent = ring_grads(other_ids, tied(up_products))[0]
+    line.mark(sent)
+    sent = lax.ppermute(sent, "dp", [(d, d ^ 1) for d in range(dp_size)])
     if chunks > 1:
         for step in range(1, bits):
             twos[0]["total"].advance()
@@ -1118,6 +1131,9 @@
         for step in range(bits):
             twos[0]["total"].advance()
         twos[0]["total"].gather()
+    ring_first, ring_rest = ring_grads(mine_ids, tied(up_products), sent)
+    line.mark(ring_rest)
+    ring = Ring(line, ring_first, ring_rest, dp_size)
     for step in range(1, bits):
         twos[0]["total"].gather()
     for c in range(1, chunks):
@@ -1125,7 +1141,6 @@
     totals = every(twos, "total")
     result = result_part(jnp.concatenate(orders), [line.tie(lows[0])] + lows[1:], down_weight)
     line.mark(result)
-    result = lax.psum(line.tie(result), "tensor")
 
     for c in range(chunks):
         one, two = ones[c], twos[c]
@@ -1151,6 +1166,10 @@
                     total.advance()
                 for step in range(bits):
                     total.gather()
+            for total in totals[1:]:
+                line.mark(*line.last, *total.got)
+            up_part = ring.advance()
+            result = lax.psum(line.tie(result), "tensor")
             parts = [line.tie(part) for part in parts]
         three["total"] = Total(line, parts, bits)
         threes.append(three)
@@ -1162,17 +1181,13 @@
     pad = lambda v: jnp.pad(v, ((0, 0), (0, D - v.shape[1])))
     wide = add(threes, "wide", 2)
     got = flip(wide, 0, blocks)
-    grads_of = lambda ids, sent: attention_grads(
-        ids, [line.tie(ones[0]["first"])] + every(ones, "first")[1:], every(threes, "dproj"), every(threes, "low"),
-        every(threes, "mix_low"), sent,
+    attention_grad = full(
+        [(every(ones, "first"), every(threes, "dproj")), (every(threes, "low"), every(threes, "mix_low"))]
     )
-    sent = grads_of(other_ids, None)[0]
-    line.mark(sent)
-    sent = lax.ppermute(sent, "dp", [(d, d ^ 1) for d in range(dp_size)])
-    line.mark(*line.last, down_part)
-    ring_first, ring_rest = grads_of(mine_ids, sent)
-    line.mark(ring_rest)
-    ring = Ring(line, ring_first, ring_rest, dp_size)
+    attention_part = lax.psum_scatter(attention_grad, "dp", scatter_dimension=0, tiled=True)
+    if chunks == 1:
+        up_part = ring.advance()
+        result = lax.psum(line.tie(result), "tensor")
     for step in range(1 if chunks > 1 else 0, bits):
         first.advance()
     first.gather()
@@ -1180,7 +1195,8 @@
         last.advance()
     for step in range(1, bits):
         first.gather()
-    attention_part = ring.advance()
+    line.mark(*line.last, down_part)
+    up_part = ring.advance()
     if chunks > 1:
         for step in range(1, bits):
             last.advance()
@@ -1212,18 +1228,15 @@
             vecs = line.tie(vecs) + got
             line.mark(vecs)
             got = hop(vecs, 1)
-            attention_part = ring.advance()
     for bit in range(2, dp_bits):
         vecs = line.tie(vecs) + got
         line.mark(vecs)
         got = hop(vecs, bit)
-    for step in range(2, count - 2):
-        attention_part = ring.advance()
+    for step in range(2, count - 1):
+        up_part = ring.advance()
     for c in range(chunks):
         output = output_of(orders[c], line.tie(twos[c]["middle"]), result, down_bias, output)
         line.mark(output)
-    line.mark(*line.last, up_part)
-    attention_part = ring.advance()
     vecs = vecs + got
     hid_vecs, mid_vecs, narrow, wide = vecs[:3], vecs[3:7], vecs[7:10], vecs[10:12]
     qkv_part = jnp.swapaxes(attention_part[:, : 3 * width].reshape(-1, 3, width), 0, 1)

time: 776 us -> 739 us (0.952)
  waiting for transfers between devices: 337 us -> 289 us
    ppermute x3, waiting for transfers between devices: 35.8 us -> 0.01 us  [send(): lax.ppermute(value, 'dp', [(d, (d + 2) % self.size) for d in range(self.s...]
    ppermute x1, waiting for transfers between devices: 8.13 us -> 0.01 us  [body(): sent = lax.ppermute(sent, 'dp', [(d, d ^ 1) for d in range(dp_size)])]
  transfers between devices with their start and end apart: 70 -> 70, of which waited for: 30 -> 30; matrix products, arithmetic and copies ran while one was open for 5% -> 5% of each run, Pallas kernels for 33% -> 35%
where the time goes in v6:
time: 739 us; the launch traced here: 729 us
  waiting for transfers between devices  289 us (39%)
  Pallas kernels  286 us (39%)
  starting transfers between devices  80.3 us (11%)
  other arithmetic  28.7 us (4%)
  local copies, waits for them, and re-layouts  27.4 us (4%)
  between operations  17.1 us (2%)
    pallas_call x24, Pallas kernels, run(): pl.pallas_call(body, grid_spec=pltpu.PrefetchScalarGridSpec(num_scalar_pr...  286 us
    ppermute x54, waiting for transfers between devices, flip(): lax.ppermute(value, 'tensor', [(t, t ^ 1 << bit) for t in range(size)])  272 us
    ppermute x54, starting transfers between devices, flip(): lax.ppermute(value, 'tensor', [(t, t ^ 1 << bit) for t in range(size)])  59 us
  transfers between devices with their start and end apart: 70, of which 30 were waited for; matrix products, arithmetic and copies ran while one was open for 5% of the time, Pallas kernels for 35%

profile of v6, /device:TPU:0, one launch (start us, length us, event | category | flops | bytes accessed | tf_op | source)
XLA Modules:
  0.0 728.6 jit_solution(563143288358315726)
XLA Ops:
  10.7 15.7 %front.2 = (bf16[512,2048]{1,0:T(8,128)(2,1)}, bf16[512,2048]{1,0:T(8,128)(2,1)}, bf16[512,1536]{1,0:T(8,128)(2,1)}, f32[512,512]{1,0:T(8,128)}, f32[16,512]{1,0...) custom-call(s32[4]{0:T(128)} %get-tuple-element.429.refs_0_, ...), custom_call_target="tpu_custom_call" | custom-call | flops 858000000 | bytes 1000 | tf_op jit(solution)/shard_map/front/pallas_call | solution.py:132
  31.5 15.9 %front.3 = (bf16[512,2048]{1,0:T(8,128)(2,1)}, bf16[512,2048]{1,0:T(8,128)(2,1)}, bf16[512,1536]{1,0:T(8,128)(2,1)}, f32[512,512]{1,0:T(8,128)}, f32[16,512]{1,0...) custom-call(s32[4]{0:T(128)} %get-tuple-element.430.refs_0_, ...), custom_call_target="tpu_custom_call" | custom-call | flops 858000000 | bytes 1000 | tf_op jit(solution)/shard_map/front/pallas_call | solution.py:132
  78.1 13.5 %hidden_back.1.refs_3_.refs_2_ = bf16[1024,2048]{1,0:T(8,128)(2,1)} custom-call(bf16[512,2048]{1,0:T(8,128)(2,1)} %bitcast.110, bf16[512,2048]{1,0:T(8,128)(2,1)} %bitcast.107, bf16[2048,2048]{1,0:T(8,128)(2,1)} %refs_3_.1), custom_call_target="tpu_custom_call" | custom-call | flops 22000001024 | bytes 1000 | tf_op jit(solution)/shard_map/hidden_back/pallas_call | solution.py:132
  110.8 28.7 %collective-permute-done.11 = f32[2,16,512]{2,1,0:T(8,128)S(1)} collective-permute-done((f32[2,16,512]{2,1,0:T(8,128)S(1)}, f32[2,16,512]{2,1,0:T(8,128)S(1)}, u32[]{:S(2)}, u32[]{:S(2)}) %collective-permute-start.11) | collective-permute-done | bytes 65568 | tf_op jit(solution)/shard_map/ppermute | solution.py:152
  151.4 13.6 %hidden_front.2 = (bf16[512,2048]{1,0:T(8,128)(2,1)}, bf16[512,2048]{1,0:T(8,128)(2,1)}, f32[8,512]{1,0:T(8,128)}) custom-call(bf16[512,2048]{1,0:T(8,128)(2,1)} %get-tuple-element.260.refs_0_.refs_1_, bf16[2048,2048]{1,0:T(8,128)(2,1)} %refs_1_.13, f32[1,2048]{1,0:T(1,128)} %bitcast.153, bf16[1024,2048]{1,0:T(8,128)(2,1)} %hidden_back.1.refs_3_.refs_2_, ...), custom_call_target="tpu_custom_call" | custom-call | flops 808499968 | bytes 1000 | tf_op jit(solution)/shard_map/hidden_front/pallas_call | solution.py:132
  181.2 9.7 %hidden_grad.2 = (f32[2,128,1024]{2,1,0:T(8,128)}, f32[2,128,1024]{2,1,0:T(8,128)}, f32[2,128,1024]{2,1,0:T(8,128)}, f32[2,128,1024]{2,1,0:T(8,128)}) custom-call(bf16[512,2048]{1,0:T(8,128)(2,1)} %get-tuple-element.231.refs_0_.refs_3_, bf16[2048,2048]{1,0:T(8,128)(2,1)} %refs_1_.13), custom_call_target="tpu_custom_call" | custom-call | flops 385000000 | bytes 1000 | tf_op jit(solution)/shard_map/hidden_grad/pallas_call | solution.py:132
  205.4 13.8 %hidden_front.3 = (bf16[512,2048]{1,0:T(8,128)(2,1)}, bf16[512,2048]{1,0:T(8,128)(2,1)}, f32[8,512]{1,0:T(8,128)}) custom-call(bf16[512,2048]{1,0:T(8,128)(2,1)} %get-tuple-element.238.refs_0_.refs_2_, bf16[2048,2048]{1,0:T(8,128)(2,1)} %refs_1_.13, f32[1,2048]{1,0:T(1,128)} %bitcast.154, bf16[1024,2048]{1,0:T(8,128)(2,1)} %hidden_back.1.refs_3_.refs_2_, ...), custom_call_target="tpu_custom_call" | custom-call | flops 808499968 | bytes 1000 | tf_op jit(solution)/shard_map/hidden_front/pallas_call | solution.py:132
  233.4 14.1 %full_grad.2 = f32[2048,2048]{1,0:T(8,128)} custom-call(bf16[512,2048]{1,0:T(8,128)(2,1)} %get-tuple-element.264.refs_0_.refs_1_, bf16[512,2048]{1,0:T(8,128)(2,1)} %get-tuple-element.254.refs_1_.refs_2_, bf16[512,2048]{1,0:T(8,128)(2,1)} %bitcast.111, bf16[512,2048]{1,0:T(8,128)(2,1)} %bitcast.108), custom_call_target="tpu_custom_call" | custom-call | flops 825000000 | bytes 1000 | tf_op jit(solution)/shard_map/full_grad/pallas_call | solution.py:132
  248.1 9.8 %ring_grads.2 = f32[4,256,2048]{2,1,0:T(8,128)} custom-call(s32[4]{0:T(128)} %add_subtract_fusion.refs_0_, bf16[512,2048]{1,0:T(8,128)(2,1)} %get-tuple-element.260.refs_0_.refs_1_, bf16[512,2048]{1,0:T(8,128)(2,1)} %get-tuple-element.238.refs_0_.refs_2_, bf16[512,2048]{1,0:T(8,128)(2,1)} %get-tuple-element.231.refs_0_.refs_3_, ...), custom_call_target="tpu_custom_call" | custom-call | flops 660000000 | bytes 1000 | tf_op jit(solution)/shard_map/ring_grads/pallas_call | solution.py:132
  272.3 12.9 %ring_grads.3 = (f32[256,2048]{1,0:T(8,128)}, f32[3,256,2048]{2,1,0:T(8,128)}) custom-call(s32[4]{0:T(128)} %broadcast_add_fusion.refs_0_, bf16[512,2048]{1,0:T(8,128)(2,1)} %get-tuple-element.260.refs_0_.refs_1_, bf16[512,2048]{1,0:T(8,128)(2,1)} %get-tuple-element.238.refs_0_.refs_2_, bf16[512,2048]{1,0:T(8,128)(2,1)} %get-tuple-element.231.refs_0_.refs_3_, ...), custom_call_target="tpu_custom_call" | custom-call | flops 660000000 | bytes 1000 | tf_op jit(solution)/shard_map/ring_grads/pallas_call | solution.py:132
  291.0 16.1 %result_part.1 = f32[8,128,2048]{2,1,0:T(8,128)} custom-call(s32[8]{0:T(128)} %pad_add_fusion.refs_0_, bf16[512,2048]{1,0:T(8,128)(2,1)} %get-tuple-element.264.refs_0_.refs_1_, bf16[512,2048]{1,0:T(8,128)(2,1)} %get-tuple-element.254.refs_1_.refs_2_, bf16[2048,2048]{1,0:T(8,128)(2,1)} %refs_3_.1), custom_call_target="tpu_custom_call" | custom-call | flops 22000001024 | bytes 1000 | tf_op jit(solution)/shard_map/result_part/pallas_call | solution.py:132
  312.8 11.2 %middle_back.2 = (f32[512,2048]{1,0:T(8,128)}, bf16[512,2048]{1,0:T(8,128)(2,1)}, f32[512,128]{1,0:T(8,128)}, f32[4,8,2048]{2,1,0:T(8,128)}) custom-call(bf16[512,2048]{1,0:T(8,128)(2,1)} %get-tuple-element.335.refs_0_.refs_6_.refs_1_, bf16[512,2048]{1,0:T(8,128)(2,1)} %bitcast.112, f32[2,128,1024]{2,1,0:T(8,128)} %copy-done.5, ...), custom_call_target="tpu_custom_call" | custom-call | flops 605000000 | bytes 1000 | tf_op jit(solution)/shard_map/middle_back/pallas_call | solution.py:132
  323.9 10.1 %collective-permute-done.35 = f32[2,128,1024]{2,1,0:T(8,128)S(1)} collective-permute-done((f32[2,128,1024]{2,1,0:T(8,128)}, f32[2,128,1024]{2,1,0:T(8,128)S(1)}, u32[]{:S(2)}, u32[]{:S(2)}) %collective-permute-start.35) | collective-permute-done | bytes 1048608 | tf_op jit(solution)/shard_map/ppermute | solution.py:152
  338.7 21.5 %attention_back.2 = (bf16[512,512]{1,0:T(8,128)(2,1)}, bf16[512,1536]{1,0:T(8,128)(2,1)}, f32[2,8,1536]{2,1,0:T(8,128)}, f32[2,8,2048]{2,1,0:T(8,128)}, f32[2,12...) custom-call(s32[4]{0:T(128)} %get-tuple-element.429.refs_0_, ...), custom_call_target="tpu_custom_call" | custom-call | flops 1193500032 | bytes 1000 | tf_op jit(solution)/shard_map/attention_back/pallas_call | solution.py:132
  362.2 10.5 %collective-permute-done.39 = f32[1,128,1024]{2,1,0:T(8,128)S(1)} collective-permute-done((f32[1,128,1024]{2,1,0:T(8,128)S(1)}, f32[1,128,1024]{2,1,0:T(8,128)S(1)}, u32[]{:S(2)}, u32[]{:S(2)}) %collective-permute-start.39) | collective-permute-done | bytes 524320 | tf_op jit(solution)/shard_map/ppermute | solution.py:152
  375.0 21.6 %collective-permute-done.42.refs_5_ = f32[2,128,1024]{2,1,0:T(8,128)S(1)} collective-permute-done((f32[2,128,1024]{2,1,0:T(8,128)S(1)}, f32[2,128,1024]{2,1,0:T(8,128)S(1)}, u32[]{:S(2)}, u32[]{:S(2)}) %collective-permute-start.42) | collective-permute-done | bytes 1048608 | tf_op jit(solution)/shard_map/ppermute | solution.py:152
  404.1 11.2 %middle_back.3 = (f32[512,2048]{1,0:T(8,128)}, bf16[512,2048]{1,0:T(8,128)(2,1)}, f32[512,128]{1,0:T(8,128)}, f32[4,8,2048]{2,1,0:T(8,128)}) custom-call(bf16[512,2048]{1,0:T(8,128)(2,1)} %get-tuple-element.341.refs_0_.refs_6_.refs_1_, bf16[512,2048]{1,0:T(8,128)(2,1)} %bitcast.109, f32[2,128,1024]{2,1,0:T(8,128)} %copy-done.7, f32[2,128,1024]{2,1,0:T(8,128)} %copy-done.30, ...), custom_call_target="tpu_custom_call" | custom-call | flops 605000000 | bytes 1000 | tf_op jit(solution)/shard_map/middle_back/pallas_call | solution.py:132
  415.3 22.1 %attention_back.3 = (bf16[512,512]{1,0:T(8,128)(2,1)}, bf16[512,1536]{1,0:T(8,128)(2,1)}, f32[2,8,1536]{2,1,0:T(8,128)}, f32[2,8,2048]{2,1,0:T(8,128)}, f32[2,12...) custom-call(s32[4]{0:T(128)} %get-tuple-element.430.refs_0_, ...), custom_call_target="tpu_custom_call" | custom-call | flops 1193500032 | bytes 1000 | tf_op jit(solution)/shard_map/attention_back/pallas_call | solution.py:132
  443.5 15.7 %full_grad.3 = f32[2048,2048]{1,0:T(8,128)} custom-call(bf16[512,2048]{1,0:T(8,128)(2,1)} %get-tuple-element.315.refs_0_, bf16[512,2048]{1,0:T(8,128)(2,1)} %get-tuple-element.316.refs_1_, bf16[512,1536]{1,0:T(8,128)(2,1)} %get-tuple-element.317.refs_2_, bf16[512,1536]{1,0:T(8,128)(2,1)} %get-tuple-element.318.refs_3_, ...), custom_call_target="tpu_custom_call" | custom-call | flops 825000000 | bytes 1000 | tf_op jit(solution)/shard_map/full_grad/pallas_call | solution.py:132
  467.6 53.2 %collective-permute-done.46 = f32[1,128,1024]{2,1,0:T(8,128)S(1)} collective-permute-done((f32[1,128,1024]{2,1,0:T(8,128)S(1)}, f32[1,128,1024]{2,1,0:T(8,128)S(1)}, u32[]{:S(2)}, u32[]{:S(2)}) %collective-permute-start.46) | collective-permute-done | bytes 524320 | tf_op jit(solution)/shard_map/ppermute | solution.py:152
  527.8 10.9 %collective-permute-done.50 = f32[1,128,1024]{2,1,0:T(8,128)S(1)} collective-permute-done((f32[1,128,1024]{2,1,0:T(8,128)S(1)}, f32[1,128,1024]{2,1,0:T(8,128)S(1)}, u32[]{:S(2)}, u32[]{:S(2)}) %collective-permute-start.50) | collective-permute-done | bytes 524320 | tf_op jit(solution)/shard_map/ppermute | solution.py:152
  539.3 21.7 %collective-permute-done.51 = f32[1,128,1024]{2,1,0:T(8,128)S(1)} collective-permute-done((f32[1,128,1024]{2,1,0:T(8,128)S(1)}, f32[1,128,1024]{2,1,0:T(8,128)S(1)}, u32[]{:S(2)}, u32[]{:S(2)}) %collective-permute-start.51) | collective-permute-done | bytes 524320 | tf_op jit(solution)/shard_map/ppermute | solution.py:152
  575.1 42.5 %collective-permute-done.57 = f32[1,128,1024]{2,1,0:T(8,128)S(1)} collective-permute-done((f32[1,128,1024]{2,1,0:T(8,128)S(1)}, f32[1,128,1024]{2,1,0:T(8,128)S(1)}, u32[]{:S(2)}, u32[]{:S(2)}) %collective-permute-start.57) | collective-permute-done | bytes 524320 | tf_op jit(solution)/shard_map/ppermute | solution.py:152
  634.6 37.4 %collective-permute-done.63.refs_6_ = f32[2,128,1024]{2,1,0:T(8,128)S(1)} collective-permute-done((f32[2,128,1024]{2,1,0:T(8,128)S(1)}, f32[2,128,1024]{2,1,0:T(8,128)S(1)}, u32[]{:S(2)}, u32[]{:S(2)}) %collective-permute-start.63) | collective-permute-done | bytes 1048608 | tf_op jit(solution)/shard_map/ppermute | solution.py:152
  (372 shorter events, 258.4 us)
Async XLA Ops:
  8.0 554.7 %reduce-scatter.3.cloned.1.call-start = ((), (), s32[]{:S(2)}) async-start(), calls=%async_computation.2 | async-start | bytes 18874368 | tf_op jit(solution)/shard_map/reduce_scatter | solution.py:1119
  106.5 42.4 %collective-permute-start.14 = (f32[1,128,1024]{2,1,0:T(8,128)}, f32[1,128,1024]{2,1,0:T(8,128)S(1)}, u32[]{:S(2)}, u32[]{:S(2)}) collective-permute-start(f32[1,128,1024]{2,1,0:T(8,128)} %slice_add_fusion.19), channel_id=1, source_target_pairs={{0,2},{1,3},{2,0},{3,1},{4,6},{5,7},{6,4},{7,5},{8,10},{9,11},{10,... | collective-permute-start | bytes 1572872 | tf_op jit(solution)/shard_map/ppermute | solution.py:152
  108.7 41.9 %collective-permute-start.15 = (f32[1,128,1024]{2,1,0:T(8,128)S(1)}, f32[1,128,1024]{2,1,0:T(8,128)S(1)}, u32[]{:S(2)}, u32[]{:S(2)}) collective-permute-start(f32[1,128,1024]{2,1,0:T(8,128)S(1)} %slice_add_fusion.18), channel_id=1, source_target_pairs={{0,1},{1,0},{2,3},{3,2},{4,5},{5,4},{6,7},{7,6},{8,9},{9,8},{10,11... | collective-permute-start | bytes 1572872 | tf_op jit(solution)/shard_map/ppermute | solution.py:152
  247.5 452.6 %all-reduce.3.cloned.1.call-start = ((), (), s32[]{:S(2)}) async-start(), calls=%async_computation.3 | async-start | bytes 16777216 | tf_op jit(solution)/shard_map/psum | solution.py:1172
  288.3 45.7 %collective-permute-start.35 = (f32[2,128,1024]{2,1,0:T(8,128)}, f32[2,128,1024]{2,1,0:T(8,128)S(1)}, u32[]{:S(2)}, u32[]{:S(2)}) collective-permute-start(f32[2,128,1024]{2,1,0:T(8,128)} %get-tuple-element.273), channel_id=1, source_target_pairs={{0,1},{1,0},{2,3},{3,2},{4,5},{5,4},{6,7},{7,6},{8,9},{9,8},{10,11... | collective-permute-start | bytes 3145736 | tf_op jit(solution)/shard_map/ppermute | solution.py:152
  288.6 45.4 %collective-permute-start.36 = (f32[2,128,1024]{2,1,0:T(8,128)}, f32[2,128,1024]{2,1,0:T(8,128)}, u32[]{:S(2)}, u32[]{:S(2)}) collective-permute-start(f32[2,128,1024]{2,1,0:T(8,128)} %get-tuple-element.276), channel_id=1, source_target_pairs={{0,2},{1,3},{2,0},{3,1},{4,6},{5,7},{6,4},{7,5},{8,10},{9,11},{10,... | collective-permute-start | bytes 3145736 | tf_op jit(solution)/shard_map/ppermute | solution.py:152
  289.5 108.5 %collective-permute-start.43 = (f32[256,2048]{1,0:T(8,128)}, f32[256,2048]{1,0:T(8,128)}, u32[]{:S(2)}, u32[]{:S(2)}) collective-permute-start(f32[256,2048]{1,0:T(8,128)} %get-tuple-element.289), channel_id=1, source_target_pairs={{0,8},{4,12},{8,16},{12,20},{16,24},{20,28},{24,0},{28,4},{1,9},{5... | collective-permute-start | bytes 6291464 | tf_op jit(solution)/shard_map/ppermute | solution.py:240
  402.0 313.1 %reduce-scatter.5.cloned.1.call-start = ((), (), s32[]{:S(2)}) async-start(), calls=%async_computation.4 | async-start | bytes 18874368 | tf_op jit(solution)/shard_map/reduce_scatter | solution.py:1187
  402.7 40.6 %collective-permute-start.45 = (f32[2,128,1024]{2,1,0:T(8,128)}, f32[2,128,1024]{2,1,0:T(8,128)S(1)}, u32[]{:S(2)}, u32[]{:S(2)}) collective-permute-start(f32[2,128,1024]{2,1,0:T(8,128)} %get-tuple-element.311), channel_id=1, source_target_pairs={{0,2},{1,3},{2,0},{3,1},{4,6},{5,7},{6,4},{7,5},{8,10},{9,11},{10,... | collective-permute-start | bytes 3145736 | tf_op jit(solution)/shard_map/ppermute | solution.py:152
  461.1 101.7 %collective-permute-start.52 = (f32[256,2048]{1,0:T(8,128)}, f32[256,2048]{1,0:T(8,128)}, u32[]{:S(2)}, u32[]{:S(2)}) collective-permute-start(f32[256,2048]{1,0:T(8,128)} %bitcast_add_fusion.2), channel_id=1, source_target_pairs={{0,8},{4,12},{8,16},{12,20},{16,24},{20,28},{24,0},{28,4},{1,9},{5... | collective-permute-start | bytes 6291464 | tf_op jit(solution)/shard_map/ppermute | solution.py:240
  463.3 59.1 %collective-permute-start.48 = (f32[2,128,1024]{2,1,0:T(8,128)}, f32[2,128,1024]{2,1,0:T(8,128)S(1)}, u32[]{:S(2)}, u32[]{:S(2)}) collective-permute-start(f32[2,128,1024]{2,1,0:T(8,128)} %get-tuple-element.324), channel_id=1, source_target_pairs={{0,1},{1,0},{2,3},{3,2},{4,5},{5,4},{6,7},{7,6},{8,9},{9,8},{10,11... | collective-permute-start | bytes 3145736 | tf_op jit(solution)/shard_map/ppermute | solution.py:152
  465.1 58.3 %collective-permute-start.49 = (f32[2,128,1024]{2,1,0:T(8,128)S(1)}, f32[2,128,1024]{2,1,0:T(8,128)S(1)}, u32[]{:S(2)}, u32[]{:S(2)}) collective-permute-start(f32[2,128,1024]{2,1,0:T(8,128)S(1)} %copy-done.53), channel_id=1, source_target_pairs={{0,2},{1,3},{2,0},{3,1},{4,6},{5,7},{6,4},{7,5},{8,10},{9,11},{10,... | collective-permute-start | bytes 3145736 | tf_op jit(solution)/shard_map/ppermute | solution.py:152
  466.9 55.5 %collective-permute-start.47 = (f32[1,128,1024]{2,1,0:T(8,128)S(1)}, f32[1,128,1024]{2,1,0:T(8,128)S(1)}, u32[]{:S(2)}, u32[]{:S(2)}) collective-permute-start(f32[1,128,1024]{2,1,0:T(8,128)S(1)} %slice_add_fusion.6), channel_id=1, source_target_pairs={{0,1},{1,0},{2,3},{3,2},{4,5},{5,4},{6,7},{7,6},{8,9},{9,8},{10,11... | collective-permute-start | bytes 1572872 | tf_op jit(solution)/shard_map/ppermute | solution.py:152
  467.2 53.7 %collective-permute-start.46 = (f32[1,128,1024]{2,1,0:T(8,128)S(1)}, f32[1,128,1024]{2,1,0:T(8,128)S(1)}, u32[]{:S(2)}, u32[]{:S(2)}) collective-permute-start(f32[1,128,1024]{2,1,0:T(8,128)S(1)} %slice_add_fusion.7), channel_id=1, source_target_pairs={{0,2},{1,3},{2,0},{3,1},{4,6},{5,7},{6,4},{7,5},{8,10},{9,11},{10,... | collective-permute-start | bytes 1572872 | tf_op jit(solution)/shard_map/ppermute | solution.py:152
  520.9 50.6 %collective-permute-start.55 = (f32[2,2048]{1,0:T(2,128)S(1)}, f32[2,2048]{1,0:T(2,128)S(1)}, u32[]{:S(2)}, u32[]{:S(2)}) collective-permute-start(f32[2,2048]{1,0:T(2,128)S(1)} %fusion.12), channel_id=1, source_target_pairs={{0,1},{1,0},{2,3},{3,2},{4,5},{5,4},{6,7},{7,6},{8,9},{9,8},{10,11... | collective-permute-start | bytes 49160 | tf_op jit(solution)/shard_map/ppermute | solution.py:152
  524.2 44.0 %collective-permute-start.54 = (f32[1,128,1024]{2,1,0:T(8,128)}, f32[1,128,1024]{2,1,0:T(8,128)}, u32[]{:S(2)}, u32[]{:S(2)}) collective-permute-start(f32[1,128,1024]{2,1,0:T(8,128)} %slice_add_fusion.2), channel_id=1, source_target_pairs={{0,1},{1,0},{2,3},{3,2},{4,5},{5,4},{6,7},{7,6},{8,9},{9,8},{10,11... | collective-permute-start | bytes 1572872 | tf_op jit(solution)/shard_map/ppermute | solution.py:152
  561.0 57.6 %collective-permute-start.59 = (f32[2,128,1024]{2,1,0:T(8,128)S(1)}, f32[2,128,1024]{2,1,0:T(8,128)}, u32[]{:S(2)}, u32[]{:S(2)}) collective-permute-start(f32[2,128,1024]{2,1,0:T(8,128)S(1)} %constant_dynamic-update-slice_fusion.18.refs_5_), channel_id=1, source_target_pairs={{0,2},{1,3},{2,0},{3,1},{4,6},{5,7},{6,4},{7,5},{8,10},{9,11},{10,... | collective-permute-start | bytes 3145736 | tf_op jit(solution)/shard_map/ppermute | solution.py:152
  562.7 55.9 %collective-permute-start.58 = (f32[2,128,1024]{2,1,0:T(8,128)S(1)}, f32[2,128,1024]{2,1,0:T(8,128)S(1)}, u32[]{:S(2)}, u32[]{:S(2)}) collective-permute-start(f32[2,128,1024]{2,1,0:T(8,128)S(1)} %constant_dynamic-update-slice_fusion.16.refs_3_), channel_id=1, source_target_pairs={{0,1},{1,0},{2,3},{3,2},{4,5},{5,4},{6,7},{7,6},{8,9},{9,8},{10,11... | collective-permute-start | bytes 3145736 | tf_op jit(solution)/shard_map/ppermute | solution.py:152
  567.9 50.7 %collective-permute-start.56 = (f32[1,128,1024]{2,1,0:T(8,128)S(1)}, f32[1,128,1024]{2,1,0:T(8,128)S(1)}, u32[]{:S(2)}, u32[]{:S(2)}) collective-permute-start(f32[1,128,1024]{2,1,0:T(8,128)S(1)} %add.373), channel_id=1, source_target_pairs={{0,2},{1,3},{2,0},{3,1},{4,6},{5,7},{6,4},{7,5},{8,10},{9,11},{10,... | collective-permute-start | bytes 1572872 | tf_op jit(solution)/shard_map/ppermute | solution.py:152
  569.3 48.3 %collective-permute-start.57 = (f32[1,128,1024]{2,1,0:T(8,128)S(1)}, f32[1,128,1024]{2,1,0:T(8,128)S(1)}, u32[]{:S(2)}, u32[]{:S(2)}) collective-permute-start(f32[1,128,1024]{2,1,0:T(8,128)S(1)} %add.374), channel_id=1, source_target_pairs={{0,1},{1,0},{2,3},{3,2},{4,5},{5,4},{6,7},{7,6},{8,9},{9,8},{10,11... | collective-permute-start | bytes 1572872 | tf_op jit(solution)/shard_map/ppermute | solution.py:152
  571.4 124.8 %collective-permute-start.65 = (f32[256,2048]{1,0:T(8,128)}, f32[256,2048]{1,0:T(8,128)}, u32[]{:S(2)}, u32[]{:S(2)}) collective-permute-start(f32[256,2048]{1,0:T(8,128)} %bitcast_add_fusion.1), channel_id=1, source_target_pairs={{0,8},{4,12},{8,16},{12,20},{16,24},{20,28},{24,0},{28,4},{1,9},{5... | collective-permute-start | bytes 6291464 | tf_op jit(solution)/shard_map/ppermute | solution.py:240
  628.9 43.1 %collective-permute-start.63 = (f32[2,128,1024]{2,1,0:T(8,128)S(1)}, f32[2,128,1024]{2,1,0:T(8,128)S(1)}, u32[]{:S(2)}, u32[]{:S(2)}) collective-permute-start(f32[2,128,1024]{2,1,0:T(8,128)S(1)} %constant_dynamic-update-slice_fusion.22.refs_5_), channel_id=1, source_target_pairs={{0,2},{1,3},{2,0},{3,1},{4,6},{5,7},{6,4},{7,5},{8,10},{9,11},{10,... | collective-permute-start | bytes 3145736 | tf_op jit(solution)/shard_map/ppermute | solution.py:152
  630.1 41.9 %collective-permute-start.62 = (f32[2,128,1024]{2,1,0:T(8,128)S(1)}, f32[2,128,1024]{2,1,0:T(8,128)S(1)}, u32[]{:S(2)}, u32[]{:S(2)}) collective-permute-start(f32[2,128,1024]{2,1,0:T(8,128)S(1)} %constant_dynamic-update-slice_fusion.20.refs_3_), channel_id=1, source_target_pairs={{0,1},{1,0},{2,3},{3,2},{4,5},{5,4},{6,7},{7,6},{8,9},{9,8},{10,11... | collective-permute-start | bytes 3145736 | tf_op jit(solution)/shard_map/ppermute | solution.py:152
  631.6 50.3 %collective-permute-start.64 = (f32[12,2048]{1,0:T(8,128)S(1)}, f32[12,2048]{1,0:T(8,128)S(1)}, u32[]{:S(2)}, u32[]{:S(2)}) collective-permute-start(f32[12,2048]{1,0:T(8,128)S(1)} %add.377), channel_id=1, source_target_pairs={{0,8},{4,12},{8,0},{12,4},{16,24},{20,28},{24,16},{28,20},{1,9},{5... | collective-permute-start | bytes 294920 | tf_op jit(solution)/shard_map/ppermute | solution.py:1210
  (101 other events, 1715.9 us)
Sparse Core Ops, SparseCore 0:
  247.6 216.9 reduce-scatter.2
  467.1 247.9 reduce-scatter.4
Sparse Core Ops, SparseCore 1:
  402.1 269.9 all-reduce.2

commit v7 on v6

--- a/solution.py
+++ b/solution.py
@@ -28,7 +28,7 @@
     "middle_norm": 7.5,
     "hidden_back": 400.0,
     "hidden_front": 14.7,
-    "hidden_mid": 6.0,
+    "hidden_mid": 400.0,
     "hidden_grad": 7.0,
     "full_grad": 15.0,
     "ring_grads": 12.0,
@@ -1086,8 +1086,6 @@
         return parts
 
     totals[0].gather()
-    for other in ones[1:]:
-        line.mark(*line.last, *other["sums"].pieces())
     for c in range(chunks):
         one = ones[c]
         mid, second, stat = middle_norm(
@@ -1098,14 +1096,16 @@
             for total in totals[1:]:
                 total.advance()
                 total.gather()
+            for other in ones[1:]:
+                line.mark(*line.last, *other["sums"].pieces())
         active, slope, sums = hidden_front(c, line.tie(second), up_weight, up_bias, back, hid_gain)
         line.mark(sums)
         twos.append(dict(middle=mid, second=second, stat=stat, active=active, slope=slope, sums=all_pieces(sums, bits)))
         if c == 0:
-            line.mark(sums, *twos[0]["sums"][1:])
             for total in totals[1:]:
                 for step in range(1, bits):
                     total.gather()
+            line.mark(*line.last, *twos[0]["sums"][1:])
         else:
             twos[0]["total"].advance()
             line.mark(*line.last, *twos[c]["sums"][1:])
@@ -1175,8 +1175,6 @@
         threes.append(three)
 
     first, last = threes[0]["total"], threes[-1]["total"]
-    if chunks > 1:
-        first.advance()
     add = lambda items, name, size: functools.reduce(jnp.add, [item[name] for item in items])[:size]
     pad = lambda v: jnp.pad(v, ((0, 0), (0, D - v.shape[1])))
     wide = add(threes, "wide", 2)
@@ -1184,19 +1182,19 @@
     attention_grad = full(
         [(every(ones, "first"), every(threes, "dproj")), (every(threes, "low"), every(threes, "mix_low"))]
     )
-    attention_part = lax.psum_scatter(attention_grad, "dp", scatter_dimension=0, tiled=True)
     if chunks == 1:
         up_part = ring.advance()
         result = lax.psum(line.tie(result), "tensor")
-    for step in range(1 if chunks > 1 else 0, bits):
+    for step in range(bits):
         first.advance()
     first.gather()
     if chunks > 1:
         last.advance()
+    line.mark(*line.last, down_part)
+    up_part = ring.advance()
+    attention_part = lax.psum_scatter(line.tie(attention_grad), "dp", scatter_dimension=0, tiled=True)
     for step in range(1, bits):
         first.gather()
-    line.mark(*line.last, down_part)
-    up_part = ring.advance()
     if chunks > 1:
         for step in range(1, bits):
             last.advance()
@@ -1222,6 +1220,8 @@
             )
             line.mark(vecs)
             got = hop(vecs, 0)
+            for step in range(2, count - 1):
+                up_part = ring.advance()
             if chunks > 1:
                 for step in range(1, bits):
                     last.gather()
@@ -1232,8 +1232,6 @@
         vecs = line.tie(vecs) + got
         line.mark(vecs)
         got = hop(vecs, bit)
-    for step in range(2, count - 1):
-        up_part = ring.advance()
     for c in range(chunks):
         output = output_of(orders[c], line.tie(twos[c]["middle"]), result, down_bias, output)
         line.mark(output)

time: 739 us -> 753 us (1.019)
  waiting for transfers between devices: 289 us -> 298 us
    reduce_scatter x1, waiting for transfers between devices: 3.18 us -> 19.5 us  [body(): lax.psum_scatter(line.tie(attention_grad), 'dp', scatter_dimension=0, til...]
    ppermute x3, waiting for transfers between devices: 10.2 us -> 1.69 us  [body(): lax.ppermute(v, 'dp', [(d, d ^ 1 << bit) for d in range(dp_size)])]
  transfers between devices with their start and end apart: 70 -> 70, of which waited for: 30 -> 27; matrix products, arithmetic and copies ran while one was open for 5% -> 6% of each run, Pallas kernels for 35% -> 35%
where the time goes in v7:
time: 753 us; the launch traced here: 742 us
  waiting for transfers between devices  298 us (40%)
  Pallas kernels  286 us (38%)
  starting transfers between devices  76.8 us (10%)
  other arithmetic  32.8 us (4%)
  local copies, waits for them, and re-layouts  31 us (4%)
  between operations  17.3 us (2%)
    pallas_call x24, Pallas kernels, run(): pl.pallas_call(body, grid_spec=pltpu.PrefetchScalarGridSpec(num_scalar_pr...  286 us
    ppermute x54, waiting for transfers between devices, flip(): lax.ppermute(value, 'tensor', [(t, t ^ 1 << bit) for t in range(size)])  276 us
    ppermute x54, starting transfers between devices, flip(): lax.ppermute(value, 'tensor', [(t, t ^ 1 << bit) for t in range(size)])  59.2 us
    reduce_scatter x1, waiting for transfers between devices, body(): lax.psum_scatter(line.tie(attention_grad), 'dp', scatter_dimension=0, til...  19.5 us
  transfers between devices with their start and end apart: 70, of which 27 were waited for; matrix products, arithmetic and copies ran while one was open for 6% of the time, Pallas kernels for 35%

profile of v7, /device:TPU:0, one launch (start us, length us, event | category | flops | bytes accessed | tf_op | source)
XLA Modules:
  0.0 742.3 jit_solution(1216383732673047308)
XLA Ops:
  10.7 15.7 %front.2 = (bf16[512,2048]{1,0:T(8,128)(2,1)}, bf16[512,2048]{1,0:T(8,128)(2,1)}, bf16[512,1536]{1,0:T(8,128)(2,1)}, f32[512,512]{1,0:T(8,128)}, f32[16,512]{1,0...) custom-call(s32[4]{0:T(128)} %get-tuple-element.431.refs_0_, ...), custom_call_target="tpu_custom_call" | custom-call | flops 858000000 | bytes 1000 | tf_op jit(solution)/shard_map/front/pallas_call | solution.py:132
  31.5 15.9 %front.3 = (bf16[512,2048]{1,0:T(8,128)(2,1)}, bf16[512,2048]{1,0:T(8,128)(2,1)}, bf16[512,1536]{1,0:T(8,128)(2,1)}, f32[512,512]{1,0:T(8,128)}, f32[16,512]{1,0...) custom-call(s32[4]{0:T(128)} %get-tuple-element.432.refs_0_, ...), custom_call_target="tpu_custom_call" | custom-call | flops 858000000 | bytes 1000 | tf_op jit(solution)/shard_map/front/pallas_call | solution.py:132
  78.1 13.5 %hidden_back.1.refs_3_.refs_2_ = bf16[1024,2048]{1,0:T(8,128)(2,1)} custom-call(bf16[512,2048]{1,0:T(8,128)(2,1)} %bitcast.110, bf16[512,2048]{1,0:T(8,128)(2,1)} %bitcast.107, bf16[2048,2048]{1,0:T(8,128)(2,1)} %refs_3_.1), custom_call_target="tpu_custom_call" | custom-call | flops 22000001024 | bytes 1000 | tf_op jit(solution)/shard_map/hidden_back/pallas_call | solution.py:132
  109.1 21.3 %collective-permute-done.12.refs_4_ = f32[2,128,1024]{2,1,0:T(8,128)S(1)} collective-permute-done((f32[2,128,1024]{2,1,0:T(8,128)S(1)}, f32[2,128,1024]{2,1,0:T(8,128)S(1)}, u32[]{:S(2)}, u32[]{:S(2)}) %collective-permute-start.12) | collective-permute-done | bytes 1048608 | tf_op jit(solution)/shard_map/ppermute | solution.py:152
  151.3 13.6 %hidden_front.2 = (bf16[512,2048]{1,0:T(8,128)(2,1)}, bf16[512,2048]{1,0:T(8,128)(2,1)}, f32[8,512]{1,0:T(8,128)}) custom-call(bf16[512,2048]{1,0:T(8,128)(2,1)} %get-tuple-element.261.refs_0_.refs_1_, bf16[2048,2048]{1,0:T(8,128)(2,1)} %refs_1_.13, f32[1,2048]{1,0:T(1,128)} %bitcast.149, bf16[1024,2048]{1,0:T(8,128)(2,1)} %hidden_back.1.refs_3_.refs_2_, ...), custom_call_target="tpu_custom_call" | custom-call | flops 808499968 | bytes 1000 | tf_op jit(solution)/shard_map/hidden_front/pallas_call | solution.py:132
  201.3 13.8 %hidden_front.3 = (bf16[512,2048]{1,0:T(8,128)(2,1)}, bf16[512,2048]{1,0:T(8,128)(2,1)}, f32[8,512]{1,0:T(8,128)}) custom-call(bf16[512,2048]{1,0:T(8,128)(2,1)} %get-tuple-element.239.refs_0_.refs_2_, bf16[2048,2048]{1,0:T(8,128)(2,1)} %refs_1_.13, f32[1,2048]{1,0:T(1,128)} %bitcast.150, bf16[1024,2048]{1,0:T(8,128)(2,1)} %hidden_back.1.refs_3_.refs_2_, ...), custom_call_target="tpu_custom_call" | custom-call | flops 808499968 | bytes 1000 | tf_op jit(solution)/shard_map/hidden_front/pallas_call | solution.py:132
  231.0 14.1 %full_grad.2 = f32[2048,2048]{1,0:T(8,128)} custom-call(bf16[512,2048]{1,0:T(8,128)(2,1)} %get-tuple-element.265.refs_0_.refs_1_, bf16[512,2048]{1,0:T(8,128)(2,1)} %get-tuple-element.254.refs_1_.refs_2_, bf16[512,2048]{1,0:T(8,128)(2,1)} %bitcast.111, bf16[512,2048]{1,0:T(8,128)(2,1)} %bitcast.108), custom_call_target="tpu_custom_call" | custom-call | flops 825000000 | bytes 1000 | tf_op jit(solution)/shard_map/full_grad/pallas_call | solution.py:132
  245.7 9.8 %ring_grads.2 = f32[4,256,2048]{2,1,0:T(8,128)} custom-call(s32[4]{0:T(128)} %add_subtract_fusion.refs_0_, bf16[512,2048]{1,0:T(8,128)(2,1)} %get-tuple-element.261.refs_0_.refs_1_, bf16[512,2048]{1,0:T(8,128)(2,1)} %get-tuple-element.239.refs_0_.refs_2_, bf16[512,2048]{1,0:T(8,128)(2,1)} %get-tuple-element.232.refs_0_.refs_3_, ...), custom_call_target="tpu_custom_call" | custom-call | flops 660000000 | bytes 1000 | tf_op jit(solution)/shard_map/ring_grads/pallas_call | solution.py:132
  258.5 9.7 %hidden_grad.3 = (f32[2,128,1024]{2,1,0:T(8,128)}, f32[2,128,1024]{2,1,0:T(8,128)}, f32[2,128,1024]{2,1,0:T(8,128)}, f32[2,128,1024]{2,1,0:T(8,128)}) custom-call(bf16[512,2048]{1,0:T(8,128)(2,1)} %get-tuple-element.259.refs_4_.refs_0_, bf16[2048,2048]{1,0:T(8,128)(2,1)} %refs_1_.13), custom_call_target="tpu_custom_call" | custom-call | flops 385000000 | bytes 1000 | tf_op jit(solution)/shard_map/hidden_grad/pallas_call | solution.py:132
  269.1 12.8 %ring_grads.3 = (f32[256,2048]{1,0:T(8,128)}, f32[3,256,2048]{2,1,0:T(8,128)}) custom-call(s32[4]{0:T(128)} %broadcast_add_fusion.refs_0_, bf16[512,2048]{1,0:T(8,128)(2,1)} %get-tuple-element.261.refs_0_.refs_1_, bf16[512,2048]{1,0:T(8,128)(2,1)} %get-tuple-element.239.refs_0_.refs_2_, bf16[512,2048]{1,0:T(8,128)(2,1)} %get-tuple-element.232.refs_0_.refs_3_, ...), custom_call_target="tpu_custom_call" | custom-call | flops 660000000 | bytes 1000 | tf_op jit(solution)/shard_map/ring_grads/pallas_call | solution.py:132
  288.2 16.0 %result_part.1 = f32[8,128,2048]{2,1,0:T(8,128)} custom-call(s32[8]{0:T(128)} %pad_add_fusion.refs_0_, bf16[512,2048]{1,0:T(8,128)(2,1)} %get-tuple-element.265.refs_0_.refs_1_, bf16[512,2048]{1,0:T(8,128)(2,1)} %get-tuple-element.254.refs_1_.refs_2_, bf16[2048,2048]{1,0:T(8,128)(2,1)} %refs_3_.1), custom_call_target="tpu_custom_call" | custom-call | flops 22000001024 | bytes 1000 | tf_op jit(solution)/shard_map/result_part/pallas_call | solution.py:132
  309.9 11.0 %middle_back.2 = (f32[512,2048]{1,0:T(8,128)}, bf16[512,2048]{1,0:T(8,128)(2,1)}, f32[512,128]{1,0:T(8,128)}, f32[4,8,2048]{2,1,0:T(8,128)}) custom-call(bf16[512,2048]{1,0:T(8,128)(2,1)} %get-tuple-element.336.refs_0_.refs_6_.refs_1_, bf16[512,2048]{1,0:T(8,128)(2,1)} %bitcast.112, f32[2,128,1024]{2,1,0:T(8,128)} %copy-done.6, ...), custom_call_target="tpu_custom_call" | custom-call | flops 605000000 | bytes 1000 | tf_op jit(solution)/shard_map/middle_back/pallas_call | solution.py:132
  321.0 10.3 %collective-permute-done.35 = f32[2,128,1024]{2,1,0:T(8,128)S(1)} collective-permute-done((f32[2,128,1024]{2,1,0:T(8,128)}, f32[2,128,1024]{2,1,0:T(8,128)S(1)}, u32[]{:S(2)}, u32[]{:S(2)}) %collective-permute-start.35) | collective-permute-done | bytes 1048608 | tf_op jit(solution)/shard_map/ppermute | solution.py:152
  335.1 21.5 %attention_back.2 = (bf16[512,512]{1,0:T(8,128)(2,1)}, bf16[512,1536]{1,0:T(8,128)(2,1)}, f32[2,8,1536]{2,1,0:T(8,128)}, f32[2,8,2048]{2,1,0:T(8,128)}, f32[2,12...) custom-call(s32[4]{0:T(128)} %get-tuple-element.431.refs_0_, ...), custom_call_target="tpu_custom_call" | custom-call | flops 1193500032 | bytes 1000 | tf_op jit(solution)/shard_map/attention_back/pallas_call | solution.py:132
  372.2 20.7 %collective-permute-done.42.refs_5_ = f32[2,128,1024]{2,1,0:T(8,128)S(1)} collective-permute-done((f32[2,128,1024]{2,1,0:T(8,128)S(1)}, f32[2,128,1024]{2,1,0:T(8,128)S(1)}, u32[]{:S(2)}, u32[]{:S(2)}) %collective-permute-start.42) | collective-permute-done | bytes 1048608 | tf_op jit(solution)/shard_map/ppermute | solution.py:152
  402.9 12.1 %middle_back.3 = (f32[512,2048]{1,0:T(8,128)}, bf16[512,2048]{1,0:T(8,128)(2,1)}, f32[512,128]{1,0:T(8,128)}, f32[4,8,2048]{2,1,0:T(8,128)}) custom-call(bf16[512,2048]{1,0:T(8,128)(2,1)} %get-tuple-element.343.refs_0_.refs_6_.refs_1_, bf16[512,2048]{1,0:T(8,128)(2,1)} %bitcast.109, f32[2,128,1024]{2,1,0:T(8,128)} %copy-done.8, f32[2,128,1024]{2,1,0:T(8,128)} %copy-done.31, ...), custom_call_target="tpu_custom_call" | custom-call | flops 605000000 | bytes 1000 | tf_op jit(solution)/shard_map/middle_back/pallas_call | solution.py:132
  415.1 21.6 %attention_back.3 = (bf16[512,512]{1,0:T(8,128)(2,1)}, bf16[512,1536]{1,0:T(8,128)(2,1)}, f32[2,8,1536]{2,1,0:T(8,128)}, f32[2,8,2048]{2,1,0:T(8,128)}, f32[2,12...) custom-call(s32[4]{0:T(128)} %get-tuple-element.432.refs_0_, ...), custom_call_target="tpu_custom_call" | custom-call | flops 1193500032 | bytes 1000 | tf_op jit(solution)/shard_map/attention_back/pallas_call | solution.py:132
  438.6 15.3 %full_grad.3 = f32[2048,2048]{1,0:T(8,128)} custom-call(bf16[512,2048]{1,0:T(8,128)(2,1)} %get-tuple-element.308.refs_0_, bf16[512,2048]{1,0:T(8,128)(2,1)} %get-tuple-element.309.refs_1_, bf16[512,1536]{1,0:T(8,128)(2,1)} %get-tuple-element.310.refs_2_, bf16[512,1536]{1,0:T(8,128)(2,1)} %get-tuple-element.311.refs_3_, ...), custom_call_target="tpu_custom_call" | custom-call | flops 825000000 | bytes 1000 | tf_op jit(solution)/shard_map/full_grad/pallas_call | solution.py:132
  458.7 42.4 %collective-permute-done.46 = f32[1,128,1024]{2,1,0:T(8,128)S(1)} collective-permute-done((f32[1,128,1024]{2,1,0:T(8,128)S(1)}, f32[1,128,1024]{2,1,0:T(8,128)S(1)}, u32[]{:S(2)}, u32[]{:S(2)}) %collective-permute-start.46) | collective-permute-done | bytes 524320 | tf_op jit(solution)/shard_map/ppermute | solution.py:152
  520.0 29.7 %collective-permute-done.51 = f32[1,128,1024]{2,1,0:T(8,128)S(1)} collective-permute-done((f32[1,128,1024]{2,1,0:T(8,128)S(1)}, f32[1,128,1024]{2,1,0:T(8,128)S(1)}, u32[]{:S(2)}, u32[]{:S(2)}) %collective-permute-start.51) | collective-permute-done | bytes 524320 | tf_op jit(solution)/shard_map/ppermute | solution.py:152
  552.2 23.5 %collective-permute-done.54 = f32[1,128,1024]{2,1,0:T(8,128)S(1)} collective-permute-done((f32[1,128,1024]{2,1,0:T(8,128)S(1)}, f32[1,128,1024]{2,1,0:T(8,128)S(1)}, u32[]{:S(2)}, u32[]{:S(2)}) %collective-permute-start.54) | collective-permute-done | bytes 524320 | tf_op jit(solution)/shard_map/ppermute | solution.py:152
  577.4 53.6 %collective-permute-done.57 = f32[1,128,1024]{2,1,0:T(8,128)S(1)} collective-permute-done((f32[1,128,1024]{2,1,0:T(8,128)S(1)}, f32[1,128,1024]{2,1,0:T(8,128)S(1)}, u32[]{:S(2)}, u32[]{:S(2)}) %collective-permute-start.57) | collective-permute-done | bytes 524320 | tf_op jit(solution)/shard_map/ppermute | solution.py:152
  654.0 22.2 %collective-permute-done.64.refs_6_ = f32[2,128,1024]{2,1,0:T(8,128)S(1)} collective-permute-done((f32[2,128,1024]{2,1,0:T(8,128)S(1)}, f32[2,128,1024]{2,1,0:T(8,128)S(1)}, u32[]{:S(2)}, u32[]{:S(2)}) %collective-permute-start.64) | collective-permute-done | bytes 1048608 | tf_op jit(solution)/shard_map/ppermute | solution.py:152
  709.4 19.5 %reduce-scatter.5.cloned.1.call-done = f32[256,2048]{1,0:T(8,128)} async-done(((f32[2048,2048]{1,0:T(8,128)}), f32[256,2048]{1,0:T(8,128)}) %reduce-scatter.5.cloned.1.call-update) | async-done | bytes 2097168 | tf_op jit(solution)/shard_map/reduce_scatter | solution.py:1195
  (384 shorter events, 265.4 us)
Async XLA Ops:
  8.0 500.9 %reduce-scatter.3.cloned.1.call-start = ((), (), s32[]{:S(2)}) async-start(), calls=%async_computation.2 | async-start | bytes 18874368 | tf_op jit(solution)/shard_map/reduce_scatter | solution.py:1119
  59.4 36.2 %collective-permute-start.7 = (f32[2,128,1024]{2,1,0:T(8,128)}, f32[2,128,1024]{2,1,0:T(8,128)S(1)}, u32[]{:S(2)}, u32[]{:S(2)}) collective-permute-start(f32[2,128,1024]{2,1,0:T(8,128)} %get-tuple-element.212), channel_id=1, source_target_pairs={{0,2},{1,3},{2,0},{3,1},{4,6},{5,7},{6,4},{7,5},{8,10},{9,11},{10,... | collective-permute-start | bytes 3145736 | tf_op jit(solution)/shard_map/ppermute | solution.py:152
  107.0 35.7 %collective-permute-start.14 = (f32[1,128,1024]{2,1,0:T(8,128)S(1)}, f32[1,128,1024]{2,1,0:T(8,128)S(1)}, u32[]{:S(2)}, u32[]{:S(2)}) collective-permute-start(f32[1,128,1024]{2,1,0:T(8,128)S(1)} %slice_add_fusion.18), channel_id=1, source_target_pairs={{0,1},{1,0},{2,3},{3,2},{4,5},{5,4},{6,7},{7,6},{8,9},{9,8},{10,11... | collective-permute-start | bytes 1572872 | tf_op jit(solution)/shard_map/ppermute | solution.py:152
  245.1 450.2 %all-reduce.3.cloned.1.call-start = ((), (), s32[]{:S(2)}) async-start(), calls=%async_computation.3 | async-start | bytes 16777216 | tf_op jit(solution)/shard_map/psum | solution.py:1172
  284.5 46.7 %collective-permute-start.35 = (f32[2,128,1024]{2,1,0:T(8,128)}, f32[2,128,1024]{2,1,0:T(8,128)S(1)}, u32[]{:S(2)}, u32[]{:S(2)}) collective-permute-start(f32[2,128,1024]{2,1,0:T(8,128)} %get-tuple-element.274), channel_id=1, source_target_pairs={{0,1},{1,0},{2,3},{3,2},{4,5},{5,4},{6,7},{7,6},{8,9},{9,8},{10,11... | collective-permute-start | bytes 3145736 | tf_op jit(solution)/shard_map/ppermute | solution.py:152
  285.8 45.5 %collective-permute-start.36 = (f32[2,128,1024]{2,1,0:T(8,128)}, f32[2,128,1024]{2,1,0:T(8,128)}, u32[]{:S(2)}, u32[]{:S(2)}) collective-permute-start(f32[2,128,1024]{2,1,0:T(8,128)} %get-tuple-element.277), channel_id=1, source_target_pairs={{0,2},{1,3},{2,0},{3,1},{4,6},{5,7},{6,4},{7,5},{8,10},{9,11},{10,... | collective-permute-start | bytes 3145736 | tf_op jit(solution)/shard_map/ppermute | solution.py:152
  286.3 108.6 %collective-permute-start.43 = (f32[256,2048]{1,0:T(8,128)}, f32[256,2048]{1,0:T(8,128)}, u32[]{:S(2)}, u32[]{:S(2)}) collective-permute-start(f32[256,2048]{1,0:T(8,128)} %get-tuple-element.290), channel_id=1, source_target_pairs={{0,8},{4,12},{8,16},{12,20},{16,24},{20,28},{24,0},{28,4},{1,9},{5... | collective-permute-start | bytes 6291464 | tf_op jit(solution)/shard_map/ppermute | solution.py:240
  398.9 330.0 %reduce-scatter.5.cloned.1.call-start = ((), (), s32[]{:S(2)}) async-start(), calls=%async_computation.4 | async-start | bytes 18874368 | tf_op jit(solution)/shard_map/reduce_scatter | solution.py:1195
  399.0 54.9 %collective-permute-start.44 = (f32[2,128,1024]{2,1,0:T(8,128)}, f32[2,128,1024]{2,1,0:T(8,128)S(1)}, u32[]{:S(2)}, u32[]{:S(2)}) collective-permute-start(f32[2,128,1024]{2,1,0:T(8,128)} %get-tuple-element.316), channel_id=1, source_target_pairs={{0,1},{1,0},{2,3},{3,2},{4,5},{5,4},{6,7},{7,6},{8,9},{9,8},{10,11... | collective-permute-start | bytes 3145736 | tf_op jit(solution)/shard_map/ppermute | solution.py:152
  400.4 53.6 %collective-permute-start.45 = (f32[2,128,1024]{2,1,0:T(8,128)}, f32[2,128,1024]{2,1,0:T(8,128)}, u32[]{:S(2)}, u32[]{:S(2)}) collective-permute-start(f32[2,128,1024]{2,1,0:T(8,128)} %get-tuple-element.319), channel_id=1, source_target_pairs={{0,2},{1,3},{2,0},{3,1},{4,6},{5,7},{6,4},{7,5},{8,10},{9,11},{10,... | collective-permute-start | bytes 3145736 | tf_op jit(solution)/shard_map/ppermute | solution.py:152
  401.1 107.9 %collective-permute-start.50 = (f32[256,2048]{1,0:T(8,128)}, f32[256,2048]{1,0:T(8,128)}, u32[]{:S(2)}, u32[]{:S(2)}) collective-permute-start(f32[256,2048]{1,0:T(8,128)} %bitcast_add_fusion.2), channel_id=1, source_target_pairs={{0,8},{4,12},{8,16},{12,20},{16,24},{20,28},{24,0},{28,4},{1,9},{5... | collective-permute-start | bytes 6291464 | tf_op jit(solution)/shard_map/ppermute | solution.py:240
  436.6 66.2 %collective-permute-start.48 = (f32[2,128,1024]{2,1,0:T(8,128)}, f32[2,128,1024]{2,1,0:T(8,128)}, u32[]{:S(2)}, u32[]{:S(2)}) collective-permute-start(f32[2,128,1024]{2,1,0:T(8,128)} %get-tuple-element.325), channel_id=1, source_target_pairs={{0,1},{1,0},{2,3},{3,2},{4,5},{5,4},{6,7},{7,6},{8,9},{9,8},{10,11... | collective-permute-start | bytes 3145736 | tf_op jit(solution)/shard_map/ppermute | solution.py:152
  437.6 67.1 %collective-permute-start.49 = (f32[2,128,1024]{2,1,0:T(8,128)}, f32[2,128,1024]{2,1,0:T(8,128)}, u32[]{:S(2)}, u32[]{:S(2)}) collective-permute-start(f32[2,128,1024]{2,1,0:T(8,128)} %get-tuple-element.327), channel_id=1, source_target_pairs={{0,2},{1,3},{2,0},{3,1},{4,6},{5,7},{6,4},{7,5},{8,10},{9,11},{10,... | collective-permute-start | bytes 3145736 | tf_op jit(solution)/shard_map/ppermute | solution.py:152
  455.1 46.9 %collective-permute-start.47 = (f32[1,128,1024]{2,1,0:T(8,128)S(1)}, f32[1,128,1024]{2,1,0:T(8,128)S(1)}, u32[]{:S(2)}, u32[]{:S(2)}) collective-permute-start(f32[1,128,1024]{2,1,0:T(8,128)S(1)} %slice_add_fusion.6), channel_id=1, source_target_pairs={{0,1},{1,0},{2,3},{3,2},{4,5},{5,4},{6,7},{7,6},{8,9},{9,8},{10,11... | collective-permute-start | bytes 1572872 | tf_op jit(solution)/shard_map/ppermute | solution.py:152
  456.6 44.4 %collective-permute-start.46 = (f32[1,128,1024]{2,1,0:T(8,128)S(1)}, f32[1,128,1024]{2,1,0:T(8,128)S(1)}, u32[]{:S(2)}, u32[]{:S(2)}) collective-permute-start(f32[1,128,1024]{2,1,0:T(8,128)S(1)} %slice_add_fusion.7), channel_id=1, source_target_pairs={{0,2},{1,3},{2,0},{3,1},{4,6},{5,7},{6,4},{7,5},{8,10},{9,11},{10,... | collective-permute-start | bytes 1572872 | tf_op jit(solution)/shard_map/ppermute | solution.py:152
  514.0 38.1 %collective-permute-start.53 = (f32[1,128,1024]{2,1,0:T(8,128)S(1)}, f32[1,128,1024]{2,1,0:T(8,128)S(1)}, u32[]{:S(2)}, u32[]{:S(2)}) collective-permute-start(f32[1,128,1024]{2,1,0:T(8,128)S(1)} %copy-done.37), channel_id=1, source_target_pairs={{0,2},{1,3},{2,0},{3,1},{4,6},{5,7},{6,4},{7,5},{8,10},{9,11},{10,... | collective-permute-start | bytes 1572872 | tf_op jit(solution)/shard_map/ppermute | solution.py:152
  514.1 37.2 %collective-permute-start.52 = (f32[1,128,1024]{2,1,0:T(8,128)S(1)}, f32[1,128,1024]{2,1,0:T(8,128)S(1)}, u32[]{:S(2)}, u32[]{:S(2)}) collective-permute-start(f32[1,128,1024]{2,1,0:T(8,128)S(1)} %copy-done.12), channel_id=1, source_target_pairs={{0,1},{1,0},{2,3},{3,2},{4,5},{5,4},{6,7},{7,6},{8,9},{9,8},{10,11... | collective-permute-start | bytes 1572872 | tf_op jit(solution)/shard_map/ppermute | solution.py:152
  516.8 59.0 %collective-permute-start.55 = (f32[2,2048]{1,0:T(2,128)S(1)}, f32[2,2048]{1,0:T(2,128)S(1)}, u32[]{:S(2)}, u32[]{:S(2)}) collective-permute-start(f32[2,2048]{1,0:T(2,128)S(1)} %fusion.12), channel_id=1, source_target_pairs={{0,1},{1,0},{2,3},{3,2},{4,5},{5,4},{6,7},{7,6},{8,9},{9,8},{10,11... | collective-permute-start | bytes 49160 | tf_op jit(solution)/shard_map/ppermute | solution.py:152
  518.2 126.1 %collective-permute-start.61 = (f32[256,2048]{1,0:T(8,128)S(1)}, f32[256,2048]{1,0:T(8,128)S(1)}, u32[]{:S(2)}, u32[]{:S(2)}) collective-permute-start(f32[256,2048]{1,0:T(8,128)S(1)} %bitcast_add_fusion.1), channel_id=1, source_target_pairs={{0,8},{4,12},{8,16},{12,20},{16,24},{20,28},{24,0},{28,4},{1,9},{5... | collective-permute-start | bytes 6291464 | tf_op jit(solution)/shard_map/ppermute | solution.py:240
  551.4 81.1 %collective-permute-start.58 = (f32[2,128,1024]{2,1,0:T(8,128)S(1)}, f32[2,128,1024]{2,1,0:T(8,128)S(1)}, u32[]{:S(2)}, u32[]{:S(2)}) collective-permute-start(f32[2,128,1024]{2,1,0:T(8,128)S(1)} %constant_dynamic-update-slice_fusion.16.refs_3_), channel_id=1, source_target_pairs={{0,1},{1,0},{2,3},{3,2},{4,5},{5,4},{6,7},{7,6},{8,9},{9,8},{10,11... | collective-permute-start | bytes 3145736 | tf_op jit(solution)/shard_map/ppermute | solution.py:152
  552.0 80.4 %collective-permute-start.59 = (f32[2,128,1024]{2,1,0:T(8,128)S(1)}, f32[2,128,1024]{2,1,0:T(8,128)S(1)}, u32[]{:S(2)}, u32[]{:S(2)}) collective-permute-start(f32[2,128,1024]{2,1,0:T(8,128)S(1)} %constant_dynamic-update-slice_fusion.18.refs_5_), channel_id=1, source_target_pairs={{0,2},{1,3},{2,0},{3,1},{4,6},{5,7},{6,4},{7,5},{8,10},{9,11},{10,... | collective-permute-start | bytes 3145736 | tf_op jit(solution)/shard_map/ppermute | solution.py:152
  575.7 56.7 %collective-permute-start.56 = (f32[1,128,1024]{2,1,0:T(8,128)S(1)}, f32[1,128,1024]{2,1,0:T(8,128)S(1)}, u32[]{:S(2)}, u32[]{:S(2)}) collective-permute-start(f32[1,128,1024]{2,1,0:T(8,128)S(1)} %add.370), channel_id=1, source_target_pairs={{0,2},{1,3},{2,0},{3,1},{4,6},{5,7},{6,4},{7,5},{8,10},{9,11},{10,... | collective-permute-start | bytes 1572872 | tf_op jit(solution)/shard_map/ppermute | solution.py:152
  575.8 55.1 %collective-permute-start.57 = (f32[1,128,1024]{2,1,0:T(8,128)S(1)}, f32[1,128,1024]{2,1,0:T(8,128)S(1)}, u32[]{:S(2)}, u32[]{:S(2)}) collective-permute-start(f32[1,128,1024]{2,1,0:T(8,128)S(1)} %add.371), channel_id=1, source_target_pairs={{0,1},{1,0},{2,3},{3,2},{4,5},{5,4},{6,7},{7,6},{8,9},{9,8},{10,11... | collective-permute-start | bytes 1572872 | tf_op jit(solution)/shard_map/ppermute | solution.py:152
  652.1 40.8 %collective-permute-start.65 = (f32[12,2048]{1,0:T(8,128)S(1)}, f32[12,2048]{1,0:T(8,128)S(1)}, u32[]{:S(2)}, u32[]{:S(2)}) collective-permute-start(f32[12,2048]{1,0:T(8,128)S(1)} %add.375), channel_id=1, source_target_pairs={{0,8},{4,12},{8,0},{12,4},{16,24},{20,28},{24,16},{28,20},{1,9},{5... | collective-permute-start | bytes 294920 | tf_op jit(solution)/shard_map/ppermute | solution.py:1208
  (107 other events, 1797.2 us)
Sparse Core Ops, SparseCore 0:
  245.3 258.0 reduce-scatter.2
  511.6 217.2 reduce-scatter.4
Sparse Core Ops, SparseCore 1:
  399.0 272.0 all-reduce.2

commit v8 on v7

--- a/solution.py
+++ b/solution.py
@@ -25,7 +25,7 @@
 
 COST = {
     "front": 15.6,
-    "middle_norm": 7.5,
+    "middle_norm": 400.0,
     "hidden_back": 400.0,
     "hidden_front": 14.7,
     "hidden_mid": 400.0,
@@ -1086,6 +1086,8 @@
         return parts
 
     totals[0].gather()
+    for other in ones[1:]:
+        line.mark(*line.last, *other["sums"].pieces())
     for c in range(chunks):
         one = ones[c]
         mid, second, stat = middle_norm(
@@ -1096,8 +1098,6 @@
             for total in totals[1:]:
                 total.advance()
                 total.gather()
-            for other in ones[1:]:
-                line.mark(*line.last, *other["sums"].pieces())
         active, slope, sums = hidden_front(c, line.tie(second), up_weight, up_bias, back, hid_gain)
         line.mark(sums)
         twos.append(dict(middle=mid, second=second, stat=stat, active=active, slope=slope, sums=all_pieces(sums, bits)))
@@ -1185,14 +1185,14 @@
     if chunks == 1:
         up_part = ring.advance()
         result = lax.psum(line.tie(result), "tensor")
+    line.mark(*line.last, down_part, *(first.got + last.got if chunks > 1 else []))
+    up_part = ring.advance()
+    attention_part = lax.psum_scatter(line.tie(attention_grad), "dp", scatter_dimension=0, tiled=True)
     for step in range(bits):
         first.advance()
     first.gather()
     if chunks > 1:
         last.advance()
-    line.mark(*line.last, down_part)
-    up_part = ring.advance()
-    attention_part = lax.psum_scatter(line.tie(attention_grad), "dp", scatter_dimension=0, tiled=True)
     for step in range(1, bits):
         first.gather()
     if chunks > 1:

time: 753 us -> 740 us (0.983)
  other arithmetic: 32.8 us -> 24.4 us
    ppermute x54, waiting for transfers between devices: 276 us -> 268 us  [flip(): lax.ppermute(value, 'tensor', [(t, t ^ 1 << bit) for t in range(size)])]
  transfers between devices with their start and end apart: 70 -> 70, of which waited for: 27 -> 32; matrix products, arithmetic and copies ran while one was open for 6% -> 5% of each run, Pallas kernels for 35% -> 35%
where the time goes in v8:
time: 740 us; the launch traced here: 730 us
  waiting for transfers between devices  291 us (39%)
  Pallas kernels  286 us (39%)
  starting transfers between devices  78.7 us (11%)
  local copies, waits for them, and re-layouts  32.6 us (4%)
  other arithmetic  24.4 us (3%)
  between operations  17.2 us (2%)
    pallas_call x24, Pallas kernels, run(): pl.pallas_call(body, grid_spec=pltpu.PrefetchScalarGridSpec(num_scalar_pr...  286 us
    ppermute x54, waiting for transfers between devices, flip(): lax.ppermute(value, 'tensor', [(t, t ^ 1 << bit) for t in range(size)])  268 us
    ppermute x54, starting transfers between devices, flip(): lax.ppermute(value, 'tensor', [(t, t ^ 1 << bit) for t in range(size)])  60.9 us
  transfers between devices with their start and end apart: 70, of which 32 were waited for; matrix products, arithmetic and copies ran while one was open for 5% of the time, Pallas kernels for 35%

profile of v8, /device:TPU:0, one launch (start us, length us, event | category | flops | bytes accessed | tf_op | source)
XLA Modules:
  0.0 729.7 jit_solution(12888704237702336622)
XLA Ops:
  10.7 15.7 %front.2 = (bf16[512,2048]{1,0:T(8,128)(2,1)}, bf16[512,2048]{1,0:T(8,128)(2,1)}, bf16[512,1536]{1,0:T(8,128)(2,1)}, f32[512,512]{1,0:T(8,128)}, f32[16,512]{1,0...) custom-call(s32[4]{0:T(128)} %get-tuple-element.431.refs_0_, ...), custom_call_target="tpu_custom_call" | custom-call | flops 858000000 | bytes 1000 | tf_op jit(solution)/shard_map/front/pallas_call | solution.py:132
  31.4 15.9 %front.3 = (bf16[512,2048]{1,0:T(8,128)(2,1)}, bf16[512,2048]{1,0:T(8,128)(2,1)}, bf16[512,1536]{1,0:T(8,128)(2,1)}, f32[512,512]{1,0:T(8,128)}, f32[16,512]{1,0...) custom-call(s32[4]{0:T(128)} %get-tuple-element.432.refs_0_, ...), custom_call_target="tpu_custom_call" | custom-call | flops 858000000 | bytes 1000 | tf_op jit(solution)/shard_map/front/pallas_call | solution.py:132
  78.1 13.5 %hidden_back.1.refs_3_.refs_2_ = bf16[1024,2048]{1,0:T(8,128)(2,1)} custom-call(bf16[512,2048]{1,0:T(8,128)(2,1)} %bitcast.110, bf16[512,2048]{1,0:T(8,128)(2,1)} %bitcast.107, bf16[2048,2048]{1,0:T(8,128)(2,1)} %refs_3_.1), custom_call_target="tpu_custom_call" | custom-call | flops 22000001024 | bytes 1000 | tf_op jit(solution)/shard_map/hidden_back/pallas_call | solution.py:132
  108.9 20.5 %collective-permute-done.11 = f32[2,16,512]{2,1,0:T(8,128)S(1)} collective-permute-done((f32[2,16,512]{2,1,0:T(8,128)S(1)}, f32[2,16,512]{2,1,0:T(8,128)S(1)}, u32[]{:S(2)}, u32[]{:S(2)}) %collective-permute-start.11) | collective-permute-done | bytes 65568 | tf_op jit(solution)/shard_map/ppermute | solution.py:152
  145.8 13.6 %hidden_front.2 = (bf16[512,2048]{1,0:T(8,128)(2,1)}, bf16[512,2048]{1,0:T(8,128)(2,1)}, f32[8,512]{1,0:T(8,128)}) custom-call(bf16[512,2048]{1,0:T(8,128)(2,1)} %get-tuple-element.261.refs_0_.refs_1_, bf16[2048,2048]{1,0:T(8,128)(2,1)} %refs_1_.13, f32[1,2048]{1,0:T(1,128)} %bitcast.136, bf16[1024,2048]{1,0:T(8,128)(2,1)} %hidden_back.1.refs_3_.refs_2_, ...), custom_call_target="tpu_custom_call" | custom-call | flops 808499968 | bytes 1000 | tf_op jit(solution)/shard_map/hidden_front/pallas_call | solution.py:132
  194.5 13.8 %hidden_front.3 = (bf16[512,2048]{1,0:T(8,128)(2,1)}, bf16[512,2048]{1,0:T(8,128)(2,1)}, f32[8,512]{1,0:T(8,128)}) custom-call(bf16[512,2048]{1,0:T(8,128)(2,1)} %get-tuple-element.239.refs_0_.refs_2_, bf16[2048,2048]{1,0:T(8,128)(2,1)} %refs_1_.13, f32[1,2048]{1,0:T(1,128)} %bitcast.137, bf16[1024,2048]{1,0:T(8,128)(2,1)} %hidden_back.1.refs_3_.refs_2_, ...), custom_call_target="tpu_custom_call" | custom-call | flops 808499968 | bytes 1000 | tf_op jit(solution)/shard_map/hidden_front/pallas_call | solution.py:132
  222.9 14.1 %full_grad.2 = f32[2048,2048]{1,0:T(8,128)} custom-call(bf16[512,2048]{1,0:T(8,128)(2,1)} %get-tuple-element.265.refs_0_.refs_1_, bf16[512,2048]{1,0:T(8,128)(2,1)} %get-tuple-element.254.refs_1_.refs_2_, bf16[512,2048]{1,0:T(8,128)(2,1)} %bitcast.111, bf16[512,2048]{1,0:T(8,128)(2,1)} %bitcast.108), custom_call_target="tpu_custom_call" | custom-call | flops 825000000 | bytes 1000 | tf_op jit(solution)/shard_map/full_grad/pallas_call | solution.py:132
  261.6 12.9 %ring_grads.3 = (f32[256,2048]{1,0:T(8,128)}, f32[3,256,2048]{2,1,0:T(8,128)}) custom-call(s32[4]{0:T(128)} %broadcast_add_fusion.refs_0_, bf16[512,2048]{1,0:T(8,128)(2,1)} %get-tuple-element.261.refs_0_.refs_1_, bf16[512,2048]{1,0:T(8,128)(2,1)} %get-tuple-element.239.refs_0_.refs_2_, bf16[512,2048]{1,0:T(8,128)(2,1)} %get-tuple-element.232.refs_0_.refs_3_, ...), custom_call_target="tpu_custom_call" | custom-call | flops 660000000 | bytes 1000 | tf_op jit(solution)/shard_map/ring_grads/pallas_call | solution.py:132
  280.3 16.1 %result_part.1 = f32[8,128,2048]{2,1,0:T(8,128)} custom-call(s32[8]{0:T(128)} %pad_add_fusion.refs_0_, bf16[512,2048]{1,0:T(8,128)(2,1)} %get-tuple-element.265.refs_0_.refs_1_, bf16[512,2048]{1,0:T(8,128)(2,1)} %get-tuple-element.254.refs_1_.refs_2_, bf16[2048,2048]{1,0:T(8,128)(2,1)} %refs_3_.1), custom_call_target="tpu_custom_call" | custom-call | flops 22000001024 | bytes 1000 | tf_op jit(solution)/shard_map/result_part/pallas_call | solution.py:132
  302.0 11.2 %middle_back.2 = (f32[512,2048]{1,0:T(8,128)}, bf16[512,2048]{1,0:T(8,128)(2,1)}, f32[512,128]{1,0:T(8,128)}, f32[4,8,2048]{2,1,0:T(8,128)}) custom-call(bf16[512,2048]{1,0:T(8,128)(2,1)} %get-tuple-element.336.refs_0_.refs_6_.refs_1_, bf16[512,2048]{1,0:T(8,128)(2,1)} %bitcast.112, f32[2,128,1024]{2,1,0:T(8,128)} %copy-done.2, ...), custom_call_target="tpu_custom_call" | custom-call | flops 605000000 | bytes 1000 | tf_op jit(solution)/shard_map/middle_back/pallas_call | solution.py:132
  313.2 10.1 %collective-permute-done.35 = f32[2,128,1024]{2,1,0:T(8,128)S(1)} collective-permute-done((f32[2,128,1024]{2,1,0:T(8,128)}, f32[2,128,1024]{2,1,0:T(8,128)S(1)}, u32[]{:S(2)}, u32[]{:S(2)}) %collective-permute-start.35) | collective-permute-done | bytes 1048608 | tf_op jit(solution)/shard_map/ppermute | solution.py:152
  327.8 21.5 %attention_back.2 = (bf16[512,512]{1,0:T(8,128)(2,1)}, bf16[512,1536]{1,0:T(8,128)(2,1)}, f32[2,8,1536]{2,1,0:T(8,128)}, f32[2,8,2048]{2,1,0:T(8,128)}, f32[2,12...) custom-call(s32[4]{0:T(128)} %get-tuple-element.431.refs_0_, ...), custom_call_target="tpu_custom_call" | custom-call | flops 1193500032 | bytes 1000 | tf_op jit(solution)/shard_map/attention_back/pallas_call | solution.py:132
  351.5 10.3 %collective-permute-done.39 = f32[1,128,1024]{2,1,0:T(8,128)S(1)} collective-permute-done((f32[1,128,1024]{2,1,0:T(8,128)S(1)}, f32[1,128,1024]{2,1,0:T(8,128)S(1)}, u32[]{:S(2)}, u32[]{:S(2)}) %collective-permute-start.39) | collective-permute-done | bytes 524320 | tf_op jit(solution)/shard_map/ppermute | solution.py:152
  364.6 20.9 %collective-permute-done.42.refs_5_ = f32[2,128,1024]{2,1,0:T(8,128)S(1)} collective-permute-done((f32[2,128,1024]{2,1,0:T(8,128)S(1)}, f32[2,128,1024]{2,1,0:T(8,128)S(1)}, u32[]{:S(2)}, u32[]{:S(2)}) %collective-permute-start.42) | collective-permute-done | bytes 1048608 | tf_op jit(solution)/shard_map/ppermute | solution.py:152
  393.3 11.2 %middle_back.3 = (f32[512,2048]{1,0:T(8,128)}, bf16[512,2048]{1,0:T(8,128)(2,1)}, f32[512,128]{1,0:T(8,128)}, f32[4,8,2048]{2,1,0:T(8,128)}) custom-call(bf16[512,2048]{1,0:T(8,128)(2,1)} %get-tuple-element.343.refs_0_.refs_6_.refs_1_, bf16[512,2048]{1,0:T(8,128)(2,1)} %bitcast.109, f32[2,128,1024]{2,1,0:T(8,128)} %copy-done.4, f32[2,128,1024]{2,1,0:T(8,128)} %copy-done.27, ...), custom_call_target="tpu_custom_call" | custom-call | flops 605000000 | bytes 1000 | tf_op jit(solution)/shard_map/middle_back/pallas_call | solution.py:132
  406.9 21.9 %attention_back.3 = (bf16[512,512]{1,0:T(8,128)(2,1)}, bf16[512,1536]{1,0:T(8,128)(2,1)}, f32[2,8,1536]{2,1,0:T(8,128)}, f32[2,8,2048]{2,1,0:T(8,128)}, f32[2,12...) custom-call(s32[4]{0:T(128)} %get-tuple-element.432.refs_0_, ...), custom_call_target="tpu_custom_call" | custom-call | flops 1193500032 | bytes 1000 | tf_op jit(solution)/shard_map/attention_back/pallas_call | solution.py:132
  430.6 15.6 %full_grad.3 = f32[2048,2048]{1,0:T(8,128)} custom-call(bf16[512,2048]{1,0:T(8,128)(2,1)} %get-tuple-element.308.refs_0_, bf16[512,2048]{1,0:T(8,128)(2,1)} %get-tuple-element.309.refs_1_, bf16[512,1536]{1,0:T(8,128)(2,1)} %get-tuple-element.310.refs_2_, bf16[512,1536]{1,0:T(8,128)(2,1)} %get-tuple-element.311.refs_3_, ...), custom_call_target="tpu_custom_call" | custom-call | flops 825000000 | bytes 1000 | tf_op jit(solution)/shard_map/full_grad/pallas_call | solution.py:132
  454.1 35.4 %collective-permute-done.46 = f32[2,128,1024]{2,1,0:T(8,128)S(1)} collective-permute-done((f32[2,128,1024]{2,1,0:T(8,128)}, f32[2,128,1024]{2,1,0:T(8,128)S(1)}, u32[]{:S(2)}, u32[]{:S(2)}) %collective-permute-start.46) | collective-permute-done | bytes 1048608 | tf_op jit(solution)/shard_map/ppermute | solution.py:152
  508.9 19.7 %collective-permute-done.49 = f32[1,128,1024]{2,1,0:T(8,128)S(1)} collective-permute-done((f32[1,128,1024]{2,1,0:T(8,128)S(1)}, f32[1,128,1024]{2,1,0:T(8,128)S(1)}, u32[]{:S(2)}, u32[]{:S(2)}) %collective-permute-start.49) | collective-permute-done | bytes 524320 | tf_op jit(solution)/shard_map/ppermute | solution.py:152
  532.8 15.2 %collective-permute-done.51 = f32[1,128,1024]{2,1,0:T(8,128)S(1)} collective-permute-done((f32[1,128,1024]{2,1,0:T(8,128)S(1)}, f32[1,128,1024]{2,1,0:T(8,128)S(1)}, u32[]{:S(2)}, u32[]{:S(2)}) %collective-permute-start.51) | collective-permute-done | bytes 524320 | tf_op jit(solution)/shard_map/ppermute | solution.py:152
  550.9 18.2 %collective-permute-done.53 = f32[1,128,1024]{2,1,0:T(8,128)S(1)} collective-permute-done((f32[1,128,1024]{2,1,0:T(8,128)S(1)}, f32[1,128,1024]{2,1,0:T(8,128)S(1)}, u32[]{:S(2)}, u32[]{:S(2)}) %collective-permute-start.53) | collective-permute-done | bytes 524320 | tf_op jit(solution)/shard_map/ppermute | solution.py:152
  575.7 53.0 %collective-permute-done.57 = f32[1,128,1024]{2,1,0:T(8,128)S(1)} collective-permute-done((f32[1,128,1024]{2,1,0:T(8,128)S(1)}, f32[1,128,1024]{2,1,0:T(8,128)S(1)}, u32[]{:S(2)}, u32[]{:S(2)}) %collective-permute-start.57) | collective-permute-done | bytes 524320 | tf_op jit(solution)/shard_map/ppermute | solution.py:152
  652.8 22.6 %collective-permute-done.64.refs_6_ = f32[2,128,1024]{2,1,0:T(8,128)S(1)} collective-permute-done((f32[2,128,1024]{2,1,0:T(8,128)S(1)}, f32[2,128,1024]{2,1,0:T(8,128)S(1)}, u32[]{:S(2)}, u32[]{:S(2)}) %collective-permute-start.64) | collective-permute-done | bytes 1048608 | tf_op jit(solution)/shard_map/ppermute | solution.py:152
  703.5 12.8 %reduce-scatter.5.cloned.1.call-done = f32[256,2048]{1,0:T(8,128)} async-done(((f32[2048,2048]{1,0:T(8,128)}), f32[256,2048]{1,0:T(8,128)}) %reduce-scatter.5.cloned.1.call-update) | async-done | bytes 2097168 | tf_op jit(solution)/shard_map/reduce_scatter | solution.py:1190
  (382 shorter events, 276.9 us)
Async XLA Ops:
  8.0 488.4 %reduce-scatter.3.cloned.1.call-start = ((), (), s32[]{:S(2)}) async-start(), calls=%async_computation.2 | async-start | bytes 18874368 | tf_op jit(solution)/shard_map/reduce_scatter | solution.py:1119
  58.9 34.3 %collective-permute-start.6 = (f32[2,128,1024]{2,1,0:T(8,128)}, f32[2,128,1024]{2,1,0:T(8,128)S(1)}, u32[]{:S(2)}, u32[]{:S(2)}) collective-permute-start(f32[2,128,1024]{2,1,0:T(8,128)} %get-tuple-element.209), channel_id=1, source_target_pairs={{0,1},{1,0},{2,3},{3,2},{4,5},{5,4},{6,7},{7,6},{8,9},{9,8},{10,11... | collective-permute-start | bytes 3145736 | tf_op jit(solution)/shard_map/ppermute | solution.py:152
  59.4 36.2 %collective-permute-start.7 = (f32[2,128,1024]{2,1,0:T(8,128)}, f32[2,128,1024]{2,1,0:T(8,128)S(1)}, u32[]{:S(2)}, u32[]{:S(2)}) collective-permute-start(f32[2,128,1024]{2,1,0:T(8,128)} %get-tuple-element.212), channel_id=1, source_target_pairs={{0,2},{1,3},{2,0},{3,1},{4,6},{5,7},{6,4},{7,5},{8,10},{9,11},{10,... | collective-permute-start | bytes 3145736 | tf_op jit(solution)/shard_map/ppermute | solution.py:152
  75.9 29.4 %collective-permute-start.10 = (f32[1,128,1024]{2,1,0:T(8,128)S(1)}, f32[1,128,1024]{2,1,0:T(8,128)S(1)}, u32[]{:S(2)}, u32[]{:S(2)}) collective-permute-start(f32[1,128,1024]{2,1,0:T(8,128)S(1)} %add.313), channel_id=1, source_target_pairs={{0,1},{1,0},{2,3},{3,2},{4,5},{5,4},{6,7},{7,6},{8,9},{9,8},{10,11... | collective-permute-start | bytes 1572872 | tf_op jit(solution)/shard_map/ppermute | solution.py:152
  237.1 452.5 %all-reduce.3.cloned.1.call-start = ((), (), s32[]{:S(2)}) async-start(), calls=%async_computation.3 | async-start | bytes 16777216 | tf_op jit(solution)/shard_map/psum | solution.py:1172
  277.3 46.0 %collective-permute-start.35 = (f32[2,128,1024]{2,1,0:T(8,128)}, f32[2,128,1024]{2,1,0:T(8,128)S(1)}, u32[]{:S(2)}, u32[]{:S(2)}) collective-permute-start(f32[2,128,1024]{2,1,0:T(8,128)} %get-tuple-element.274), channel_id=1, source_target_pairs={{0,1},{1,0},{2,3},{3,2},{4,5},{5,4},{6,7},{7,6},{8,9},{9,8},{10,11... | collective-permute-start | bytes 3145736 | tf_op jit(solution)/shard_map/ppermute | solution.py:152
  277.9 45.4 %collective-permute-start.36 = (f32[2,128,1024]{2,1,0:T(8,128)}, f32[2,128,1024]{2,1,0:T(8,128)}, u32[]{:S(2)}, u32[]{:S(2)}) collective-permute-start(f32[2,128,1024]{2,1,0:T(8,128)} %get-tuple-element.277), channel_id=1, source_target_pairs={{0,2},{1,3},{2,0},{3,1},{4,6},{5,7},{6,4},{7,5},{8,10},{9,11},{10,... | collective-permute-start | bytes 3145736 | tf_op jit(solution)/shard_map/ppermute | solution.py:152
  278.8 108.1 %collective-permute-start.43 = (f32[256,2048]{1,0:T(8,128)}, f32[256,2048]{1,0:T(8,128)}, u32[]{:S(2)}, u32[]{:S(2)}) collective-permute-start(f32[256,2048]{1,0:T(8,128)} %get-tuple-element.290), channel_id=1, source_target_pairs={{0,8},{4,12},{8,16},{12,20},{16,24},{20,28},{24,0},{28,4},{1,9},{5... | collective-permute-start | bytes 6291464 | tf_op jit(solution)/shard_map/ppermute | solution.py:240
  390.9 325.4 %reduce-scatter.5.cloned.1.call-start = ((), (), s32[]{:S(2)}) async-start(), calls=%async_computation.4 | async-start | bytes 18874368 | tf_op jit(solution)/shard_map/reduce_scatter | solution.py:1190
  390.9 105.5 %collective-permute-start.48 = (f32[256,2048]{1,0:T(8,128)}, f32[256,2048]{1,0:T(8,128)}, u32[]{:S(2)}, u32[]{:S(2)}) collective-permute-start(f32[256,2048]{1,0:T(8,128)} %bitcast_add_fusion.2), channel_id=1, source_target_pairs={{0,8},{4,12},{8,16},{12,20},{16,24},{20,28},{24,0},{28,4},{1,9},{5... | collective-permute-start | bytes 6291464 | tf_op jit(solution)/shard_map/ppermute | solution.py:240
  404.5 48.7 %collective-permute-start.44 = (f32[2,128,1024]{2,1,0:T(8,128)}, f32[2,128,1024]{2,1,0:T(8,128)S(1)}, u32[]{:S(2)}, u32[]{:S(2)}) collective-permute-start(f32[2,128,1024]{2,1,0:T(8,128)} %get-tuple-element.315), channel_id=1, source_target_pairs={{0,1},{1,0},{2,3},{3,2},{4,5},{5,4},{6,7},{7,6},{8,9},{9,8},{10,11... | collective-permute-start | bytes 3145736 | tf_op jit(solution)/shard_map/ppermute | solution.py:152
  405.4 48.8 %collective-permute-start.45 = (f32[2,128,1024]{2,1,0:T(8,128)}, f32[2,128,1024]{2,1,0:T(8,128)}, u32[]{:S(2)}, u32[]{:S(2)}) collective-permute-start(f32[2,128,1024]{2,1,0:T(8,128)} %get-tuple-element.317), channel_id=1, source_target_pairs={{0,2},{1,3},{2,0},{3,1},{4,6},{5,7},{6,4},{7,5},{8,10},{9,11},{10,... | collective-permute-start | bytes 3145736 | tf_op jit(solution)/shard_map/ppermute | solution.py:152
  428.8 60.7 %collective-permute-start.46 = (f32[2,128,1024]{2,1,0:T(8,128)}, f32[2,128,1024]{2,1,0:T(8,128)S(1)}, u32[]{:S(2)}, u32[]{:S(2)}) collective-permute-start(f32[2,128,1024]{2,1,0:T(8,128)} %get-tuple-element.318), channel_id=1, source_target_pairs={{0,1},{1,0},{2,3},{3,2},{4,5},{5,4},{6,7},{7,6},{8,9},{9,8},{10,11... | collective-permute-start | bytes 3145736 | tf_op jit(solution)/shard_map/ppermute | solution.py:152
  429.9 59.6 %collective-permute-start.47 = (f32[2,128,1024]{2,1,0:T(8,128)}, f32[2,128,1024]{2,1,0:T(8,128)S(1)}, u32[]{:S(2)}, u32[]{:S(2)}) collective-permute-start(f32[2,128,1024]{2,1,0:T(8,128)} %get-tuple-element.319), channel_id=1, source_target_pairs={{0,2},{1,3},{2,0},{3,1},{4,6},{5,7},{6,4},{7,5},{8,10},{9,11},{10,... | collective-permute-start | bytes 3145736 | tf_op jit(solution)/shard_map/ppermute | solution.py:152
  502.2 71.9 %collective-permute-start.55 = (f32[2,2048]{1,0:T(2,128)S(1)}, f32[2,2048]{1,0:T(2,128)S(1)}, u32[]{:S(2)}, u32[]{:S(2)}) collective-permute-start(f32[2,2048]{1,0:T(2,128)S(1)} %fusion.12), channel_id=1, source_target_pairs={{0,1},{1,0},{2,3},{3,2},{4,5},{5,4},{6,7},{7,6},{8,9},{9,8},{10,11... | collective-permute-start | bytes 49160 | tf_op jit(solution)/shard_map/ppermute | solution.py:152
  507.3 133.0 %collective-permute-start.61 = (f32[256,2048]{1,0:T(8,128)S(1)}, f32[256,2048]{1,0:T(8,128)S(1)}, u32[]{:S(2)}, u32[]{:S(2)}) collective-permute-start(f32[256,2048]{1,0:T(8,128)S(1)} %bitcast_add_fusion.1), channel_id=1, source_target_pairs={{0,8},{4,12},{8,16},{12,20},{16,24},{20,28},{24,0},{28,4},{1,9},{5... | collective-permute-start | bytes 6291464 | tf_op jit(solution)/shard_map/ppermute | solution.py:240
  530.6 38.5 %collective-permute-start.53 = (f32[1,128,1024]{2,1,0:T(8,128)S(1)}, f32[1,128,1024]{2,1,0:T(8,128)S(1)}, u32[]{:S(2)}, u32[]{:S(2)}) collective-permute-start(f32[1,128,1024]{2,1,0:T(8,128)S(1)} %slice_add_fusion.3), channel_id=1, source_target_pairs={{0,2},{1,3},{2,0},{3,1},{4,6},{5,7},{6,4},{7,5},{8,10},{9,11},{10,... | collective-permute-start | bytes 1572872 | tf_op jit(solution)/shard_map/ppermute | solution.py:152
  549.6 79.2 %collective-permute-start.58 = (f32[2,128,1024]{2,1,0:T(8,128)S(1)}, f32[2,128,1024]{2,1,0:T(8,128)S(1)}, u32[]{:S(2)}, u32[]{:S(2)}) collective-permute-start(f32[2,128,1024]{2,1,0:T(8,128)S(1)} %constant_dynamic-update-slice_fusion.16.refs_3_), channel_id=1, source_target_pairs={{0,1},{1,0},{2,3},{3,2},{4,5},{5,4},{6,7},{7,6},{8,9},{9,8},{10,11... | collective-permute-start | bytes 3145736 | tf_op jit(solution)/shard_map/ppermute | solution.py:152
  569.1 59.6 %collective-permute-start.59 = (f32[2,128,1024]{2,1,0:T(8,128)S(1)}, f32[2,128,1024]{2,1,0:T(8,128)S(1)}, u32[]{:S(2)}, u32[]{:S(2)}) collective-permute-start(f32[2,128,1024]{2,1,0:T(8,128)S(1)} %constant_dynamic-update-slice_fusion.18.refs_5_), channel_id=1, source_target_pairs={{0,2},{1,3},{2,0},{3,1},{4,6},{5,7},{6,4},{7,5},{8,10},{9,11},{10,... | collective-permute-start | bytes 3145736 | tf_op jit(solution)/shard_map/ppermute | solution.py:152
  574.0 54.7 %collective-permute-start.56 = (f32[1,128,1024]{2,1,0:T(8,128)S(1)}, f32[1,128,1024]{2,1,0:T(8,128)S(1)}, u32[]{:S(2)}, u32[]{:S(2)}) collective-permute-start(f32[1,128,1024]{2,1,0:T(8,128)S(1)} %add.370), channel_id=1, source_target_pairs={{0,2},{1,3},{2,0},{3,1},{4,6},{5,7},{6,4},{7,5},{8,10},{9,11},{10,... | collective-permute-start | bytes 1572872 | tf_op jit(solution)/shard_map/ppermute | solution.py:152
  574.1 54.6 %collective-permute-start.57 = (f32[1,128,1024]{2,1,0:T(8,128)S(1)}, f32[1,128,1024]{2,1,0:T(8,128)S(1)}, u32[]{:S(2)}, u32[]{:S(2)}) collective-permute-start(f32[1,128,1024]{2,1,0:T(8,128)S(1)} %add.371), channel_id=1, source_target_pairs={{0,1},{1,0},{2,3},{3,2},{4,5},{5,4},{6,7},{7,6},{8,9},{9,8},{10,11... | collective-permute-start | bytes 1572872 | tf_op jit(solution)/shard_map/ppermute | solution.py:152
  644.9 30.5 %collective-permute-start.64 = (f32[2,128,1024]{2,1,0:T(8,128)S(1)}, f32[2,128,1024]{2,1,0:T(8,128)S(1)}, u32[]{:S(2)}, u32[]{:S(2)}) collective-permute-start(f32[2,128,1024]{2,1,0:T(8,128)S(1)} %constant_dynamic-update-slice_fusion.22.refs_5_), channel_id=1, source_target_pairs={{0,2},{1,3},{2,0},{3,1},{4,6},{5,7},{6,4},{7,5},{8,10},{9,11},{10,... | collective-permute-start | bytes 3145736 | tf_op jit(solution)/shard_map/ppermute | solution.py:152
  646.5 29.5 %collective-permute-start.63 = (f32[2,128,1024]{2,1,0:T(8,128)S(1)}, f32[2,128,1024]{2,1,0:T(8,128)S(1)}, u32[]{:S(2)}, u32[]{:S(2)}) collective-permute-start(f32[2,128,1024]{2,1,0:T(8,128)S(1)} %constant_dynamic-update-slice_fusion.20.refs_3_), channel_id=1, source_target_pairs={{0,1},{1,0},{2,3},{3,2},{4,5},{5,4},{6,7},{7,6},{8,9},{9,8},{10,11... | collective-permute-start | bytes 3145736 | tf_op jit(solution)/shard_map/ppermute | solution.py:152
  650.3 35.4 %collective-permute-start.65 = (f32[12,2048]{1,0:T(8,128)S(1)}, f32[12,2048]{1,0:T(8,128)S(1)}, u32[]{:S(2)}, u32[]{:S(2)}) collective-permute-start(f32[12,2048]{1,0:T(8,128)S(1)} %add.375), channel_id=1, source_target_pairs={{0,8},{4,12},{8,0},{12,4},{16,24},{20,28},{24,16},{28,20},{1,9},{5... | collective-permute-start | bytes 294920 | tf_op jit(solution)/shard_map/ppermute | solution.py:1208
  (106 other events, 1630.1 us)
Sparse Core Ops, SparseCore 0:
  237.2 259.1 reduce-scatter.2
  499.1 217.1 reduce-scatter.4
Sparse Core Ops, SparseCore 1:
  391.0 272.7 all-reduce.2

commit v9 on v8

--- a/solution.py
+++ b/solution.py
@@ -1179,15 +1179,15 @@
     pad = lambda v: jnp.pad(v, ((0, 0), (0, D - v.shape[1])))
     wide = add(threes, "wide", 2)
     got = flip(wide, 0, blocks)
+    if chunks > 1:
+        line.mark(*line.last, *first.got)
     attention_grad = full(
         [(every(ones, "first"), every(threes, "dproj")), (every(threes, "low"), every(threes, "mix_low"))]
     )
     if chunks == 1:
         up_part = ring.advance()
         result = lax.psum(line.tie(result), "tensor")
-    line.mark(*line.last, down_part, *(first.got + last.got if chunks > 1 else []))
-    up_part = ring.advance()
-    attention_part = lax.psum_scatter(line.tie(attention_grad), "dp", scatter_dimension=0, tiled=True)
+    attention_part = lax.psum_scatter(attention_grad, "dp", scatter_dimension=0, tiled=True)
     for step in range(bits):
         first.advance()
     first.gather()
@@ -1195,6 +1195,8 @@
         last.advance()
     for step in range(1, bits):
         first.gather()
+    line.mark(*line.last, down_part)
+    up_part = ring.advance()
     if chunks > 1:
         for step in range(1, bits):
             last.advance()

time: 740 us -> 728 us (0.984)
  waiting for transfers between devices: 291 us -> 281 us
  transfers between devices with their start and end apart: 70 -> 70, of which waited for: 32 -> 30; matrix products, arithmetic and copies ran while one was open for 5% -> 5% of each run, Pallas kernels for 35% -> 36%
where the time goes in v9:
time: 728 us; the launch traced here: 718 us
  Pallas kernels  286 us (39%)
  waiting for transfers between devices  281 us (39%)
  starting transfers between devices  76.5 us (11%)
  local copies, waits for them, and re-layouts  30.3 us (4%)
  other arithmetic  26.6 us (4%)
  between operations  17.2 us (2%)
    pallas_call x24, Pallas kernels, run(): pl.pallas_call(body, grid_spec=pltpu.PrefetchScalarGridSpec(num_scalar_pr...  286 us
    ppermute x54, waiting for transfers between devices, flip(): lax.ppermute(value, 'tensor', [(t, t ^ 1 << bit) for t in range(size)])  262 us
    ppermute x54, starting transfers between devices, flip(): lax.ppermute(value, 'tensor', [(t, t ^ 1 << bit) for t in range(size)])  59.6 us
  transfers between devices with their start and end apart: 70, of which 30 were waited for; matrix products, arithmetic and copies ran while one was open for 5% of the time, Pallas kernels for 36%

profile of v9, /device:TPU:0, one launch (start us, length us, event | category | flops | bytes accessed | tf_op | source)
XLA Modules:
  0.0 717.9 jit_solution(11996277343801444288)
XLA Ops:
  10.7 15.7 %front.2 = (bf16[512,2048]{1,0:T(8,128)(2,1)}, bf16[512,2048]{1,0:T(8,128)(2,1)}, bf16[512,1536]{1,0:T(8,128)(2,1)}, f32[512,512]{1,0:T(8,128)}, f32[16,512]{1,0...) custom-call(s32[4]{0:T(128)} %get-tuple-element.429.refs_0_, ...), custom_call_target="tpu_custom_call" | custom-call | flops 858000000 | bytes 1000 | tf_op jit(solution)/shard_map/front/pallas_call | solution.py:132
  31.4 15.9 %front.3 = (bf16[512,2048]{1,0:T(8,128)(2,1)}, bf16[512,2048]{1,0:T(8,128)(2,1)}, bf16[512,1536]{1,0:T(8,128)(2,1)}, f32[512,512]{1,0:T(8,128)}, f32[16,512]{1,0...) custom-call(s32[4]{0:T(128)} %get-tuple-element.430.refs_0_, ...), custom_call_target="tpu_custom_call" | custom-call | flops 858000000 | bytes 1000 | tf_op jit(solution)/shard_map/front/pallas_call | solution.py:132
  78.1 13.5 %hidden_back.1.refs_3_.refs_2_ = bf16[1024,2048]{1,0:T(8,128)(2,1)} custom-call(bf16[512,2048]{1,0:T(8,128)(2,1)} %bitcast.110, bf16[512,2048]{1,0:T(8,128)(2,1)} %bitcast.107, bf16[2048,2048]{1,0:T(8,128)(2,1)} %refs_3_.1), custom_call_target="tpu_custom_call" | custom-call | flops 22000001024 | bytes 1000 | tf_op jit(solution)/shard_map/hidden_back/pallas_call | solution.py:132
  108.9 20.5 %collective-permute-done.11 = f32[2,16,512]{2,1,0:T(8,128)S(1)} collective-permute-done((f32[2,16,512]{2,1,0:T(8,128)S(1)}, f32[2,16,512]{2,1,0:T(8,128)S(1)}, u32[]{:S(2)}, u32[]{:S(2)}) %collective-permute-start.11) | collective-permute-done | bytes 65568 | tf_op jit(solution)/shard_map/ppermute | solution.py:152
  145.8 13.6 %hidden_front.2 = (bf16[512,2048]{1,0:T(8,128)(2,1)}, bf16[512,2048]{1,0:T(8,128)(2,1)}, f32[8,512]{1,0:T(8,128)}) custom-call(bf16[512,2048]{1,0:T(8,128)(2,1)} %get-tuple-element.260.refs_0_.refs_1_, bf16[2048,2048]{1,0:T(8,128)(2,1)} %refs_1_.13, f32[1,2048]{1,0:T(1,128)} %bitcast.136, bf16[1024,2048]{1,0:T(8,128)(2,1)} %hidden_back.1.refs_3_.refs_2_, ...), custom_call_target="tpu_custom_call" | custom-call | flops 808499968 | bytes 1000 | tf_op jit(solution)/shard_map/hidden_front/pallas_call | solution.py:132
  194.5 13.8 %hidden_front.3 = (bf16[512,2048]{1,0:T(8,128)(2,1)}, bf16[512,2048]{1,0:T(8,128)(2,1)}, f32[8,512]{1,0:T(8,128)}) custom-call(bf16[512,2048]{1,0:T(8,128)(2,1)} %get-tuple-element.238.refs_0_.refs_2_, bf16[2048,2048]{1,0:T(8,128)(2,1)} %refs_1_.13, f32[1,2048]{1,0:T(1,128)} %bitcast.137, bf16[1024,2048]{1,0:T(8,128)(2,1)} %hidden_back.1.refs_3_.refs_2_, ...), custom_call_target="tpu_custom_call" | custom-call | flops 808499968 | bytes 1000 | tf_op jit(solution)/shard_map/hidden_front/pallas_call | solution.py:132
  223.1 14.1 %full_grad.2 = f32[2048,2048]{1,0:T(8,128)} custom-call(bf16[512,2048]{1,0:T(8,128)(2,1)} %get-tuple-element.264.refs_0_.refs_1_, bf16[512,2048]{1,0:T(8,128)(2,1)} %get-tuple-element.253.refs_1_.refs_2_, bf16[512,2048]{1,0:T(8,128)(2,1)} %bitcast.111, bf16[512,2048]{1,0:T(8,128)(2,1)} %bitcast.108), custom_call_target="tpu_custom_call" | custom-call | flops 825000000 | bytes 1000 | tf_op jit(solution)/shard_map/full_grad/pallas_call | solution.py:132
  237.8 9.8 %ring_grads.2 = f32[4,256,2048]{2,1,0:T(8,128)} custom-call(s32[4]{0:T(128)} %add_subtract_fusion.refs_0_, bf16[512,2048]{1,0:T(8,128)(2,1)} %get-tuple-element.260.refs_0_.refs_1_, bf16[512,2048]{1,0:T(8,128)(2,1)} %get-tuple-element.238.refs_0_.refs_2_, bf16[512,2048]{1,0:T(8,128)(2,1)} %get-tuple-element.231.refs_0_.refs_3_, ...), custom_call_target="tpu_custom_call" | custom-call | flops 660000000 | bytes 1000 | tf_op jit(solution)/shard_map/ring_grads/pallas_call | solution.py:132
  261.6 12.9 %ring_grads.3 = (f32[256,2048]{1,0:T(8,128)}, f32[3,256,2048]{2,1,0:T(8,128)}) custom-call(s32[4]{0:T(128)} %broadcast_add_fusion.refs_0_, bf16[512,2048]{1,0:T(8,128)(2,1)} %get-tuple-element.260.refs_0_.refs_1_, bf16[512,2048]{1,0:T(8,128)(2,1)} %get-tuple-element.238.refs_0_.refs_2_, bf16[512,2048]{1,0:T(8,128)(2,1)} %get-tuple-element.231.refs_0_.refs_3_, ...), custom_call_target="tpu_custom_call" | custom-call | flops 660000000 | bytes 1000 | tf_op jit(solution)/shard_map/ring_grads/pallas_call | solution.py:132
  280.3 16.1 %result_part.1 = f32[8,128,2048]{2,1,0:T(8,128)} custom-call(s32[8]{0:T(128)} %pad_add_fusion.refs_0_, bf16[512,2048]{1,0:T(8,128)(2,1)} %get-tuple-element.264.refs_0_.refs_1_, bf16[512,2048]{1,0:T(8,128)(2,1)} %get-tuple-element.253.refs_1_.refs_2_, bf16[2048,2048]{1,0:T(8,128)(2,1)} %refs_3_.1), custom_call_target="tpu_custom_call" | custom-call | flops 22000001024 | bytes 1000 | tf_op jit(solution)/shard_map/result_part/pallas_call | solution.py:132
  302.3 11.2 %middle_back.2 = (f32[512,2048]{1,0:T(8,128)}, bf16[512,2048]{1,0:T(8,128)(2,1)}, f32[512,128]{1,0:T(8,128)}, f32[4,8,2048]{2,1,0:T(8,128)}) custom-call(bf16[512,2048]{1,0:T(8,128)(2,1)} %get-tuple-element.335.refs_0_.refs_6_.refs_1_, bf16[512,2048]{1,0:T(8,128)(2,1)} %bitcast.112, f32[2,128,1024]{2,1,0:T(8,128)} %copy-done, ...), custom_call_target="tpu_custom_call" | custom-call | flops 605000000 | bytes 1000 | tf_op jit(solution)/shard_map/middle_back/pallas_call | solution.py:132
  313.5 10.1 %collective-permute-done.35 = f32[2,128,1024]{2,1,0:T(8,128)S(1)} collective-permute-done((f32[2,128,1024]{2,1,0:T(8,128)}, f32[2,128,1024]{2,1,0:T(8,128)S(1)}, u32[]{:S(2)}, u32[]{:S(2)}) %collective-permute-start.35) | collective-permute-done | bytes 1048608 | tf_op jit(solution)/shard_map/ppermute | solution.py:152
  328.0 21.5 %attention_back.2 = (bf16[512,512]{1,0:T(8,128)(2,1)}, bf16[512,1536]{1,0:T(8,128)(2,1)}, f32[2,8,1536]{2,1,0:T(8,128)}, f32[2,8,2048]{2,1,0:T(8,128)}, f32[2,12...) custom-call(s32[4]{0:T(128)} %get-tuple-element.429.refs_0_, ...), custom_call_target="tpu_custom_call" | custom-call | flops 1193500032 | bytes 1000 | tf_op jit(solution)/shard_map/attention_back/pallas_call | solution.py:132
  351.8 10.2 %collective-permute-done.39 = f32[1,128,1024]{2,1,0:T(8,128)S(1)} collective-permute-done((f32[1,128,1024]{2,1,0:T(8,128)S(1)}, f32[1,128,1024]{2,1,0:T(8,128)S(1)}, u32[]{:S(2)}, u32[]{:S(2)}) %collective-permute-start.39) | collective-permute-done | bytes 524320 | tf_op jit(solution)/shard_map/ppermute | solution.py:152
  364.6 21.3 %collective-permute-done.42.refs_5_ = f32[2,128,1024]{2,1,0:T(8,128)S(1)} collective-permute-done((f32[2,128,1024]{2,1,0:T(8,128)S(1)}, f32[2,128,1024]{2,1,0:T(8,128)S(1)}, u32[]{:S(2)}, u32[]{:S(2)}) %collective-permute-start.42) | collective-permute-done | bytes 1048608 | tf_op jit(solution)/shard_map/ppermute | solution.py:152
  393.5 11.2 %middle_back.3 = (f32[512,2048]{1,0:T(8,128)}, bf16[512,2048]{1,0:T(8,128)(2,1)}, f32[512,128]{1,0:T(8,128)}, f32[4,8,2048]{2,1,0:T(8,128)}) custom-call(bf16[512,2048]{1,0:T(8,128)(2,1)} %get-tuple-element.342.refs_0_.refs_6_.refs_1_, bf16[512,2048]{1,0:T(8,128)(2,1)} %bitcast.109, f32[2,128,1024]{2,1,0:T(8,128)} %copy-done.2, f32[2,128,1024]{2,1,0:T(8,128)} %copy-done.24, ...), custom_call_target="tpu_custom_call" | custom-call | flops 605000000 | bytes 1000 | tf_op jit(solution)/shard_map/middle_back/pallas_call | solution.py:132
  404.7 21.9 %attention_back.3 = (bf16[512,512]{1,0:T(8,128)(2,1)}, bf16[512,1536]{1,0:T(8,128)(2,1)}, f32[2,8,1536]{2,1,0:T(8,128)}, f32[2,8,2048]{2,1,0:T(8,128)}, f32[2,12...) custom-call(s32[4]{0:T(128)} %get-tuple-element.430.refs_0_, ...), custom_call_target="tpu_custom_call" | custom-call | flops 1193500032 | bytes 1000 | tf_op jit(solution)/shard_map/attention_back/pallas_call | solution.py:132
  432.6 16.0 %full_grad.3 = f32[2048,2048]{1,0:T(8,128)} custom-call(bf16[512,2048]{1,0:T(8,128)(2,1)} %get-tuple-element.311.refs_0_, bf16[512,2048]{1,0:T(8,128)(2,1)} %get-tuple-element.312.refs_1_, bf16[512,1536]{1,0:T(8,128)(2,1)} %get-tuple-element.313.refs_2_, bf16[512,1536]{1,0:T(8,128)(2,1)} %get-tuple-element.314.refs_3_, ...), custom_call_target="tpu_custom_call" | custom-call | flops 825000000 | bytes 1000 | tf_op jit(solution)/shard_map/full_grad/pallas_call | solution.py:132
  459.0 54.0 %collective-permute-done.46 = f32[1,128,1024]{2,1,0:T(8,128)S(1)} collective-permute-done((f32[1,128,1024]{2,1,0:T(8,128)S(1)}, f32[1,128,1024]{2,1,0:T(8,128)S(1)}, u32[]{:S(2)}, u32[]{:S(2)}) %collective-permute-start.46) | collective-permute-done | bytes 524320 | tf_op jit(solution)/shard_map/ppermute | solution.py:152
  518.3 12.5 %collective-permute-done.50 = f32[1,128,1024]{2,1,0:T(8,128)S(1)} collective-permute-done((f32[1,128,1024]{2,1,0:T(8,128)S(1)}, f32[1,128,1024]{2,1,0:T(8,128)S(1)}, u32[]{:S(2)}, u32[]{:S(2)}) %collective-permute-start.50) | collective-permute-done | bytes 524320 | tf_op jit(solution)/shard_map/ppermute | solution.py:152
  540.2 11.4 %collective-permute-done.53 = f32[1,128,1024]{2,1,0:T(8,128)} collective-permute-done((f32[1,128,1024]{2,1,0:T(8,128)}, f32[1,128,1024]{2,1,0:T(8,128)}, u32[]{:S(2)}, u32[]{:S(2)}) %collective-permute-start.53) | collective-permute-done | bytes 524320 | tf_op jit(solution)/shard_map/ppermute | solution.py:152
  565.9 48.3 %collective-permute-done.57 = f32[1,128,1024]{2,1,0:T(8,128)S(1)} collective-permute-done((f32[1,128,1024]{2,1,0:T(8,128)S(1)}, f32[1,128,1024]{2,1,0:T(8,128)S(1)}, u32[]{:S(2)}, u32[]{:S(2)}) %collective-permute-start.57) | collective-permute-done | bytes 524320 | tf_op jit(solution)/shard_map/ppermute | solution.py:152
  636.8 24.6 %collective-permute-done.64.refs_6_ = f32[2,128,1024]{2,1,0:T(8,128)S(1)} collective-permute-done((f32[2,128,1024]{2,1,0:T(8,128)S(1)}, f32[2,128,1024]{2,1,0:T(8,128)S(1)}, u32[]{:S(2)}, u32[]{:S(2)}) %collective-permute-start.64) | collective-permute-done | bytes 1048608 | tf_op jit(solution)/shard_map/ppermute | solution.py:152
  691.9 12.6 %reduce-scatter.5.cloned.1.call-done = f32[256,2048]{1,0:T(8,128)} async-done(((f32[2048,2048]{1,0:T(8,128)}), f32[256,2048]{1,0:T(8,128)}) %reduce-scatter.5.cloned.1.call-update) | async-done | bytes 2097168 | tf_op jit(solution)/shard_map/reduce_scatter | solution.py:1190
  (386 shorter events, 268.1 us)
Async XLA Ops:
  8.0 523.0 %reduce-scatter.3.cloned.1.call-start = ((), (), s32[]{:S(2)}) async-start(), calls=%async_computation.2 | async-start | bytes 18874368 | tf_op jit(solution)/shard_map/reduce_scatter | solution.py:1119
  58.9 34.3 %collective-permute-start.6 = (f32[2,128,1024]{2,1,0:T(8,128)}, f32[2,128,1024]{2,1,0:T(8,128)S(1)}, u32[]{:S(2)}, u32[]{:S(2)}) collective-permute-start(f32[2,128,1024]{2,1,0:T(8,128)} %get-tuple-element.208), channel_id=1, source_target_pairs={{0,1},{1,0},{2,3},{3,2},{4,5},{5,4},{6,7},{7,6},{8,9},{9,8},{10,11... | collective-permute-start | bytes 3145736 | tf_op jit(solution)/shard_map/ppermute | solution.py:152
  59.4 36.2 %collective-permute-start.7 = (f32[2,128,1024]{2,1,0:T(8,128)}, f32[2,128,1024]{2,1,0:T(8,128)S(1)}, u32[]{:S(2)}, u32[]{:S(2)}) collective-permute-start(f32[2,128,1024]{2,1,0:T(8,128)} %get-tuple-element.211), channel_id=1, source_target_pairs={{0,2},{1,3},{2,0},{3,1},{4,6},{5,7},{6,4},{7,5},{8,10},{9,11},{10,... | collective-permute-start | bytes 3145736 | tf_op jit(solution)/shard_map/ppermute | solution.py:152
  237.2 440.9 %all-reduce.3.cloned.1.call-start = ((), (), s32[]{:S(2)}) async-start(), calls=%async_computation.3 | async-start | bytes 16777216 | tf_op jit(solution)/shard_map/psum | solution.py:1172
  277.7 46.0 %collective-permute-start.35 = (f32[2,128,1024]{2,1,0:T(8,128)}, f32[2,128,1024]{2,1,0:T(8,128)S(1)}, u32[]{:S(2)}, u32[]{:S(2)}) collective-permute-start(f32[2,128,1024]{2,1,0:T(8,128)} %get-tuple-element.273), channel_id=1, source_target_pairs={{0,1},{1,0},{2,3},{3,2},{4,5},{5,4},{6,7},{7,6},{8,9},{9,8},{10,11... | collective-permute-start | bytes 3145736 | tf_op jit(solution)/shard_map/ppermute | solution.py:152
  278.2 45.5 %collective-permute-start.36 = (f32[2,128,1024]{2,1,0:T(8,128)}, f32[2,128,1024]{2,1,0:T(8,128)}, u32[]{:S(2)}, u32[]{:S(2)}) collective-permute-start(f32[2,128,1024]{2,1,0:T(8,128)} %get-tuple-element.276), channel_id=1, source_target_pairs={{0,2},{1,3},{2,0},{3,1},{4,6},{5,7},{6,4},{7,5},{8,10},{9,11},{10,... | collective-permute-start | bytes 3145736 | tf_op jit(solution)/shard_map/ppermute | solution.py:152
  278.8 108.5 %collective-permute-start.43 = (f32[256,2048]{1,0:T(8,128)}, f32[256,2048]{1,0:T(8,128)}, u32[]{:S(2)}, u32[]{:S(2)}) collective-permute-start(f32[256,2048]{1,0:T(8,128)} %get-tuple-element.289), channel_id=1, source_target_pairs={{0,8},{4,12},{8,16},{12,20},{16,24},{20,28},{24,0},{28,4},{1,9},{5... | collective-permute-start | bytes 6291464 | tf_op jit(solution)/shard_map/ppermute | solution.py:240
  391.2 313.3 %reduce-scatter.5.cloned.1.call-start = ((), (), s32[]{:S(2)}) async-start(), calls=%async_computation.4 | async-start | bytes 18874368 | tf_op jit(solution)/shard_map/reduce_scatter | solution.py:1190
  391.3 39.9 %collective-permute-start.44 = (f32[2,128,1024]{2,1,0:T(8,128)}, f32[2,128,1024]{2,1,0:T(8,128)S(1)}, u32[]{:S(2)}, u32[]{:S(2)}) collective-permute-start(f32[2,128,1024]{2,1,0:T(8,128)} %get-tuple-element.308), channel_id=1, source_target_pairs={{0,1},{1,0},{2,3},{3,2},{4,5},{5,4},{6,7},{7,6},{8,9},{9,8},{10,11... | collective-permute-start | bytes 3145736 | tf_op jit(solution)/shard_map/ppermute | solution.py:152
  392.1 40.5 %collective-permute-start.45 = (f32[2,128,1024]{2,1,0:T(8,128)}, f32[2,128,1024]{2,1,0:T(8,128)S(1)}, u32[]{:S(2)}, u32[]{:S(2)}) collective-permute-start(f32[2,128,1024]{2,1,0:T(8,128)} %get-tuple-element.310), channel_id=1, source_target_pairs={{0,2},{1,3},{2,0},{3,1},{4,6},{5,7},{6,4},{7,5},{8,10},{9,11},{10,... | collective-permute-start | bytes 3145736 | tf_op jit(solution)/shard_map/ppermute | solution.py:152
  451.1 81.6 %collective-permute-start.52 = (f32[256,2048]{1,0:T(8,128)}, f32[256,2048]{1,0:T(8,128)}, u32[]{:S(2)}, u32[]{:S(2)}) collective-permute-start(f32[256,2048]{1,0:T(8,128)} %bitcast_add_fusion.2), channel_id=1, source_target_pairs={{0,8},{4,12},{8,16},{12,20},{16,24},{20,28},{24,0},{28,4},{1,9},{5... | collective-permute-start | bytes 6291464 | tf_op jit(solution)/shard_map/ppermute | solution.py:240
  453.3 62.5 %collective-permute-start.48 = (f32[2,128,1024]{2,1,0:T(8,128)}, f32[2,128,1024]{2,1,0:T(8,128)S(1)}, u32[]{:S(2)}, u32[]{:S(2)}) collective-permute-start(f32[2,128,1024]{2,1,0:T(8,128)} %get-tuple-element.324), channel_id=1, source_target_pairs={{0,1},{1,0},{2,3},{3,2},{4,5},{5,4},{6,7},{7,6},{8,9},{9,8},{10,11... | collective-permute-start | bytes 3145736 | tf_op jit(solution)/shard_map/ppermute | solution.py:152
  454.5 62.7 %collective-permute-start.49 = (f32[2,128,1024]{2,1,0:T(8,128)}, f32[2,128,1024]{2,1,0:T(8,128)S(1)}, u32[]{:S(2)}, u32[]{:S(2)}) collective-permute-start(f32[2,128,1024]{2,1,0:T(8,128)} %get-tuple-element.326), channel_id=1, source_target_pairs={{0,2},{1,3},{2,0},{3,1},{4,6},{5,7},{6,4},{7,5},{8,10},{9,11},{10,... | collective-permute-start | bytes 3145736 | tf_op jit(solution)/shard_map/ppermute | solution.py:152
  456.8 58.5 %collective-permute-start.47 = (f32[1,128,1024]{2,1,0:T(8,128)S(1)}, f32[1,128,1024]{2,1,0:T(8,128)S(1)}, u32[]{:S(2)}, u32[]{:S(2)}) collective-permute-start(f32[1,128,1024]{2,1,0:T(8,128)S(1)} %slice_add_fusion.6), channel_id=1, source_target_pairs={{0,1},{1,0},{2,3},{3,2},{4,5},{5,4},{6,7},{7,6},{8,9},{9,8},{10,11... | collective-permute-start | bytes 1572872 | tf_op jit(solution)/shard_map/ppermute | solution.py:152
  457.4 55.6 %collective-permute-start.46 = (f32[1,128,1024]{2,1,0:T(8,128)S(1)}, f32[1,128,1024]{2,1,0:T(8,128)S(1)}, u32[]{:S(2)}, u32[]{:S(2)}) collective-permute-start(f32[1,128,1024]{2,1,0:T(8,128)S(1)} %slice_add_fusion.7), channel_id=1, source_target_pairs={{0,2},{1,3},{2,0},{3,1},{4,6},{5,7},{6,4},{7,5},{8,10},{9,11},{10,... | collective-permute-start | bytes 1572872 | tf_op jit(solution)/shard_map/ppermute | solution.py:152
  516.7 34.8 %collective-permute-start.53 = (f32[1,128,1024]{2,1,0:T(8,128)}, f32[1,128,1024]{2,1,0:T(8,128)}, u32[]{:S(2)}, u32[]{:S(2)}) collective-permute-start(f32[1,128,1024]{2,1,0:T(8,128)} %slice_add_fusion.3), channel_id=1, source_target_pairs={{0,2},{1,3},{2,0},{3,1},{4,6},{5,7},{6,4},{7,5},{8,10},{9,11},{10,... | collective-permute-start | bytes 1572872 | tf_op jit(solution)/shard_map/ppermute | solution.py:152
  535.4 92.6 %collective-permute-start.61 = (f32[256,2048]{1,0:T(8,128)S(1)}, f32[256,2048]{1,0:T(8,128)S(1)}, u32[]{:S(2)}, u32[]{:S(2)}) collective-permute-start(f32[256,2048]{1,0:T(8,128)S(1)} %bitcast_add_fusion.1), channel_id=1, source_target_pairs={{0,8},{4,12},{8,16},{12,20},{16,24},{20,28},{24,0},{28,4},{1,9},{5... | collective-permute-start | bytes 6291464 | tf_op jit(solution)/shard_map/ppermute | solution.py:240
  539.3 75.1 %collective-permute-start.59 = (f32[2,128,1024]{2,1,0:T(8,128)S(1)}, f32[2,128,1024]{2,1,0:T(8,128)S(1)}, u32[]{:S(2)}, u32[]{:S(2)}) collective-permute-start(f32[2,128,1024]{2,1,0:T(8,128)S(1)} %constant_dynamic-update-slice_fusion.18.refs_5_), channel_id=1, source_target_pairs={{0,2},{1,3},{2,0},{3,1},{4,6},{5,7},{6,4},{7,5},{8,10},{9,11},{10,... | collective-permute-start | bytes 3145736 | tf_op jit(solution)/shard_map/ppermute | solution.py:152
  551.6 62.9 %collective-permute-start.58 = (f32[2,128,1024]{2,1,0:T(8,128)S(1)}, f32[2,128,1024]{2,1,0:T(8,128)S(1)}, u32[]{:S(2)}, u32[]{:S(2)}) collective-permute-start(f32[2,128,1024]{2,1,0:T(8,128)S(1)} %constant_dynamic-update-slice_fusion.16.refs_3_), channel_id=1, source_target_pairs={{0,1},{1,0},{2,3},{3,2},{4,5},{5,4},{6,7},{7,6},{8,9},{9,8},{10,11... | collective-permute-start | bytes 3145736 | tf_op jit(solution)/shard_map/ppermute | solution.py:152
  563.2 51.2 %collective-permute-start.56 = (f32[1,128,1024]{2,1,0:T(8,128)S(1)}, f32[1,128,1024]{2,1,0:T(8,128)S(1)}, u32[]{:S(2)}, u32[]{:S(2)}) collective-permute-start(f32[1,128,1024]{2,1,0:T(8,128)S(1)} %add.370), channel_id=1, source_target_pairs={{0,2},{1,3},{2,0},{3,1},{4,6},{5,7},{6,4},{7,5},{8,10},{9,11},{10,... | collective-permute-start | bytes 1572872 | tf_op jit(solution)/shard_map/ppermute | solution.py:152
  564.1 50.1 %collective-permute-start.57 = (f32[1,128,1024]{2,1,0:T(8,128)S(1)}, f32[1,128,1024]{2,1,0:T(8,128)S(1)}, u32[]{:S(2)}, u32[]{:S(2)}) collective-permute-start(f32[1,128,1024]{2,1,0:T(8,128)S(1)} %add.371), channel_id=1, source_target_pairs={{0,1},{1,0},{2,3},{3,2},{4,5},{5,4},{6,7},{7,6},{8,9},{9,8},{10,11... | collective-permute-start | bytes 1572872 | tf_op jit(solution)/shard_map/ppermute | solution.py:152
  631.5 29.9 %collective-permute-start.64 = (f32[2,128,1024]{2,1,0:T(8,128)S(1)}, f32[2,128,1024]{2,1,0:T(8,128)S(1)}, u32[]{:S(2)}, u32[]{:S(2)}) collective-permute-start(f32[2,128,1024]{2,1,0:T(8,128)S(1)} %constant_dynamic-update-slice_fusion.22.refs_5_), channel_id=1, source_target_pairs={{0,2},{1,3},{2,0},{3,1},{4,6},{5,7},{6,4},{7,5},{8,10},{9,11},{10,... | collective-permute-start | bytes 3145736 | tf_op jit(solution)/shard_map/ppermute | solution.py:152
  633.1 32.5 %collective-permute-start.63 = (f32[2,128,1024]{2,1,0:T(8,128)S(1)}, f32[2,128,1024]{2,1,0:T(8,128)S(1)}, u32[]{:S(2)}, u32[]{:S(2)}) collective-permute-start(f32[2,128,1024]{2,1,0:T(8,128)S(1)} %constant_dynamic-update-slice_fusion.20.refs_3_), channel_id=1, source_target_pairs={{0,1},{1,0},{2,3},{3,2},{4,5},{5,4},{6,7},{7,6},{8,9},{9,8},{10,11... | collective-permute-start | bytes 3145736 | tf_op jit(solution)/shard_map/ppermute | solution.py:152
  635.6 39.7 %collective-permute-start.65 = (f32[12,2048]{1,0:T(8,128)S(1)}, f32[12,2048]{1,0:T(8,128)S(1)}, u32[]{:S(2)}, u32[]{:S(2)}) collective-permute-start(f32[12,2048]{1,0:T(8,128)S(1)} %add.375), channel_id=1, source_target_pairs={{0,8},{4,12},{8,0},{12,4},{16,24},{20,28},{24,16},{28,20},{1,9},{5... | collective-permute-start | bytes 294920 | tf_op jit(solution)/shard_map/ppermute | solution.py:1210
  (108 other events, 1663.4 us)
Sparse Core Ops, SparseCore 0:
  237.3 216.2 reduce-scatter.2
  456.1 248.3 reduce-scatter.4
Sparse Core Ops, SparseCore 1:
  391.3 267.4 all-reduce.2

commit v10 on v9

--- a/solution.py
+++ b/solution.py
@@ -35,7 +35,7 @@
     "result_part": 400.0,
     "middle_back": 11.0,
     "attention_back": 21.7,
-    "tokens_back": 8.5,
+    "tokens_back": 2450.0,
     "output": 6.0,
 }
 WORK = 5.5e+07

time: 728 us -> 740 us (1.016)
  other arithmetic: 26.6 us -> 35 us
    ppermute x3, waiting for transfers between devices: 3.6 us -> 32.3 us  [send(): lax.ppermute(value, 'dp', [(d, (d + 2) % self.size) for d in range(self.s...]
    ppermute x54, waiting for transfers between devices: 262 us -> 235 us  [flip(): lax.ppermute(value, 'tensor', [(t, t ^ 1 << bit) for t in range(size)])]
  transfers between devices with their start and end apart: 70 -> 70, of which waited for: 30 -> 28; matrix products, arithmetic and copies ran while one was open for 5% -> 7% of each run, Pallas kernels for 36% -> 35%
where the time goes in v10:
time: 740 us; the launch traced here: 729 us
  Pallas kernels  287 us (39%)
  waiting for transfers between devices  285 us (39%)
  starting transfers between devices  72.1 us (10%)
  other arithmetic  35 us (5%)
  local copies, waits for them, and re-layouts  33.2 us (4%)
  between operations  17.2 us (2%)
    pallas_call x24, Pallas kernels, run(): pl.pallas_call(body, grid_spec=pltpu.PrefetchScalarGridSpec(num_scalar_pr...  287 us
    ppermute x54, waiting for transfers between devices, flip(): lax.ppermute(value, 'tensor', [(t, t ^ 1 << bit) for t in range(size)])  235 us
    ppermute x54, starting transfers between devices, flip(): lax.ppermute(value, 'tensor', [(t, t ^ 1 << bit) for t in range(size)])  59.2 us
    ppermute x3, waiting for transfers between devices, send(): lax.ppermute(value, 'dp', [(d, (d + 2) % self.size) for d in range(self.s...  32.3 us
    reduce_scatter x1, waiting for transfers between devices, body(): lax.psum_scatter(attention_grad, 'dp', scatter_dimension=0, tiled=True)  15.1 us
  transfers between devices with their start and end apart: 70, of which 28 were waited for; matrix products, arithmetic and copies ran while one was open for 7% of the time, Pallas kernels for 35%

profile of v10, /device:TPU:0, one launch (start us, length us, event | category | flops | bytes accessed | tf_op | source)
XLA Modules:
  0.0 729.4 jit_solution(3486007325004130596)
XLA Ops:
  10.7 15.7 %front.2 = (bf16[512,2048]{1,0:T(8,128)(2,1)}, bf16[512,2048]{1,0:T(8,128)(2,1)}, bf16[512,1536]{1,0:T(8,128)(2,1)}, f32[512,512]{1,0:T(8,128)}, f32[16,512]{1,0...) custom-call(s32[4]{0:T(128)} %get-tuple-element.429.refs_0_, ...), custom_call_target="tpu_custom_call" | custom-call | flops 858000000 | bytes 1000 | tf_op jit(solution)/shard_map/front/pallas_call | solution.py:132
  31.4 15.9 %front.3 = (bf16[512,2048]{1,0:T(8,128)(2,1)}, bf16[512,2048]{1,0:T(8,128)(2,1)}, bf16[512,1536]{1,0:T(8,128)(2,1)}, f32[512,512]{1,0:T(8,128)}, f32[16,512]{1,0...) custom-call(s32[4]{0:T(128)} %get-tuple-element.430.refs_0_, ...), custom_call_target="tpu_custom_call" | custom-call | flops 858000000 | bytes 1000 | tf_op jit(solution)/shard_map/front/pallas_call | solution.py:132
  78.1 13.5 %hidden_back.1.refs_3_.refs_2_ = bf16[1024,2048]{1,0:T(8,128)(2,1)} custom-call(bf16[512,2048]{1,0:T(8,128)(2,1)} %bitcast.109, bf16[512,2048]{1,0:T(8,128)(2,1)} %bitcast.106, bf16[2048,2048]{1,0:T(8,128)(2,1)} %refs_3_.1), custom_call_target="tpu_custom_call" | custom-call | flops 22000001024 | bytes 1000 | tf_op jit(solution)/shard_map/hidden_back/pallas_call | solution.py:132
  108.9 20.5 %collective-permute-done.11 = f32[2,16,512]{2,1,0:T(8,128)S(1)} collective-permute-done((f32[2,16,512]{2,1,0:T(8,128)S(1)}, f32[2,16,512]{2,1,0:T(8,128)S(1)}, u32[]{:S(2)}, u32[]{:S(2)}) %collective-permute-start.11) | collective-permute-done | bytes 65568 | tf_op jit(solution)/shard_map/ppermute | solution.py:152
  145.8 13.6 %hidden_front.2 = (bf16[512,2048]{1,0:T(8,128)(2,1)}, bf16[512,2048]{1,0:T(8,128)(2,1)}, f32[8,512]{1,0:T(8,128)}) custom-call(bf16[512,2048]{1,0:T(8,128)(2,1)} %get-tuple-element.260.refs_0_.refs_1_, bf16[2048,2048]{1,0:T(8,128)(2,1)} %refs_1_.13, f32[1,2048]{1,0:T(1,128)} %bitcast.131, bf16[1024,2048]{1,0:T(8,128)(2,1)} %hidden_back.1.refs_3_.refs_2_, ...), custom_call_target="tpu_custom_call" | custom-call | flops 808499968 | bytes 1000 | tf_op jit(solution)/shard_map/hidden_front/pallas_call | solution.py:132
  194.5 13.8 %hidden_front.3 = (bf16[512,2048]{1,0:T(8,128)(2,1)}, bf16[512,2048]{1,0:T(8,128)(2,1)}, f32[8,512]{1,0:T(8,128)}) custom-call(bf16[512,2048]{1,0:T(8,128)(2,1)} %get-tuple-element.238.refs_0_.refs_2_, bf16[2048,2048]{1,0:T(8,128)(2,1)} %refs_1_.13, f32[1,2048]{1,0:T(1,128)} %bitcast.132, bf16[1024,2048]{1,0:T(8,128)(2,1)} %hidden_back.1.refs_3_.refs_2_, ...), custom_call_target="tpu_custom_call" | custom-call | flops 808499968 | bytes 1000 | tf_op jit(solution)/shard_map/hidden_front/pallas_call | solution.py:132
  223.1 14.1 %full_grad.2 = f32[2048,2048]{1,0:T(8,128)} custom-call(bf16[512,2048]{1,0:T(8,128)(2,1)} %get-tuple-element.264.refs_0_.refs_1_, bf16[512,2048]{1,0:T(8,128)(2,1)} %get-tuple-element.253.refs_1_.refs_2_, bf16[512,2048]{1,0:T(8,128)(2,1)} %bitcast.110, bf16[512,2048]{1,0:T(8,128)(2,1)} %bitcast.107), custom_call_target="tpu_custom_call" | custom-call | flops 825000000 | bytes 1000 | tf_op jit(solution)/shard_map/full_grad/pallas_call | solution.py:132
  261.5 12.9 %ring_grads.3 = (f32[256,2048]{1,0:T(8,128)}, f32[3,256,2048]{2,1,0:T(8,128)}) custom-call(s32[4]{0:T(128)} %broadcast_add_fusion.refs_0_, bf16[512,2048]{1,0:T(8,128)(2,1)} %get-tuple-element.260.refs_0_.refs_1_, bf16[512,2048]{1,0:T(8,128)(2,1)} %get-tuple-element.238.refs_0_.refs_2_, bf16[512,2048]{1,0:T(8,128)(2,1)} %get-tuple-element.231.refs_0_.refs_3_, ...), custom_call_target="tpu_custom_call" | custom-call | flops 660000000 | bytes 1000 | tf_op jit(solution)/shard_map/ring_grads/pallas_call | solution.py:132
  280.3 16.1 %result_part.1 = f32[8,128,2048]{2,1,0:T(8,128)} custom-call(s32[8]{0:T(128)} %pad_add_fusion.refs_0_, bf16[512,2048]{1,0:T(8,128)(2,1)} %get-tuple-element.264.refs_0_.refs_1_, bf16[512,2048]{1,0:T(8,128)(2,1)} %get-tuple-element.253.refs_1_.refs_2_, bf16[2048,2048]{1,0:T(8,128)(2,1)} %refs_3_.1), custom_call_target="tpu_custom_call" | custom-call | flops 22000001024 | bytes 1000 | tf_op jit(solution)/shard_map/result_part/pallas_call | solution.py:132
  302.3 11.1 %middle_back.2 = (f32[512,2048]{1,0:T(8,128)}, bf16[512,2048]{1,0:T(8,128)(2,1)}, f32[512,128]{1,0:T(8,128)}, f32[4,8,2048]{2,1,0:T(8,128)}) custom-call(bf16[512,2048]{1,0:T(8,128)(2,1)} %get-tuple-element.335.refs_0_.refs_6_.refs_1_, bf16[512,2048]{1,0:T(8,128)(2,1)} %bitcast.111, f32[2,128,1024]{2,1,0:T(8,128)} %copy-done, ...), custom_call_target="tpu_custom_call" | custom-call | flops 605000000 | bytes 1000 | tf_op jit(solution)/shard_map/middle_back/pallas_call | solution.py:132
  313.4 10.2 %collective-permute-done.35 = f32[2,128,1024]{2,1,0:T(8,128)S(1)} collective-permute-done((f32[2,128,1024]{2,1,0:T(8,128)}, f32[2,128,1024]{2,1,0:T(8,128)S(1)}, u32[]{:S(2)}, u32[]{:S(2)}) %collective-permute-start.35) | collective-permute-done | bytes 1048608 | tf_op jit(solution)/shard_map/ppermute | solution.py:152
  328.0 21.5 %attention_back.2 = (bf16[512,512]{1,0:T(8,128)(2,1)}, bf16[512,1536]{1,0:T(8,128)(2,1)}, f32[2,8,1536]{2,1,0:T(8,128)}, f32[2,8,2048]{2,1,0:T(8,128)}, f32[2,12...) custom-call(s32[4]{0:T(128)} %get-tuple-element.429.refs_0_, ...), custom_call_target="tpu_custom_call" | custom-call | flops 1193500032 | bytes 1000 | tf_op jit(solution)/shard_map/attention_back/pallas_call | solution.py:132
  364.7 21.2 %collective-permute-done.42.refs_5_ = f32[2,128,1024]{2,1,0:T(8,128)S(1)} collective-permute-done((f32[2,128,1024]{2,1,0:T(8,128)S(1)}, f32[2,128,1024]{2,1,0:T(8,128)S(1)}, u32[]{:S(2)}, u32[]{:S(2)}) %collective-permute-start.42) | collective-permute-done | bytes 1048608 | tf_op jit(solution)/shard_map/ppermute | solution.py:152
  396.1 12.5 %middle_back.3 = (f32[512,2048]{1,0:T(8,128)}, bf16[512,2048]{1,0:T(8,128)(2,1)}, f32[512,128]{1,0:T(8,128)}, f32[4,8,2048]{2,1,0:T(8,128)}) custom-call(bf16[512,2048]{1,0:T(8,128)(2,1)} %get-tuple-element.342.refs_0_.refs_6_.refs_1_, bf16[512,2048]{1,0:T(8,128)(2,1)} %bitcast.108, f32[2,128,1024]{2,1,0:T(8,128)} %copy-done.2, f32[2,128,1024]{2,1,0:T(8,128)} %copy-done.14, ...), custom_call_target="tpu_custom_call" | custom-call | flops 605000000 | bytes 1000 | tf_op jit(solution)/shard_map/middle_back/pallas_call | solution.py:132
  410.4 22.0 %attention_back.3 = (bf16[512,512]{1,0:T(8,128)(2,1)}, bf16[512,1536]{1,0:T(8,128)(2,1)}, f32[2,8,1536]{2,1,0:T(8,128)}, f32[2,8,2048]{2,1,0:T(8,128)}, f32[2,12...) custom-call(s32[4]{0:T(128)} %get-tuple-element.430.refs_0_, ...), custom_call_target="tpu_custom_call" | custom-call | flops 1193500032 | bytes 1000 | tf_op jit(solution)/shard_map/attention_back/pallas_call | solution.py:132
  435.6 21.6 %collective-permute-done.44 = f32[2,128,1024]{2,1,0:T(8,128)} collective-permute-done((f32[2,128,1024]{2,1,0:T(8,128)S(1)}, f32[2,128,1024]{2,1,0:T(8,128)}, u32[]{:S(2)}, u32[]{:S(2)}) %collective-permute-start.44) | collective-permute-done | bytes 1048608 | tf_op jit(solution)/shard_map/ppermute | solution.py:152
  457.3 15.3 %full_grad.3 = f32[2048,2048]{1,0:T(8,128)} custom-call(bf16[512,2048]{1,0:T(8,128)(2,1)} %get-tuple-element.311.refs_0_, bf16[512,2048]{1,0:T(8,128)(2,1)} %get-tuple-element.312.refs_1_, bf16[512,1536]{1,0:T(8,128)(2,1)} %get-tuple-element.313.refs_2_, bf16[512,1536]{1,0:T(8,128)(2,1)} %get-tuple-element.314.refs_3_, ...), custom_call_target="tpu_custom_call" | custom-call | flops 825000000 | bytes 1000 | tf_op jit(solution)/shard_map/full_grad/pallas_call | solution.py:132
  481.8 29.7 %collective-permute-done.46 = f32[1,128,1024]{2,1,0:T(8,128)S(1)} collective-permute-done((f32[1,128,1024]{2,1,0:T(8,128)S(1)}, f32[1,128,1024]{2,1,0:T(8,128)S(1)}, u32[]{:S(2)}, u32[]{:S(2)}) %collective-permute-start.46) | collective-permute-done | bytes 524320 | tf_op jit(solution)/shard_map/ppermute | solution.py:152
  521.6 13.1 %collective-permute-done.50 = f32[1,128,1024]{2,1,0:T(8,128)S(1)} collective-permute-done((f32[1,128,1024]{2,1,0:T(8,128)S(1)}, f32[1,128,1024]{2,1,0:T(8,128)S(1)}, u32[]{:S(2)}, u32[]{:S(2)}) %collective-permute-start.50) | collective-permute-done | bytes 524320 | tf_op jit(solution)/shard_map/ppermute | solution.py:152
  535.7 17.0 %collective-permute-done.51 = f32[1,128,1024]{2,1,0:T(8,128)S(1)} collective-permute-done((f32[1,128,1024]{2,1,0:T(8,128)S(1)}, f32[1,128,1024]{2,1,0:T(8,128)S(1)}, u32[]{:S(2)}, u32[]{:S(2)}) %collective-permute-start.51) | collective-permute-done | bytes 524320 | tf_op jit(solution)/shard_map/ppermute | solution.py:152
  564.1 47.4 %collective-permute-done.57 = f32[1,128,1024]{2,1,0:T(8,128)S(1)} collective-permute-done((f32[1,128,1024]{2,1,0:T(8,128)S(1)}, f32[1,128,1024]{2,1,0:T(8,128)S(1)}, u32[]{:S(2)}, u32[]{:S(2)}) %collective-permute-start.57) | collective-permute-done | bytes 524320 | tf_op jit(solution)/shard_map/ppermute | solution.py:152
  623.1 32.3 %collective-permute-done.61 = f32[256,2048]{1,0:T(8,128)S(1)} collective-permute-done((f32[256,2048]{1,0:T(8,128)S(1)}, f32[256,2048]{1,0:T(8,128)S(1)}, u32[]{:S(2)}, u32[]{:S(2)}) %collective-permute-start.61) | collective-permute-done | bytes 2097184 | tf_op jit(solution)/shard_map/ppermute | solution.py:240
  662.0 13.8 %collective-permute-done.64.refs_6_ = f32[2,128,1024]{2,1,0:T(8,128)S(1)} collective-permute-done((f32[2,128,1024]{2,1,0:T(8,128)S(1)}, f32[2,128,1024]{2,1,0:T(8,128)S(1)}, u32[]{:S(2)}, u32[]{:S(2)}) %collective-permute-start.64) | collective-permute-done | bytes 1048608 | tf_op jit(solution)/shard_map/ppermute | solution.py:152
  700.9 15.1 %reduce-scatter.5.cloned.1.call-done = f32[256,2048]{1,0:T(8,128)} async-done(((f32[2048,2048]{1,0:T(8,128)}), f32[256,2048]{1,0:T(8,128)}) %reduce-scatter.5.cloned.1.call-update) | async-done | bytes 2097168 | tf_op jit(solution)/shard_map/reduce_scatter | solution.py:1190
  (370 shorter events, 272.6 us)
Async XLA Ops:
  8.0 547.1 %reduce-scatter.3.cloned.1.call-start = ((), (), s32[]{:S(2)}) async-start(), calls=%async_computation.2 | async-start | bytes 18874368 | tf_op jit(solution)/shard_map/reduce_scatter | solution.py:1119
  58.9 34.3 %collective-permute-start.6 = (f32[2,128,1024]{2,1,0:T(8,128)}, f32[2,128,1024]{2,1,0:T(8,128)S(1)}, u32[]{:S(2)}, u32[]{:S(2)}) collective-permute-start(f32[2,128,1024]{2,1,0:T(8,128)} %get-tuple-element.208), channel_id=1, source_target_pairs={{0,1},{1,0},{2,3},{3,2},{4,5},{5,4},{6,7},{7,6},{8,9},{9,8},{10,11... | collective-permute-start | bytes 3145736 | tf_op jit(solution)/shard_map/ppermute | solution.py:152
  59.4 36.2 %collective-permute-start.7 = (f32[2,128,1024]{2,1,0:T(8,128)}, f32[2,128,1024]{2,1,0:T(8,128)S(1)}, u32[]{:S(2)}, u32[]{:S(2)}) collective-permute-start(f32[2,128,1024]{2,1,0:T(8,128)} %get-tuple-element.211), channel_id=1, source_target_pairs={{0,2},{1,3},{2,0},{3,1},{4,6},{5,7},{6,4},{7,5},{8,10},{9,11},{10,... | collective-permute-start | bytes 3145736 | tf_op jit(solution)/shard_map/ppermute | solution.py:152
  76.0 29.4 %collective-permute-start.10 = (f32[1,128,1024]{2,1,0:T(8,128)S(1)}, f32[1,128,1024]{2,1,0:T(8,128)S(1)}, u32[]{:S(2)}, u32[]{:S(2)}) collective-permute-start(f32[1,128,1024]{2,1,0:T(8,128)S(1)} %add.313), channel_id=1, source_target_pairs={{0,1},{1,0},{2,3},{3,2},{4,5},{5,4},{6,7},{7,6},{8,9},{9,8},{10,11... | collective-permute-start | bytes 1572872 | tf_op jit(solution)/shard_map/ppermute | solution.py:152
  237.2 450.0 %all-reduce.3.cloned.1.call-start = ((), (), s32[]{:S(2)}) async-start(), calls=%async_computation.3 | async-start | bytes 16777216 | tf_op jit(solution)/shard_map/psum | solution.py:1172
  277.6 46.0 %collective-permute-start.35 = (f32[2,128,1024]{2,1,0:T(8,128)}, f32[2,128,1024]{2,1,0:T(8,128)S(1)}, u32[]{:S(2)}, u32[]{:S(2)}) collective-permute-start(f32[2,128,1024]{2,1,0:T(8,128)} %get-tuple-element.273), channel_id=1, source_target_pairs={{0,1},{1,0},{2,3},{3,2},{4,5},{5,4},{6,7},{7,6},{8,9},{9,8},{10,11... | collective-permute-start | bytes 3145736 | tf_op jit(solution)/shard_map/ppermute | solution.py:152
  278.2 45.5 %collective-permute-start.36 = (f32[2,128,1024]{2,1,0:T(8,128)}, f32[2,128,1024]{2,1,0:T(8,128)}, u32[]{:S(2)}, u32[]{:S(2)}) collective-permute-start(f32[2,128,1024]{2,1,0:T(8,128)} %get-tuple-element.276), channel_id=1, source_target_pairs={{0,2},{1,3},{2,0},{3,1},{4,6},{5,7},{6,4},{7,5},{8,10},{9,11},{10,... | collective-permute-start | bytes 3145736 | tf_op jit(solution)/shard_map/ppermute | solution.py:152
  278.7 108.5 %collective-permute-start.43 = (f32[256,2048]{1,0:T(8,128)}, f32[256,2048]{1,0:T(8,128)}, u32[]{:S(2)}, u32[]{:S(2)}) collective-permute-start(f32[256,2048]{1,0:T(8,128)} %get-tuple-element.289), channel_id=1, source_target_pairs={{0,8},{4,12},{8,16},{12,20},{16,24},{20,28},{24,0},{28,4},{1,9},{5... | collective-permute-start | bytes 6291464 | tf_op jit(solution)/shard_map/ppermute | solution.py:240
  391.2 324.8 %reduce-scatter.5.cloned.1.call-start = ((), (), s32[]{:S(2)}) async-start(), calls=%async_computation.4 | async-start | bytes 18874368 | tf_op jit(solution)/shard_map/reduce_scatter | solution.py:1190
  394.1 161.0 %collective-permute-start.52 = (f32[256,2048]{1,0:T(8,128)S(1)}, f32[256,2048]{1,0:T(8,128)}, u32[]{:S(2)}, u32[]{:S(2)}) collective-permute-start(f32[256,2048]{1,0:T(8,128)S(1)} %copy-done.4), channel_id=1, source_target_pairs={{0,8},{4,12},{8,16},{12,20},{16,24},{20,28},{24,0},{28,4},{1,9},{5... | collective-permute-start | bytes 6291464 | tf_op jit(solution)/shard_map/ppermute | solution.py:240
  408.6 48.6 %collective-permute-start.44 = (f32[2,128,1024]{2,1,0:T(8,128)S(1)}, f32[2,128,1024]{2,1,0:T(8,128)}, u32[]{:S(2)}, u32[]{:S(2)}) collective-permute-start(f32[2,128,1024]{2,1,0:T(8,128)S(1)} %copy-done.39), channel_id=1, source_target_pairs={{0,1},{1,0},{2,3},{3,2},{4,5},{5,4},{6,7},{7,6},{8,9},{9,8},{10,11... | collective-permute-start | bytes 3145736 | tf_op jit(solution)/shard_map/ppermute | solution.py:152
  408.8 48.6 %collective-permute-start.45 = (f32[2,128,1024]{2,1,0:T(8,128)S(1)}, f32[2,128,1024]{2,1,0:T(8,128)}, u32[]{:S(2)}, u32[]{:S(2)}) collective-permute-start(f32[2,128,1024]{2,1,0:T(8,128)S(1)} %copy-done.38), channel_id=1, source_target_pairs={{0,2},{1,3},{2,0},{3,1},{4,6},{5,7},{6,4},{7,5},{8,10},{9,11},{10,... | collective-permute-start | bytes 3145736 | tf_op jit(solution)/shard_map/ppermute | solution.py:152
  433.3 80.0 %collective-permute-start.48 = (f32[2,128,1024]{2,1,0:T(8,128)}, f32[2,128,1024]{2,1,0:T(8,128)}, u32[]{:S(2)}, u32[]{:S(2)}) collective-permute-start(f32[2,128,1024]{2,1,0:T(8,128)} %get-tuple-element.324), channel_id=1, source_target_pairs={{0,1},{1,0},{2,3},{3,2},{4,5},{5,4},{6,7},{7,6},{8,9},{9,8},{10,11... | collective-permute-start | bytes 3145736 | tf_op jit(solution)/shard_map/ppermute | solution.py:152
  434.9 80.4 %collective-permute-start.49 = (f32[2,128,1024]{2,1,0:T(8,128)}, f32[2,128,1024]{2,1,0:T(8,128)}, u32[]{:S(2)}, u32[]{:S(2)}) collective-permute-start(f32[2,128,1024]{2,1,0:T(8,128)} %get-tuple-element.326), channel_id=1, source_target_pairs={{0,2},{1,3},{2,0},{3,1},{4,6},{5,7},{6,4},{7,5},{8,10},{9,11},{10,... | collective-permute-start | bytes 3145736 | tf_op jit(solution)/shard_map/ppermute | solution.py:152
  476.1 37.2 %collective-permute-start.47 = (f32[1,128,1024]{2,1,0:T(8,128)S(1)}, f32[1,128,1024]{2,1,0:T(8,128)S(1)}, u32[]{:S(2)}, u32[]{:S(2)}) collective-permute-start(f32[1,128,1024]{2,1,0:T(8,128)S(1)} %slice_add_fusion.6), channel_id=1, source_target_pairs={{0,1},{1,0},{2,3},{3,2},{4,5},{5,4},{6,7},{7,6},{8,9},{9,8},{10,11... | collective-permute-start | bytes 1572872 | tf_op jit(solution)/shard_map/ppermute | solution.py:152
  478.1 33.4 %collective-permute-start.46 = (f32[1,128,1024]{2,1,0:T(8,128)S(1)}, f32[1,128,1024]{2,1,0:T(8,128)S(1)}, u32[]{:S(2)}, u32[]{:S(2)}) collective-permute-start(f32[1,128,1024]{2,1,0:T(8,128)S(1)} %slice_add_fusion.7), channel_id=1, source_target_pairs={{0,2},{1,3},{2,0},{3,1},{4,6},{5,7},{6,4},{7,5},{8,10},{9,11},{10,... | collective-permute-start | bytes 1572872 | tf_op jit(solution)/shard_map/ppermute | solution.py:152
  511.5 51.2 %collective-permute-start.55 = (f32[2,2048]{1,0:T(2,128)S(1)}, f32[2,2048]{1,0:T(2,128)S(1)}, u32[]{:S(2)}, u32[]{:S(2)}) collective-permute-start(f32[2,2048]{1,0:T(2,128)S(1)} %fusion.12), channel_id=1, source_target_pairs={{0,1},{1,0},{2,3},{3,2},{4,5},{5,4},{6,7},{7,6},{8,9},{9,8},{10,11... | collective-permute-start | bytes 49160 | tf_op jit(solution)/shard_map/ppermute | solution.py:152
  517.3 42.2 %collective-permute-start.54 = (f32[1,128,1024]{2,1,0:T(8,128)}, f32[1,128,1024]{2,1,0:T(8,128)}, u32[]{:S(2)}, u32[]{:S(2)}) collective-permute-start(f32[1,128,1024]{2,1,0:T(8,128)} %slice_add_fusion.2), channel_id=1, source_target_pairs={{0,1},{1,0},{2,3},{3,2},{4,5},{5,4},{6,7},{7,6},{8,9},{9,8},{10,11... | collective-permute-start | bytes 1572872 | tf_op jit(solution)/shard_map/ppermute | solution.py:152
  517.5 35.1 %collective-permute-start.51 = (f32[1,128,1024]{2,1,0:T(8,128)S(1)}, f32[1,128,1024]{2,1,0:T(8,128)S(1)}, u32[]{:S(2)}, u32[]{:S(2)}) collective-permute-start(f32[1,128,1024]{2,1,0:T(8,128)S(1)} %add.364), channel_id=1, source_target_pairs={{0,1},{1,0},{2,3},{3,2},{4,5},{5,4},{6,7},{7,6},{8,9},{9,8},{10,11... | collective-permute-start | bytes 1572872 | tf_op jit(solution)/shard_map/ppermute | solution.py:152
  553.5 59.4 %collective-permute-start.59 = (f32[2,128,1024]{2,1,0:T(8,128)}, f32[2,128,1024]{2,1,0:T(8,128)}, u32[]{:S(2)}, u32[]{:S(2)}) collective-permute-start(f32[2,128,1024]{2,1,0:T(8,128)} %constant_dynamic-update-slice_fusion.18.refs_5_), channel_id=1, source_target_pairs={{0,2},{1,3},{2,0},{3,1},{4,6},{5,7},{6,4},{7,5},{8,10},{9,11},{10,... | collective-permute-start | bytes 3145736 | tf_op jit(solution)/shard_map/ppermute | solution.py:152
  555.1 57.8 %collective-permute-start.58 = (f32[2,128,1024]{2,1,0:T(8,128)}, f32[2,128,1024]{2,1,0:T(8,128)S(1)}, u32[]{:S(2)}, u32[]{:S(2)}) collective-permute-start(f32[2,128,1024]{2,1,0:T(8,128)} %copy-done.21), channel_id=1, source_target_pairs={{0,1},{1,0},{2,3},{3,2},{4,5},{5,4},{6,7},{7,6},{8,9},{9,8},{10,11... | collective-permute-start | bytes 3145736 | tf_op jit(solution)/shard_map/ppermute | solution.py:152
  559.0 53.9 %collective-permute-start.56 = (f32[1,128,1024]{2,1,0:T(8,128)S(1)}, f32[1,128,1024]{2,1,0:T(8,128)S(1)}, u32[]{:S(2)}, u32[]{:S(2)}) collective-permute-start(f32[1,128,1024]{2,1,0:T(8,128)S(1)} %add.370), channel_id=1, source_target_pairs={{0,2},{1,3},{2,0},{3,1},{4,6},{5,7},{6,4},{7,5},{8,10},{9,11},{10,... | collective-permute-start | bytes 1572872 | tf_op jit(solution)/shard_map/ppermute | solution.py:152
  560.5 50.9 %collective-permute-start.57 = (f32[1,128,1024]{2,1,0:T(8,128)S(1)}, f32[1,128,1024]{2,1,0:T(8,128)S(1)}, u32[]{:S(2)}, u32[]{:S(2)}) collective-permute-start(f32[1,128,1024]{2,1,0:T(8,128)S(1)} %add.371), channel_id=1, source_target_pairs={{0,1},{1,0},{2,3},{3,2},{4,5},{5,4},{6,7},{7,6},{8,9},{9,8},{10,11... | collective-permute-start | bytes 1572872 | tf_op jit(solution)/shard_map/ppermute | solution.py:152
  562.7 92.7 %collective-permute-start.61 = (f32[256,2048]{1,0:T(8,128)S(1)}, f32[256,2048]{1,0:T(8,128)S(1)}, u32[]{:S(2)}, u32[]{:S(2)}) collective-permute-start(f32[256,2048]{1,0:T(8,128)S(1)} %bitcast_add_fusion.1), channel_id=1, source_target_pairs={{0,8},{4,12},{8,16},{12,20},{16,24},{20,28},{24,0},{28,4},{1,9},{5... | collective-permute-start | bytes 6291464 | tf_op jit(solution)/shard_map/ppermute | solution.py:240
  (100 other events, 1453.6 us)
Sparse Core Ops, SparseCore 0:
  237.3 258.9 reduce-scatter.2
  498.8 217.1 reduce-scatter.4
Sparse Core Ops, SparseCore 1:
  391.3 256.5 all-reduce.2

commit v11 on v9

--- a/solution.py
+++ b/solution.py
@@ -37,6 +37,7 @@
     "attention_back": 21.7,
     "tokens_back": 8.5,
     "output": 6.0,
+    "attention_outputs": 2.0,
 }
 WORK = 5.5e+07
 
@@ -965,6 +966,26 @@
         for at in range(len(totals)):
             if done[at] < limits[at]:
                 step(at)
+
+
+def attention_outputs(part, width):
+    rows = part.shape[0]
+
+    def kernel(p, qkv, out):
+        for c in range(3):
+            qkv[c] = p[:, c * width : (c + 1) * width]
+        out[...] = jnp.transpose(p[:, 3 * width :])
+
+    return run(
+        kernel,
+        (1,),
+        [whole(part)],
+        [
+            ((3, rows, width), F32, (3, rows, width), lambda i: (0, 0, 0)),
+            ((width, rows), F32, (width, rows), lambda i: (0, 0)),
+        ],
+        name="attention_outputs",
+    )
 
 
 def split_rows(value):
@@ -1239,8 +1260,7 @@
         line.mark(output)
     vecs = vecs + got
     hid_vecs, mid_vecs, narrow, wide = vecs[:3], vecs[3:7], vecs[7:10], vecs[10:12]
-    qkv_part = jnp.swapaxes(attention_part[:, : 3 * width].reshape(-1, 3, width), 0, 1)
-    out_part = jnp.transpose(attention_part[:, 3 * width :])
+    qkv_part, out_part = attention_outputs(attention_part, width)
     units = hid_gain.shape[1]
     return (
         output.reshape(-1, D),

time: 728 us -> 726 us (level)
    pallas_call x24 -> x25, Pallas kernels: 286 us -> 290 us  [run(): pl.pallas_call(body, grid_spec=pltpu.PrefetchScalarGridSpec(num_scalar_pr...]
where the time goes in v11:
time: 726 us; the launch traced here: 716 us
  Pallas kernels  290 us (40%)
  waiting for transfers between devices  280 us (39%)
  starting transfers between devices  76.8 us (11%)
  other arithmetic  26.5 us (4%)
  local copies, waits for them, and re-layouts  25.8 us (4%)
  between operations  17.2 us (2%)
    pallas_call x25, Pallas kernels, run(): pl.pallas_call(body, grid_spec=pltpu.PrefetchScalarGridSpec(num_scalar_pr...  290 us
    ppermute x54, waiting for transfers between devices, flip(): lax.ppermute(value, 'tensor', [(t, t ^ 1 << bit) for t in range(size)])  260 us
    ppermute x54, starting transfers between devices, flip(): lax.ppermute(value, 'tensor', [(t, t ^ 1 << bit) for t in range(size)])  60.3 us
  transfers between devices with their start and end apart: 70, of which 30 were waited for; matrix products, arithmetic and copies ran while one was open for 5% of the time, Pallas kernels for 36%

profile of v11, /device:TPU:0, one launch (start us, length us, event | category | flops | bytes accessed | tf_op | source)
XLA Modules:
  0.0 715.6 jit_solution(14759402079755616245)
XLA Ops:
  10.7 15.7 %front.2 = (bf16[512,2048]{1,0:T(8,128)(2,1)}, bf16[512,2048]{1,0:T(8,128)(2,1)}, bf16[512,1536]{1,0:T(8,128)(2,1)}, f32[512,512]{1,0:T(8,128)}, f32[16,512]{1,0...) custom-call(s32[4]{0:T(128)} %get-tuple-element.397.refs_0_, ...), custom_call_target="tpu_custom_call" | custom-call | flops 858000000 | bytes 1000 | tf_op jit(solution)/shard_map/front/pallas_call | solution.py:133
  31.5 15.9 %front.3 = (bf16[512,2048]{1,0:T(8,128)(2,1)}, bf16[512,2048]{1,0:T(8,128)(2,1)}, bf16[512,1536]{1,0:T(8,128)(2,1)}, f32[512,512]{1,0:T(8,128)}, f32[16,512]{1,0...) custom-call(s32[4]{0:T(128)} %get-tuple-element.398.refs_0_, ...), custom_call_target="tpu_custom_call" | custom-call | flops 858000000 | bytes 1000 | tf_op jit(solution)/shard_map/front/pallas_call | solution.py:133
  78.1 13.5 %hidden_back.1.refs_3_.refs_2_ = bf16[1024,2048]{1,0:T(8,128)(2,1)} custom-call(bf16[512,2048]{1,0:T(8,128)(2,1)} %bitcast.105, bf16[512,2048]{1,0:T(8,128)(2,1)} %bitcast.102, bf16[2048,2048]{1,0:T(8,128)(2,1)} %refs_3_.1), custom_call_target="tpu_custom_call" | custom-call | flops 22000001024 | bytes 1000 | tf_op jit(solution)/shard_map/hidden_back/pallas_call | solution.py:133
  108.9 20.5 %collective-permute-done.11 = f32[2,16,512]{2,1,0:T(8,128)S(1)} collective-permute-done((f32[2,16,512]{2,1,0:T(8,128)S(1)}, f32[2,16,512]{2,1,0:T(8,128)S(1)}, u32[]{:S(2)}, u32[]{:S(2)}) %collective-permute-start.11) | collective-permute-done | bytes 65568 | tf_op jit(solution)/shard_map/ppermute | solution.py:153
  145.8 13.6 %hidden_front.2 = (bf16[512,2048]{1,0:T(8,128)(2,1)}, bf16[512,2048]{1,0:T(8,128)(2,1)}, f32[8,512]{1,0:T(8,128)}) custom-call(bf16[512,2048]{1,0:T(8,128)(2,1)} %get-tuple-element.262.refs_0_.refs_1_, bf16[2048,2048]{1,0:T(8,128)(2,1)} %refs_1_.13, f32[1,2048]{1,0:T(1,128)} %bitcast.130, bf16[1024,2048]{1,0:T(8,128)(2,1)} %hidden_back.1.refs_3_.refs_2_, ...), custom_call_target="tpu_custom_call" | custom-call | flops 808499968 | bytes 1000 | tf_op jit(solution)/shard_map/hidden_front/pallas_call | solution.py:133
  194.5 13.8 %hidden_front.3 = (bf16[512,2048]{1,0:T(8,128)(2,1)}, bf16[512,2048]{1,0:T(8,128)(2,1)}, f32[8,512]{1,0:T(8,128)}) custom-call(bf16[512,2048]{1,0:T(8,128)(2,1)} %get-tuple-element.240.refs_0_.refs_2_, bf16[2048,2048]{1,0:T(8,128)(2,1)} %refs_1_.13, f32[1,2048]{1,0:T(1,128)} %bitcast.131, bf16[1024,2048]{1,0:T(8,128)(2,1)} %hidden_back.1.refs_3_.refs_2_, ...), custom_call_target="tpu_custom_call" | custom-call | flops 808499968 | bytes 1000 | tf_op jit(solution)/shard_map/hidden_front/pallas_call | solution.py:133
  223.1 14.1 %full_grad.2 = f32[2048,2048]{1,0:T(8,128)} custom-call(bf16[512,2048]{1,0:T(8,128)(2,1)} %get-tuple-element.266.refs_0_.refs_1_, bf16[512,2048]{1,0:T(8,128)(2,1)} %get-tuple-element.255.refs_1_.refs_2_, bf16[512,2048]{1,0:T(8,128)(2,1)} %bitcast.106, bf16[512,2048]{1,0:T(8,128)(2,1)} %bitcast.103), custom_call_target="tpu_custom_call" | custom-call | flops 825000000 | bytes 1000 | tf_op jit(solution)/shard_map/full_grad/pallas_call | solution.py:133
  237.8 9.8 %ring_grads.2 = f32[4,256,2048]{2,1,0:T(8,128)} custom-call(s32[4]{0:T(128)} %add_subtract_fusion.refs_0_, bf16[512,2048]{1,0:T(8,128)(2,1)} %get-tuple-element.262.refs_0_.refs_1_, bf16[512,2048]{1,0:T(8,128)(2,1)} %get-tuple-element.240.refs_0_.refs_2_, bf16[512,2048]{1,0:T(8,128)(2,1)} %get-tuple-element.233.refs_0_.refs_3_, ...), custom_call_target="tpu_custom_call" | custom-call | flops 660000000 | bytes 1000 | tf_op jit(solution)/shard_map/ring_grads/pallas_call | solution.py:133
  261.6 12.9 %ring_grads.3 = (f32[256,2048]{1,0:T(8,128)}, f32[3,256,2048]{2,1,0:T(8,128)}) custom-call(s32[4]{0:T(128)} %broadcast_add_fusion.refs_0_, bf16[512,2048]{1,0:T(8,128)(2,1)} %get-tuple-element.262.refs_0_.refs_1_, bf16[512,2048]{1,0:T(8,128)(2,1)} %get-tuple-element.240.refs_0_.refs_2_, bf16[512,2048]{1,0:T(8,128)(2,1)} %get-tuple-element.233.refs_0_.refs_3_, ...), custom_call_target="tpu_custom_call" | custom-call | flops 660000000 | bytes 1000 | tf_op jit(solution)/shard_map/ring_grads/pallas_call | solution.py:133
  280.4 16.1 %result_part.1 = f32[8,128,2048]{2,1,0:T(8,128)} custom-call(s32[8]{0:T(128)} %pad_add_fusion.refs_0_, bf16[512,2048]{1,0:T(8,128)(2,1)} %get-tuple-element.266.refs_0_.refs_1_, bf16[512,2048]{1,0:T(8,128)(2,1)} %get-tuple-element.255.refs_1_.refs_2_, bf16[2048,2048]{1,0:T(8,128)(2,1)} %refs_3_.1), custom_call_target="tpu_custom_call" | custom-call | flops 22000001024 | bytes 1000 | tf_op jit(solution)/shard_map/result_part/pallas_call | solution.py:133
  302.4 11.1 %middle_back.2 = (f32[512,2048]{1,0:T(8,128)}, bf16[512,2048]{1,0:T(8,128)(2,1)}, f32[512,128]{1,0:T(8,128)}, f32[4,8,2048]{2,1,0:T(8,128)}) custom-call(bf16[512,2048]{1,0:T(8,128)(2,1)} %get-tuple-element.337.refs_0_.refs_6_.refs_1_, bf16[512,2048]{1,0:T(8,128)(2,1)} %bitcast.107, f32[2,128,1024]{2,1,0:T(8,128)} %copy-done, ...), custom_call_target="tpu_custom_call" | custom-call | flops 605000000 | bytes 1000 | tf_op jit(solution)/shard_map/middle_back/pallas_call | solution.py:133
  313.5 10.2 %collective-permute-done.35 = f32[2,128,1024]{2,1,0:T(8,128)S(1)} collective-permute-done((f32[2,128,1024]{2,1,0:T(8,128)}, f32[2,128,1024]{2,1,0:T(8,128)S(1)}, u32[]{:S(2)}, u32[]{:S(2)}) %collective-permute-start.35) | collective-permute-done | bytes 1048608 | tf_op jit(solution)/shard_map/ppermute | solution.py:153
  328.1 21.5 %attention_back.2 = (bf16[512,512]{1,0:T(8,128)(2,1)}, bf16[512,1536]{1,0:T(8,128)(2,1)}, f32[2,8,1536]{2,1,0:T(8,128)}, f32[2,8,2048]{2,1,0:T(8,128)}, f32[2,12...) custom-call(s32[4]{0:T(128)} %get-tuple-element.397.refs_0_, ...), custom_call_target="tpu_custom_call" | custom-call | flops 1193500032 | bytes 1000 | tf_op jit(solution)/shard_map/attention_back/pallas_call | solution.py:133
  351.9 10.2 %collective-permute-done.39 = f32[1,128,1024]{2,1,0:T(8,128)S(1)} collective-permute-done((f32[1,128,1024]{2,1,0:T(8,128)S(1)}, f32[1,128,1024]{2,1,0:T(8,128)S(1)}, u32[]{:S(2)}, u32[]{:S(2)}) %collective-permute-start.39) | collective-permute-done | bytes 524320 | tf_op jit(solution)/shard_map/ppermute | solution.py:153
  364.7 21.3 %collective-permute-done.42.refs_5_ = f32[2,128,1024]{2,1,0:T(8,128)S(1)} collective-permute-done((f32[2,128,1024]{2,1,0:T(8,128)S(1)}, f32[2,128,1024]{2,1,0:T(8,128)S(1)}, u32[]{:S(2)}, u32[]{:S(2)}) %collective-permute-start.42) | collective-permute-done | bytes 1048608 | tf_op jit(solution)/shard_map/ppermute | solution.py:153
  393.6 11.2 %middle_back.3 = (f32[512,2048]{1,0:T(8,128)}, bf16[512,2048]{1,0:T(8,128)(2,1)}, f32[512,128]{1,0:T(8,128)}, f32[4,8,2048]{2,1,0:T(8,128)}) custom-call(bf16[512,2048]{1,0:T(8,128)(2,1)} %get-tuple-element.344.refs_0_.refs_6_.refs_1_, bf16[512,2048]{1,0:T(8,128)(2,1)} %bitcast.104, f32[2,128,1024]{2,1,0:T(8,128)} %copy-done.2, f32[2,128,1024]{2,1,0:T(8,128)} %copy-done.24, ...), custom_call_target="tpu_custom_call" | custom-call | flops 605000000 | bytes 1000 | tf_op jit(solution)/shard_map/middle_back/pallas_call | solution.py:133
  404.8 21.9 %attention_back.3 = (bf16[512,512]{1,0:T(8,128)(2,1)}, bf16[512,1536]{1,0:T(8,128)(2,1)}, f32[2,8,1536]{2,1,0:T(8,128)}, f32[2,8,2048]{2,1,0:T(8,128)}, f32[2,12...) custom-call(s32[4]{0:T(128)} %get-tuple-element.398.refs_0_, ...), custom_call_target="tpu_custom_call" | custom-call | flops 1193500032 | bytes 1000 | tf_op jit(solution)/shard_map/attention_back/pallas_call | solution.py:133
  432.8 15.9 %full_grad.3 = f32[2048,2048]{1,0:T(8,128)} custom-call(bf16[512,2048]{1,0:T(8,128)(2,1)} %get-tuple-element.313.refs_0_, bf16[512,2048]{1,0:T(8,128)(2,1)} %get-tuple-element.314.refs_1_, bf16[512,1536]{1,0:T(8,128)(2,1)} %get-tuple-element.315.refs_2_, bf16[512,1536]{1,0:T(8,128)(2,1)} %get-tuple-element.316.refs_3_, ...), custom_call_target="tpu_custom_call" | custom-call | flops 825000000 | bytes 1000 | tf_op jit(solution)/shard_map/full_grad/pallas_call | solution.py:133
  459.1 53.8 %collective-permute-done.46 = f32[1,128,1024]{2,1,0:T(8,128)S(1)} collective-permute-done((f32[1,128,1024]{2,1,0:T(8,128)S(1)}, f32[1,128,1024]{2,1,0:T(8,128)S(1)}, u32[]{:S(2)}, u32[]{:S(2)}) %collective-permute-start.46) | collective-permute-done | bytes 524320 | tf_op jit(solution)/shard_map/ppermute | solution.py:153
  518.2 12.7 %collective-permute-done.50 = f32[1,128,1024]{2,1,0:T(8,128)S(1)} collective-permute-done((f32[1,128,1024]{2,1,0:T(8,128)S(1)}, f32[1,128,1024]{2,1,0:T(8,128)S(1)}, u32[]{:S(2)}, u32[]{:S(2)}) %collective-permute-start.50) | collective-permute-done | bytes 524320 | tf_op jit(solution)/shard_map/ppermute | solution.py:153
  540.4 11.0 %collective-permute-done.53 = f32[1,128,1024]{2,1,0:T(8,128)} collective-permute-done((f32[1,128,1024]{2,1,0:T(8,128)}, f32[1,128,1024]{2,1,0:T(8,128)}, u32[]{:S(2)}, u32[]{:S(2)}) %collective-permute-start.53) | collective-permute-done | bytes 524320 | tf_op jit(solution)/shard_map/ppermute | solution.py:153
  566.3 47.9 %collective-permute-done.57 = f32[1,128,1024]{2,1,0:T(8,128)S(1)} collective-permute-done((f32[1,128,1024]{2,1,0:T(8,128)S(1)}, f32[1,128,1024]{2,1,0:T(8,128)S(1)}, u32[]{:S(2)}, u32[]{:S(2)}) %collective-permute-start.57) | collective-permute-done | bytes 524320 | tf_op jit(solution)/shard_map/ppermute | solution.py:153
  638.0 23.5 %collective-permute-done.64.refs_6_ = f32[2,128,1024]{2,1,0:T(8,128)S(1)} collective-permute-done((f32[2,128,1024]{2,1,0:T(8,128)S(1)}, f32[2,128,1024]{2,1,0:T(8,128)S(1)}, u32[]{:S(2)}, u32[]{:S(2)}) %collective-permute-start.64) | collective-permute-done | bytes 1048608 | tf_op jit(solution)/shard_map/ppermute | solution.py:153
  692.0 12.6 %reduce-scatter.5.cloned.1.call-done.refs_0_ = f32[256,2048]{1,0:T(8,128)} async-done(((f32[2048,2048]{1,0:T(8,128)}), f32[256,2048]{1,0:T(8,128)}) %reduce-scatter.5.cloned.1.call-update) | async-done | bytes 2097168 | tf_op jit(solution)/shard_map/reduce_scatter | solution.py:1211
  (385 shorter events, 267.8 us)
Async XLA Ops:
  8.0 523.1 %reduce-scatter.3.cloned.1.call-start = ((), (), s32[]{:S(2)}) async-start(), calls=%async_computation.2 | async-start | bytes 18874368 | tf_op jit(solution)/shard_map/reduce_scatter | solution.py:1140
  58.9 34.3 %collective-permute-start.6 = (f32[2,128,1024]{2,1,0:T(8,128)}, f32[2,128,1024]{2,1,0:T(8,128)S(1)}, u32[]{:S(2)}, u32[]{:S(2)}) collective-permute-start(f32[2,128,1024]{2,1,0:T(8,128)} %get-tuple-element.210), channel_id=1, source_target_pairs={{0,1},{1,0},{2,3},{3,2},{4,5},{5,4},{6,7},{7,6},{8,9},{9,8},{10,11... | collective-permute-start | bytes 3145736 | tf_op jit(solution)/shard_map/ppermute | solution.py:153
  59.4 36.2 %collective-permute-start.7 = (f32[2,128,1024]{2,1,0:T(8,128)}, f32[2,128,1024]{2,1,0:T(8,128)S(1)}, u32[]{:S(2)}, u32[]{:S(2)}) collective-permute-start(f32[2,128,1024]{2,1,0:T(8,128)} %get-tuple-element.213), channel_id=1, source_target_pairs={{0,2},{1,3},{2,0},{3,1},{4,6},{5,7},{6,4},{7,5},{8,10},{9,11},{10,... | collective-permute-start | bytes 3145736 | tf_op jit(solution)/shard_map/ppermute | solution.py:153
  76.0 29.4 %collective-permute-start.10 = (f32[1,128,1024]{2,1,0:T(8,128)S(1)}, f32[1,128,1024]{2,1,0:T(8,128)S(1)}, u32[]{:S(2)}, u32[]{:S(2)}) collective-permute-start(f32[1,128,1024]{2,1,0:T(8,128)S(1)} %add.313), channel_id=1, source_target_pairs={{0,1},{1,0},{2,3},{3,2},{4,5},{5,4},{6,7},{7,6},{8,9},{9,8},{10,11... | collective-permute-start | bytes 1572872 | tf_op jit(solution)/shard_map/ppermute | solution.py:153
  237.2 441.0 %all-reduce.3.cloned.1.call-start = ((), (), s32[]{:S(2)}) async-start(), calls=%async_computation.3 | async-start | bytes 16777216 | tf_op jit(solution)/shard_map/psum | solution.py:1193
  277.7 46.0 %collective-permute-start.35 = (f32[2,128,1024]{2,1,0:T(8,128)}, f32[2,128,1024]{2,1,0:T(8,128)S(1)}, u32[]{:S(2)}, u32[]{:S(2)}) collective-permute-start(f32[2,128,1024]{2,1,0:T(8,128)} %get-tuple-element.275), channel_id=1, source_target_pairs={{0,1},{1,0},{2,3},{3,2},{4,5},{5,4},{6,7},{7,6},{8,9},{9,8},{10,11... | collective-permute-start | bytes 3145736 | tf_op jit(solution)/shard_map/ppermute | solution.py:153
  278.3 45.5 %collective-permute-start.36 = (f32[2,128,1024]{2,1,0:T(8,128)}, f32[2,128,1024]{2,1,0:T(8,128)}, u32[]{:S(2)}, u32[]{:S(2)}) collective-permute-start(f32[2,128,1024]{2,1,0:T(8,128)} %get-tuple-element.278), channel_id=1, source_target_pairs={{0,2},{1,3},{2,0},{3,1},{4,6},{5,7},{6,4},{7,5},{8,10},{9,11},{10,... | collective-permute-start | bytes 3145736 | tf_op jit(solution)/shard_map/ppermute | solution.py:153
  278.8 108.6 %collective-permute-start.43 = (f32[256,2048]{1,0:T(8,128)}, f32[256,2048]{1,0:T(8,128)}, u32[]{:S(2)}, u32[]{:S(2)}) collective-permute-start(f32[256,2048]{1,0:T(8,128)} %get-tuple-element.291), channel_id=1, source_target_pairs={{0,8},{4,12},{8,16},{12,20},{16,24},{20,28},{24,0},{28,4},{1,9},{5... | collective-permute-start | bytes 6291464 | tf_op jit(solution)/shard_map/ppermute | solution.py:241
  391.3 313.2 %reduce-scatter.5.cloned.1.call-start = ((), (), s32[]{:S(2)}) async-start(), calls=%async_computation.4 | async-start | bytes 18874368 | tf_op jit(solution)/shard_map/reduce_scatter | solution.py:1211
  391.4 40.0 %collective-permute-start.44 = (f32[2,128,1024]{2,1,0:T(8,128)}, f32[2,128,1024]{2,1,0:T(8,128)S(1)}, u32[]{:S(2)}, u32[]{:S(2)}) collective-permute-start(f32[2,128,1024]{2,1,0:T(8,128)} %get-tuple-element.310), channel_id=1, source_target_pairs={{0,1},{1,0},{2,3},{3,2},{4,5},{5,4},{6,7},{7,6},{8,9},{9,8},{10,11... | collective-permute-start | bytes 3145736 | tf_op jit(solution)/shard_map/ppermute | solution.py:153
  392.2 40.6 %collective-permute-start.45 = (f32[2,128,1024]{2,1,0:T(8,128)}, f32[2,128,1024]{2,1,0:T(8,128)S(1)}, u32[]{:S(2)}, u32[]{:S(2)}) collective-permute-start(f32[2,128,1024]{2,1,0:T(8,128)} %get-tuple-element.312), channel_id=1, source_target_pairs={{0,2},{1,3},{2,0},{3,1},{4,6},{5,7},{6,4},{7,5},{8,10},{9,11},{10,... | collective-permute-start | bytes 3145736 | tf_op jit(solution)/shard_map/ppermute | solution.py:153
  451.2 81.9 %collective-permute-start.52 = (f32[256,2048]{1,0:T(8,128)}, f32[256,2048]{1,0:T(8,128)}, u32[]{:S(2)}, u32[]{:S(2)}) collective-permute-start(f32[256,2048]{1,0:T(8,128)} %bitcast_add_fusion.2), channel_id=1, source_target_pairs={{0,8},{4,12},{8,16},{12,20},{16,24},{20,28},{24,0},{28,4},{1,9},{5... | collective-permute-start | bytes 6291464 | tf_op jit(solution)/shard_map/ppermute | solution.py:241
  453.5 62.3 %collective-permute-start.48 = (f32[2,128,1024]{2,1,0:T(8,128)}, f32[2,128,1024]{2,1,0:T(8,128)S(1)}, u32[]{:S(2)}, u32[]{:S(2)}) collective-permute-start(f32[2,128,1024]{2,1,0:T(8,128)} %get-tuple-element.326), channel_id=1, source_target_pairs={{0,1},{1,0},{2,3},{3,2},{4,5},{5,4},{6,7},{7,6},{8,9},{9,8},{10,11... | collective-permute-start | bytes 3145736 | tf_op jit(solution)/shard_map/ppermute | solution.py:153
  454.8 62.4 %collective-permute-start.49 = (f32[2,128,1024]{2,1,0:T(8,128)}, f32[2,128,1024]{2,1,0:T(8,128)S(1)}, u32[]{:S(2)}, u32[]{:S(2)}) collective-permute-start(f32[2,128,1024]{2,1,0:T(8,128)} %get-tuple-element.328), channel_id=1, source_target_pairs={{0,2},{1,3},{2,0},{3,1},{4,6},{5,7},{6,4},{7,5},{8,10},{9,11},{10,... | collective-permute-start | bytes 3145736 | tf_op jit(solution)/shard_map/ppermute | solution.py:153
  457.1 58.1 %collective-permute-start.47 = (f32[1,128,1024]{2,1,0:T(8,128)S(1)}, f32[1,128,1024]{2,1,0:T(8,128)S(1)}, u32[]{:S(2)}, u32[]{:S(2)}) collective-permute-start(f32[1,128,1024]{2,1,0:T(8,128)S(1)} %slice_add_fusion.6), channel_id=1, source_target_pairs={{0,1},{1,0},{2,3},{3,2},{4,5},{5,4},{6,7},{7,6},{8,9},{9,8},{10,11... | collective-permute-start | bytes 1572872 | tf_op jit(solution)/shard_map/ppermute | solution.py:153
  457.5 55.4 %collective-permute-start.46 = (f32[1,128,1024]{2,1,0:T(8,128)S(1)}, f32[1,128,1024]{2,1,0:T(8,128)S(1)}, u32[]{:S(2)}, u32[]{:S(2)}) collective-permute-start(f32[1,128,1024]{2,1,0:T(8,128)S(1)} %slice_add_fusion.7), channel_id=1, source_target_pairs={{0,2},{1,3},{2,0},{3,1},{4,6},{5,7},{6,4},{7,5},{8,10},{9,11},{10,... | collective-permute-start | bytes 1572872 | tf_op jit(solution)/shard_map/ppermute | solution.py:153
  516.6 34.8 %collective-permute-start.53 = (f32[1,128,1024]{2,1,0:T(8,128)}, f32[1,128,1024]{2,1,0:T(8,128)}, u32[]{:S(2)}, u32[]{:S(2)}) collective-permute-start(f32[1,128,1024]{2,1,0:T(8,128)} %slice_add_fusion.3), channel_id=1, source_target_pairs={{0,2},{1,3},{2,0},{3,1},{4,6},{5,7},{6,4},{7,5},{8,10},{9,11},{10,... | collective-permute-start | bytes 1572872 | tf_op jit(solution)/shard_map/ppermute | solution.py:153
  535.7 92.6 %collective-permute-start.61 = (f32[256,2048]{1,0:T(8,128)S(1)}, f32[256,2048]{1,0:T(8,128)S(1)}, u32[]{:S(2)}, u32[]{:S(2)}) collective-permute-start(f32[256,2048]{1,0:T(8,128)S(1)} %bitcast_add_fusion.1), channel_id=1, source_target_pairs={{0,8},{4,12},{8,16},{12,20},{16,24},{20,28},{24,0},{28,4},{1,9},{5... | collective-permute-start | bytes 6291464 | tf_op jit(solution)/shard_map/ppermute | solution.py:241
  539.5 75.1 %collective-permute-start.59 = (f32[2,128,1024]{2,1,0:T(8,128)S(1)}, f32[2,128,1024]{2,1,0:T(8,128)S(1)}, u32[]{:S(2)}, u32[]{:S(2)}) collective-permute-start(f32[2,128,1024]{2,1,0:T(8,128)S(1)} %constant_dynamic-update-slice_fusion.18.refs_5_), channel_id=1, source_target_pairs={{0,2},{1,3},{2,0},{3,1},{4,6},{5,7},{6,4},{7,5},{8,10},{9,11},{10,... | collective-permute-start | bytes 3145736 | tf_op jit(solution)/shard_map/ppermute | solution.py:153
  551.4 63.1 %collective-permute-start.58 = (f32[2,128,1024]{2,1,0:T(8,128)S(1)}, f32[2,128,1024]{2,1,0:T(8,128)S(1)}, u32[]{:S(2)}, u32[]{:S(2)}) collective-permute-start(f32[2,128,1024]{2,1,0:T(8,128)S(1)} %constant_dynamic-update-slice_fusion.16.refs_3_), channel_id=1, source_target_pairs={{0,1},{1,0},{2,3},{3,2},{4,5},{5,4},{6,7},{7,6},{8,9},{9,8},{10,11... | collective-permute-start | bytes 3145736 | tf_op jit(solution)/shard_map/ppermute | solution.py:153
  563.3 51.2 %collective-permute-start.56 = (f32[1,128,1024]{2,1,0:T(8,128)S(1)}, f32[1,128,1024]{2,1,0:T(8,128)S(1)}, u32[]{:S(2)}, u32[]{:S(2)}) collective-permute-start(f32[1,128,1024]{2,1,0:T(8,128)S(1)} %add.370), channel_id=1, source_target_pairs={{0,2},{1,3},{2,0},{3,1},{4,6},{5,7},{6,4},{7,5},{8,10},{9,11},{10,... | collective-permute-start | bytes 1572872 | tf_op jit(solution)/shard_map/ppermute | solution.py:153
  564.4 49.8 %collective-permute-start.57 = (f32[1,128,1024]{2,1,0:T(8,128)S(1)}, f32[1,128,1024]{2,1,0:T(8,128)S(1)}, u32[]{:S(2)}, u32[]{:S(2)}) collective-permute-start(f32[1,128,1024]{2,1,0:T(8,128)S(1)} %add.371), channel_id=1, source_target_pairs={{0,1},{1,0},{2,3},{3,2},{4,5},{5,4},{6,7},{7,6},{8,9},{9,8},{10,11... | collective-permute-start | bytes 1572872 | tf_op jit(solution)/shard_map/ppermute | solution.py:153
  634.2 31.5 %collective-permute-start.63 = (f32[2,128,1024]{2,1,0:T(8,128)S(1)}, f32[2,128,1024]{2,1,0:T(8,128)S(1)}, u32[]{:S(2)}, u32[]{:S(2)}) collective-permute-start(f32[2,128,1024]{2,1,0:T(8,128)S(1)} %constant_dynamic-update-slice_fusion.20.refs_3_), channel_id=1, source_target_pairs={{0,1},{1,0},{2,3},{3,2},{4,5},{5,4},{6,7},{7,6},{8,9},{9,8},{10,11... | collective-permute-start | bytes 3145736 | tf_op jit(solution)/shard_map/ppermute | solution.py:153
  637.0 38.3 %collective-permute-start.65 = (f32[12,2048]{1,0:T(8,128)S(1)}, f32[12,2048]{1,0:T(8,128)S(1)}, u32[]{:S(2)}, u32[]{:S(2)}) collective-permute-start(f32[12,2048]{1,0:T(8,128)S(1)} %add.375), channel_id=1, source_target_pairs={{0,8},{4,12},{8,0},{12,4},{16,24},{20,28},{24,16},{28,20},{1,9},{5... | collective-permute-start | bytes 294920 | tf_op jit(solution)/shard_map/ppermute | solution.py:1231
  (109 other events, 1663.0 us)
Sparse Core Ops, SparseCore 0:
  237.4 216.3 reduce-scatter.2
  456.2 248.3 reduce-scatter.4
Sparse Core Ops, SparseCore 1:
  391.4 266.4 all-reduce.2

commit v12 on v11

--- a/solution.py
+++ b/solution.py
@@ -29,6 +29,7 @@
     "hidden_back": 400.0,
     "hidden_front": 14.7,
     "hidden_mid": 400.0,
+    "hidden_low": 400.0,
     "hidden_grad": 7.0,
     "full_grad": 15.0,
     "ring_grads": 12.0,
@@ -559,6 +560,39 @@
         after=after,
         name="hidden_front",
     )
+
+
+def hidden_low(active, sums, gain, shift):
+    blocks = len(sums)
+    rows, units = active.shape
+
+    def kernel(act, *refs):
+        stats = refs[:blocks]
+        g, b, low, tot8 = refs[blocks:]
+        step = pl.program_id(0)
+        for block in range(blocks):
+
+            @pl.when(step == block)
+            def _(block=block):
+                tot8[...] = combine(stats, block, blocks)
+
+        cols = columns_of(tot8[...]) * (1.0 / FF)
+        mean = cols[:, 0:1]
+        inverse = lax.rsqrt(cols[:, 1:2] - mean * mean + eps)
+        for at in range(0, units, 256):
+            c = slice(at, at + 256)
+            hat = (act[:, c].astype(F32) - mean) * inverse
+            low[:, c] = rounded(hat * g[:, c] + b[:, c])
+
+    row = lambda k: (k, 0)
+    return run(
+        kernel,
+        (blocks,),
+        [(active, (SLOT, units), row)] + [whole(part) for part in sums] + [whole(gain), whole(shift)],
+        [((rows, units), BF16, (SLOT, units), row)],
+        scratch=[pltpu.VMEM((8, SLOT), F32)],
+        name="hidden_low",
+    )[0]
 
 
 def hidden_mid(chunk, active, slope, back, sums, gain, shift):
@@ -1130,7 +1164,12 @@
         else:
             twos[0]["total"].advance()
             line.mark(*line.last, *twos[c]["sums"][1:])
-        mid_of(c)
+        if c == chunks - 1 and c > 0:
+            two = twos[c]
+            two["low"] = hidden_low(line.tie(two["active"]), two["sums"], hid_gain, hid_shift)
+            line.mark(two["low"])
+        else:
+            mid_of(c)
         if c > 0:
             line.mark(*line.last, *twos[0]["total"].got)
         if c == 0 and chunks > 1:
@@ -1138,6 +1177,10 @@
     lows = every(twos, "low")
     down_grad = full([(lows, cots)])
     down_part = lax.psum_scatter(down_grad, "dp", scatter_dimension=1, tiled=True)
+    if chunks > 1:
+        low = twos[-1]["low"]
+        mid_of(chunks - 1)
+        twos[-1]["low"] = low
     up_products = [(every(twos, "second"), every(twos, "grad"))]
     sent = ring_grads(other_ids, tied(up_products))[0]
     line.mark(sent)

time: 726 us -> 727 us (level)
    pallas_call x25 -> x26, Pallas kernels: 290 us -> 294 us  [run(): pl.pallas_call(body, grid_spec=pltpu.PrefetchScalarGridSpec(num_scalar_pr...]
  transfers between devices with their start and end apart: 70 -> 70, of which waited for: 30 -> 32; matrix products, arithmetic and copies ran while one was open for 5% -> 5% of each run, Pallas kernels for 36% -> 36%
where the time goes in v12:
time: 727 us; the launch traced here: 717 us
  Pallas kernels  294 us (40%)
  waiting for transfers between devices  279 us (38%)
  starting transfers between devices  74.7 us (10%)
  other arithmetic  26.8 us (4%)
  local copies, waits for them, and re-layouts  25.6 us (4%)
  between operations  17.2 us (2%)
    pallas_call x26, Pallas kernels, run(): pl.pallas_call(body, grid_spec=pltpu.PrefetchScalarGridSpec(num_scalar_pr...  294 us
    ppermute x54, waiting for transfers between devices, flip(): lax.ppermute(value, 'tensor', [(t, t ^ 1 << bit) for t in range(size)])  262 us
    ppermute x54, starting transfers between devices, flip(): lax.ppermute(value, 'tensor', [(t, t ^ 1 << bit) for t in range(size)])  58.7 us
  transfers between devices with their start and end apart: 70, of which 32 were waited for; matrix products, arithmetic and copies ran while one was open for 5% of the time, Pallas kernels for 36%

profile of v12, /device:TPU:0, one launch (start us, length us, event | category | flops | bytes accessed | tf_op | source)
XLA Modules:
  0.0 717.2 jit_solution(1062073277187659924)
XLA Ops:
  10.7 15.7 %front.2 = (bf16[512,2048]{1,0:T(8,128)(2,1)}, bf16[512,2048]{1,0:T(8,128)(2,1)}, bf16[512,1536]{1,0:T(8,128)(2,1)}, f32[512,512]{1,0:T(8,128)}, f32[16,512]{1,0...) custom-call(s32[4]{0:T(128)} %get-tuple-element.397.refs_0_, ...), custom_call_target="tpu_custom_call" | custom-call | flops 858000000 | bytes 1000 | tf_op jit(solution)/shard_map/front/pallas_call | solution.py:134
  31.5 15.9 %front.3 = (bf16[512,2048]{1,0:T(8,128)(2,1)}, bf16[512,2048]{1,0:T(8,128)(2,1)}, bf16[512,1536]{1,0:T(8,128)(2,1)}, f32[512,512]{1,0:T(8,128)}, f32[16,512]{1,0...) custom-call(s32[4]{0:T(128)} %get-tuple-element.398.refs_0_, ...), custom_call_target="tpu_custom_call" | custom-call | flops 858000000 | bytes 1000 | tf_op jit(solution)/shard_map/front/pallas_call | solution.py:134
  78.1 13.5 %hidden_back.1.refs_3_.refs_2_ = bf16[1024,2048]{1,0:T(8,128)(2,1)} custom-call(bf16[512,2048]{1,0:T(8,128)(2,1)} %bitcast.105, bf16[512,2048]{1,0:T(8,128)(2,1)} %bitcast.102, bf16[2048,2048]{1,0:T(8,128)(2,1)} %refs_3_.1), custom_call_target="tpu_custom_call" | custom-call | flops 22000001024 | bytes 1000 | tf_op jit(solution)/shard_map/hidden_back/pallas_call | solution.py:134
  108.9 20.5 %collective-permute-done.11 = f32[2,16,512]{2,1,0:T(8,128)S(1)} collective-permute-done((f32[2,16,512]{2,1,0:T(8,128)S(1)}, f32[2,16,512]{2,1,0:T(8,128)S(1)}, u32[]{:S(2)}, u32[]{:S(2)}) %collective-permute-start.11) | collective-permute-done | bytes 65568 | tf_op jit(solution)/shard_map/ppermute | solution.py:154
  145.8 13.6 %hidden_front.2 = (bf16[512,2048]{1,0:T(8,128)(2,1)}, bf16[512,2048]{1,0:T(8,128)(2,1)}, f32[8,512]{1,0:T(8,128)}) custom-call(bf16[512,2048]{1,0:T(8,128)(2,1)} %get-tuple-element.262.refs_0_.refs_1_, bf16[2048,2048]{1,0:T(8,128)(2,1)} %refs_1_.13, f32[1,2048]{1,0:T(1,128)} %bitcast.130, bf16[1024,2048]{1,0:T(8,128)(2,1)} %hidden_back.1.refs_3_.refs_2_, ...), custom_call_target="tpu_custom_call" | custom-call | flops 808499968 | bytes 1000 | tf_op jit(solution)/shard_map/hidden_front/pallas_call | solution.py:134
  194.6 13.8 %hidden_front.3 = (bf16[512,2048]{1,0:T(8,128)(2,1)}, bf16[512,2048]{1,0:T(8,128)(2,1)}, f32[8,512]{1,0:T(8,128)}) custom-call(bf16[512,2048]{1,0:T(8,128)(2,1)} %get-tuple-element.240.refs_0_.refs_2_, bf16[2048,2048]{1,0:T(8,128)(2,1)} %refs_1_.13, f32[1,2048]{1,0:T(1,128)} %bitcast.131, bf16[1024,2048]{1,0:T(8,128)(2,1)} %hidden_back.1.refs_3_.refs_2_, ...), custom_call_target="tpu_custom_call" | custom-call | flops 808499968 | bytes 1000 | tf_op jit(solution)/shard_map/hidden_front/pallas_call | solution.py:134
  222.0 14.1 %full_grad.2 = f32[2048,2048]{1,0:T(8,128)} custom-call(bf16[512,2048]{1,0:T(8,128)(2,1)} %get-tuple-element.266.refs_0_.refs_1_, bf16[512,2048]{1,0:T(8,128)(2,1)} %hidden_low.1.refs_1_.refs_2_, bf16[512,2048]{1,0:T(8,128)(2,1)} %bitcast.106, bf16[512,2048]{1,0:T(8,128)(2,1)} %bitcast.103), custom_call_target="tpu_custom_call" | custom-call | flops 825000000 | bytes 1000 | tf_op jit(solution)/shard_map/full_grad/pallas_call | solution.py:134
  244.4 9.8 %ring_grads.2 = f32[4,256,2048]{2,1,0:T(8,128)} custom-call(s32[4]{0:T(128)} %add_subtract_fusion.refs_0_, bf16[512,2048]{1,0:T(8,128)(2,1)} %get-tuple-element.262.refs_0_.refs_1_, bf16[512,2048]{1,0:T(8,128)(2,1)} %get-tuple-element.240.refs_0_.refs_2_, bf16[512,2048]{1,0:T(8,128)(2,1)} %get-tuple-element.233.refs_0_.refs_3_, ...), custom_call_target="tpu_custom_call" | custom-call | flops 660000000 | bytes 1000 | tf_op jit(solution)/shard_map/ring_grads/pallas_call | solution.py:134
  258.6 9.8 %hidden_grad.3 = (f32[2,128,1024]{2,1,0:T(8,128)}, f32[2,128,1024]{2,1,0:T(8,128)}, f32[2,128,1024]{2,1,0:T(8,128)}, f32[2,128,1024]{2,1,0:T(8,128)}) custom-call(bf16[512,2048]{1,0:T(8,128)(2,1)} %get-tuple-element.260.refs_4_.refs_0_, bf16[2048,2048]{1,0:T(8,128)(2,1)} %refs_1_.13), custom_call_target="tpu_custom_call" | custom-call | flops 385000000 | bytes 1000 | tf_op jit(solution)/shard_map/hidden_grad/pallas_call | solution.py:134
  268.4 12.9 %ring_grads.3 = (f32[256,2048]{1,0:T(8,128)}, f32[3,256,2048]{2,1,0:T(8,128)}) custom-call(s32[4]{0:T(128)} %broadcast_add_fusion.refs_0_, bf16[512,2048]{1,0:T(8,128)(2,1)} %get-tuple-element.262.refs_0_.refs_1_, bf16[512,2048]{1,0:T(8,128)(2,1)} %get-tuple-element.240.refs_0_.refs_2_, bf16[512,2048]{1,0:T(8,128)(2,1)} %get-tuple-element.233.refs_0_.refs_3_, ...), custom_call_target="tpu_custom_call" | custom-call | flops 660000000 | bytes 1000 | tf_op jit(solution)/shard_map/ring_grads/pallas_call | solution.py:134
  287.1 15.9 %result_part.1 = f32[8,128,2048]{2,1,0:T(8,128)} custom-call(s32[8]{0:T(128)} %pad_add_fusion.refs_0_, bf16[512,2048]{1,0:T(8,128)(2,1)} %get-tuple-element.266.refs_0_.refs_1_, bf16[512,2048]{1,0:T(8,128)(2,1)} %hidden_low.1.refs_1_.refs_2_, bf16[2048,2048]{1,0:T(8,128)(2,1)} %refs_3_.1), custom_call_target="tpu_custom_call" | custom-call | flops 22000001024 | bytes 1000 | tf_op jit(solution)/shard_map/result_part/pallas_call | solution.py:134
  308.8 11.0 %middle_back.2 = (f32[512,2048]{1,0:T(8,128)}, bf16[512,2048]{1,0:T(8,128)(2,1)}, f32[512,128]{1,0:T(8,128)}, f32[4,8,2048]{2,1,0:T(8,128)}) custom-call(bf16[512,2048]{1,0:T(8,128)(2,1)} %get-tuple-element.337.refs_0_.refs_6_.refs_1_, bf16[512,2048]{1,0:T(8,128)(2,1)} %bitcast.107, f32[2,128,1024]{2,1,0:T(8,128)} %copy-done, ...), custom_call_target="tpu_custom_call" | custom-call | flops 605000000 | bytes 1000 | tf_op jit(solution)/shard_map/middle_back/pallas_call | solution.py:134
  319.8 10.2 %collective-permute-done.35 = f32[2,128,1024]{2,1,0:T(8,128)S(1)} collective-permute-done((f32[2,128,1024]{2,1,0:T(8,128)}, f32[2,128,1024]{2,1,0:T(8,128)S(1)}, u32[]{:S(2)}, u32[]{:S(2)}) %collective-permute-start.35) | collective-permute-done | bytes 1048608 | tf_op jit(solution)/shard_map/ppermute | solution.py:154
  334.1 21.4 %attention_back.2 = (bf16[512,512]{1,0:T(8,128)(2,1)}, bf16[512,1536]{1,0:T(8,128)(2,1)}, f32[2,8,1536]{2,1,0:T(8,128)}, f32[2,8,2048]{2,1,0:T(8,128)}, f32[2,12...) custom-call(s32[4]{0:T(128)} %get-tuple-element.397.refs_0_, ...), custom_call_target="tpu_custom_call" | custom-call | flops 1193500032 | bytes 1000 | tf_op jit(solution)/shard_map/attention_back/pallas_call | solution.py:134
  358.3 10.0 %collective-permute-done.39 = f32[1,128,1024]{2,1,0:T(8,128)S(1)} collective-permute-done((f32[1,128,1024]{2,1,0:T(8,128)S(1)}, f32[1,128,1024]{2,1,0:T(8,128)S(1)}, u32[]{:S(2)}, u32[]{:S(2)}) %collective-permute-start.39) | collective-permute-done | bytes 524320 | tf_op jit(solution)/shard_map/ppermute | solution.py:154
  370.9 21.3 %collective-permute-done.42.refs_5_ = f32[2,128,1024]{2,1,0:T(8,128)S(1)} collective-permute-done((f32[2,128,1024]{2,1,0:T(8,128)S(1)}, f32[2,128,1024]{2,1,0:T(8,128)S(1)}, u32[]{:S(2)}, u32[]{:S(2)}) %collective-permute-start.42) | collective-permute-done | bytes 1048608 | tf_op jit(solution)/shard_map/ppermute | solution.py:154
  399.6 11.1 %middle_back.3 = (f32[512,2048]{1,0:T(8,128)}, bf16[512,2048]{1,0:T(8,128)(2,1)}, f32[512,128]{1,0:T(8,128)}, f32[4,8,2048]{2,1,0:T(8,128)}) custom-call(bf16[512,2048]{1,0:T(8,128)(2,1)} %get-tuple-element.344.refs_0_.refs_6_.refs_1_, bf16[512,2048]{1,0:T(8,128)(2,1)} %bitcast.104, f32[2,128,1024]{2,1,0:T(8,128)} %copy-done.2, f32[2,128,1024]{2,1,0:T(8,128)} %copy-done.24, ...), custom_call_target="tpu_custom_call" | custom-call | flops 605000000 | bytes 1000 | tf_op jit(solution)/shard_map/middle_back/pallas_call | solution.py:134
  410.8 21.8 %attention_back.3 = (bf16[512,512]{1,0:T(8,128)(2,1)}, bf16[512,1536]{1,0:T(8,128)(2,1)}, f32[2,8,1536]{2,1,0:T(8,128)}, f32[2,8,2048]{2,1,0:T(8,128)}, f32[2,12...) custom-call(s32[4]{0:T(128)} %get-tuple-element.398.refs_0_, ...), custom_call_target="tpu_custom_call" | custom-call | flops 1193500032 | bytes 1000 | tf_op jit(solution)/shard_map/attention_back/pallas_call | solution.py:134
  438.2 16.1 %full_grad.3 = f32[2048,2048]{1,0:T(8,128)} custom-call(bf16[512,2048]{1,0:T(8,128)(2,1)} %get-tuple-element.313.refs_0_, bf16[512,2048]{1,0:T(8,128)(2,1)} %get-tuple-element.314.refs_1_, bf16[512,1536]{1,0:T(8,128)(2,1)} %get-tuple-element.315.refs_2_, bf16[512,1536]{1,0:T(8,128)(2,1)} %get-tuple-element.316.refs_3_, ...), custom_call_target="tpu_custom_call" | custom-call | flops 825000000 | bytes 1000 | tf_op jit(solution)/shard_map/full_grad/pallas_call | solution.py:134
  464.4 54.1 %collective-permute-done.46 = f32[1,128,1024]{2,1,0:T(8,128)S(1)} collective-permute-done((f32[1,128,1024]{2,1,0:T(8,128)S(1)}, f32[1,128,1024]{2,1,0:T(8,128)S(1)}, u32[]{:S(2)}, u32[]{:S(2)}) %collective-permute-start.46) | collective-permute-done | bytes 524320 | tf_op jit(solution)/shard_map/ppermute | solution.py:154
  524.4 12.6 %collective-permute-done.50 = f32[1,128,1024]{2,1,0:T(8,128)S(1)} collective-permute-done((f32[1,128,1024]{2,1,0:T(8,128)S(1)}, f32[1,128,1024]{2,1,0:T(8,128)S(1)}, u32[]{:S(2)}, u32[]{:S(2)}) %collective-permute-start.50) | collective-permute-done | bytes 524320 | tf_op jit(solution)/shard_map/ppermute | solution.py:154
  546.1 10.8 %collective-permute-done.53 = f32[1,128,1024]{2,1,0:T(8,128)} collective-permute-done((f32[1,128,1024]{2,1,0:T(8,128)}, f32[1,128,1024]{2,1,0:T(8,128)}, u32[]{:S(2)}, u32[]{:S(2)}) %collective-permute-start.53) | collective-permute-done | bytes 524320 | tf_op jit(solution)/shard_map/ppermute | solution.py:154
  571.5 48.4 %collective-permute-done.57 = f32[1,128,1024]{2,1,0:T(8,128)S(1)} collective-permute-done((f32[1,128,1024]{2,1,0:T(8,128)S(1)}, f32[1,128,1024]{2,1,0:T(8,128)S(1)}, u32[]{:S(2)}, u32[]{:S(2)}) %collective-permute-start.57) | collective-permute-done | bytes 524320 | tf_op jit(solution)/shard_map/ppermute | solution.py:154
  642.6 24.8 %collective-permute-done.64.refs_6_ = f32[2,128,1024]{2,1,0:T(8,128)S(1)} collective-permute-done((f32[2,128,1024]{2,1,0:T(8,128)S(1)}, f32[2,128,1024]{2,1,0:T(8,128)S(1)}, u32[]{:S(2)}, u32[]{:S(2)}) %collective-permute-start.64) | collective-permute-done | bytes 1048608 | tf_op jit(solution)/shard_map/ppermute | solution.py:154
  (386 shorter events, 271.0 us)
Async XLA Ops:
  8.0 529.1 %reduce-scatter.3.cloned.1.call-start = ((), (), s32[]{:S(2)}) async-start(), calls=%async_computation.2 | async-start | bytes 18874368 | tf_op jit(solution)/shard_map/reduce_scatter | solution.py:1179
  58.9 34.3 %collective-permute-start.6 = (f32[2,128,1024]{2,1,0:T(8,128)}, f32[2,128,1024]{2,1,0:T(8,128)S(1)}, u32[]{:S(2)}, u32[]{:S(2)}) collective-permute-start(f32[2,128,1024]{2,1,0:T(8,128)} %get-tuple-element.210), channel_id=1, source_target_pairs={{0,1},{1,0},{2,3},{3,2},{4,5},{5,4},{6,7},{7,6},{8,9},{9,8},{10,11... | collective-permute-start | bytes 3145736 | tf_op jit(solution)/shard_map/ppermute | solution.py:154
  59.4 36.2 %collective-permute-start.7 = (f32[2,128,1024]{2,1,0:T(8,128)}, f32[2,128,1024]{2,1,0:T(8,128)S(1)}, u32[]{:S(2)}, u32[]{:S(2)}) collective-permute-start(f32[2,128,1024]{2,1,0:T(8,128)} %get-tuple-element.213), channel_id=1, source_target_pairs={{0,2},{1,3},{2,0},{3,1},{4,6},{5,7},{6,4},{7,5},{8,10},{9,11},{10,... | collective-permute-start | bytes 3145736 | tf_op jit(solution)/shard_map/ppermute | solution.py:154
  76.0 29.4 %collective-permute-start.10 = (f32[1,128,1024]{2,1,0:T(8,128)S(1)}, f32[1,128,1024]{2,1,0:T(8,128)S(1)}, u32[]{:S(2)}, u32[]{:S(2)}) collective-permute-start(f32[1,128,1024]{2,1,0:T(8,128)S(1)} %add.313), channel_id=1, source_target_pairs={{0,1},{1,0},{2,3},{3,2},{4,5},{5,4},{6,7},{7,6},{8,9},{9,8},{10,11... | collective-permute-start | bytes 1572872 | tf_op jit(solution)/shard_map/ppermute | solution.py:154
  236.2 448.4 %all-reduce.3.cloned.1.call-start = ((), (), s32[]{:S(2)}) async-start(), calls=%async_computation.3 | async-start | bytes 16777216 | tf_op jit(solution)/shard_map/psum | solution.py:1236
  284.0 46.0 %collective-permute-start.35 = (f32[2,128,1024]{2,1,0:T(8,128)}, f32[2,128,1024]{2,1,0:T(8,128)S(1)}, u32[]{:S(2)}, u32[]{:S(2)}) collective-permute-start(f32[2,128,1024]{2,1,0:T(8,128)} %get-tuple-element.275), channel_id=1, source_target_pairs={{0,1},{1,0},{2,3},{3,2},{4,5},{5,4},{6,7},{7,6},{8,9},{9,8},{10,11... | collective-permute-start | bytes 3145736 | tf_op jit(solution)/shard_map/ppermute | solution.py:154
  284.6 45.4 %collective-permute-start.36 = (f32[2,128,1024]{2,1,0:T(8,128)}, f32[2,128,1024]{2,1,0:T(8,128)}, u32[]{:S(2)}, u32[]{:S(2)}) collective-permute-start(f32[2,128,1024]{2,1,0:T(8,128)} %get-tuple-element.278), channel_id=1, source_target_pairs={{0,2},{1,3},{2,0},{3,1},{4,6},{5,7},{6,4},{7,5},{8,10},{9,11},{10,... | collective-permute-start | bytes 3145736 | tf_op jit(solution)/shard_map/ppermute | solution.py:154
  285.6 108.0 %collective-permute-start.43 = (f32[256,2048]{1,0:T(8,128)}, f32[256,2048]{1,0:T(8,128)}, u32[]{:S(2)}, u32[]{:S(2)}) collective-permute-start(f32[256,2048]{1,0:T(8,128)} %get-tuple-element.291), channel_id=1, source_target_pairs={{0,8},{4,12},{8,16},{12,20},{16,24},{20,28},{24,0},{28,4},{1,9},{5... | collective-permute-start | bytes 6291464 | tf_op jit(solution)/shard_map/ppermute | solution.py:242
  397.6 308.6 %reduce-scatter.5.cloned.1.call-start = ((), (), s32[]{:S(2)}) async-start(), calls=%async_computation.4 | async-start | bytes 18874368 | tf_op jit(solution)/shard_map/reduce_scatter | solution.py:1254
  397.7 39.8 %collective-permute-start.44 = (f32[2,128,1024]{2,1,0:T(8,128)}, f32[2,128,1024]{2,1,0:T(8,128)S(1)}, u32[]{:S(2)}, u32[]{:S(2)}) collective-permute-start(f32[2,128,1024]{2,1,0:T(8,128)} %get-tuple-element.310), channel_id=1, source_target_pairs={{0,1},{1,0},{2,3},{3,2},{4,5},{5,4},{6,7},{7,6},{8,9},{9,8},{10,11... | collective-permute-start | bytes 3145736 | tf_op jit(solution)/shard_map/ppermute | solution.py:154
  398.3 39.9 %collective-permute-start.45 = (f32[2,128,1024]{2,1,0:T(8,128)}, f32[2,128,1024]{2,1,0:T(8,128)S(1)}, u32[]{:S(2)}, u32[]{:S(2)}) collective-permute-start(f32[2,128,1024]{2,1,0:T(8,128)} %get-tuple-element.312), channel_id=1, source_target_pairs={{0,2},{1,3},{2,0},{3,1},{4,6},{5,7},{6,4},{7,5},{8,10},{9,11},{10,... | collective-permute-start | bytes 3145736 | tf_op jit(solution)/shard_map/ppermute | solution.py:154
  456.6 82.7 %collective-permute-start.52 = (f32[256,2048]{1,0:T(8,128)}, f32[256,2048]{1,0:T(8,128)}, u32[]{:S(2)}, u32[]{:S(2)}) collective-permute-start(f32[256,2048]{1,0:T(8,128)} %bitcast_add_fusion.2), channel_id=1, source_target_pairs={{0,8},{4,12},{8,16},{12,20},{16,24},{20,28},{24,0},{28,4},{1,9},{5... | collective-permute-start | bytes 6291464 | tf_op jit(solution)/shard_map/ppermute | solution.py:242
  458.7 62.5 %collective-permute-start.48 = (f32[2,128,1024]{2,1,0:T(8,128)}, f32[2,128,1024]{2,1,0:T(8,128)S(1)}, u32[]{:S(2)}, u32[]{:S(2)}) collective-permute-start(f32[2,128,1024]{2,1,0:T(8,128)} %get-tuple-element.326), channel_id=1, source_target_pairs={{0,1},{1,0},{2,3},{3,2},{4,5},{5,4},{6,7},{7,6},{8,9},{9,8},{10,11... | collective-permute-start | bytes 3145736 | tf_op jit(solution)/shard_map/ppermute | solution.py:154
  460.4 62.9 %collective-permute-start.49 = (f32[2,128,1024]{2,1,0:T(8,128)}, f32[2,128,1024]{2,1,0:T(8,128)S(1)}, u32[]{:S(2)}, u32[]{:S(2)}) collective-permute-start(f32[2,128,1024]{2,1,0:T(8,128)} %get-tuple-element.328), channel_id=1, source_target_pairs={{0,2},{1,3},{2,0},{3,1},{4,6},{5,7},{6,4},{7,5},{8,10},{9,11},{10,... | collective-permute-start | bytes 3145736 | tf_op jit(solution)/shard_map/ppermute | solution.py:154
  462.3 57.9 %collective-permute-start.47 = (f32[1,128,1024]{2,1,0:T(8,128)S(1)}, f32[1,128,1024]{2,1,0:T(8,128)S(1)}, u32[]{:S(2)}, u32[]{:S(2)}) collective-permute-start(f32[1,128,1024]{2,1,0:T(8,128)S(1)} %slice_add_fusion.6), channel_id=1, source_target_pairs={{0,1},{1,0},{2,3},{3,2},{4,5},{5,4},{6,7},{7,6},{8,9},{9,8},{10,11... | collective-permute-start | bytes 1572872 | tf_op jit(solution)/shard_map/ppermute | solution.py:154
  462.9 55.6 %collective-permute-start.46 = (f32[1,128,1024]{2,1,0:T(8,128)S(1)}, f32[1,128,1024]{2,1,0:T(8,128)S(1)}, u32[]{:S(2)}, u32[]{:S(2)}) collective-permute-start(f32[1,128,1024]{2,1,0:T(8,128)S(1)} %slice_add_fusion.7), channel_id=1, source_target_pairs={{0,2},{1,3},{2,0},{3,1},{4,6},{5,7},{6,4},{7,5},{8,10},{9,11},{10,... | collective-permute-start | bytes 1572872 | tf_op jit(solution)/shard_map/ppermute | solution.py:154
  522.0 34.9 %collective-permute-start.53 = (f32[1,128,1024]{2,1,0:T(8,128)}, f32[1,128,1024]{2,1,0:T(8,128)}, u32[]{:S(2)}, u32[]{:S(2)}) collective-permute-start(f32[1,128,1024]{2,1,0:T(8,128)} %slice_add_fusion.3), channel_id=1, source_target_pairs={{0,2},{1,3},{2,0},{3,1},{4,6},{5,7},{6,4},{7,5},{8,10},{9,11},{10,... | collective-permute-start | bytes 1572872 | tf_op jit(solution)/shard_map/ppermute | solution.py:154
  542.1 92.7 %collective-permute-start.61 = (f32[256,2048]{1,0:T(8,128)S(1)}, f32[256,2048]{1,0:T(8,128)S(1)}, u32[]{:S(2)}, u32[]{:S(2)}) collective-permute-start(f32[256,2048]{1,0:T(8,128)S(1)} %bitcast_add_fusion.1), channel_id=1, source_target_pairs={{0,8},{4,12},{8,16},{12,20},{16,24},{20,28},{24,0},{28,4},{1,9},{5... | collective-permute-start | bytes 6291464 | tf_op jit(solution)/shard_map/ppermute | solution.py:242
  545.3 74.8 %collective-permute-start.59 = (f32[2,128,1024]{2,1,0:T(8,128)S(1)}, f32[2,128,1024]{2,1,0:T(8,128)S(1)}, u32[]{:S(2)}, u32[]{:S(2)}) collective-permute-start(f32[2,128,1024]{2,1,0:T(8,128)S(1)} %constant_dynamic-update-slice_fusion.18.refs_5_), channel_id=1, source_target_pairs={{0,2},{1,3},{2,0},{3,1},{4,6},{5,7},{6,4},{7,5},{8,10},{9,11},{10,... | collective-permute-start | bytes 3145736 | tf_op jit(solution)/shard_map/ppermute | solution.py:154
  556.9 63.2 %collective-permute-start.58 = (f32[2,128,1024]{2,1,0:T(8,128)S(1)}, f32[2,128,1024]{2,1,0:T(8,128)S(1)}, u32[]{:S(2)}, u32[]{:S(2)}) collective-permute-start(f32[2,128,1024]{2,1,0:T(8,128)S(1)} %constant_dynamic-update-slice_fusion.16.refs_3_), channel_id=1, source_target_pairs={{0,1},{1,0},{2,3},{3,2},{4,5},{5,4},{6,7},{7,6},{8,9},{9,8},{10,11... | collective-permute-start | bytes 3145736 | tf_op jit(solution)/shard_map/ppermute | solution.py:154
  569.2 50.9 %collective-permute-start.56 = (f32[1,128,1024]{2,1,0:T(8,128)S(1)}, f32[1,128,1024]{2,1,0:T(8,128)S(1)}, u32[]{:S(2)}, u32[]{:S(2)}) collective-permute-start(f32[1,128,1024]{2,1,0:T(8,128)S(1)} %add.370), channel_id=1, source_target_pairs={{0,2},{1,3},{2,0},{3,1},{4,6},{5,7},{6,4},{7,5},{8,10},{9,11},{10,... | collective-permute-start | bytes 1572872 | tf_op jit(solution)/shard_map/ppermute | solution.py:154
  570.1 49.9 %collective-permute-start.57 = (f32[1,128,1024]{2,1,0:T(8,128)S(1)}, f32[1,128,1024]{2,1,0:T(8,128)S(1)}, u32[]{:S(2)}, u32[]{:S(2)}) collective-permute-start(f32[1,128,1024]{2,1,0:T(8,128)S(1)} %add.371), channel_id=1, source_target_pairs={{0,1},{1,0},{2,3},{3,2},{4,5},{5,4},{6,7},{7,6},{8,9},{9,8},{10,11... | collective-permute-start | bytes 1572872 | tf_op jit(solution)/shard_map/ppermute | solution.py:154
  640.3 31.3 %collective-permute-start.63 = (f32[2,128,1024]{2,1,0:T(8,128)S(1)}, f32[2,128,1024]{2,1,0:T(8,128)S(1)}, u32[]{:S(2)}, u32[]{:S(2)}) collective-permute-start(f32[2,128,1024]{2,1,0:T(8,128)S(1)} %constant_dynamic-update-slice_fusion.20.refs_3_), channel_id=1, source_target_pairs={{0,1},{1,0},{2,3},{3,2},{4,5},{5,4},{6,7},{7,6},{8,9},{9,8},{10,11... | collective-permute-start | bytes 3145736 | tf_op jit(solution)/shard_map/ppermute | solution.py:154
  641.8 39.5 %collective-permute-start.65 = (f32[12,2048]{1,0:T(8,128)S(1)}, f32[12,2048]{1,0:T(8,128)S(1)}, u32[]{:S(2)}, u32[]{:S(2)}) collective-permute-start(f32[12,2048]{1,0:T(8,128)S(1)} %add.375), channel_id=1, source_target_pairs={{0,8},{4,12},{8,0},{12,4},{16,24},{20,28},{24,16},{28,20},{1,9},{5... | collective-permute-start | bytes 294920 | tf_op jit(solution)/shard_map/ppermute | solution.py:1274
  (109 other events, 1656.8 us)
Sparse Core Ops, SparseCore 0:
  236.3 214.3 reduce-scatter.2
  454.4 251.7 reduce-scatter.4
Sparse Core Ops, SparseCore 1:
  397.7 266.6 all-reduce.2
